TPU v7x, 128 devices: a whole 4x4x4 slice. The times are simulated.
128 devices in a mesh: section: 2 (over z_lo), fsdp: 8 (over y, core), replica: 8 (over x, z_hi).
Axes of the slice: x: 4, y: 4, z: 4 (z_hi: 2, z_lo: 2; z = z_hi * 2 + z_lo), core: 2. Of those that a mesh axis runs over, the one named last changes fastest.
Arguments:
- inputs: bfloat16 [2, 8, 512, 1088], P(None, 'replica', 'fsdp'), may hold values from -6 to 6
- cotangent: bfloat16 [2, 8, 512, 1088], P(None, 'replica', 'fsdp'), may hold values from -6 to 6
- weight_attn: bfloat16 [2, 1088, 3264], P('section', 'fsdp'), may hold values from -0.1875 to 0.1875
- weight_out: bfloat16 [2, 1088, 1088], P('section', 'fsdp'), may hold values from -1.5 to 1.5
- weight_up: bfloat16 [2, 1088, 4352], P('section', 'fsdp'), may hold values from -0.1875 to 0.1875
- weight_down: bfloat16 [2, 4352, 1088], P('section', 'fsdp'), may hold values from -0.09375 to 0.09375
- bias_attn: bfloat16 [2, 2176], P('section', 'fsdp'), may hold values from -3 to 3
- bias_out: bfloat16 [2, 1088], P('section', 'fsdp'), may hold values from -2 to 2
- bias_up: bfloat16 [2, 4352], P('section', 'fsdp'), may hold values from -3 to 3
- bias_down: bfloat16 [2, 1088], P('section', 'fsdp'), may hold values from -2 to 2
- norm_gain: bfloat16 [2, 2, 1088], P('section', None, 'fsdp'), may hold values from 0.5 to 1.5
- norm_bias: bfloat16 [2, 2, 1088], P('section', None, 'fsdp'), may hold values from -1.5 to 1.5
Outputs:
- acts: bfloat16 [2, 2, 8, 512, 1088], P('section', None, 'replica', 'fsdp')
- in_grads: bfloat16 [2, 2, 8, 512, 1088], P('section', None, 'replica', 'fsdp')
- grad_attn: float32 [2, 1088, 3264], P('section', 'fsdp')
- grad_out: float32 [2, 1088, 1088], P('section', 'fsdp')
- grad_up: float32 [2, 1088, 4352], P('section', 'fsdp')
- grad_down: float32 [2, 4352, 1088], P('section', 'fsdp')
- grad_bias_attn: float32 [2, 2176], P('section', 'fsdp')
- grad_bias_out: float32 [2, 1088], P('section', 'fsdp')
- grad_bias_up: float32 [2, 4352], P('section', 'fsdp')
- grad_bias_down: float32 [2, 1088], P('section', 'fsdp')
- grad_gain: float32 [2, 2, 1088], P('section', None, 'fsdp')
- grad_shift: float32 [2, 2, 1088], P('section', None, 'fsdp')
All inputs are finite; a program needn't handle non-finite values.
Results may differ from a plain program's by a relative error of at most 0.02.
Values may be sent and summed in bfloat16 or wider, within the bound.
A program may use at most 192 MiB of HBM per device.

v0:
```python
import jax
import jax.numpy as jnp
from jax import lax
from jax.sharding import PartitionSpec as P

HEAD_DIM = 64


norm_epsilon = 1e-05


def from_behind(block, axis, distance):
    devices = range(lax.axis_size(axis))
    route = [(i - distance, i) for i in devices if i - distance in devices]
    return lax.ppermute(block, axis, route)


def norm_rows(values, gain_row, shift_row):
    centre = values - jnp.mean(values, axis=-1, keepdims=True)
    spread = jnp.mean(centre * centre, axis=-1, keepdims=True)
    return centre * lax.rsqrt(spread + norm_epsilon) * gain_row + shift_row


def smooth_gate(values):
    return jax.nn.gelu(values, approximate=True)


def product(left_side, right_side):
    return jnp.dot(left_side, right_side, preferred_element_type=jnp.float32)


def product_left(left_side, right_side):
    return lax.dot_general(
        left_side, right_side, (((0,), (0,)), ((), ())), preferred_element_type=jnp.float32
    )


def product_right(left_side, right_side):
    return lax.dot_general(
        left_side, right_side, (((1,), (1,)), ((), ())), preferred_element_type=jnp.float32
    )


def soft_scores(queries, keys_full, first_row):
    row_count = queries.shape[0]
    length = keys_full.shape[0]
    scores = jnp.einsum(
        "qhd,khd->hqk", queries, keys_full, preferred_element_type=jnp.float32
    ) * HEAD_DIM ** (-0.5)
    causal = (first_row + jnp.arange(row_count))[:, None] >= jnp.arange(length)[None, :]
    return jnp.where(causal[None], scores, -1e30)


def forward_layer(layer_in, params, first_row):
    (
        weight_attn,
        weight_out,
        weight_up,
        weight_down,
        bias_attn,
        bias_out,
        bias_up,
        bias_down,
        gains_all,
        shifts_all,
    ) = params
    row_count = layer_in.shape[0]
    feature_count = layer_in.shape[1]
    head_count = feature_count // HEAD_DIM
    stream = layer_in.astype(jnp.float32)
    normed = norm_rows(stream, gains_all[0], shifts_all[0]).astype(jnp.bfloat16)
    bias_full = jnp.concatenate(
        [
            bias_attn[:feature_count].astype(jnp.float32),
            jnp.zeros((feature_count,), jnp.float32),
            bias_attn[feature_count:].astype(jnp.float32),
        ]
    )
    joined = (product(normed, weight_attn) + bias_full).astype(jnp.bfloat16)
    keys_full, values_full = (
        lax.all_gather(joined[:, feature_count : 2 * feature_count], "fsdp", axis=0, tiled=True),
        lax.all_gather(joined[:, 2 * feature_count :], "fsdp", axis=0, tiled=True),
    )
    length = keys_full.shape[0]
    queries = joined[:, :feature_count].reshape(row_count, head_count, HEAD_DIM)
    keys_full = keys_full.reshape(length, head_count, HEAD_DIM)
    values_full = values_full.reshape(length, head_count, HEAD_DIM)
    masked = soft_scores(queries, keys_full, first_row)
    row_max = jnp.max(masked, axis=-1, keepdims=True)
    row_total = jnp.sum(jnp.exp(masked - row_max), axis=-1, keepdims=True)
    logsum = row_max + jnp.log(row_total)
    attention = jnp.exp(masked - logsum).astype(jnp.bfloat16)
    attended = jnp.einsum(
        "hqk,khd->qhd", attention, values_full, preferred_element_type=jnp.float32
    )
    attended = attended.reshape(row_count, feature_count).astype(jnp.bfloat16)
    middle = stream + product(attended, weight_out) + bias_out
    normed_two = norm_rows(middle, gains_all[1], shifts_all[1]).astype(jnp.bfloat16)
    hidden_pre = product(normed_two, weight_up) + bias_up
    active = smooth_gate(hidden_pre).astype(jnp.bfloat16)
    result = middle + product(active, weight_down) + bias_down
    stored = (
        stream,
        normed,
        queries,
        keys_full,
        values_full,
        logsum,
        attended,
        middle,
        normed_two,
        hidden_pre,
        active,
    )
    return (result, stored)


def backward_layer(upstream, stored, params, first_row):
    (
        weight_attn,
        weight_out,
        weight_up,
        weight_down,
        bias_attn,
        bias_out,
        bias_up,
        bias_down,
        gains_all,
        shifts_all,
    ) = params
    (
        stream,
        normed,
        queries,
        keys_full,
        values_full,
        logsum,
        attended,
        middle,
        normed_two,
        hidden_pre,
        active,
    ) = stored
    row_count = queries.shape[0]
    length = keys_full.shape[0]
    feature_count = stream.shape[1]
    head_count = feature_count // HEAD_DIM
    grad_down_in = upstream.astype(jnp.bfloat16)
    grad_active = product_right(grad_down_in, weight_down)
    unused_value, gate_back = jax.vjp(smooth_gate, hidden_pre)
    grad_hidden = gate_back(grad_active)[0].astype(jnp.bfloat16)
    grad_normed_two = product_right(grad_hidden, weight_up)
    unused_value, norm_back_two = jax.vjp(
        norm_rows, middle, gains_all[1].astype(jnp.float32), shifts_all[1].astype(jnp.float32)
    )
    middle_part, gain_two, shift_two = norm_back_two(grad_normed_two)
    grad_middle = upstream + middle_part
    grad_branch = grad_middle.astype(jnp.bfloat16)
    grad_attended = (
        product_right(grad_branch, weight_out)
        .astype(jnp.bfloat16)
        .reshape(row_count, head_count, HEAD_DIM)
    )
    masked = soft_scores(queries, keys_full, first_row)
    probs_full = jnp.exp(masked - logsum)
    attention = probs_full.astype(jnp.bfloat16)
    grad_probs = jnp.einsum(
        "qhd,khd->hqk", grad_attended, values_full, preferred_element_type=jnp.float32
    )
    row_delta = jnp.sum(probs_full * grad_probs, axis=-1, keepdims=True)
    grad_scores = (probs_full * (grad_probs - row_delta)).astype(jnp.bfloat16)
    grad_queries = jnp.einsum(
        "hqk,khd->qhd", grad_scores, keys_full, preferred_element_type=jnp.float32
    ) * HEAD_DIM ** (-0.5)
    key_part = jnp.einsum(
        "hqk,qhd->khd", grad_scores, queries, preferred_element_type=jnp.float32
    ) * HEAD_DIM ** (-0.5)
    value_part = jnp.einsum(
        "hqk,qhd->khd", attention, grad_attended, preferred_element_type=jnp.float32
    )
    grad_keys, grad_values = (
        lax.psum_scatter(
            key_part.reshape(length, feature_count).astype(jnp.bfloat16),
            "fsdp",
            scatter_dimension=0,
            tiled=True,
        ).astype(jnp.float32),
        lax.psum_scatter(
            value_part.reshape(length, feature_count).astype(jnp.bfloat16),
            "fsdp",
            scatter_dimension=0,
            tiled=True,
        ).astype(jnp.float32),
    )
    grad_joined = jnp.concatenate(
        [
            grad_queries.reshape(row_count, feature_count).astype(jnp.bfloat16),
            grad_keys.astype(jnp.bfloat16),
            grad_values.astype(jnp.bfloat16),
        ],
        axis=1,
    )
    grad_normed = product_right(grad_joined, weight_attn)
    unused_value, norm_back_one = jax.vjp(
        norm_rows, stream, gains_all[0].astype(jnp.float32), shifts_all[0].astype(jnp.float32)
    )
    stream_part, gain_one, shift_one = norm_back_one(grad_normed)
    grad_stream = grad_middle + stream_part
    row_pieces = (
        normed,
        grad_joined,
        attended,
        grad_branch,
        normed_two,
        grad_hidden,
        active,
        grad_down_in,
    )
    small_pieces = (jnp.stack([gain_one, gain_two]), jnp.stack([shift_one, shift_two]))
    return (grad_stream, row_pieces, small_pieces)


def on_device(
    inputs,
    cotangent,
    weight_attn,
    weight_out,
    weight_up,
    weight_down,
    bias_attn,
    bias_out,
    bias_up,
    bias_down,
    norm_gain,
    norm_bias,
):
    section_pos = lax.axis_index("section")
    micro_count = inputs.shape[0]
    row_count = inputs.shape[2]
    feature_count = inputs.shape[3]
    first_row = lax.axis_index("fsdp") * row_count

    def obtain():
        return (
            lax.all_gather(weight_attn[0], "fsdp", axis=0, tiled=True),
            lax.all_gather(weight_out[0], "fsdp", axis=0, tiled=True),
            lax.all_gather(weight_up[0], "fsdp", axis=0, tiled=True),
            lax.all_gather(weight_down[0], "fsdp", axis=0, tiled=True),
            lax.all_gather(bias_attn[0], "fsdp", axis=0, tiled=True),
            lax.all_gather(bias_out[0], "fsdp", axis=0, tiled=True),
            lax.all_gather(bias_up[0], "fsdp", axis=0, tiled=True),
            lax.all_gather(bias_down[0], "fsdp", axis=0, tiled=True),
            lax.all_gather(norm_gain[0], "fsdp", axis=1, tiled=True),
            lax.all_gather(norm_bias[0], "fsdp", axis=1, tiled=True),
        )

    incoming = jnp.zeros((row_count, feature_count), jnp.bfloat16)
    sent_list = []
    stored_list = []
    for moment in range(micro_count + 1):
        own_rows = inputs[min(moment, micro_count - 1), 0]
        layer_in = jnp.where(section_pos == 0, own_rows, incoming)
        result, stored = forward_layer(layer_in, obtain(), first_row)
        sent_out = result.astype(jnp.bfloat16)
        sent_list.append(sent_out)
        stored_list.append(stored)
        if moment < micro_count:
            incoming = from_behind(sent_out, "section", 1)
    stored_stack = jax.tree.map(lambda *members: jnp.stack(members), *stored_list)
    returning = jnp.zeros((row_count, feature_count), jnp.bfloat16)
    back_list = []
    row_list = []
    small_list = []
    for moment in range(micro_count + 1):
        if moment < micro_count:
            own_grad = cotangent[moment, 0].astype(jnp.float32)
        else:
            own_grad = jnp.zeros((row_count, feature_count), jnp.float32)
        upstream = jnp.where(section_pos == 1, own_grad, returning.astype(jnp.float32))
        source = jnp.clip(moment - 1 + 2 * section_pos, 0, micro_count)
        stored = jax.tree.map(
            lambda stacked: lax.dynamic_index_in_dim(stacked, source, 0, keepdims=False),
            stored_stack,
        )
        grad_stream, row_pieces, small_pieces = backward_layer(
            upstream, stored, obtain(), first_row
        )
        sent_back = grad_stream.astype(jnp.bfloat16)
        back_list.append(sent_back)
        row_list.append(row_pieces)
        small_list.append(small_pieces)
        if moment < micro_count:
            returning = from_behind(sent_back, "section", -1)
    acts = lax.dynamic_slice_in_dim(jnp.stack(sent_list), section_pos, micro_count, 0)
    acts = acts.reshape(1, micro_count, 1, row_count, feature_count)
    in_grads = lax.dynamic_slice_in_dim(jnp.stack(back_list), 1 - section_pos, micro_count, 0)
    in_grads = in_grads.reshape(1, micro_count, 1, row_count, feature_count)
    joined_rows = jax.tree.map(lambda *members: jnp.concatenate(members, 0), *row_list)
    (
        normed_all,
        joined_all,
        attended_all,
        branch_all,
        normed_two_all,
        hidden_all,
        active_all,
        down_all,
    ) = joined_rows
    joined_sum = jnp.sum(joined_all, axis=0, dtype=jnp.float32)
    grad_bias_qv = jnp.concatenate([joined_sum[:feature_count], joined_sum[2 * feature_count :]])
    grad_bias_branch = jnp.sum(branch_all, axis=0, dtype=jnp.float32)
    grad_bias_hidden = jnp.sum(hidden_all, axis=0, dtype=jnp.float32)
    grad_bias_last = jnp.sum(down_all, axis=0, dtype=jnp.float32)
    grad_gains = sum((small[0] for small in small_list))
    grad_shifts = sum((small[1] for small in small_list))
    grad_weight_attn = product_left(normed_all, joined_all)
    grad_weight_out = product_left(attended_all, branch_all)
    grad_weight_up = product_left(normed_two_all, hidden_all)
    grad_weight_down = product_left(active_all, down_all)
    pieces = (
        lax.psum_scatter(
            grad_weight_attn.astype(jnp.bfloat16), "fsdp", scatter_dimension=0, tiled=True
        ).astype(jnp.float32),
        lax.psum_scatter(
            grad_weight_out.astype(jnp.bfloat16), "fsdp", scatter_dimension=0, tiled=True
        ).astype(jnp.float32),
        lax.psum_scatter(
            grad_weight_up.astype(jnp.bfloat16), "fsdp", scatter_dimension=0, tiled=True
        ).astype(jnp.float32),
        lax.psum_scatter(
            grad_weight_down.astype(jnp.bfloat16), "fsdp", scatter_dimension=0, tiled=True
        ).astype(jnp.float32),
        lax.psum_scatter(
            grad_bias_qv.astype(jnp.bfloat16), "fsdp", scatter_dimension=0, tiled=True
        ).astype(jnp.float32),
        lax.psum_scatter(
            grad_bias_branch.astype(jnp.bfloat16), "fsdp", scatter_dimension=0, tiled=True
        ).astype(jnp.float32),
        lax.psum_scatter(
            grad_bias_hidden.astype(jnp.bfloat16), "fsdp", scatter_dimension=0, tiled=True
        ).astype(jnp.float32),
        lax.psum_scatter(
            grad_bias_last.astype(jnp.bfloat16), "fsdp", scatter_dimension=0, tiled=True
        ).astype(jnp.float32),
        lax.psum_scatter(
            grad_gains.astype(jnp.bfloat16), "fsdp", scatter_dimension=1, tiled=True
        ).astype(jnp.float32),
        lax.psum_scatter(
            grad_shifts.astype(jnp.bfloat16), "fsdp", scatter_dimension=1, tiled=True
        ).astype(jnp.float32),
    )
    summed = (
        lax.psum(pieces[0].astype(jnp.bfloat16), "replica").astype(jnp.float32),
        lax.psum(pieces[1].astype(jnp.bfloat16), "replica").astype(jnp.float32),
        lax.psum(pieces[2].astype(jnp.bfloat16), "replica").astype(jnp.float32),
        lax.psum(pieces[3].astype(jnp.bfloat16), "replica").astype(jnp.float32),
        lax.psum(pieces[4].astype(jnp.bfloat16), "replica").astype(jnp.float32),
        lax.psum(pieces[5].astype(jnp.bfloat16), "replica").astype(jnp.float32),
        lax.psum(pieces[6].astype(jnp.bfloat16), "replica").astype(jnp.float32),
        lax.psum(pieces[7].astype(jnp.bfloat16), "replica").astype(jnp.float32),
        lax.psum(pieces[8].astype(jnp.bfloat16), "replica").astype(jnp.float32),
        lax.psum(pieces[9].astype(jnp.bfloat16), "replica").astype(jnp.float32),
    )
    return (
        acts,
        in_grads,
        summed[0][None],
        summed[1][None],
        summed[2][None],
        summed[3][None],
        summed[4][None],
        summed[5][None],
        summed[6][None],
        summed[7][None],
        summed[8][None],
        summed[9][None],
    )


def solution(mesh):
    placed = (
        P(None, "replica", "fsdp", None),
        P(None, "replica", "fsdp", None),
        P("section", "fsdp", None),
        P("section", "fsdp", None),
        P("section", "fsdp", None),
        P("section", "fsdp", None),
        P("section", "fsdp"),
        P("section", "fsdp"),
        P("section", "fsdp"),
        P("section", "fsdp"),
        P("section", None, "fsdp"),
        P("section", None, "fsdp"),
    )
    return jax.shard_map(
        on_device,
        mesh=mesh,
        in_specs=placed,
        out_specs=(
            P("section", None, "replica", "fsdp", None),
            P("section", None, "replica", "fsdp", None),
            P("section", "fsdp", None),
            P("section", "fsdp", None),
            P("section", "fsdp", None),
            P("section", "fsdp", None),
            P("section", "fsdp"),
            P("section", "fsdp"),
            P("section", "fsdp"),
            P("section", "fsdp"),
            P("section", None, "fsdp"),
            P("section", None, "fsdp"),
        ),
        check_vma=False,
    )
```

profile of v0, /device:TPU:4, one launch (start us, length us, event | category | flops | bytes accessed | tf_op | source)
XLA Modules:
  0.0 1175.8 jit_solution(7179058256435751385)
XLA Ops:
  15.0 27.4 %all-reduce.14 = (bf16[2176]{0:T(1024)(128)(2,1)S(1)}, bf16[1088]{0:T(1024)(128)(2,1)S(1)}, bf16[1088]{0:T(1024)(128)(2,1)S(1)}, bf16[4352]{0:T(1024)(128)(2,1)S(1)}) all-reduce(bf16[2176]{0:T(1024)(128)(2,1)S(1)} %dynamic-update-slice, ...), channel_id=5, replica_groups=mesh['section'=2,'fsdp'=8,'replica'=8] {'fsdp'}, use_global_device_ids=true, to_apply=%add | all-reduce | flops 8704 | bytes 34816
  44.2 14.2 %all-gather.1 = bf16[1,2,1088]{1,0,2:T(2,128)(2,1)S(1)} all-gather(bf16[1,2,136]{1,0,2:T(2,128)(2,1)S(1)} %copy.120), channel_id=3, replica_groups=mesh['section'=2,'fsdp'=8,'replica'=8] {'fsdp'}, dimensions={2}, use_global_device_ids=true | all-gather | bytes 4896 | tf_op jit(solution)/shard_map/all_gather | solution.py:254
  58.4 13.1 %all-gather = bf16[1,2,1088]{1,0,2:T(2,128)(2,1)S(1)} all-gather(bf16[1,2,136]{1,0,2:T(2,128)(2,1)S(1)} %copy.119), channel_id=2, replica_groups=mesh['section'=2,'fsdp'=8,'replica'=8] {'fsdp'}, dimensions={2}, use_global_device_ids=true | all-gather | bytes 4896 | tf_op jit(solution)/shard_map/all_gather | solution.py:253
  71.9 17.8 %fusion.258 = (f32[1088]{0:T(1024)S(1)}, f32[1088]{0:T(1024)S(1)}) fusion(bf16[1,2,1088]{1,0,2:T(2,128)(2,1)S(1)} %all-gather.1), kind=kLoop, calls=%fused_computation.254 | loop fusion | flops 2176 | bytes 13056 | tf_op jit(solution)/shard_map/add | solution.py:21
  89.8 18.1 %fusion.259 = (f32[1088]{0:T(1024)S(1)}, f32[1088]{0:T(1024)S(1)}) fusion(bf16[1,2,1088]{1,0,2:T(2,128)(2,1)S(1)} %all-gather), kind=kLoop, calls=%fused_computation.256 | loop fusion | flops 2176 | bytes 13056 | tf_op jit(solution)/shard_map/mul | solution.py:21
  108.0 4.3 fusion.60
  116.0 21.5 %all-gather.23.cloned.1.call-done = bf16[512,1088]{1,0:T(8,128)(2,1)} async-done(((bf16[64,1088]{1,0:T(8,128)(2,1)}), bf16[512,1088]{1,0:T(8,128)(2,1)}) %all-gather.23.cloned.1.call-update) | async-done | bytes 1114128 | tf_op jit(solution)/shard_map/all_gather | solution.py:81
  139.5 23.9 %all-gather.21.cloned.1.call-done = bf16[512,1088]{1,0:T(8,128)(2,1)} async-done(((bf16[64,1088]{1,0:T(8,128)(2,1)}), bf16[512,1088]{1,0:T(8,128)(2,1)}) %all-gather.21.cloned.1.call-update) | async-done | bytes 1114128 | tf_op jit(solution)/shard_map/all_gather | solution.py:82
  167.1 24.1 %all-gather.35.cloned.1.call-done = bf16[1,1088,1088]{2,1,0:T(8,128)(2,1)} async-done(((bf16[1,136,1088]{2,1,0:T(8,128)(2,1)}), bf16[1,1088,1088]{2,1,0:T(8,128)(2,1)}) %all-gather.35.cloned.1.call-update) | async-done | bytes 2367504 | tf_op jit(solution)/shard_map/all_gather | solution.py:246
  193.8 53.7 %all-gather.37.cloned.1.call-done = bf16[1,1088,4352]{2,1,0:T(8,128)(2,1)} async-done(((bf16[1,136,4352]{2,1,0:T(8,128)(2,1)}), bf16[1,1088,4352]{2,1,0:T(8,128)(2,1)}) %all-gather.37.cloned.1.call-update) | async-done | bytes 9469968 | tf_op jit(solution)/shard_map/all_gather | solution.py:247
  247.5 5.2 fusion.36
  252.8 53.1 %all-gather.39.cloned.1.call-done = bf16[1,4352,1088]{2,1,0:T(8,128)(2,1)} async-done(((bf16[1,544,1088]{2,1,0:T(8,128)(2,1)}), bf16[1,4352,1088]{2,1,0:T(8,128)(2,1)}) %all-gather.39.cloned.1.call-update) | async-done | bytes 9469968 | tf_op jit(solution)/shard_map/all_gather | solution.py:248
  305.9 5.7 fusion.117
  315.1 3.5 collective-permute-done
  319.8 4.3 fusion.57
  325.9 23.8 %all-gather.27.cloned.1.call-done = bf16[512,1088]{1,0:T(8,128)(2,1)} async-done(((bf16[64,1088]{1,0:T(8,128)(2,1)}), bf16[512,1088]{1,0:T(8,128)(2,1)}) %all-gather.27.cloned.1.call-update) | async-done | bytes 1114128 | tf_op jit(solution)/shard_map/all_gather | solution.py:81
  354.4 21.2 %all-gather.25.cloned.1.call-done = bf16[512,1088]{1,0:T(8,128)(2,1)} async-done(((bf16[64,1088]{1,0:T(8,128)(2,1)}), bf16[512,1088]{1,0:T(8,128)(2,1)}) %all-gather.25.cloned.1.call-update) | async-done | bytes 1114128 | tf_op jit(solution)/shard_map/all_gather | solution.py:82
  382.8 5.4 fusion.39
  404.0 20.3 %all-gather.31.cloned.1.call-done = bf16[512,1088]{1,0:T(8,128)(2,1)} async-done(((bf16[64,1088]{1,0:T(8,128)(2,1)}), bf16[512,1088]{1,0:T(8,128)(2,1)}) %all-gather.31.cloned.1.call-update) | async-done | bytes 1114128 | tf_op jit(solution)/shard_map/all_gather | solution.py:81
  428.9 20.7 %all-gather.29.cloned.1.call-done = bf16[512,1088]{1,0:T(8,128)(2,1)} async-done(((bf16[64,1088]{1,0:T(8,128)(2,1)}), bf16[512,1088]{1,0:T(8,128)(2,1)}) %all-gather.29.cloned.1.call-update) | async-done | bytes 1114128 | tf_op jit(solution)/shard_map/all_gather | solution.py:82
  460.1 5.4 fusion.42
  467.8 6.5 fusion.414
  474.4 4.9 multiply_reduce_fusion.7
  511.3 19.5 %reduce-scatter.35.cloned.1.call-done = bf16[64,1088]{1,0:T(8,128)(2,1)} async-done(((bf16[512,1088]{1,0:T(8,128)(2,1)}), bf16[64,1088]{1,0:T(8,128)(2,1)}) %reduce-scatter.35.cloned.1.call-update) | async-done | bytes 139280
  531.9 32.8 %reduce-scatter.33.cloned.1.call-done = bf16[64,1088]{1,0:T(8,128)(2,1)} async-done(((bf16[512,1088]{1,0:T(8,128)(2,1)}), bf16[64,1088]{1,0:T(8,128)(2,1)}) %reduce-scatter.33.cloned.1.call-update) | async-done | bytes 139280
  566.6 5.9 multiply_reduce_fusion.8
  576.1 5.7 collective-permute-done.2
  582.5 7.8 fusion.415
  590.4 3.7 multiply_reduce_fusion.5
  617.1 19.9 %reduce-scatter.39.cloned.1.call-done = bf16[64,1088]{1,0:T(8,128)(2,1)} async-done(((bf16[512,1088]{1,0:T(8,128)(2,1)}), bf16[64,1088]{1,0:T(8,128)(2,1)}) %reduce-scatter.39.cloned.1.call-update) | async-done | bytes 139280
  638.1 32.6 %reduce-scatter.37.cloned.1.call-done = bf16[64,1088]{1,0:T(8,128)(2,1)} async-done(((bf16[512,1088]{1,0:T(8,128)(2,1)}), bf16[64,1088]{1,0:T(8,128)(2,1)}) %reduce-scatter.37.cloned.1.call-update) | async-done | bytes 139280
  672.5 6.5 multiply_reduce_fusion.6
  681.7 5.7 collective-permute-done.3
  688.1 7.8 fusion.413
  695.9 3.5 multiply_reduce_fusion.3
  727.2 17.0 %reduce-scatter.41.cloned.1.call-done = bf16[64,1088]{1,0:T(8,128)(2,1)} async-done(((bf16[512,1088]{1,0:T(8,128)(2,1)}), bf16[64,1088]{1,0:T(8,128)(2,1)}) %reduce-scatter.41.cloned.1.call-update) | async-done | bytes 139280
  745.4 32.7 %reduce-scatter.43.cloned.1.call-done = bf16[64,1088]{1,0:T(8,128)(2,1)} async-done(((bf16[512,1088]{1,0:T(8,128)(2,1)}), bf16[64,1088]{1,0:T(8,128)(2,1)}) %reduce-scatter.43.cloned.1.call-update) | async-done | bytes 139280
  779.1 7.5 convolution_convert_fusion.2
  788.3 6.3 convolution_convert_fusion.1
  798.2 5.6 convolution_convert_fusion
  807.4 6.0 fusion.129
  815.4 48.4 %reduce-scatter.27.cloned.1.call-done = bf16[136,3264]{1,0:T(8,128)(2,1)} async-done(((bf16[1088,3264]{1,0:T(8,128)(2,1)}), bf16[136,3264]{1,0:T(8,128)(2,1)}) %reduce-scatter.27.cloned.1.call-update) | async-done | bytes 887824 | tf_op jit(solution)/shard_map/reduce_scatter | solution.py:321
  863.8 59.8 %reduce-scatter.29.cloned.1.call-done = bf16[136,4352]{1,0:T(8,128)(2,1)} async-done(((bf16[1088,4352]{1,0:T(8,128)(2,1)}), bf16[136,4352]{1,0:T(8,128)(2,1)}) %reduce-scatter.29.cloned.1.call-update) | async-done | bytes 1183760 | tf_op jit(solution)/shard_map/reduce_scatter | solution.py:327
  923.5 62.1 %reduce-scatter.31.cloned.1.call-done = bf16[544,1088]{1,0:T(8,128)(2,1)} async-done(((bf16[4352,1088]{1,0:T(8,128)(2,1)}), bf16[544,1088]{1,0:T(8,128)(2,1)}) %reduce-scatter.31.cloned.1.call-update) | async-done | bytes 1183760 | tf_op jit(solution)/shard_map/reduce_scatter | solution.py:330
  987.1 5.5 multiply_reduce_fusion.4
  993.2 25.4 %all-reduce.13 = (bf16[2176]{0:T(1024)(128)(2,1)S(1)}, bf16[1088]{0:T(1024)(128)(2,1)S(1)}, bf16[4352]{0:T(1024)(128)(2,1)S(1)}, bf16[1088]{0:T(1024)(128)(2,1)S...) all-reduce(bf16[2176]{0:T(1024)(128)(2,1)S(1)} %pad_maximum_fusion., ...), channel_id=22, replica_groups=mesh['section'=2,'fsdp'=8,'replica'=8] {'fsdp'}, use_global_device_ids=true, to_apply=%region_60.61.clone | all-reduce | flops 13056 | bytes 52224
  1019.0 21.7 %all-reduce.11 = (bf16[1,272]{1,0:T(2,128)(2,1)S(1)}, bf16[1,136]{1,0:T(2,128)(2,1)S(1)}, bf16[1,544]{1,0:T(2,128)(2,1)S(1)}, bf16[1,136]{1,0:T(2,128)(2,1)S(1)}...) all-reduce(bf16[1,272]{1,0:T(2,128)(2,1)S(1)} %broadcast_in_dim.232, ...), channel_id=1, replica_groups=mesh['section'=2,'fsdp'=8,'replica'=8] {'replica'}, use_global_device_ids=true, to_apply=%region_61.62 | all-reduce | flops 1632 | bytes 6528 | tf_op jit(solution)/shard_map/psum | solution.py:357
  1045.5 115.1 %all-reduce.17.cloned.1.call-done = (bf16[1,136,3264]{2,1,0:T(8,128)(2,1)}, bf16[1,136,1088]{2,1,0:T(8,128)(2,1)}, bf16[1,136,4352]{2,1,0:T(8,128)(2,1)}, bf16[1,544,1088]{2,1,0:T(8,128)(2,1)}) async-done(((bf16[1,136,3264]{2,1,0:T(8,128)(2,1)}, bf16[1,136,1088]{2,1,0:T(8,128)(2,1)}, bf16[1,136,4352]{2,1,0:T(8,128)(2,1)}, bf16[1,544,1088]{2,1,0:T(8,128)(2,1)}), (bf16[1,136,3264]{2,1,0:T(8,128)(2,1)}, ...) | async-done | bytes 3551248 | tf_op jit(solution)/shard_map/psum | solution.py:353
  (690 shorter events, 191.5 us)
Async XLA Ops:
  7.2 64.4 %copy-start.45 = (bf16[2,1,64,1088]{3,2,1,0:T(8,128)(2,1)S(1)}, bf16[2,1,64,1088]{3,2,1,0:T(8,128)(2,1)}, u32[]{:S(2)}) copy-start(bf16[2,1,64,1088]{3,2,1,0:T(8,128)(2,1)} %param.12) | copy-start | bytes 835588
  7.2 100.8 %all-gather.33.cloned.1.call-start = ((), (), s32[]{:S(2)}) async-start(), calls=%async_computation.19 | async-start | bytes 8146944 | tf_op jit(solution)/shard_map/all_gather | solution.py:245
  7.9 129.5 %all-gather.23.cloned.1.call-start = ((), (), s32[]{:S(2)}) async-start(), calls=%async_computation.11 | async-start | bytes 1327104 | tf_op jit(solution)/shard_map/all_gather | solution.py:81
  44.2 275.5 %copy-start.113 = (f32[3264]{0:T(1024)}, f32[3264]{0:T(1024)S(1)}, u32[]{:S(2)}) copy-start(f32[3264]{0:T(1024)S(1)} %concatenate.42) | copy-start | bytes 39172
  89.8 292.2 %copy-start.105 = (f32[1088]{0:T(1024)}, f32[1088]{0:T(1024)S(1)}, u32[]{:S(2)}) copy-start(f32[1088]{0:T(1024)S(1)} %get-tuple-element.36) | copy-start | bytes 13060
  89.8 307.8 %copy-start.111 = (f32[1088]{0:T(1024)}, f32[1088]{0:T(1024)S(1)}, u32[]{:S(2)}) copy-start(f32[1088]{0:T(1024)S(1)} %get-tuple-element.37) | copy-start | bytes 13060
  107.9 274.0 %copy-start.77 = (f32[1088]{0:T(1024)}, f32[1088]{0:T(1024)S(1)}, u32[]{:S(2)}) copy-start(f32[1088]{0:T(1024)S(1)} %get-tuple-element.34) | copy-start | bytes 13060
  107.9 289.7 %copy-start.86 = (f32[1088]{0:T(1024)}, f32[1088]{0:T(1024)S(1)}, u32[]{:S(2)}) copy-start(f32[1088]{0:T(1024)S(1)} %get-tuple-element.35) | copy-start | bytes 13060
  113.1 50.4 %all-gather.21.cloned.1.call-start = ((), (), s32[]{:S(2)}) async-start(), calls=%async_computation.10 | async-start | bytes 1327104 | tf_op jit(solution)/shard_map/all_gather | solution.py:82
  113.8 77.4 %all-gather.35.cloned.1.call-start = ((), (), s32[]{:S(2)}) async-start(), calls=%async_computation.20 | async-start | bytes 2820096 | tf_op jit(solution)/shard_map/all_gather | solution.py:246
  114.4 133.1 %all-gather.37.cloned.1.call-start = ((), (), s32[]{:S(2)}) async-start(), calls=%async_computation.21 | async-start | bytes 10653696 | tf_op jit(solution)/shard_map/all_gather | solution.py:247
  115.0 190.9 %all-gather.39.cloned.1.call-start = ((), (), s32[]{:S(2)}) async-start(), calls=%async_computation.22 | async-start | bytes 11280384 | tf_op jit(solution)/shard_map/all_gather | solution.py:248
  115.5 234.1 %all-gather.27.cloned.1.call-start = ((), (), s32[]{:S(2)}) async-start(), calls=%async_computation.13 | async-start | bytes 1327104 | tf_op jit(solution)/shard_map/all_gather | solution.py:81
  115.6 75.6 %copy-start.123 = (f32[1088]{0:T(1024)}, f32[1088]{0:T(1024)S(1)}, u32[]{:S(2)}) copy-start(f32[1088]{0:T(1024)S(1)} %convert_element_type.539) | copy-start | bytes 13060
  115.6 190.3 %copy-start.120 = (f32[1088]{0:T(1024)}, f32[1088]{0:T(1024)S(1)}, u32[]{:S(2)}) copy-start(f32[1088]{0:T(1024)S(1)} %convert_element_type.541) | copy-start | bytes 13060
  115.6 131.9 %copy-start.108 = (f32[4352]{0:T(1024)}, f32[4352]{0:T(1024)S(1)}, u32[]{:S(2)}) copy-start(f32[4352]{0:T(1024)S(1)} %convert_element_type.540) | copy-start | bytes 52228
  115.8 336.3 %copy-start.47 = (pred[64,512]{1,0:T(8,128)(4,1)}, pred[64,512]{1,0:T(8,128)(4,1)S(1)}, u32[]{:S(2)}) copy-start(pred[64,512]{1,0:T(8,128)(4,1)S(1)} %iota_compare_fusion) | copy-start | bytes 98308
  116.0 49.0 %copy-start.68 = (bf16[64,1088]{0,1:T(8,128)(2,1)}, bf16[64,1088]{0,1:T(8,128)(2,1)S(1)}, u32[]{:S(2)}) copy-start(bf16[64,1088]{0,1:T(8,128)(2,1)S(1)} %copy.122) | copy-start | bytes 417796
  193.6 59.2 %copy-start.154 = (f32[64]{0:T(128)}, f32[64]{0:T(128)S(1)}, u32[]{:S(2)}) copy-start(f32[64]{0:T(128)S(1)} %broadcast_multiply_fusion.10) | copy-start | bytes 772
  193.8 59.0 %copy-start.166 = (f32[64]{0:T(128)}, f32[64]{0:T(128)S(1)}, u32[]{:S(2)}) copy-start(f32[64]{0:T(128)S(1)} %add_rsqrt_fusion.4) | copy-start | bytes 772
  252.7 58.9 %copy-start.4 = (f32[64,4352]{1,0:T(8,128)}, f32[64,4352]{1,0:T(8,128)S(1)}, u32[]{:S(2)}) copy-start(f32[64,4352]{1,0:T(8,128)S(1)} %fusion.36) | copy-start | bytes 3342340
  311.7 7.0 collective-permute-start
  319.4 61.6 %copy-start.40 = (bf16[64,1088]{1,0:T(8,128)(2,1)}, bf16[64,1088]{1,0:T(8,128)(2,1)S(1)}, u32[]{:S(2)}) copy-start(bf16[64,1088]{1,0:T(8,128)(2,1)S(1)} %get-tuple-element.89) | copy-start | bytes 417796
  324.9 50.8 %all-gather.25.cloned.1.call-start = ((), (), s32[]{:S(2)}) async-start(), calls=%async_computation.12 | async-start | bytes 1327104 | tf_op jit(solution)/shard_map/all_gather | solution.py:82
  325.6 98.7 %all-gather.31.cloned.1.call-start = ((), (), s32[]{:S(2)}) async-start(), calls=%async_computation.15 | async-start | bytes 1327104 | tf_op jit(solution)/shard_map/all_gather | solution.py:81
  390.2 7.0 collective-permute-start.1
  399.8 49.8 %all-gather.29.cloned.1.call-start = ((), (), s32[]{:S(2)}) async-start(), calls=%async_computation.14 | async-start | bytes 1327104 | tf_op jit(solution)/shard_map/all_gather | solution.py:82
  400.3 130.5 %reduce-scatter.35.cloned.1.call-start = ((), (), s32[]{:S(2)}) async-start(), calls=%async_computation.24 | async-start | bytes 1327104
  498.5 66.2 %reduce-scatter.33.cloned.1.call-start = ((), (), s32[]{:S(2)}) async-start(), calls=%async_computation.23 | async-start | bytes 1327104
  506.9 130.2 %reduce-scatter.39.cloned.1.call-start = ((), (), s32[]{:S(2)}) async-start(), calls=%async_computation.26 | async-start | bytes 1327104
  508.6 57.9 %copy-start.87 = (f32[1088]{0:T(1024)S(1)}, f32[1088]{0:T(1024)}, u32[]{:S(2)}) copy-start(f32[1088]{0:T(1024)} %copy-done.86) | copy-start | bytes 13060
  574.8 7.0 collective-permute-start.2
  605.7 65.0 %reduce-scatter.37.cloned.1.call-start = ((), (), s32[]{:S(2)}) async-start(), calls=%async_computation.25 | async-start | bytes 1327104
  614.1 130.1 %reduce-scatter.41.cloned.1.call-start = ((), (), s32[]{:S(2)}) async-start(), calls=%async_computation.27 | async-start | bytes 1327104
  614.4 58.2 %copy-start.164 = (f32[64]{0:T(128)}, f32[64]{0:T(128)S(1)}, u32[]{:S(2)}) copy-start(f32[64]{0:T(128)S(1)} %broadcast_multiply_fusion) | copy-start | bytes 772
  638.1 40.9 %copy-start.58 = (bf16[64,1088]{0,1:T(8,128)(2,1)}, bf16[64,1088]{0,1:T(8,128)(2,1)S(1)}, u32[]{:S(2)}) copy-start(bf16[64,1088]{0,1:T(8,128)(2,1)S(1)} %copy.176) | copy-start | bytes 417796
  680.4 7.0 collective-permute-start.3
  712.8 65.2 %reduce-scatter.43.cloned.1.call-start = ((), (), s32[]{:S(2)}) async-start(), calls=%async_computation.28 | async-start | bytes 1327104
  718.4 96.9 %reduce-scatter.45.cloned.1.call-start = ((), (), s32[]{:S(2)}) async-start(), calls=%async_computation.29 | async-start | bytes 2820096
  722.5 141.3 %reduce-scatter.27.cloned.1.call-start = ((), (), s32[]{:S(2)}) async-start(), calls=%async_computation.16 | async-start | bytes 8146944 | tf_op jit(solution)/shard_map/reduce_scatter | solution.py:321
  745.3 41.3 %copy-start.61 = (bf16[64,1088]{0,1:T(8,128)(2,1)}, bf16[64,1088]{0,1:T(8,128)(2,1)S(1)}, u32[]{:S(2)}) copy-start(bf16[64,1088]{0,1:T(8,128)(2,1)S(1)} %copy.178) | copy-start | bytes 417796
  786.7 136.8 %reduce-scatter.29.cloned.1.call-start = ((), (), s32[]{:S(2)}) async-start(), calls=%async_computation.17 | async-start | bytes 10653696 | tf_op jit(solution)/shard_map/reduce_scatter | solution.py:327
  794.7 191.0 %reduce-scatter.31.cloned.1.call-start = ((), (), s32[]{:S(2)}) async-start(), calls=%async_computation.18 | async-start | bytes 11280384 | tf_op jit(solution)/shard_map/reduce_scatter | solution.py:330
  803.9 356.8 %all-reduce.17.cloned.1.call-start = ((), (), s32[]{:S(2)}) async-start(), calls=%async_computation.30 | async-start | bytes 7311360 | tf_op jit(solution)/shard_map/psum | solution.py:353
  992.6 51.9 %copy-start.50 = (f32[64,1088]{1,0:T(8,128)S(1)}, f32[64,1088]{1,0:T(8,128)}, u32[]{:S(2)}) copy-start(f32[64,1088]{1,0:T(8,128)} %copy-done.49) | copy-start | bytes 835588
  992.6 51.9 %copy-start.180 = (f32[64]{0:T(128)S(1)}, f32[64]{0:T(128)}, u32[]{:S(2)}) copy-start(f32[64]{0:T(128)} %copy-done.179) | copy-start | bytes 772
  992.6 52.0 %copy-start.89 = (bf16[64,1088]{1,0:T(8,128)(2,1)S(1)}, bf16[64,1088]{1,0:T(8,128)(2,1)}, u32[]{:S(2)}) copy-start(bf16[64,1088]{1,0:T(8,128)(2,1)} %copy-done.88) | copy-start | bytes 417796
  992.6 52.0 %copy-start.100 = (bf16[64,1088]{1,0:T(8,128)(2,1)S(1)}, bf16[64,1088]{1,0:T(8,128)(2,1)}, u32[]{:S(2)}) copy-start(bf16[64,1088]{1,0:T(8,128)(2,1)} %copy-done.99) | copy-start | bytes 417796
  (184 other events, 988.9 us)
Sparse Core Ops, SparseCore 0:
  9.7 49.7 all-gather.32
  113.2 24.2 all-gather.22
  139.7 23.6 all-gather.20
  165.0 26.1 all-gather.34
  192.7 54.7 all-gather.36
  249.0 56.8 all-gather.38
  325.0 24.6 all-gather.26
  351.9 23.6 all-gather.24
  399.9 24.3 all-gather.30
  425.8 23.6 all-gather.28
  498.6 32.1 reduce-scatter.34
  533.6 31.0 reduce-scatter.32
  605.8 31.1 reduce-scatter.38
  639.9 30.8 reduce-scatter.36
  712.9 31.2 reduce-scatter.40
  747.1 30.9 reduce-scatter.42
  780.9 34.4 reduce-scatter.44
  817.8 45.9 reduce-scatter.26
  866.2 57.2 reduce-scatter.28
  925.8 59.8 reduce-scatter.30
  988.4 172.1 all-reduce.16
where the time goes:
time: 1180 us
  waiting for transfers between devices  725 us (61%)
  matrix products  159 us (13%)
  blocking collectives  102 us (9%)
  other arithmetic  89 us (8%)
  local copies, waits for them, and re-layouts  67.3 us (6%)
  between operations  21.6 us (2%)
    unnamed x28, waiting for transfers between devices  159 us
    psum x1, waiting for transfers between devices, on_device(): lax.psum(pieces[0].astype(jnp.bfloat16), 'replica').astype(jnp.float32)  115 us
    all_gather x3, waiting for transfers between devices, forward_layer(): lax.all_gather(joined[:, 2 * feature_count:], 'fsdp', axis=0, tiled=True)  65.9 us
    all_gather x3, waiting for transfers between devices, forward_layer(): lax.all_gather(joined[:, feature_count:2 * feature_count], 'fsdp', axis=0...  65.5 us
    reduce_scatter x1, waiting for transfers between devices, on_device(): lax.psum_scatter(grad_weight_down.astype(jnp.bfloat16), 'fsdp', scatter_d...  62.1 us
    reduce_scatter x1, waiting for transfers between devices, on_device(): lax.psum_scatter(grad_weight_up.astype(jnp.bfloat16), 'fsdp', scatter_dim...  59.8 us
    dot_general x12, matrix products, product_right(): lax.dot_general(left_side, right_side, (((1,), (1,)), ((), ())), preferre...  54.6 us
    all_gather x1, waiting for transfers between devices, obtain(): lax.all_gather(weight_up[0], 'fsdp', axis=0, tiled=True)  53.7 us
  transfers between devices with their start and end apart: 25, of which 23 were waited for; matrix products, arithmetic and copies ran while one was open for 12% of the time, Pallas kernels for 0%

commit v1 on v0

v1 whole, which is shorter than its diff:
```python
import functools

import jax
import jax.numpy as jnp
from jax import lax
from jax.experimental import pallas as pl
from jax.experimental.pallas import tpu as pltpu
from jax.sharding import PartitionSpec as P

D = 1088
FF = 4352
HEADS = 17
HD = 64
BLK = 64
CHIPS = 4
ROWS = BLK * CHIPS
SLOTS = 5
TH = SLOTS * HD
TQKV = 3 * TH
SCALE = HD**-0.5
EPS = 1e-5
MESH = pl.DeviceIdType.MESH
BF = jnp.bfloat16
F32 = jnp.float32
ANY = pl.BlockSpec(memory_space=pl.ANY)
VMEM = pl.BlockSpec(memory_space=pltpu.VMEM)
DMA = pltpu.SemaphoreType.DMA
LIMIT = 56 * 1024 * 1024


def dot(a, b):
    return lax.dot_general(a, b, (((1,), (0,)), ((), ())), preferred_element_type=F32)


def dot_nt(a, b):
    return lax.dot_general(a, b, (((1,), (1,)), ((), ())), preferred_element_type=F32)


def dot_tn(a, b):
    return lax.dot_general(a, b, (((0,), (0,)), ((), ())), preferred_element_type=F32)


def chunks(n, size=256):
    return [(i, min(size, n - i)) for i in range(0, n, size)]


def place():
    f = lax.axis_index("fsdp")
    return f // 2, f % 2


def ring(y, k):
    return lax.rem(y + k, CHIPS)


def at_chip(y, c):
    return {"fsdp": 2 * y + c}


def greet(targets):
    barrier = pltpu.get_barrier_semaphore()
    for target in targets:
        pl.semaphore_signal(barrier, inc=1, device_id=target, device_id_type=MESH)
    return functools.partial(pl.semaphore_wait, barrier, len(targets))


def remote(src, dst, send, recv, target):
    return pltpu.make_async_remote_copy(
        src_ref=src, dst_ref=dst, send_sem=send, recv_sem=recv, device_id=target, device_id_type=MESH
    )


def slot(ref, y):
    return ref.at[pl.ds(pl.multiple_of(y * BLK, BLK), BLK)]


ORDER = (2, 1, 3)


def gather_start(full, y, c, send, recv):
    for k in ORDER:
        remote(slot(full, y), slot(full, y), send.at[k - 1], recv.at[k - 1], at_chip(ring(y, k), c)).start()


def gather_wait(full, y, c, send, recv):
    for k in (1, 3, 2):
        source = ring(y, 4 - k)
        remote(slot(full, source), slot(full, source), send.at[k - 1], recv.at[k - 1], at_chip(ring(y, k), c)).wait()


def scatter_start(acc, out_buf, in_buf, y, c, send, recv):
    for k in ORDER:
        target = ring(y, k)
        out_buf[k - 1] = slot(acc, target)[...].astype(BF)
        remote(out_buf.at[k - 1], in_buf.at[k - 1], send.at[k - 1], recv.at[k - 1], at_chip(target, c)).start()


def scatter_wait(acc, out_buf, in_buf, y, c, send, recv):
    total = slot(acc, y)[...]
    for k in (1, 3, 2):
        remote(out_buf.at[k - 1], in_buf.at[k - 1], send.at[k - 1], recv.at[k - 1], at_chip(ring(y, k), c)).wait()
        total = total + in_buf[k - 1].astype(F32)
    return total


def stats(v):
    centre = v - jnp.mean(v, axis=-1, keepdims=True)
    scale = lax.rsqrt(jnp.mean(centre * centre, axis=-1, keepdims=True) + EPS)
    return centre * scale, scale


def norm(v, gain, shift):
    return stats(v)[0] * gain + shift


def norm_back(d, v, gain):
    vh, scale = stats(v)
    q = d * gain
    grad = scale * (q - jnp.mean(q, axis=-1, keepdims=True) - vh * jnp.mean(q * vh, axis=-1, keepdims=True))
    return grad, jnp.sum(d * vh, axis=0, keepdims=True), jnp.sum(d, axis=0, keepdims=True)


GELU_A = 0.7978845608028654
GELU_B = 0.044715


def gelu(h):
    return 0.5 * h * (1.0 + jnp.tanh(GELU_A * (h + GELU_B * h * h * h)))


def gelu_slope(h):
    t = jnp.tanh(GELU_A * (h + GELU_B * h * h * h))
    return 0.5 * (1.0 + t) + 0.5 * h * (1.0 - t * t) * (GELU_A * (1.0 + 3.0 * GELU_B * h * h))


def masks(c):
    row = lax.broadcasted_iota(jnp.int32, (ROWS, ROWS), 0)
    col = lax.broadcasted_iota(jnp.int32, (ROWS, ROWS), 1)
    own = row >= col
    other = (row // BLK) >= (col // BLK) + (1 - c)
    return own, other


def load(pairs, sems):
    copies = [pltpu.make_async_copy(src, dst, sems.at[i]) for i, (src, dst) in enumerate(pairs)]
    for copy in copies:
        copy.start()
    return copies


def attend_forward(x, w_hbm, wo_hbm, vecs, bias, middle, normed, queries, kv, kv_other, logsum, attended,
                   w, wo, acc, out_buf, in_buf, ls, gs, gr, ss, sr, ks, kr):
    y, c = place()
    peers = [at_chip(ring(y, k), c) for k in (1, 2, 3)]
    sibling = at_chip(y, 1 - c)
    arrived = greet(peers + [sibling])
    weights = load([(w_hbm, w), (wo_hbm, wo)], ls)
    slot(normed, y)[...] = norm(x[...], vecs[0:1], vecs[1:2]).astype(BF)
    arrived()
    gather_start(normed, y, c, gs, gr)
    own, other = masks(c)
    weights[0].wait()
    gather_wait(normed, y, c, gs, gr)
    rows = normed[...]
    for at, size in chunks(2 * TH):
        kv[:, at : at + size] = (dot(rows, w[:, at : at + size]) + bias[0:1, at : at + size]).astype(BF)
    swap = remote(kv, kv_other, ks, kr, sibling)
    swap.start()
    queries[...] = (dot(rows, w[:, 2 * TH :]) + bias[0:1, 2 * TH :]).astype(BF)
    swap.wait()
    for h in range(SLOTS):
        at = h * HD
        q = queries[:, at : at + HD]
        s_own = jnp.where(own, dot_nt(q, kv[:, at : at + HD]) * SCALE, -1e30)
        s_other = jnp.where(other, dot_nt(q, kv_other[:, at : at + HD]) * SCALE, -1e30)
        top = jnp.maximum(jnp.max(s_own, axis=-1, keepdims=True), jnp.max(s_other, axis=-1, keepdims=True))
        e_own = jnp.exp(s_own - top)
        e_other = jnp.exp(s_other - top)
        total = jnp.sum(e_own, axis=-1, keepdims=True) + jnp.sum(e_other, axis=-1, keepdims=True)
        logsum[:, h : h + 1] = top + jnp.log(total)
        inverse = 1.0 / total
        a_own = (e_own * inverse).astype(BF)
        a_other = (e_other * inverse).astype(BF)
        out = dot(a_own, kv[:, TH + at : TH + at + HD]) + dot(a_other, kv_other[:, TH + at : TH + at + HD])
        attended[:, at : at + HD] = out.astype(BF)
    weights[1].wait()
    mixed = attended[...]
    for at, size in chunks(D):
        acc[:, at : at + size] = dot(mixed, wo[:, at : at + size])
    scatter_start(acc, out_buf, in_buf, y, c, ss, sr)
    base = x[...] + vecs[4:5]
    middle[...] = base + scatter_wait(acc, out_buf, in_buf, y, c, ss, sr)


def feed_forward(middle, wu_hbm, wd_hbm, vecs, result, normed, hidden, active,
                 wu, wd, acc, out_buf, in_buf, ls, gs, gr, ss, sr):
    y, c = place()
    arrived = greet([at_chip(ring(y, k), c) for k in (1, 2, 3)])
    weights = load([(wu_hbm, wu), (wd_hbm, wd)], ls)
    slot(normed, y)[...] = norm(middle[...], vecs[2:3], vecs[3:4]).astype(BF)
    arrived()
    gather_start(normed, y, c, gs, gr)
    weights[0].wait()
    gather_wait(normed, y, c, gs, gr)
    rows = normed[...]
    for at, size in chunks(D):
        h = dot(rows, wu[:, at : at + size]) + vecs[6:7, at : at + size]
        hidden[:, at : at + size] = h
        active[:, at : at + size] = gelu(h).astype(BF)
    weights[1].wait()
    rows = active[...]
    for at, size in chunks(D):
        acc[:, at : at + size] = dot(rows, wd[:, at : at + size])
    scatter_start(acc, out_buf, in_buf, y, c, ss, sr)
    base = middle[...] + vecs[5:6]
    result[...] = base + scatter_wait(acc, out_buf, in_buf, y, c, ss, sr)


def feed_back(grad, wu_hbm, wd_hbm, vecs, middle, normed, hidden, active, grad_middle, grad_up, grad_down, small,
              wu, wd, full, gh, acc, out_buf, in_buf, ls, gs, gr, ss, sr):
    y, c = place()
    arrived = greet([at_chip(ring(y, k), c) for k in (1, 2, 3)])
    weights = load([(wu_hbm, wu), (wd_hbm, wd)], ls)
    own_rows = grad[...].astype(BF)
    slot(full, y)[...] = own_rows
    arrived()
    gather_start(full, y, c, gs, gr)
    small[...] = jnp.zeros_like(small)
    small[3:4] = jnp.sum(own_rows.astype(F32), axis=0, keepdims=True)
    weights[1].wait()
    gather_wait(full, y, c, gs, gr)
    rows = full[...]
    for at, size in chunks(D):
        slope = gelu_slope(hidden[:, at : at + size])
        part = (dot_nt(rows, wd[at : at + size, :]) * slope).astype(BF)
        gh[:, at : at + size] = part
        small[2:3, at : at + size] = jnp.sum(part.astype(F32), axis=0, keepdims=True)
    weights[0].wait()
    rows = gh[...]
    for at, size in chunks(D):
        acc[:, at : at + size] = dot_nt(rows, wu[at : at + size, :])
    scatter_start(acc, out_buf, in_buf, y, c, ss, sr)
    for at, size in chunks(D):
        grad_up[at : at + size, :] = dot_tn(normed[:, at : at + size], gh[...]).astype(BF)
        grad_down[at : at + size, :] = dot_tn(active[:, at : at + size], full[...]).astype(BF)
    d = scatter_wait(acc, out_buf, in_buf, y, c, ss, sr)
    back, gain, shift = norm_back(d, middle[...], vecs[2:3])
    small[0:1] = gain
    small[1:2] = shift
    grad_middle[...] = grad[...] + back


def attend_back(grad, w_hbm, wo_hbm, vecs, x, normed, queries, kv, kv_other, logsum, attended,
                grad_x, grad_attn, grad_out, small, small_bias,
                w, wo, full, ga, gj, part_out, part_in, part_own, acc, out_buf, in_buf, ls, gs, gr, ss, sr, ks, kr):
    y, c = place()
    peers = [at_chip(ring(y, k), c) for k in (1, 2, 3)]
    sibling = at_chip(y, 1 - c)
    arrived = greet(peers + [sibling])
    weights = load([(w_hbm, w), (wo_hbm, wo)], ls)
    own_rows = grad[...].astype(BF)
    slot(full, y)[...] = own_rows
    arrived()
    gather_start(full, y, c, gs, gr)
    small[...] = jnp.zeros_like(small)
    small[2:3] = jnp.sum(own_rows.astype(F32), axis=0, keepdims=True)
    own, other = masks(c)
    weights[1].wait()
    gather_wait(full, y, c, gs, gr)
    ga[...] = dot_nt(full[...], wo[...]).astype(BF)
    for h in range(SLOTS):
        at = h * HD
        q = queries[:, at : at + HD]
        g = ga[:, at : at + HD]
        lse = logsum[:, h : h + 1]
        k_own, k_other = kv[:, at : at + HD], kv_other[:, at : at + HD]
        v_own, v_other = kv[:, TH + at : TH + at + HD], kv_other[:, TH + at : TH + at + HD]
        p_own = jnp.exp(jnp.where(own, dot_nt(q, k_own) * SCALE, -1e30) - lse)
        p_other = jnp.exp(jnp.where(other, dot_nt(q, k_other) * SCALE, -1e30) - lse)
        gp_own = dot_nt(g, v_own)
        gp_other = dot_nt(g, v_other)
        delta = jnp.sum(p_own * gp_own, axis=-1, keepdims=True) + jnp.sum(p_other * gp_other, axis=-1, keepdims=True)
        s_own = (p_own * (gp_own - delta)).astype(BF)
        s_other = (p_other * (gp_other - delta)).astype(BF)
        gj[:, 2 * TH + at : 2 * TH + at + HD] = ((dot(s_own, k_own) + dot(s_other, k_other)) * SCALE).astype(BF)
        part_own[:, at : at + HD] = dot_tn(s_own, q) * SCALE
        part_out[:, at : at + HD] = (dot_tn(s_other, q) * SCALE).astype(BF)
        part_own[:, TH + at : TH + at + HD] = dot_tn(p_own.astype(BF), g)
        part_out[:, TH + at : TH + at + HD] = dot_tn(p_other.astype(BF), g).astype(BF)
    swap = remote(part_out, part_in, ks, kr, sibling)
    swap.start()
    for at, size in chunks(D):
        grad_out[:, at : at + size] = dot_tn(attended[...], full[:, at : at + size]).astype(BF)
    weights[0].wait()
    swap.wait()
    gj[:, : 2 * TH] = (part_own[...] + part_in[...].astype(F32)).astype(BF)
    rows = gj[...]
    for at, size in chunks(D):
        acc[:, at : at + size] = dot_nt(rows, w[at : at + size, :])
    scatter_start(acc, out_buf, in_buf, y, c, ss, sr)
    for at, size in chunks(D):
        grad_attn[at : at + size, :] = dot_tn(normed[:, at : at + size], gj[...]).astype(BF)
    small_bias[...] = jnp.zeros_like(small_bias)
    small_bias[0:1] = jnp.sum(gj[...].astype(F32), axis=0, keepdims=True)
    d = scatter_wait(acc, out_buf, in_buf, y, c, ss, sr)
    back, gain, shift = norm_back(d, x[...], vecs[0:1])
    small[0:1] = gain
    small[1:2] = shift
    grad_x[...] = grad[...] + back


def shape(dims, kind):
    return jax.ShapeDtypeStruct(dims, kind)


MOVE = [
    pltpu.VMEM((ROWS, D), F32),
    pltpu.VMEM((3, BLK, D), BF),
    pltpu.VMEM((3, BLK, D), BF),
    DMA((2,)),
    DMA((3,)),
    DMA((3,)),
    DMA((3,)),
    DMA((3,)),
]


def call(body, name, number, outs, ins, scratch):
    return pl.pallas_call(
        body,
        name=name,
        out_shape=outs,
        in_specs=ins,
        out_specs=[VMEM] * len(outs),
        scratch_shapes=scratch,
        compiler_params=pltpu.CompilerParams(collective_id=number, has_side_effects=True, vmem_limit_bytes=LIMIT),
    )


def run_attend_forward(x, w, wo, vecs, bias):
    outs = [
        shape((BLK, D), F32),
        shape((ROWS, D), BF),
        shape((ROWS, TH), BF),
        shape((ROWS, 2 * TH), BF),
        shape((ROWS, 2 * TH), BF),
        shape((ROWS, 128), F32),
        shape((ROWS, TH), BF),
    ]
    scratch = [pltpu.VMEM((D, TQKV), BF), pltpu.VMEM((TH, D), BF)] + MOVE + [DMA, DMA]
    return call(attend_forward, "attend_forward", 0, outs, [VMEM, ANY, ANY, VMEM, VMEM], scratch)(x, w, wo, vecs, bias)


def run_feed_forward(middle, wu, wd, vecs):
    outs = [shape((BLK, D), F32), shape((ROWS, D), BF), shape((ROWS, D), F32), shape((ROWS, D), BF)]
    scratch = [pltpu.VMEM((D, D), BF), pltpu.VMEM((D, D), BF)] + MOVE
    return call(feed_forward, "feed_forward", 1, outs, [VMEM, ANY, ANY, VMEM], scratch)(middle, wu, wd, vecs)


def run_feed_back(grad, wu, wd, vecs, middle, normed, hidden, active):
    outs = [shape((BLK, D), F32), shape((D, D), BF), shape((D, D), BF), shape((8, D), F32)]
    scratch = [
        pltpu.VMEM((D, D), BF),
        pltpu.VMEM((D, D), BF),
        pltpu.VMEM((ROWS, D), BF),
        pltpu.VMEM((ROWS, D), BF),
    ] + MOVE
    return call(feed_back, "feed_back", 2, outs, [VMEM, ANY, ANY] + [VMEM] * 5, scratch)(
        grad, wu, wd, vecs, middle, normed, hidden, active
    )


def run_attend_back(grad, w, wo, vecs, x, saved):
    outs = [
        shape((BLK, D), F32),
        shape((D, TQKV), BF),
        shape((TH, D), BF),
        shape((8, D), F32),
        shape((8, TQKV), F32),
    ]
    scratch = [
        pltpu.VMEM((D, TQKV), BF),
        pltpu.VMEM((TH, D), BF),
        pltpu.VMEM((ROWS, D), BF),
        pltpu.VMEM((ROWS, TH), BF),
        pltpu.VMEM((ROWS, TQKV), BF),
        pltpu.VMEM((ROWS, 2 * TH), BF),
        pltpu.VMEM((ROWS, 2 * TH), BF),
        pltpu.VMEM((ROWS, 2 * TH), F32),
    ] + MOVE + [DMA, DMA]
    return call(attend_back, "attend_back", 3, outs, [VMEM, ANY, ANY] + [VMEM] * 8, scratch)(
        grad, w, wo, vecs, x, *saved
    )


def spread(send_a, send_u, send_d, send_o, send_v, wa, wu, wd, wo, wv, local, ysend, yrecv, zsend, zrecv, csend, crecv):
    s = lax.axis_index("section")
    y, c = place()
    replica = lax.axis_index("replica")
    flipped = replica // 2 * 2 + (1 - replica % 2)
    near = {"section": 1 - s}
    far = {"section": 1 - s, "replica": flipped}
    sibling = at_chip(y, 1 - c)
    peers = [at_chip(ring(y, k), c) for k in (1, 2, 3)]
    arrived = greet(peers + [sibling, near, far])
    keeps = load(
        [
            (send_a.at[y], wa.at[s, y, c]),
            (send_u.at[y], wu.at[s, y, c]),
            (send_d, wd.at[s, c]),
            (send_o, wo.at[s, c]),
            (send_v, wv.at[s, y, c]),
        ],
        local,
    )
    arrived()

    def along_y(k, back):
        target = ring(y, k)
        place_in = ring(y, 4 - k) if back else y
        return [
            remote(send_v, wv.at[s, place_in, c], ysend.at[0, k - 1], yrecv.at[0, k - 1], at_chip(target, c)),
            remote(send_a.at[target], wa.at[s, place_in, c], ysend.at[1, k - 1], yrecv.at[1, k - 1], at_chip(target, c)),
            remote(send_u.at[target], wu.at[s, place_in, c], ysend.at[2, k - 1], yrecv.at[2, k - 1], at_chip(target, c)),
        ]

    def along_z(layer):
        return [
            remote(wv.at[layer, :, c], wv.at[layer, :, c], zsend.at[0], zrecv.at[0], near),
            remote(wa.at[layer, 0:2, c], wa.at[layer, 0:2, c], zsend.at[1], zrecv.at[1], near),
            remote(wa.at[layer, 2:4, c], wa.at[layer, 2:4, c], zsend.at[2], zrecv.at[2], far),
            remote(wo.at[layer, c], wo.at[layer, c], zsend.at[3], zrecv.at[3], far),
            remote(wu.at[layer, 0:2, c], wu.at[layer, 0:2, c], zsend.at[4], zrecv.at[4], near),
            remote(wu.at[layer, 2:4, c], wu.at[layer, 2:4, c], zsend.at[5], zrecv.at[5], far),
            remote(wd.at[layer, c, 0:272], wd.at[layer, c, 0:272], zsend.at[6], zrecv.at[6], near),
            remote(wd.at[layer, c, 272:544], wd.at[layer, c, 272:544], zsend.at[7], zrecv.at[7], far),
        ]

    def across(layer, i, core):
        return [
            remote(wv.at[layer, :, core], wv.at[layer, :, core], csend.at[i, 0], crecv.at[i, 0], sibling),
            remote(wa.at[layer, :, core], wa.at[layer, :, core], csend.at[i, 1], crecv.at[i, 1], sibling),
            remote(wo.at[layer, core], wo.at[layer, core], csend.at[i, 2], crecv.at[i, 2], sibling),
            remote(wu.at[layer, :, core], wu.at[layer, :, core], csend.at[i, 3], crecv.at[i, 3], sibling),
            remote(wd.at[layer, core], wd.at[layer, core], csend.at[i, 4], crecv.at[i, 4], sibling),
        ]

    sent_y = [along_y(k, False) for k in (1, 2, 3)]
    got_y = [along_y(k, True) for k in (1, 2, 3)]
    sent_z, got_z = along_z(s), along_z(1 - s)
    sent_c = [across(s, 0, c), across(1 - s, 1, c)]
    got_c = [across(s, 0, 1 - c), across(1 - s, 1, 1 - c)]
    for kind in range(3):
        for k in (1, 0, 2):
            sent_y[k][kind].start()
    keeps[2].wait()
    keeps[3].wait()
    sent_z[3].start()
    sent_c[0][2].start()
    for kind, keep, zs, cross in ((0, 4, (0,), 0), (1, 0, (1, 2), 1), (2, 1, (4, 5, 6, 7), 3)):
        keeps[keep].wait()
        for k in range(3):
            got_y[k][kind].wait_recv()
        for z in zs:
            sent_z[z].start()
        sent_c[0][cross].start()
    sent_c[0][4].start()
    for zs, cross in (((0,), 0), ((1, 2), 1), ((3,), 2), ((4, 5), 3), ((6, 7), 4)):
        for z in zs:
            got_z[z].wait_recv()
        sent_c[1][cross].start()
    for i in range(2):
        for cross in range(5):
            got_c[i][cross].wait_recv()
    for k in range(3):
        for kind in range(3):
            sent_y[k][kind].wait_send()
    for z in range(8):
        sent_z[z].wait_send()
    for i in range(2):
        for cross in range(5):
            sent_c[i][cross].wait_send()


def run_spread(a, u, d, o, v):
    outs = [
        shape((2, 4, 2, 136, TQKV), BF),
        shape((2, 4, 2, 136, D), BF),
        shape((2, 2, 544, D), BF),
        shape((2, 2, 192, D), BF),
        shape((2, 4, 2, 16, 128), BF),
    ]
    return pl.pallas_call(
        spread,
        name="spread",
        out_shape=outs,
        in_specs=[ANY] * 5,
        out_specs=[ANY] * 5,
        scratch_shapes=[DMA((5,)), DMA((3, 3)), DMA((3, 3)), DMA((8,)), DMA((8,)), DMA((2, 5)), DMA((2, 5))],
        compiler_params=pltpu.CompilerParams(collective_id=4, has_side_effects=True),
    )(a, u, d, o, v)


def collect(wide, tall, out_wide, out_tall, own_w, own_t, in_w, in_t, out_w, local, csend, crecv, ysend, yrecv):
    y, c = place()
    sibling = at_chip(y, 1 - c)
    arrived = greet([at_chip(ring(y, k), c) for k in (1, 2, 3)] + [sibling])
    keeps = load([(wide.at[:, c], own_w), (tall.at[c], own_t)], local)
    arrived()
    swaps = [
        remote(wide.at[:, 1 - c], in_w, csend.at[0], crecv.at[0], sibling),
        remote(tall.at[1 - c], in_t, csend.at[1], crecv.at[1], sibling),
    ]
    for swap in swaps:
        swap.start()
    keeps[0].wait()
    swaps[0].wait()
    for k in ORDER:
        target = ring(y, k)
        out_w[target] = (own_w[target].astype(F32) + in_w[target].astype(F32)).astype(BF)
        remote(out_w.at[target], out_wide.at[y], ysend.at[k - 1], yrecv.at[k - 1], at_chip(target, c)).start()
    out_wide[y] = (own_w[y].astype(F32) + in_w[y].astype(F32)).astype(BF)
    keeps[1].wait()
    swaps[1].wait()
    out_tall[...] = (own_t[...].astype(F32) + in_t[...].astype(F32)).astype(BF)
    for k in (1, 3, 2):
        remote(out_w.at[ring(y, k)], out_wide.at[ring(y, 4 - k)], ysend.at[k - 1], yrecv.at[k - 1],
               at_chip(ring(y, k), c)).wait()


def run_collect(wide, tall, number):
    width = wide.shape[-1]
    rows = tall.shape[1]
    outs = [shape((4, 136, width), BF), shape((rows, D), BF)]
    wide_buf, tall_buf = pltpu.VMEM((4, 136, width), BF), pltpu.VMEM((rows, D), BF)
    return pl.pallas_call(
        collect,
        name="collect_%d" % number,
        out_shape=outs,
        in_specs=[ANY] * 2,
        out_specs=[VMEM] * 2,
        scratch_shapes=[wide_buf, tall_buf, wide_buf, tall_buf, wide_buf, DMA((2,)), DMA((2,)), DMA((2,)), DMA((3,)), DMA((3,))],
        compiler_params=pltpu.CompilerParams(collective_id=number, has_side_effects=True, vmem_limit_bytes=LIMIT),
    )(wide, tall)


def by_chip(options, y):
    return lax.dynamic_index_in_dim(jnp.stack(options), y, 0, keepdims=False)


def split_heads(block):
    zero = jnp.zeros(block.shape[:-1] + (HD,), block.dtype)
    return [
        jnp.concatenate([block[..., 256 * j : 256 * j + 256], block[..., 1024:] if j == 3 else zero], axis=-1)
        for j in range(CHIPS)
    ]


def join_heads(blocks):
    return jnp.concatenate([blocks[j][..., :256] for j in range(CHIPS)] + [blocks[3][..., 256:]], axis=-1)


def on_device(inputs, cotangent, weight_attn, weight_out, weight_up, weight_down, bias_attn, bias_out, bias_up,
              bias_down, norm_gain, norm_bias):
    s = lax.axis_index("section")
    f = lax.axis_index("fsdp")
    y, c = f // 2, f % 2
    wa = weight_attn[0]
    q_blocks, k_blocks, v_blocks = (split_heads(wa[:, i * D : (i + 1) * D]) for i in range(3))
    send_a = jnp.stack(
        [jnp.concatenate([k_blocks[j], v_blocks[j], q_blocks[j]], axis=-1) for j in range(CHIPS)]
    )
    send_u = jnp.stack([weight_up[0][:, j * D : (j + 1) * D] for j in range(CHIPS)])
    tail = lax.ppermute(weight_out[0, 88:], "fsdp", [(i, (i + 2) % 8) for i in range(8)])
    send_o = jnp.concatenate([weight_out[0], tail, jnp.zeros((8, D), BF)], axis=0)
    send_v = jnp.concatenate(
        [bias_attn[0], bias_out[0], bias_up[0], bias_down[0], norm_gain[0].reshape(-1), norm_bias[0].reshape(-1),
         jnp.zeros((416,), BF)]
    ).reshape(16, 128)
    wa, wu, wd, wo, wv = run_spread(send_a, send_u, weight_down[0], send_o, send_v)
    wa = wa.reshape(2, D, TQKV)
    wu = wu.reshape(2, D, D)
    wd = wd.reshape(2, D, D)
    wv = wv.reshape(2, 8, 2048).astype(F32)

    def layer_params(e):
        rows = jnp.concatenate([wo[e, 1, 136:184], wo[e, 0, :136], wo[e, 1, :136]], axis=0)
        main = lax.dynamic_slice_in_dim(rows, 48 - 16 * y, 256, 0)
        extra = jnp.where(y == 3, rows[256:320], jnp.zeros((HD, D), BF))
        out_rows = jnp.concatenate([main, extra], axis=0)
        v = wv[e]
        attn = v[:, :272].reshape(-1)
        gains = v[:, 1088:1360].reshape(8, 2, 136).transpose(1, 0, 2).reshape(2, D)
        shifts = v[:, 1360:1632].reshape(8, 2, 136).transpose(1, 0, 2).reshape(2, D)
        up = lax.dynamic_slice_in_dim(v, 2 * y, 2, 0)[:, 408:952].reshape(1, D)
        vecs = jnp.concatenate(
            [gains[0:1], shifts[0:1], gains[1:2], shifts[1:2], v[:, 272:408].reshape(1, D), v[:, 952:1088].reshape(1, D),
             up, jnp.zeros((1, D), F32)], axis=0
        )
        bq, bv = by_chip(split_heads(attn[:D]), y), by_chip(split_heads(attn[D:]), y)
        bias = jnp.concatenate([jnp.zeros((TH,), F32), bv, bq])[None]
        return wa[e], out_rows, wu[e], wd[e], vecs, jnp.pad(bias, ((0, 7), (0, 0)))

    params = [layer_params(e) for e in range(2)]
    micro = lax.dynamic_index_in_dim(inputs, s, 0, keepdims=False)[0]
    stream = micro.astype(F32)
    saved, acts = [], []
    for e in range(2):
        w, wo_e, wu_e, wd_e, vecs, bias = params[e]
        middle, *kept = run_attend_forward(stream, w, wo_e, vecs, bias)
        result, *kept_two = run_feed_forward(middle, wu_e, wd_e, vecs)
        saved.append((stream, kept, middle, kept_two))
        acts.append(result.astype(BF))
        stream = acts[-1].astype(F32)
    grad = lax.dynamic_index_in_dim(cotangent, s, 0, keepdims=False)[0].astype(F32)
    in_grads, weight_grads, small_grads = [None, None], [None, None], [None, None]
    for e in (1, 0):
        w, wo_e, wu_e, wd_e, vecs, bias = params[e]
        x, kept, middle, kept_two = saved[e]
        grad_middle, grad_up, grad_down, small_two = run_feed_back(grad, wu_e, wd_e, vecs, middle, *kept_two)
        up, down = run_collect(grad_up.reshape(4, 2, 136, D), grad_down.reshape(2, 544, D), 5)
        up = lax.psum(up, ("section", "replica"))
        down = lax.psum(down, ("section", "replica"))
        grad_x, grad_attn, grad_out, small_one, small_bias = run_attend_back(grad_middle, w, wo_e, vecs, x, kept)
        in_grads[e] = grad_x.astype(BF)
        grad = in_grads[e].astype(F32)
        after = lax.ppermute(grad_out[:64], "fsdp", [(i, (i - 2) % 8) for i in range(8)])
        after = jnp.where(y == 3, grad_out[256:], after)
        chip_rows = lax.dynamic_slice_in_dim(jnp.concatenate([grad_out[:256], after], axis=0), 16 * y, 272, 0)
        attn, out = run_collect(grad_attn.reshape(4, 2, 136, TQKV), chip_rows.reshape(2, 136, D), 6)
        attn = lax.psum(attn, ("section", "replica"))
        out = lax.psum(out, ("section", "replica"))
        weight_grads[e] = (attn, out, up, down)
        bq = lax.dynamic_update_slice(jnp.zeros((4, TH), F32), small_bias[0:1, 2 * TH :], (y, 0))
        bv = lax.dynamic_update_slice(jnp.zeros((4, TH), F32), small_bias[0:1, TH : 2 * TH], (y, 0))
        bu = lax.dynamic_update_slice(jnp.zeros((4, D), F32), small_two[2:3], (y, 0))
        small_grads[e] = jnp.concatenate(
            [join_heads(bq), join_heads(bv), small_one[2], bu.reshape(-1), small_two[3],
             small_one[0], small_two[0], small_one[1], small_two[1]]
        )
    small = lax.psum(jnp.stack(small_grads), ("section", "fsdp", "replica"))
    attn, out, up, down = (jnp.where(s == 0, a, b).astype(F32) for a, b in zip(weight_grads[0], weight_grads[1]))
    small = lax.dynamic_index_in_dim(small, s, 0, keepdims=False)
    attn = jnp.concatenate(
        [join_heads([attn[j][:, i * TH : (i + 1) * TH] for j in range(CHIPS)]) for i in (2, 0, 1)], axis=-1
    )
    up = jnp.concatenate([up[j] for j in range(CHIPS)], axis=-1)

    def piece(at, total):
        size = total // 8
        return lax.dynamic_slice_in_dim(small, at + f * size, size, 0)

    def pair(at):
        return jnp.stack([piece(at, D), piece(at + D, D)])

    def swap_layers(values):
        mine = jnp.where(s == 0, values[0], values[1])
        theirs = jnp.where(s == 0, values[1], values[0])
        received = lax.ppermute(theirs, "section", [(0, 1), (1, 0)])
        pair_up = jnp.stack([jnp.where(s == 0, mine, received), jnp.where(s == 0, received, mine)])
        return pair_up[None, :, None]

    return (
        swap_layers(acts),
        swap_layers(in_grads),
        attn[None],
        out[None],
        up[None],
        down[None],
        piece(0, 2176)[None],
        piece(2176, D)[None],
        piece(3264, FF)[None],
        piece(7616, D)[None],
        pair(8704)[None],
        pair(10880)[None],
    )


def solution(mesh):
    placed = (
        P(None, "replica", "fsdp", None),
        P(None, "replica", "fsdp", None),
        P("section", "fsdp", None),
        P("section", "fsdp", None),
        P("section", "fsdp", None),
        P("section", "fsdp", None),
        P("section", "fsdp"),
        P("section", "fsdp"),
        P("section", "fsdp"),
        P("section", "fsdp"),
        P("section", None, "fsdp"),
        P("section", None, "fsdp"),
    )
    return jax.shard_map(
        on_device,
        mesh=mesh,
        in_specs=placed,
        out_specs=(
            P("section", None, "replica", "fsdp", None),
            P("section", None, "replica", "fsdp", None),
        )
        + placed[2:],
        check_vma=False,
    )
```

time: 1180 us -> 724 us (0.61)
  waiting for transfers between devices: 725 us -> 196 us
  Pallas kernels: 0 us -> 422 us
  matrix products: 159 us -> 0 us
  blocking collectives: 102 us -> 0 us
  other arithmetic: 89 us -> 25.5 us
  local copies, waits for them, and re-layouts: 67.3 us -> 46.2 us
    pallas_call x0 -> x13, Pallas kernels: none -> 422 us  [the longest x1 127 us: run_spread(): pl.pallas_call(spread, name='spread', out_shape=outs, in_specs=[ANY] * 5,...]
    all_gather x10 -> x0, waiting for transfers between devices: 262 us -> none  [the longest x3 65.9 us: forward_layer(): lax.all_gather(joined[:, 2 * feature_count:], 'fsdp', axis=0, tiled=True)]
    reduce_scatter x3 -> x0, waiting for transfers between devices: 170 us -> none  [the longest x1 62.1 us: on_device(): lax.psum_scatter(grad_weight_down.astype(jnp.bfloat16), 'fsdp', scatter_d...]
    dot_general x49 -> x0, matrix products: 159 us -> none  [the longest x12 54.6 us: product_right(): lax.dot_general(left_side, right_side, (((1,), (1,)), ((), ())), preferre...]
    unnamed x28 -> x2, waiting for transfers between devices: 159 us -> 0.03 us
    psum x1 -> x2, waiting for transfers between devices: 115 us -> 196 us  [the longest x1 136 us: on_device(): attn = lax.psum(attn, ('section', 'replica'))]
    unnamed x2 -> x0, blocking collectives: 52.7 us -> none
    unnamed x442 -> x52, local copies, waits for them, and re-layouts: 48.2 us -> 2.95 us
  transfers between devices with their start and end apart: 25 -> 7, of which waited for: 23 -> 2; matrix products, arithmetic and copies ran while one was open for 12% -> 3% of each run, Pallas kernels for 0% -> 12%
where the time goes in v1:
time: 724 us; the launch traced here: 712 us
  Pallas kernels  422 us (58%)
  waiting for transfers between devices  196 us (27%)
  local copies, waits for them, and re-layouts  46.2 us (6%)
  other arithmetic  25.5 us (4%)
  between operations  15.8 us (2%)
    psum x1, waiting for transfers between devices, on_device(): attn = lax.psum(attn, ('section', 'replica'))  136 us
    pallas_call x1, Pallas kernels, run_spread(): pl.pallas_call(spread, name='spread', out_shape=outs, in_specs=[ANY] * 5,...  127 us
    pallas_call x4, Pallas kernels, run_collect(): pl.pallas_call(collect, name='collect_%d' % number, out_shape=outs, in_sp...  86.6 us
    psum x1, waiting for transfers between devices, on_device(): small = lax.psum(jnp.stack(small_grads), ('section', 'fsdp', 'replica'))  60.7 us
    pallas_call x2, Pallas kernels, run_attend_back(): call(attend_back, 'attend_back', 3, outs, [VMEM, ANY, ANY] + [VMEM] * 8,...  58.7 us
    pallas_call x2, Pallas kernels, run_attend_forward(): call(attend_forward, 'attend_forward', 0, outs, [VMEM, ANY, ANY, VMEM, VM...  54.6 us
    pallas_call x2, Pallas kernels, run_feed_back(): call(feed_back, 'feed_back', 2, outs, [VMEM, ANY, ANY] + [VMEM] * 5, scra...  49.9 us
    pallas_call x2, Pallas kernels, run_feed_forward(): call(feed_forward, 'feed_forward', 1, outs, [VMEM, ANY, ANY, VMEM], scratch)  45.7 us
  transfers between devices with their start and end apart: 7, of which 2 were waited for; matrix products, arithmetic and copies ran while one was open for 3% of the time, Pallas kernels for 12%

profile of v1, /device:TPU:4, one launch (start us, length us, event | category | flops | bytes accessed | tf_op | source)
XLA Modules:
  0.0 712.3 jit_solution(10126778908951480468)
XLA Ops:
  7.2 1.0 slice_bitcast_fusion.18
  8.2 1.6 collective-permute-start
  9.9 1.1 fusion.28
  11.0 1.3 fusion.27
  13.4 1.6 bitcast_convert_fusion.3.x
  15.0 1.7 bitcast_convert_fusion.2.grad
  17.3 1.3 pad_maximum_fusion.send_u
  19.3 1.1 pad_maximum_fusion.1.send_a
  20.4 1.8 maximum_maximum_fusion.send_o
  22.2 126.9 %spread.1 = (bf16[2,4,2,136,960]{4,3,2,1,0:T(8,128)(2,1)}, bf16[2,4,2,136,1088]{4,3,2,1,0:T(8,128)(2,1)}, bf16[2,2,544,1088]{3,2,1,0:T(8,128)(2,1)}, bf16[2,2,19...) custom-call(bf16[4,136,960]{2,1,0:T(8,128)(2,1)} %pad_maximum_fusion.1.send_a, ...), custom_call_target="tpu_custom_call" | custom-call | tf_op jit(solution)/shard_map/spread/pallas_call | solution.py:493
  149.1 1.0 slice_bitcast_fusion.16
  150.1 1.4 slice_bitcast_fusion.12
  151.9 5.0 fusion.26
  157.0 1.0 select_bitcast_fusion.4
  159.6 5.3 fusion.25
  164.9 2.6 fusion.24
  169.3 1.3 pad_maximum_fusion.2
  171.2 28.0 %attend_forward.2 = (f32[64,1088]{1,0:T(8,128)}, bf16[256,1088]{1,0:T(8,128)(2,1)}, bf16[256,320]{1,0:T(8,128)(2,1)}, bf16[256,640]{1,0:T(8,128)(2,1)}, bf16[256...) custom-call(f32[64,1088]{1,0:T(8,128)} %bitcast_convert_fusion.3.x, bf16[1088,960]{1,0:T(8,128)(2,1)} %bitcast.164, ...), custom_call_target="tpu_custom_call" | custom-call | tf_op jit(solution)/shard_map/attend_forward/pallas_call | solution.py:351
  199.2 22.5 %feed_forward.2 = (f32[64,1088]{1,0:T(8,128)}, bf16[256,1088]{1,0:T(8,128)(2,1)}, f32[256,1088]{1,0:T(8,128)}, bf16[256,1088]{1,0:T(8,128)(2,1)}) custom-call(f32[64,1088]{1,0:T(8,128)} %get-tuple-element.68.middle, bf16[1088,1088]{1,0:T(8,128)(2,1)} %bitcast.156, bf16[1088,1088]{1,0:T(8,128)(2,1)} %bitcast.158, f32[8,1088]{1,0:T(8,128)} %concatenate.118.vecs), custom_call_target="tpu_custom_call" | custom-call | tf_op jit(solution)/shard_map/feed_forward/pallas_call | solution.py:357
  221.7 1.7 convert_convert_fusion.1.x
  226.0 26.7 %attend_forward.3 = (f32[64,1088]{1,0:T(8,128)}, bf16[256,1088]{1,0:T(8,128)(2,1)}, bf16[256,320]{1,0:T(8,128)(2,1)}, bf16[256,640]{1,0:T(8,128)(2,1)}, bf16[256...) custom-call(f32[64,1088]{1,0:T(8,128)} %convert_convert_fusion.1.x, bf16[1088,960]{1,0:T(8,128)(2,1)} %bitcast.166, ...), custom_call_target="tpu_custom_call" | custom-call | tf_op jit(solution)/shard_map/attend_forward/pallas_call | solution.py:351
  252.6 23.1 %feed_forward.3 = (f32[64,1088]{1,0:T(8,128)}, bf16[256,1088]{1,0:T(8,128)(2,1)}, f32[256,1088]{1,0:T(8,128)}, bf16[256,1088]{1,0:T(8,128)(2,1)}) custom-call(f32[64,1088]{1,0:T(8,128)} %get-tuple-element.72.middle, bf16[1088,1088]{1,0:T(8,128)(2,1)} %bitcast.160, bf16[1088,1088]{1,0:T(8,128)(2,1)} %bitcast.162, f32[8,1088]{1,0:T(8,128)} %concatenate.130.vecs), custom_call_target="tpu_custom_call" | custom-call | tf_op jit(solution)/shard_map/feed_forward/pallas_call | solution.py:357
  275.8 24.7 %feed_back.2 = (f32[64,1088]{1,0:T(8,128)}, bf16[1088,1088]{1,0:T(8,128)(2,1)}, bf16[1088,1088]{1,0:T(8,128)(2,1)}, f32[8,1088]{1,0:T(8,128)}) custom-call(f32[64,1088]{1,0:T(8,128)} %bitcast_convert_fusion.2.grad, bf16[1088,1088]{1,0:T(8,128)(2,1)} %bitcast.161, bf16[1088,1088]{1,0:T(8,128)(2,1)} %bitcast.163, f32[8,1088]{1,0:T(8,128)} %concatenate.130.vecs, ...), custom_call_target="tpu_custom_call" | custom-call | tf_op jit(solution)/shard_map/feed_back/pallas_call | solution.py:368
  300.6 29.5 %attend_back.2 = (f32[64,1088]{1,0:T(8,128)}, bf16[1088,960]{1,0:T(8,128)(2,1)}, bf16[320,1088]{1,0:T(8,128)(2,1)}, f32[8,1088]{1,0:T(8,128)}, f32[8,960]{1,0:T(8,128)}) custom-call(f32[64,1088]{1,0:T(8,128)} %get-tuple-element.77.grad, bf16[1088,960]{1,0:T(8,128)(2,1)} %bitcast.167, bf16[320,1088]{1,0:T(8,128)(2,1)} %get-tuple-element.281.wo_hbm, ...), custom_call_target="tpu_custom_call" | custom-call | tf_op jit(solution)/shard_map/attend_back/pallas_call | solution.py:391
  330.0 1.7 convert_convert_fusion.grad
  331.7 25.1 %feed_back.3 = (f32[64,1088]{1,0:T(8,128)}, bf16[1088,1088]{1,0:T(8,128)(2,1)}, bf16[1088,1088]{1,0:T(8,128)(2,1)}, f32[8,1088]{1,0:T(8,128)}) custom-call(f32[64,1088]{1,0:T(8,128)} %convert_convert_fusion.grad, bf16[1088,1088]{1,0:T(8,128)(2,1)} %bitcast.157, bf16[1088,1088]{1,0:T(8,128)(2,1)} %bitcast.159, f32[8,1088]{1,0:T(8,128)} %concatenate.118.vecs, ...), custom_call_target="tpu_custom_call" | custom-call | tf_op jit(solution)/shard_map/feed_back/pallas_call | solution.py:368
  356.9 29.2 %attend_back.3 = (f32[64,1088]{1,0:T(8,128)}, bf16[1088,960]{1,0:T(8,128)(2,1)}, bf16[320,1088]{1,0:T(8,128)(2,1)}, f32[8,1088]{1,0:T(8,128)}, f32[8,960]{1,0:T(8,128)}) custom-call(f32[64,1088]{1,0:T(8,128)} %get-tuple-element.88.grad, bf16[1088,960]{1,0:T(8,128)(2,1)} %bitcast.165, bf16[320,1088]{1,0:T(8,128)(2,1)} %get-tuple-element.280.wo_hbm, ...), custom_call_target="tpu_custom_call" | custom-call | tf_op jit(solution)/shard_map/attend_back/pallas_call | solution.py:391
  386.1 1.2 slice.713
  387.3 0.9 slice.715
  390.3 1.7 collective-permute-start.3
  393.9 0.9 slice_reduce_fusion.7
  396.1 22.9 %collect_5.2 = (bf16[4,136,1088]{2,1,0:T(8,128)(2,1)}, bf16[544,1088]{1,0:T(8,128)(2,1)}) custom-call(bf16[4,2,136,1088]{3,2,1,0:T(8,128)(2,1)} %bitcast.172, bf16[2,544,1088]{2,1,0:T(8,128)(2,1)} %bitcast.173), custom_call_target="tpu_custom_call" | custom-call | tf_op jit(solution)/shard_map/collect_5/pallas_call | solution.py:536
  418.9 22.6 %collect_5.3 = (bf16[4,136,1088]{2,1,0:T(8,128)(2,1)}, bf16[544,1088]{1,0:T(8,128)(2,1)}) custom-call(bf16[4,2,136,1088]{3,2,1,0:T(8,128)(2,1)} %bitcast.170, bf16[2,544,1088]{2,1,0:T(8,128)(2,1)} %bitcast.171), custom_call_target="tpu_custom_call" | custom-call | tf_op jit(solution)/shard_map/collect_5/pallas_call | solution.py:536
  441.5 0.9 slice_select_fusion.1
  442.5 1.2 fusion.1
  443.7 1.2 fusion
  444.9 20.6 %collect_6.2 = (bf16[4,136,960]{2,1,0:T(8,128)(2,1)}, bf16[136,1088]{1,0:T(8,128)(2,1)}) custom-call(bf16[4,2,136,960]{3,2,1,0:T(8,128)(2,1)} %bitcast.178, bf16[2,136,1088]{2,1,0:T(8,128)(2,1)} %bitcast.174), custom_call_target="tpu_custom_call" | custom-call | tf_op jit(solution)/shard_map/collect_6/pallas_call | solution.py:536
  465.4 20.6 %collect_6.3 = (bf16[4,136,960]{2,1,0:T(8,128)(2,1)}, bf16[136,1088]{1,0:T(8,128)(2,1)}) custom-call(bf16[4,2,136,960]{3,2,1,0:T(8,128)(2,1)} %bitcast.177, bf16[2,136,1088]{2,1,0:T(8,128)(2,1)} %bitcast.175), custom_call_target="tpu_custom_call" | custom-call | tf_op jit(solution)/shard_map/collect_6/pallas_call | solution.py:536
  487.3 2.0 collective-permute-start.2
  489.3 60.7 %all-reduce.14.cloned.1.call-done = f32[2,13056]{1,0:T(2,128)} async-done(((f32[2,13056]{1,0:T(2,128)}), f32[2,13056]{1,0:T(2,128)}) %all-reduce.14.cloned.1.call-update) | async-done | bytes 104464 | tf_op jit(solution)/shard_map/psum | solution.py:641
  550.0 1.3 fusion.33
  551.9 1.3 dynamic_slice.82
  553.2 1.3 dynamic_slice.84
  556.8 135.7 %all-reduce.16.cloned.1.call-done = (bf16[4,136,960]{2,1,0:T(8,128)(2,1)}, bf16[4,136,960]{2,1,0:T(8,128)(2,1)}, bf16[136,1088]{1,0:T(8,128)(2,1)}, bf16[136,108...) async-done(((bf16[4,136,960]{2,1,0:T(8,128)(2,1)}, ...) | async-done | bytes 7415824 | tf_op jit(solution)/shard_map/psum | solution.py:631
  692.5 1.4 select_convert_fusion.1
  698.7 1.6 bitcast_convert_fusion
  700.3 2.4 concatenate.143
  702.7 2.5 concatenate.142
  (215 shorter events, 22.3 us)
Async XLA Ops:
  7.2 5.2 copy-start.2
  7.2 542.8 %all-reduce.14.cloned.1.call-start = ((), (), s32[]{:S(2)}) async-start(), calls=%async_computation | async-start | bytes 208896 | tf_op jit(solution)/shard_map/psum | solution.py:641
  8.2 12.2 %collective-permute-start = (bf16[48,1088]{1,0:T(8,128)(2,1)S(1)}, bf16[48,1088]{1,0:T(8,128)(2,1)}, u32[]{:S(2)}, u32[]{:S(2)}) collective-permute-start(bf16[48,1088]{1,0:T(8,128)(2,1)S(1)} %slice_bitcast_fusion.18), channel_id=1, source_target_pairs={{0,16},{8,24},{16,32},{24,40},{32,48},{40,56},{48,0},{56,8},{1,17}... | collective-permute-start | bytes 313352 | tf_op jit(solution)/shard_map/ppermute | solution.py:574
  12.4 0.7 copy-start.17
  12.4 0.7 copy-start.18
  12.4 0.7 copy-start.16
  12.4 0.7 copy-start.19
  12.4 0.8 copy-start.20
  12.4 0.8 copy-start.21
  18.6 1.8 copy-start.10
  150.1 1.4 copy-start.13
  151.9 7.4 %copy-start.22 = (pred[320]{0:T(512)(128)(4,1)S(1)}, pred[320]{0:T(512)(128)(4,1)}, u32[]{:S(2)}) copy-start(pred[320]{0:T(512)(128)(4,1)} %constant.183.clone.1) | copy-start | bytes 964
  158.8 6.1 slice-start
  159.6 5.3 slice-start.1
  386.1 2.2 copy-start.9
  387.3 6.3 copy-start.15
  387.3 7.6 %copy-start.14 = (f32[8,1088]{1,0:T(8,128)S(1)}, f32[8,1088]{1,0:T(8,128)}, u32[]{:S(2)}) copy-start(f32[8,1088]{1,0:T(8,128)} %get-tuple-element.114) | copy-start | bytes 104452
  390.3 51.2 %collective-permute-start.3 = (bf16[64,1088]{1,0:T(8,128)(2,1)S(1)}, bf16[64,1088]{1,0:T(8,128)(2,1)S(1)}, u32[]{:S(2)}, u32[]{:S(2)}) collective-permute-start(bf16[64,1088]{1,0:T(8,128)(2,1)S(1)} %slice.715), channel_id=1, source_target_pairs={{0,48},{8,56},{16,0},{24,8},{32,16},{40,24},{48,32},{56,40},{1,49}... | collective-permute-start | bytes 417800 | tf_op jit(solution)/shard_map/ppermute | solution.py:627
  392.1 51.6 %collective-permute-start.4 = (bf16[64,1088]{1,0:T(8,128)(2,1)S(1)}, bf16[64,1088]{1,0:T(8,128)(2,1)S(1)}, u32[]{:S(2)}, u32[]{:S(2)}) collective-permute-start(bf16[64,1088]{1,0:T(8,128)(2,1)S(1)} %slice.718), channel_id=1, source_target_pairs={{0,48},{8,56},{16,0},{24,8},{32,16},{40,24},{48,32},{56,40},{1,49}... | collective-permute-start | bytes 417800 | tf_op jit(solution)/shard_map/ppermute | solution.py:627
  396.0 296.4 %all-reduce.16.cloned.1.call-start = ((), (), s32[]{:S(2)}) async-start(), calls=%async_computation.1 | async-start | bytes 15736832 | tf_op jit(solution)/shard_map/psum | solution.py:631
  486.0 1.0 copy-start
  486.0 1.0 copy-start.7
  486.0 1.2 copy-start.1
  486.0 1.2 copy-start.8
  487.1 68.0 %collective-permute-start.1 = (bf16[64,1088]{1,0:T(8,128)(2,1)S(1)}, bf16[64,1088]{1,0:T(8,128)(2,1)S(1)}, u32[]{:S(2)}, u32[]{:S(2)}) collective-permute-start(bf16[64,1088]{1,0:T(8,128)(2,1)S(1)} %broadcast_select_fusion.2), channel_id=1, source_target_pairs={{0,64},{64,0},{1,65},{65,1},{2,66},{66,2},{3,67},{67,3},{4,68},{68... | collective-permute-start | bytes 417800 | tf_op jit(solution)/shard_map/ppermute | solution.py:659
  487.3 68.7 %collective-permute-start.2 = (bf16[64,1088]{1,0:T(8,128)(2,1)S(1)}, bf16[64,1088]{1,0:T(8,128)(2,1)S(1)}, u32[]{:S(2)}, u32[]{:S(2)}) collective-permute-start(bf16[64,1088]{1,0:T(8,128)(2,1)S(1)} %broadcast_select_fusion), channel_id=1, source_target_pairs={{0,64},{64,0},{1,65},{65,1},{2,66},{66,2},{3,67},{67,3},{4,68},{68... | collective-permute-start | bytes 417800 | tf_op jit(solution)/shard_map/ppermute | solution.py:659
  694.2 1.7 copy-start.6
  695.0 1.5 copy-start.5
  696.8 1.0 copy-start.11
  696.8 1.1 copy-start.12
  696.8 1.9 copy-start.4
  697.0 1.7 copy-start.3
Sparse Core Ops, SparseCore 0:
  396.1 153.7 all-reduce.13
  556.1 136.2 all-reduce.15

commit v2 on v1

--- a/solution.py
+++ b/solution.py
@@ -26,6 +26,7 @@
 VMEM = pl.BlockSpec(memory_space=pltpu.VMEM)
 DMA = pltpu.SemaphoreType.DMA
 LIMIT = 56 * 1024 * 1024
+COST = pl.CostEstimate(flops=10_000_000, bytes_accessed=10_000, transcendentals=0)
 
 
 def dot(a, b):
@@ -148,13 +149,36 @@
     return copies
 
 
-def attend_forward(x, w_hbm, wo_hbm, vecs, bias, middle, normed, queries, kv, kv_other, logsum, attended,
+def out_rows(wo_hbm, wo, e, y):
+    start = pl.multiple_of(48 - 16 * y, 16)
+    return [(wo_hbm.at[e, pl.ds(start, 256)], wo.at[0:256]), (wo_hbm.at[e, 256:320], wo.at[256:320])]
+
+
+def out_wait(weights, wo, y):
+    weights[1].wait()
+    weights[2].wait()
+
+    @pl.when(y < 3)
+    def _():
+        wo[256:320] = jnp.zeros((HD, D), BF)
+
+
+def chip_row(y, rows):
+    return jnp.where(lax.broadcasted_iota(jnp.int32, (CHIPS, 1), 0) == y, rows, 0.0)
+
+
+def head_bias(vecs, row, y):
+    last = jnp.where(y == 3, vecs[row : row + 1, 1024:D], 0.0)
+    return jnp.concatenate([vecs[row : row + 1, pl.ds(pl.multiple_of(256 * y, 256), 256)], last], axis=-1)
+
+
+def attend_forward(e, x, w_hbm, wo_hbm, vecs, middle, normed, queries, kv, kv_other, logsum, attended,
                    w, wo, acc, out_buf, in_buf, ls, gs, gr, ss, sr, ks, kr):
     y, c = place()
     peers = [at_chip(ring(y, k), c) for k in (1, 2, 3)]
     sibling = at_chip(y, 1 - c)
     arrived = greet(peers + [sibling])
-    weights = load([(w_hbm, w), (wo_hbm, wo)], ls)
+    weights = load([(w_hbm.at[e], w)] + out_rows(wo_hbm, wo, e, y), ls)
     slot(normed, y)[...] = norm(x[...], vecs[0:1], vecs[1:2]).astype(BF)
     arrived()
     gather_start(normed, y, c, gs, gr)
@@ -162,11 +186,12 @@
     weights[0].wait()
     gather_wait(normed, y, c, gs, gr)
     rows = normed[...]
+    bias = jnp.concatenate([jnp.zeros((1, TH), F32), head_bias(vecs, 11, y)], axis=-1)
     for at, size in chunks(2 * TH):
-        kv[:, at : at + size] = (dot(rows, w[:, at : at + size]) + bias[0:1, at : at + size]).astype(BF)
+        kv[:, at : at + size] = (dot(rows, w[:, at : at + size]) + bias[:, at : at + size]).astype(BF)
     swap = remote(kv, kv_other, ks, kr, sibling)
     swap.start()
-    queries[...] = (dot(rows, w[:, 2 * TH :]) + bias[0:1, 2 * TH :]).astype(BF)
+    queries[...] = (dot(rows, w[:, 2 * TH :]) + head_bias(vecs, 10, y)).astype(BF)
     swap.wait()
     for h in range(SLOTS):
         at = h * HD
@@ -183,7 +208,7 @@
         a_other = (e_other * inverse).astype(BF)
         out = dot(a_own, kv[:, TH + at : TH + at + HD]) + dot(a_other, kv_other[:, TH + at : TH + at + HD])
         attended[:, at : at + HD] = out.astype(BF)
-    weights[1].wait()
+    out_wait(weights, wo, y)
     mixed = attended[...]
     for at, size in chunks(D):
         acc[:, at : at + size] = dot(mixed, wo[:, at : at + size])
@@ -192,19 +217,20 @@
     middle[...] = base + scatter_wait(acc, out_buf, in_buf, y, c, ss, sr)
 
 
-def feed_forward(middle, wu_hbm, wd_hbm, vecs, result, normed, hidden, active,
+def feed_forward(e, middle, wu_hbm, wd_hbm, vecs, result, normed, hidden, active,
                  wu, wd, acc, out_buf, in_buf, ls, gs, gr, ss, sr):
     y, c = place()
     arrived = greet([at_chip(ring(y, k), c) for k in (1, 2, 3)])
-    weights = load([(wu_hbm, wu), (wd_hbm, wd)], ls)
+    weights = load([(wu_hbm.at[e], wu), (wd_hbm.at[e], wd)], ls)
     slot(normed, y)[...] = norm(middle[...], vecs[2:3], vecs[3:4]).astype(BF)
     arrived()
     gather_start(normed, y, c, gs, gr)
+    bias = jnp.sum(chip_row(y, vecs[6:10]), axis=0, keepdims=True)
     weights[0].wait()
     gather_wait(normed, y, c, gs, gr)
     rows = normed[...]
     for at, size in chunks(D):
-        h = dot(rows, wu[:, at : at + size]) + vecs[6:7, at : at + size]
+        h = dot(rows, wu[:, at : at + size]) + bias[:, at : at + size]
         hidden[:, at : at + size] = h
         active[:, at : at + size] = gelu(h).astype(BF)
     weights[1].wait()
@@ -216,11 +242,11 @@
     result[...] = base + scatter_wait(acc, out_buf, in_buf, y, c, ss, sr)
 
 
-def feed_back(grad, wu_hbm, wd_hbm, vecs, middle, normed, hidden, active, grad_middle, grad_up, grad_down, small,
+def feed_back(e, grad, wu_hbm, wd_hbm, vecs, middle, normed, hidden, active, grad_middle, grad_up, grad_down, small,
               wu, wd, full, gh, acc, out_buf, in_buf, ls, gs, gr, ss, sr):
     y, c = place()
     arrived = greet([at_chip(ring(y, k), c) for k in (1, 2, 3)])
-    weights = load([(wu_hbm, wu), (wd_hbm, wd)], ls)
+    weights = load([(wu_hbm.at[e], wu), (wd_hbm.at[e], wd)], ls)
     own_rows = grad[...].astype(BF)
     slot(full, y)[...] = own_rows
     arrived()
@@ -250,14 +276,14 @@
     grad_middle[...] = grad[...] + back
 
 
-def attend_back(grad, w_hbm, wo_hbm, vecs, x, normed, queries, kv, kv_other, logsum, attended,
+def attend_back(e, grad, w_hbm, wo_hbm, vecs, x, normed, queries, kv, kv_other, logsum, attended,
                 grad_x, grad_attn, grad_out, small, small_bias,
                 w, wo, full, ga, gj, part_out, part_in, part_own, acc, out_buf, in_buf, ls, gs, gr, ss, sr, ks, kr):
     y, c = place()
     peers = [at_chip(ring(y, k), c) for k in (1, 2, 3)]
     sibling = at_chip(y, 1 - c)
     arrived = greet(peers + [sibling])
-    weights = load([(w_hbm, w), (wo_hbm, wo)], ls)
+    weights = load([(w_hbm.at[e], w)] + out_rows(wo_hbm, wo, e, y), ls)
     own_rows = grad[...].astype(BF)
     slot(full, y)[...] = own_rows
     arrived()
@@ -265,7 +291,7 @@
     small[...] = jnp.zeros_like(small)
     small[2:3] = jnp.sum(own_rows.astype(F32), axis=0, keepdims=True)
     own, other = masks(c)
-    weights[1].wait()
+    out_wait(weights, wo, y)
     gather_wait(full, y, c, gs, gr)
     ga[...] = dot_nt(full[...], wo[...]).astype(BF)
     for h in range(SLOTS):
@@ -317,7 +343,7 @@
     pltpu.VMEM((ROWS, D), F32),
     pltpu.VMEM((3, BLK, D), BF),
     pltpu.VMEM((3, BLK, D), BF),
-    DMA((2,)),
+    DMA((3,)),
     DMA((3,)),
     DMA((3,)),
     DMA((3,)),
@@ -333,11 +359,12 @@
         in_specs=ins,
         out_specs=[VMEM] * len(outs),
         scratch_shapes=scratch,
+        cost_estimate=COST,
         compiler_params=pltpu.CompilerParams(collective_id=number, has_side_effects=True, vmem_limit_bytes=LIMIT),
     )
 
 
-def run_attend_forward(x, w, wo, vecs, bias):
+def run_attend_forward(e, x, w, wo, vecs):
     outs = [
         shape((BLK, D), F32),
         shape((ROWS, D), BF),
@@ -348,16 +375,16 @@
         shape((ROWS, TH), BF),
     ]
     scratch = [pltpu.VMEM((D, TQKV), BF), pltpu.VMEM((TH, D), BF)] + MOVE + [DMA, DMA]
-    return call(attend_forward, "attend_forward", 0, outs, [VMEM, ANY, ANY, VMEM, VMEM], scratch)(x, w, wo, vecs, bias)
-
-
-def run_feed_forward(middle, wu, wd, vecs):
+    return call(functools.partial(attend_forward, e), "attend_forward_%d" % e, e, outs, [VMEM, ANY, ANY, VMEM], scratch)(x, w, wo, vecs)
+
+
+def run_feed_forward(e, middle, wu, wd, vecs):
     outs = [shape((BLK, D), F32), shape((ROWS, D), BF), shape((ROWS, D), F32), shape((ROWS, D), BF)]
     scratch = [pltpu.VMEM((D, D), BF), pltpu.VMEM((D, D), BF)] + MOVE
-    return call(feed_forward, "feed_forward", 1, outs, [VMEM, ANY, ANY, VMEM], scratch)(middle, wu, wd, vecs)
-
-
-def run_feed_back(grad, wu, wd, vecs, middle, normed, hidden, active):
+    return call(functools.partial(feed_forward, e), "feed_forward_%d" % e, 2 + e, outs, [VMEM, ANY, ANY, VMEM], scratch)(middle, wu, wd, vecs)
+
+
+def run_feed_back(e, grad, wu, wd, vecs, middle, normed, hidden, active):
     outs = [shape((BLK, D), F32), shape((D, D), BF), shape((D, D), BF), shape((8, D), F32)]
     scratch = [
         pltpu.VMEM((D, D), BF),
@@ -365,12 +392,12 @@
         pltpu.VMEM((ROWS, D), BF),
         pltpu.VMEM((ROWS, D), BF),
     ] + MOVE
-    return call(feed_back, "feed_back", 2, outs, [VMEM, ANY, ANY] + [VMEM] * 5, scratch)(
+    return call(functools.partial(feed_back, e), "feed_back_%d" % e, 4 + e, outs, [VMEM, ANY, ANY] + [VMEM] * 5, scratch)(
         grad, wu, wd, vecs, middle, normed, hidden, active
     )
 
 
-def run_attend_back(grad, w, wo, vecs, x, saved):
+def run_attend_back(e, grad, w, wo, vecs, x, saved):
     outs = [
         shape((BLK, D), F32),
         shape((D, TQKV), BF),
@@ -388,7 +415,7 @@
         pltpu.VMEM((ROWS, 2 * TH), BF),
         pltpu.VMEM((ROWS, 2 * TH), F32),
     ] + MOVE + [DMA, DMA]
-    return call(attend_back, "attend_back", 3, outs, [VMEM, ANY, ANY] + [VMEM] * 8, scratch)(
+    return call(functools.partial(attend_back, e), "attend_back_%d" % e, 6 + e, outs, [VMEM, ANY, ANY] + [VMEM] * 8, scratch)(
         grad, w, wo, vecs, x, *saved
     )
 
@@ -450,25 +477,38 @@
     sent_z, got_z = along_z(s), along_z(1 - s)
     sent_c = [across(s, 0, c), across(1 - s, 1, c)]
     got_c = [across(s, 0, 1 - c), across(1 - s, 1, 1 - c)]
-    for kind in range(3):
+    for kind in (0, 1):
         for k in (1, 0, 2):
             sent_y[k][kind].start()
-    keeps[2].wait()
     keeps[3].wait()
     sent_z[3].start()
     sent_c[0][2].start()
-    for kind, keep, zs, cross in ((0, 4, (0,), 0), (1, 0, (1, 2), 1), (2, 1, (4, 5, 6, 7), 3)):
+    keeps[2].wait()
+    sent_z[6].start()
+    sent_z[7].start()
+    sent_c[0][4].start()
+    for kind, keep, zs, cross in ((0, 4, (0,), 0), (1, 0, (1, 2), 1)):
         keeps[keep].wait()
         for k in range(3):
             got_y[k][kind].wait_recv()
         for z in zs:
             sent_z[z].start()
         sent_c[0][cross].start()
-    sent_c[0][4].start()
-    for zs, cross in (((0,), 0), ((1, 2), 1), ((3,), 2), ((4, 5), 3), ((6, 7), 4)):
+    for k in (1, 0, 2):
+        sent_y[k][2].start()
+    for zs, cross in (((3,), 2), ((6, 7), 4), ((0,), 0), ((1, 2), 1)):
         for z in zs:
             got_z[z].wait_recv()
         sent_c[1][cross].start()
+    keeps[1].wait()
+    for k in range(3):
+        got_y[k][2].wait_recv()
+    for z in (4, 5):
+        sent_z[z].start()
+    sent_c[0][3].start()
+    for z in (4, 5):
+        got_z[z].wait_recv()
+    sent_c[1][3].start()
     for i in range(2):
         for cross in range(5):
             got_c[i][cross].wait_recv()
@@ -488,7 +528,7 @@
         shape((2, 4, 2, 136, D), BF),
         shape((2, 2, 544, D), BF),
         shape((2, 2, 192, D), BF),
-        shape((2, 4, 2, 16, 128), BF),
+        shape((2, 4, 2, 16, D), BF),
     ]
     return pl.pallas_call(
         spread,
@@ -497,11 +537,27 @@
         in_specs=[ANY] * 5,
         out_specs=[ANY] * 5,
         scratch_shapes=[DMA((5,)), DMA((3, 3)), DMA((3, 3)), DMA((8,)), DMA((8,)), DMA((2, 5)), DMA((2, 5))],
-        compiler_params=pltpu.CompilerParams(collective_id=4, has_side_effects=True),
+        compiler_params=pltpu.CompilerParams(collective_id=8, has_side_effects=True),
     )(a, u, d, o, v)
 
 
-def collect(wide, tall, out_wide, out_tall, own_w, own_t, in_w, in_t, out_w, local, csend, crecv, ysend, yrecv):
+def wide_start(wide, own_w, in_w, out_w, out_wide, keep, swap, y, c, ysend, yrecv):
+    keep.wait()
+    swap.wait()
+    for k in ORDER:
+        target = ring(y, k)
+        out_w[target] = (own_w[target].astype(F32) + in_w[target].astype(F32)).astype(BF)
+        remote(out_w.at[target], out_wide.at[y], ysend.at[k - 1], yrecv.at[k - 1], at_chip(target, c)).start()
+    out_wide[y] = (own_w[y].astype(F32) + in_w[y].astype(F32)).astype(BF)
+
+
+def wide_wait(out_w, out_wide, y, c, ysend, yrecv):
+    for k in (1, 3, 2):
+        remote(out_w.at[ring(y, k)], out_wide.at[ring(y, 4 - k)], ysend.at[k - 1], yrecv.at[k - 1],
+               at_chip(ring(y, k), c)).wait()
+
+
+def collect_feed(wide, tall, out_wide, out_tall, own_w, own_t, in_w, in_t, out_w, local, csend, crecv, ysend, yrecv):
     y, c = place()
     sibling = at_chip(y, 1 - c)
     arrived = greet([at_chip(ring(y, k), c) for k in (1, 2, 3)] + [sibling])
@@ -513,39 +569,82 @@
     ]
     for swap in swaps:
         swap.start()
-    keeps[0].wait()
-    swaps[0].wait()
-    for k in ORDER:
-        target = ring(y, k)
-        out_w[target] = (own_w[target].astype(F32) + in_w[target].astype(F32)).astype(BF)
-        remote(out_w.at[target], out_wide.at[y], ysend.at[k - 1], yrecv.at[k - 1], at_chip(target, c)).start()
-    out_wide[y] = (own_w[y].astype(F32) + in_w[y].astype(F32)).astype(BF)
+    wide_start(wide, own_w, in_w, out_w, out_wide, keeps[0], swaps[0], y, c, ysend, yrecv)
     keeps[1].wait()
     swaps[1].wait()
     out_tall[...] = (own_t[...].astype(F32) + in_t[...].astype(F32)).astype(BF)
-    for k in (1, 3, 2):
-        remote(out_w.at[ring(y, k)], out_wide.at[ring(y, 4 - k)], ysend.at[k - 1], yrecv.at[k - 1],
-               at_chip(ring(y, k), c)).wait()
-
-
-def run_collect(wide, tall, number):
-    width = wide.shape[-1]
-    rows = tall.shape[1]
-    outs = [shape((4, 136, width), BF), shape((rows, D), BF)]
-    wide_buf, tall_buf = pltpu.VMEM((4, 136, width), BF), pltpu.VMEM((rows, D), BF)
-    return pl.pallas_call(
-        collect,
-        name="collect_%d" % number,
-        out_shape=outs,
-        in_specs=[ANY] * 2,
-        out_specs=[VMEM] * 2,
-        scratch_shapes=[wide_buf, tall_buf, wide_buf, tall_buf, wide_buf, DMA((2,)), DMA((2,)), DMA((2,)), DMA((3,)), DMA((3,))],
-        compiler_params=pltpu.CompilerParams(collective_id=number, has_side_effects=True, vmem_limit_bytes=LIMIT),
-    )(wide, tall)
-
-
-def by_chip(options, y):
-    return lax.dynamic_index_in_dim(jnp.stack(options), y, 0, keepdims=False)
+    wide_wait(out_w, out_wide, y, c, ysend, yrecv)
+
+
+def collect_attend(wide, rows, one, two, heads, out_wide, out_rows_ref, out_small,
+                   own_w, own_r, in_w, in_r, out_w, edge, small, in_small, in_small_y,
+                   local, csend, crecv, ysend, yrecv, esend, erecv, ssend, srecv):
+    y, c = place()
+    sibling = at_chip(y, 1 - c)
+    arrived = greet([at_chip(ring(y, k), c) for k in (1, 2, 3)] + [sibling])
+    keeps = load([(wide.at[:, c], own_w), (rows, own_r)], local)
+    small[...] = jnp.zeros_like(small)
+    small[0:2] = one[0:2]
+    small[2:4] = two[0:2]
+    small[4:5] = one[2:3]
+    small[5:6] = two[3:4]
+    small[6:10] = chip_row(y, two[2:3])
+    for row, at in ((10, 2 * TH), (11, TH)):
+        small[row : row + 1, pl.ds(pl.multiple_of(256 * y, 256), 256)] = heads[0:1, at : at + 256]
+
+        @pl.when(y == 3)
+        def _():
+            small[row : row + 1, 1024:D] = heads[0:1, at + 256 : at + TH]
+
+    arrived()
+    swaps = [
+        remote(wide.at[:, 1 - c], in_w, csend.at[0], crecv.at[0], sibling),
+        remote(rows, in_r, csend.at[1], crecv.at[1], sibling),
+        remote(small, in_small, csend.at[2], crecv.at[2], sibling),
+    ]
+    for swap in swaps:
+        swap.start()
+    wide_start(wide, own_w, in_w, out_w, out_wide, keeps[0], swaps[0], y, c, ysend, yrecv)
+    keeps[1].wait()
+    swaps[1].wait()
+    own_r[...] = (own_r[...].astype(F32) + in_r[...].astype(F32)).astype(BF)
+    shift = remote(own_r.at[0:HD], edge, esend, erecv, at_chip(ring(y, 3), c))
+    shift.start()
+    swaps[2].wait()
+    small[...] = small[...] + in_small[...]
+    for k in (1, 2, 3):
+        remote(small, in_small_y.at[k - 1], ssend.at[k - 1], srecv.at[k - 1], at_chip(ring(y, k), c)).start()
+    shift.wait()
+
+    @pl.when(y < 3)
+    def _():
+        own_r[256:320] = edge[...]
+
+    out_rows_ref[...] = own_r[pl.ds(pl.multiple_of(16 * y, 16), 272)]
+    total = small[...]
+    for k in (1, 2, 3):
+        remote(small, in_small_y.at[k - 1], ssend.at[k - 1], srecv.at[k - 1], at_chip(ring(y, k), c)).wait()
+        total = total + in_small_y[k - 1]
+    out_small[...] = total
+    wide_wait(out_w, out_wide, y, c, ysend, yrecv)
+
+
+def run_collect_feed(e, wide, tall):
+    outs = [shape((4, 136, D), BF), shape((544, D), BF)]
+    wide_buf, tall_buf = pltpu.VMEM((4, 136, D), BF), pltpu.VMEM((544, D), BF)
+    scratch = [wide_buf, tall_buf, wide_buf, tall_buf, wide_buf, DMA((2,)), DMA((2,)), DMA((2,)), DMA((3,)), DMA((3,))]
+    return call(collect_feed, "collect_feed_%d" % e, 9 + e, outs, [ANY] * 2, scratch)(wide, tall)
+
+
+def run_collect_attend(e, wide, rows, one, two, heads):
+    outs = [shape((4, 136, TQKV), BF), shape((272, D), BF), shape((16, D), F32)]
+    wide_buf, rows_buf, small_buf = pltpu.VMEM((4, 136, TQKV), BF), pltpu.VMEM((TH, D), BF), pltpu.VMEM((16, D), F32)
+    scratch = [wide_buf, rows_buf, wide_buf, rows_buf, wide_buf, pltpu.VMEM((HD, D), BF), small_buf, small_buf,
+               pltpu.VMEM((3, 16, D), F32), DMA((2,)), DMA((3,)), DMA((3,)), DMA((3,)), DMA((3,)), DMA, DMA,
+               DMA((3,)), DMA((3,))]
+    return call(collect_attend, "collect_attend_%d" % e, 11 + e, outs, [ANY] * 2 + [VMEM] * 3, scratch)(
+        wide, rows, one, two, heads
+    )
 
 
 def split_heads(block):
@@ -573,85 +672,59 @@
     send_u = jnp.stack([weight_up[0][:, j * D : (j + 1) * D] for j in range(CHIPS)])
     tail = lax.ppermute(weight_out[0, 88:], "fsdp", [(i, (i + 2) % 8) for i in range(8)])
     send_o = jnp.concatenate([weight_out[0], tail, jnp.zeros((8, D), BF)], axis=0)
+    vectors = jnp.stack([norm_gain[0, 0], norm_bias[0, 0], norm_gain[0, 1], norm_bias[0, 1], bias_out[0], bias_down[0]])
     send_v = jnp.concatenate(
-        [bias_attn[0], bias_out[0], bias_up[0], bias_down[0], norm_gain[0].reshape(-1), norm_bias[0].reshape(-1),
-         jnp.zeros((416,), BF)]
-    ).reshape(16, 128)
+        [
+            lax.dynamic_update_slice(jnp.zeros((6, D), BF), vectors, (0, 136 * f)),
+            lax.dynamic_update_slice(jnp.zeros((4, D), BF), bias_up, (y, 544 * c)),
+            lax.dynamic_update_slice(jnp.zeros((6, D), BF), bias_attn, (f // 4, 272 * (f % 4))),
+        ]
+    )
     wa, wu, wd, wo, wv = run_spread(send_a, send_u, weight_down[0], send_o, send_v)
     wa = wa.reshape(2, D, TQKV)
     wu = wu.reshape(2, D, D)
     wd = wd.reshape(2, D, D)
-    wv = wv.reshape(2, 8, 2048).astype(F32)
-
-    def layer_params(e):
-        rows = jnp.concatenate([wo[e, 1, 136:184], wo[e, 0, :136], wo[e, 1, :136]], axis=0)
-        main = lax.dynamic_slice_in_dim(rows, 48 - 16 * y, 256, 0)
-        extra = jnp.where(y == 3, rows[256:320], jnp.zeros((HD, D), BF))
-        out_rows = jnp.concatenate([main, extra], axis=0)
-        v = wv[e]
-        attn = v[:, :272].reshape(-1)
-        gains = v[:, 1088:1360].reshape(8, 2, 136).transpose(1, 0, 2).reshape(2, D)
-        shifts = v[:, 1360:1632].reshape(8, 2, 136).transpose(1, 0, 2).reshape(2, D)
-        up = lax.dynamic_slice_in_dim(v, 2 * y, 2, 0)[:, 408:952].reshape(1, D)
-        vecs = jnp.concatenate(
-            [gains[0:1], shifts[0:1], gains[1:2], shifts[1:2], v[:, 272:408].reshape(1, D), v[:, 952:1088].reshape(1, D),
-             up, jnp.zeros((1, D), F32)], axis=0
-        )
-        bq, bv = by_chip(split_heads(attn[:D]), y), by_chip(split_heads(attn[D:]), y)
-        bias = jnp.concatenate([jnp.zeros((TH,), F32), bv, bq])[None]
-        return wa[e], out_rows, wu[e], wd[e], vecs, jnp.pad(bias, ((0, 7), (0, 0)))
-
-    params = [layer_params(e) for e in range(2)]
+    wo = jnp.concatenate([wo[:, 1, 136:184], wo[:, 0, :136], wo[:, 1, :136]], axis=1)
+    vecs = jnp.sum(wv.astype(F32), axis=(1, 2))
     micro = lax.dynamic_index_in_dim(inputs, s, 0, keepdims=False)[0]
     stream = micro.astype(F32)
     saved, acts = [], []
     for e in range(2):
-        w, wo_e, wu_e, wd_e, vecs, bias = params[e]
-        middle, *kept = run_attend_forward(stream, w, wo_e, vecs, bias)
-        result, *kept_two = run_feed_forward(middle, wu_e, wd_e, vecs)
+        middle, *kept = run_attend_forward(e, stream, wa, wo, vecs[e])
+        result, *kept_two = run_feed_forward(e, middle, wu, wd, vecs[e])
         saved.append((stream, kept, middle, kept_two))
         acts.append(result.astype(BF))
         stream = acts[-1].astype(F32)
     grad = lax.dynamic_index_in_dim(cotangent, s, 0, keepdims=False)[0].astype(F32)
-    in_grads, weight_grads, small_grads = [None, None], [None, None], [None, None]
+    in_grads, weight_grads = [None, None], [None, None]
     for e in (1, 0):
-        w, wo_e, wu_e, wd_e, vecs, bias = params[e]
         x, kept, middle, kept_two = saved[e]
-        grad_middle, grad_up, grad_down, small_two = run_feed_back(grad, wu_e, wd_e, vecs, middle, *kept_two)
-        up, down = run_collect(grad_up.reshape(4, 2, 136, D), grad_down.reshape(2, 544, D), 5)
-        up = lax.psum(up, ("section", "replica"))
-        down = lax.psum(down, ("section", "replica"))
-        grad_x, grad_attn, grad_out, small_one, small_bias = run_attend_back(grad_middle, w, wo_e, vecs, x, kept)
+        grad_middle, grad_up, grad_down, two = run_feed_back(e, grad, wu, wd, vecs[e], middle, *kept_two)
+        if e == 0:
+            grad_up, weight_grads[1] = lax.optimization_barrier((grad_up, weight_grads[1]))
+        up, down = run_collect_feed(e, grad_up.reshape(4, 2, 136, D), grad_down.reshape(2, 544, D))
+        grad_middle, up, down = lax.optimization_barrier((grad_middle, up, down))
+        up, down = lax.psum((up, down), ("replica", "section"))
+        grad_x, grad_attn, grad_out, one, heads = run_attend_back(e, grad_middle, wa, wo, vecs[e], x, kept)
         in_grads[e] = grad_x.astype(BF)
         grad = in_grads[e].astype(F32)
-        after = lax.ppermute(grad_out[:64], "fsdp", [(i, (i - 2) % 8) for i in range(8)])
-        after = jnp.where(y == 3, grad_out[256:], after)
-        chip_rows = lax.dynamic_slice_in_dim(jnp.concatenate([grad_out[:256], after], axis=0), 16 * y, 272, 0)
-        attn, out = run_collect(grad_attn.reshape(4, 2, 136, TQKV), chip_rows.reshape(2, 136, D), 6)
-        attn = lax.psum(attn, ("section", "replica"))
-        out = lax.psum(out, ("section", "replica"))
-        weight_grads[e] = (attn, out, up, down)
-        bq = lax.dynamic_update_slice(jnp.zeros((4, TH), F32), small_bias[0:1, 2 * TH :], (y, 0))
-        bv = lax.dynamic_update_slice(jnp.zeros((4, TH), F32), small_bias[0:1, TH : 2 * TH], (y, 0))
-        bu = lax.dynamic_update_slice(jnp.zeros((4, D), F32), small_two[2:3], (y, 0))
-        small_grads[e] = jnp.concatenate(
-            [join_heads(bq), join_heads(bv), small_one[2], bu.reshape(-1), small_two[3],
-             small_one[0], small_two[0], small_one[1], small_two[1]]
-        )
-    small = lax.psum(jnp.stack(small_grads), ("section", "fsdp", "replica"))
-    attn, out, up, down = (jnp.where(s == 0, a, b).astype(F32) for a, b in zip(weight_grads[0], weight_grads[1]))
-    small = lax.dynamic_index_in_dim(small, s, 0, keepdims=False)
+        attn, out, small = run_collect_attend(e, grad_attn.reshape(4, 2, 136, TQKV), grad_out, one, two, heads)
+        out = lax.dynamic_slice_in_dim(out, 136 * c, 136, 0)
+        out = jnp.concatenate([out, small.astype(BF)], axis=0)
+        grad, attn, out, up, down = lax.optimization_barrier((grad, attn, out, up, down))
+        attn, out = lax.psum((attn, out), ("section", "replica"))
+        out, small = out[:136], out[136:]
+        weight_grads[e] = (attn, out, up, down, small)
+    attn, out, up, down, small = (
+        jnp.where(s == 0, a, b).astype(F32) for a, b in zip(weight_grads[0], weight_grads[1])
+    )
     attn = jnp.concatenate(
         [join_heads([attn[j][:, i * TH : (i + 1) * TH] for j in range(CHIPS)]) for i in (2, 0, 1)], axis=-1
     )
     up = jnp.concatenate([up[j] for j in range(CHIPS)], axis=-1)
-
-    def piece(at, total):
-        size = total // 8
-        return lax.dynamic_slice_in_dim(small, at + f * size, size, 0)
-
-    def pair(at):
-        return jnp.stack([piece(at, D), piece(at + D, D)])
+    pieces = lax.dynamic_slice(small, (0, 136 * f), (6, 136))
+    piece_up = lax.dynamic_slice(small, (6 + y, 544 * c), (1, 544))
+    piece_attn = lax.dynamic_slice(small, (10 + f // 4, 272 * (f % 4)), (1, 272))
 
     def swap_layers(values):
         mine = jnp.where(s == 0, values[0], values[1])
@@ -667,12 +740,12 @@
         out[None],
         up[None],
         down[None],
-        piece(0, 2176)[None],
-        piece(2176, D)[None],
-        piece(3264, FF)[None],
-        piece(7616, D)[None],
-        pair(8704)[None],
-        pair(10880)[None],
+        piece_attn,
+        pieces[4:5],
+        piece_up,
+        pieces[5:6],
+        pieces[0:4:2][None],
+        pieces[1:4:2][None],
     )
 
 

time: 724 us -> 722 us (level)
  local copies, waits for them, and re-layouts: 46.2 us -> 22.8 us
  waiting for transfers between devices: 196 us -> 214 us
  Pallas kernels: 422 us -> 435 us
    slice x44 -> x5, local copies, waits for them, and re-layouts: 20.3 us -> 3.59 us  [the longest x2 1.76 us: on_device(): out, small = (out[:136], out[136:])]
    psum x2 -> x4, waiting for transfers between devices: 196 us -> 210 us  [the longest x2 149 us: on_device(): attn, out = lax.psum((attn, out), ('section', 'replica'))]
    pallas_call x12, Pallas kernels: 295 us -> 307 us  [the longest x2 58.3 us: run_attend_back(): call(functools.partial(attend_back, e), 'attend_back_%d' % e, 6 + e, outs...]
  transfers between devices with their start and end apart: 7 -> 7, of which waited for: 2 -> 5; matrix products, arithmetic and copies ran while one was open for 3% -> 4% of each run, Pallas kernels for 12% -> 19%
where the time goes in v2:
time: 722 us; the launch traced here: 714 us
  Pallas kernels  435 us (60%)
  waiting for transfers between devices  214 us (30%)
  other arithmetic  24.4 us (3%)
  local copies, waits for them, and re-layouts  22.8 us (3%)
  between operations  14.5 us (2%)
    psum x2, waiting for transfers between devices, on_device(): attn, out = lax.psum((attn, out), ('section', 'replica'))  149 us
    pallas_call x1, Pallas kernels, run_spread(): pl.pallas_call(spread, name='spread', out_shape=outs, in_specs=[ANY] * 5,...  128 us
    psum x2, waiting for transfers between devices, on_device(): up, down = lax.psum((up, down), ('replica', 'section'))  60.9 us
    pallas_call x2, Pallas kernels, run_attend_back(): call(functools.partial(attend_back, e), 'attend_back_%d' % e, 6 + e, outs...  58.3 us
    pallas_call x2, Pallas kernels, run_attend_forward(): call(functools.partial(attend_forward, e), 'attend_forward_%d' % e, e, ou...  55.2 us
    pallas_call x2, Pallas kernels, run_collect_attend(): call(collect_attend, 'collect_attend_%d' % e, 11 + e, outs, [ANY] * 2 + [...  54 us
    pallas_call x2, Pallas kernels, run_feed_back(): call(functools.partial(feed_back, e), 'feed_back_%d' % e, 4 + e, outs, [V...  47.4 us
    pallas_call x2, Pallas kernels, run_feed_forward(): call(functools.partial(feed_forward, e), 'feed_forward_%d' % e, 2 + e, ou...  46.1 us
  transfers between devices with their start and end apart: 7, of which 5 were waited for; matrix products, arithmetic and copies ran while one was open for 4% of the time, Pallas kernels for 19%

profile of v2, /device:TPU:4, one launch (start us, length us, event | category | flops | bytes accessed | tf_op | source)
XLA Modules:
  0.0 714.1 jit_solution(7322596158997679644)
XLA Ops:
  7.2 1.0 slice_bitcast_fusion.15
  8.2 1.6 collective-permute-start
  9.9 1.1 fusion.4
  11.0 1.3 fusion.3
  12.7 1.6 bitcast_convert_fusion.2.x
  14.4 1.6 bitcast_convert_fusion.1.grad
  18.2 1.3 pad_maximum_fusion.1.send_u
  19.5 1.1 pad_maximum_fusion.2.send_a
  20.6 1.8 maximum_maximum_fusion.send_o
  22.4 127.5 %spread.1 = (bf16[2,4,2,136,960]{4,3,2,1,0:T(8,128)(2,1)}, bf16[2,4,2,136,1088]{4,3,2,1,0:T(8,128)(2,1)}, bf16[2,2,544,1088]{3,2,1,0:T(8,128)(2,1)}, bf16[2,2,19...) custom-call(bf16[4,136,960]{2,1,0:T(8,128)(2,1)} %pad_maximum_fusion.2.send_a, ...), custom_call_target="tpu_custom_call" | custom-call | tf_op jit(solution)/shard_map/spread/pallas_call | solution.py:533
  149.9 1.4 slice_bitcast_fusion.5
  151.4 1.0 slice_bitcast_fusion.14
  153.1 1.2 pad_maximum_fusion.wo_hbm
  154.3 28.1 %attend_forward_0.1 = (f32[64,1088]{1,0:T(8,128)}, bf16[256,1088]{1,0:T(8,128)(2,1)}, bf16[256,320]{1,0:T(8,128)(2,1)}, bf16[256,640]{1,0:T(8,128)(2,1)}, bf16[2...) custom-call(f32[64,1088]{1,0:T(8,128)} %bitcast_convert_fusion.2.x, ...), custom_call_target="tpu_custom_call" | custom-call | flops 10000000 | bytes 10000 | tf_op jit(solution)/shard_map/attend_forward_0/pallas_call | solution.py:378
  182.4 23.1 %feed_forward_0.1 = (f32[64,1088]{1,0:T(8,128)}, bf16[256,1088]{1,0:T(8,128)(2,1)}, f32[256,1088]{1,0:T(8,128)}, bf16[256,1088]{1,0:T(8,128)(2,1)}) custom-call(f32[64,1088]{1,0:T(8,128)} %get-tuple-element.91.middle, bf16[2,1088,1088]{2,1,0:T(8,128)(2,1)} %bitcast.96, bf16[2,1088,1088]{2,1,0:T(8,128)(2,1)} %bitcast.100, f32[16,1088]{1,0:T(8,128)} %get-tuple-element.227.vecs), custom_call_target="tpu_custom_call" | custom-call | flops 10000000 | bytes 10000 | tf_op jit(solution)/shard_map/feed_forward_0/pallas_call | solution.py:384
  205.5 1.7 convert_convert_fusion.1.x
  207.2 27.1 %attend_forward_1.1 = (f32[64,1088]{1,0:T(8,128)}, bf16[256,1088]{1,0:T(8,128)(2,1)}, bf16[256,320]{1,0:T(8,128)(2,1)}, bf16[256,640]{1,0:T(8,128)(2,1)}, bf16[2...) custom-call(f32[64,1088]{1,0:T(8,128)} %convert_convert_fusion.1.x, ...), custom_call_target="tpu_custom_call" | custom-call | flops 10000000 | bytes 10000 | tf_op jit(solution)/shard_map/attend_forward_1/pallas_call | solution.py:378
  234.3 23.1 %feed_forward_1.1 = (f32[64,1088]{1,0:T(8,128)}, bf16[256,1088]{1,0:T(8,128)(2,1)}, f32[256,1088]{1,0:T(8,128)}, bf16[256,1088]{1,0:T(8,128)(2,1)}) custom-call(f32[64,1088]{1,0:T(8,128)} %get-tuple-element.95.middle, bf16[2,1088,1088]{2,1,0:T(8,128)(2,1)} %bitcast.97, bf16[2,1088,1088]{2,1,0:T(8,128)(2,1)} %bitcast.101, f32[16,1088]{1,0:T(8,128)} %get-tuple-element.226.vecs), custom_call_target="tpu_custom_call" | custom-call | flops 10000000 | bytes 10000 | tf_op jit(solution)/shard_map/feed_forward_1/pallas_call | solution.py:384
  257.4 25.1 %feed_back_1.1 = (f32[64,1088]{1,0:T(8,128)}, bf16[1088,1088]{1,0:T(8,128)(2,1)}, bf16[1088,1088]{1,0:T(8,128)(2,1)}, f32[8,1088]{1,0:T(8,128)}) custom-call(f32[64,1088]{1,0:T(8,128)} %bitcast_convert_fusion.1.grad, bf16[2,1088,1088]{2,1,0:T(8,128)(2,1)} %bitcast.98, bf16[2,1088,1088]{2,1,0:T(8,128)(2,1)} %bitcast.102, f32[16,1088]{1,0:T(8,128)} %get-tuple-element.226.vecs, ...), custom_call_target="tpu_custom_call" | custom-call | flops 10000000 | bytes 10000 | tf_op jit(solution)/shard_map/feed_back_1/pallas_call | solution.py:395
  282.5 22.7 %collect_feed_1.1 = (bf16[4,136,1088]{2,1,0:T(8,128)(2,1)}, bf16[544,1088]{1,0:T(8,128)(2,1)}) custom-call(bf16[4,2,136,1088]{3,2,1,0:T(8,128)(2,1)} %bitcast.110, bf16[2,544,1088]{2,1,0:T(8,128)(2,1)} %bitcast.111), custom_call_target="tpu_custom_call" | custom-call | flops 10000000 | bytes 10000 | tf_op jit(solution)/shard_map/collect_feed_1/pallas_call | solution.py:636
  305.3 29.0 %attend_back_1.1 = (f32[64,1088]{1,0:T(8,128)}, bf16[1088,960]{1,0:T(8,128)(2,1)}, bf16[320,1088]{1,0:T(8,128)(2,1)}, f32[8,1088]{1,0:T(8,128)}, f32[8,960]{1,0:T(8,128)}) custom-call(f32[64,1088]{1,0:T(8,128)} %get-tuple-element.105.grad, bf16[2,1088,960]{2,1,0:T(8,128)(2,1)} %bitcast.106, bf16[2,320,1088]{2,1,0:T(8,128)(2,1)} %pad_maximum_fusion.wo_hbm, ...), custom_call_target="tpu_custom_call" | custom-call | flops 10000000 | bytes 10000 | tf_op jit(solution)/shard_map/attend_back_1/pallas_call | solution.py:418
  334.4 27.1 %collect_attend_1.1 = (bf16[4,136,960]{2,1,0:T(8,128)(2,1)}, bf16[272,1088]{1,0:T(8,128)(2,1)}, f32[16,1088]{1,0:T(8,128)}) custom-call(bf16[4,2,136,960]{3,2,1,0:T(8,128)(2,1)} %bitcast.114, bf16[320,1088]{1,0:T(8,128)(2,1)} %get-tuple-element.114.rows, f32[8,1088]{1,0:T(8,128)} %get-tuple-element.115.one, f32[8,1088]{1,0:T(8,128)} %get-tuple-element.116.two, ...), custom_call_target="tpu_custom_call" | custom-call | flops 10000000 | bytes 10000 | tf_op jit(solution)/shard_map/collect_attend_1/pallas_call | solution.py:645
  361.5 0.9 convert_element_type.59
  362.4 1.0 constant_dynamic-slice_fusion.2
  363.4 0.8 pad_maximum_fusion.3
  364.9 32.3 %all-reduce.15.cloned.1.call-done = (bf16[4,136,1088]{2,1,0:T(8,128)(2,1)}, bf16[544,1088]{1,0:T(8,128)(2,1)}) async-done(((bf16[4,136,1088]{2,1,0:T(8,128)(2,1)}, bf16[544,1088]{1,0:T(8,128)(2,1)}), (bf16[4,136,1088]{2,1,0:T(8,128)(2,1)}, bf16[544,1088]{1,0:T(8,128)(2,1)})) %all-reduce.15.cloned.1.call-update) | async-done | bytes 2367504 | tf_op jit(solution)/shard_map/psum | solution.py:707
  397.4 1.2 collective-permute-start.1
  398.5 4.2 collective-permute-done.1
  402.8 22.2 %feed_back_0.1 = (f32[64,1088]{1,0:T(8,128)}, bf16[1088,1088]{1,0:T(8,128)(2,1)}, bf16[1088,1088]{1,0:T(8,128)(2,1)}, f32[8,1088]{1,0:T(8,128)}) custom-call(f32[64,1088]{1,0:T(8,128)} %convert_convert_fusion.grad, bf16[2,1088,1088]{2,1,0:T(8,128)(2,1)} %bitcast.99, bf16[2,1088,1088]{2,1,0:T(8,128)(2,1)} %bitcast.103, f32[16,1088]{1,0:T(8,128)} %get-tuple-element.227.vecs, ...), custom_call_target="tpu_custom_call" | custom-call | flops 10000000 | bytes 10000 | tf_op jit(solution)/shard_map/feed_back_0/pallas_call | solution.py:395
  425.1 64.2 %all-reduce.11.cloned.1.call-done = (bf16[4,136,960]{2,1,0:T(8,128)(2,1)}, bf16[152,1088]{1,0:T(8,128)(2,1)}) async-done(((bf16[4,136,960]{2,1,0:T(8,128)(2,1)}, bf16[152,1088]{1,0:T(8,128)(2,1)}), (bf16[4,136,960]{2,1,0:T(8,128)(2,1)}, bf16[152,1088]{1,0:T(8,128)(2,1)})) %all-reduce.11.cloned.1.call-update) | async-done | bytes 1375248 | tf_op jit(solution)/shard_map/psum | solution.py:715
  489.3 1.0 slice.308
  490.3 0.8 slice.309
  491.1 23.3 %collect_feed_0.1 = (bf16[4,136,1088]{2,1,0:T(8,128)(2,1)}, bf16[544,1088]{1,0:T(8,128)(2,1)}) custom-call(bf16[4,2,136,1088]{3,2,1,0:T(8,128)(2,1)} %bitcast.108, bf16[2,544,1088]{2,1,0:T(8,128)(2,1)} %bitcast.109), custom_call_target="tpu_custom_call" | custom-call | flops 10000000 | bytes 10000 | tf_op jit(solution)/shard_map/collect_feed_0/pallas_call | solution.py:636
  515.2 29.3 %attend_back_0.1 = (f32[64,1088]{1,0:T(8,128)}, bf16[1088,960]{1,0:T(8,128)(2,1)}, bf16[320,1088]{1,0:T(8,128)(2,1)}, f32[8,1088]{1,0:T(8,128)}, f32[8,960]{1,0:T(8,128)}) custom-call(f32[64,1088]{1,0:T(8,128)} %get-tuple-element.137.grad, bf16[2,1088,960]{2,1,0:T(8,128)(2,1)} %bitcast.107, bf16[2,320,1088]{2,1,0:T(8,128)(2,1)} %pad_maximum_fusion.wo_hbm, ...), custom_call_target="tpu_custom_call" | custom-call | flops 10000000 | bytes 10000 | tf_op jit(solution)/shard_map/attend_back_0/pallas_call | solution.py:418
  544.5 1.0 broadcast_select_fusion
  546.1 26.9 %collect_attend_0.1 = (bf16[4,136,960]{2,1,0:T(8,128)(2,1)}, bf16[272,1088]{1,0:T(8,128)(2,1)}, f32[16,1088]{1,0:T(8,128)}) custom-call(bf16[4,2,136,960]{3,2,1,0:T(8,128)(2,1)} %bitcast.113, bf16[320,1088]{1,0:T(8,128)(2,1)} %get-tuple-element.146.rows, f32[8,1088]{1,0:T(8,128)} %get-tuple-element.147.one, f32[8,1088]{1,0:T(8,128)} %get-tuple-element.148.two, ...), custom_call_target="tpu_custom_call" | custom-call | flops 10000000 | bytes 10000 | tf_op jit(solution)/shard_map/collect_attend_0/pallas_call | solution.py:645
  573.1 0.9 convert_element_type.61
  574.0 1.0 constant_dynamic-slice_fusion.1
  575.0 0.8 pad_maximum_fusion.4
  576.6 28.6 %all-reduce.13.cloned.1.call-done = (bf16[4,136,1088]{2,1,0:T(8,128)(2,1)}, bf16[544,1088]{1,0:T(8,128)(2,1)}) async-done(((bf16[4,136,1088]{2,1,0:T(8,128)(2,1)}, bf16[544,1088]{1,0:T(8,128)(2,1)}), (bf16[4,136,1088]{2,1,0:T(8,128)(2,1)}, bf16[544,1088]{1,0:T(8,128)(2,1)})) %all-reduce.13.cloned.1.call-update) | async-done | bytes 2367504 | tf_op jit(solution)/shard_map/psum | solution.py:707
  605.3 1.3 copy-done.4
  606.9 2.4 concatenate.45
  609.3 3.0 bitcast_convert_fusion
  612.3 84.8 %all-reduce.9.cloned.1.call-done = (bf16[4,136,960]{2,1,0:T(8,128)(2,1)}, bf16[152,1088]{1,0:T(8,128)(2,1)}) async-done(((bf16[4,136,960]{2,1,0:T(8,128)(2,1)}, bf16[152,1088]{1,0:T(8,128)(2,1)}), (bf16[4,136,960]{2,1,0:T(8,128)(2,1)}, bf16[152,1088]{1,0:T(8,128)(2,1)})) %all-reduce.9.cloned.1.call-update) | async-done | bytes 1375248 | tf_op jit(solution)/shard_map/psum | solution.py:715
  697.1 0.8 fusion.2
  699.2 1.5 select_convert_fusion.1
  702.2 0.9 fusion.1
  705.0 2.4 concatenate.44
  (84 shorter events, 11.4 us)
Async XLA Ops:
  7.2 5.2 copy-start.2
  7.2 390.1 %all-reduce.15.cloned.1.call-start = ((), (), s32[]{:S(2)}) async-start(), calls=%async_computation.3 | async-start | bytes 5013504 | tf_op jit(solution)/shard_map/psum | solution.py:707
  8.2 12.4 %collective-permute-start = (bf16[48,1088]{1,0:T(8,128)(2,1)S(1)}, bf16[48,1088]{1,0:T(8,128)(2,1)}, u32[]{:S(2)}, u32[]{:S(2)}) collective-permute-start(bf16[48,1088]{1,0:T(8,128)(2,1)S(1)} %slice_bitcast_fusion.15), channel_id=1, source_target_pairs={{0,16},{8,24},{16,32},{24,40},{32,48},{40,56},{48,0},{56,8},{1,17}... | collective-permute-start | bytes 313352 | tf_op jit(solution)/shard_map/ppermute | solution.py:673
  12.4 3.7 copy-start.11
  12.4 3.7 copy-start.12
  16.0 0.7 copy-start.15
  16.0 0.7 copy-start.16
  16.1 0.9 copy-start.14
  16.1 1.2 copy-start.13
  19.5 1.1 copy-start.9
  149.9 2.4 copy-start.8
  305.3 184.0 %all-reduce.11.cloned.1.call-start = ((), (), s32[]{:S(2)}) async-start(), calls=%async_computation.1 | async-start | bytes 2928640 | tf_op jit(solution)/shard_map/psum | solution.py:715
  361.5 2.7 copy-start
  363.4 33.9 %copy-start.1 = (f32[64,1088]{1,0:T(8,128)S(1)}, f32[64,1088]{1,0:T(8,128)}, u32[]{:S(2)}) copy-start(f32[64,1088]{1,0:T(8,128)} %get-tuple-element.94) | copy-start | bytes 835588
  363.4 33.9 %copy-start.5 = (f32[64,1088]{1,0:T(8,128)S(1)}, f32[64,1088]{1,0:T(8,128)}, u32[]{:S(2)}) copy-start(f32[64,1088]{1,0:T(8,128)} %get-tuple-element.96) | copy-start | bytes 835588
  397.3 208.0 %all-reduce.13.cloned.1.call-start = ((), (), s32[]{:S(2)}) async-start(), calls=%async_computation.2 | async-start | bytes 5013504 | tf_op jit(solution)/shard_map/psum | solution.py:707
  397.4 5.4 collective-permute-start.1
  514.4 182.7 %all-reduce.9.cloned.1.call-start = ((), (), s32[]{:S(2)}) async-start(), calls=%async_computation | async-start | bytes 2928640 | tf_op jit(solution)/shard_map/psum | solution.py:715
  545.5 30.2 %collective-permute-start.2 = (bf16[64,1088]{1,0:T(8,128)(2,1)S(1)}, bf16[64,1088]{1,0:T(8,128)(2,1)S(1)}, u32[]{:S(2)}, u32[]{:S(2)}) collective-permute-start(bf16[64,1088]{1,0:T(8,128)(2,1)S(1)} %broadcast_select_fusion), channel_id=1, source_target_pairs={{0,64},{64,0},{1,65},{65,1},{2,66},{66,2},{3,67},{67,3},{4,68},{68... | collective-permute-start | bytes 417800 | tf_op jit(solution)/shard_map/ppermute | solution.py:732
  573.1 2.7 copy-start.6
  575.8 29.4 %copy-start.3 = (bf16[4,136,1088]{2,1,0:T(8,128)(2,1)S(1)}, bf16[4,136,1088]{2,1,0:T(8,128)(2,1)}, u32[]{:S(2)}) copy-start(bf16[4,136,1088]{2,1,0:T(8,128)(2,1)} %get-tuple-element.160) | copy-start | bytes 3551236
  605.2 1.3 copy-start.4
  609.3 89.9 %copy-start.7 = (bf16[4,136,960]{2,1,0:T(8,128)(2,1)S(1)}, bf16[4,136,960]{2,1,0:T(8,128)(2,1)}, u32[]{:S(2)}) copy-start(bf16[4,136,960]{2,1,0:T(8,128)(2,1)} %get-tuple-element.156) | copy-start | bytes 3133444
  701.2 1.0 copy-start.10
Sparse Core Ops, SparseCore 0:
  305.4 91.8 all-reduce.14
  401.3 87.9 all-reduce.10
  514.5 90.6 all-reduce.12
  609.1 87.9 all-reduce.8

commit v3 on v2

--- a/solution.py
+++ b/solution.py
@@ -243,18 +243,23 @@
 
 
 def feed_back(e, grad, wu_hbm, wd_hbm, vecs, middle, normed, hidden, active, grad_middle, grad_up, grad_down, small,
-              wu, wd, full, gh, acc, out_buf, in_buf, ls, gs, gr, ss, sr):
+              wu, wd, full, gh, acc, out_buf, in_buf, ls, gs, gr, ss, sr, reduce=None):
     y, c = place()
-    arrived = greet([at_chip(ring(y, k), c) for k in (1, 2, 3)])
+    peers = [at_chip(ring(y, k), c) for k in (1, 2, 3)]
+    arrived = greet(peers) if reduce is None else greet_owners(peers + [at_chip(y, 1 - c)], reduce.pieces.layer)
     weights = load([(wu_hbm.at[e], wu), (wd_hbm.at[e], wd)], ls)
     own_rows = grad[...].astype(BF)
     slot(full, y)[...] = own_rows
     arrived()
     gather_start(full, y, c, gs, gr)
+    if reduce is not None:
+        reduce.begin(y, c)
     small[...] = jnp.zeros_like(small)
     small[3:4] = jnp.sum(own_rows.astype(F32), axis=0, keepdims=True)
     weights[1].wait()
     gather_wait(full, y, c, gs, gr)
+    if reduce is not None:
+        reduce.middle(y, c)
     rows = full[...]
     for at, size in chunks(D):
         slope = gelu_slope(hidden[:, at : at + size])
@@ -274,25 +279,30 @@
     small[0:1] = gain
     small[1:2] = shift
     grad_middle[...] = grad[...] + back
+    if reduce is not None:
+        reduce.finish()
 
 
 def attend_back(e, grad, w_hbm, wo_hbm, vecs, x, normed, queries, kv, kv_other, logsum, attended,
                 grad_x, grad_attn, grad_out, small, small_bias,
-                w, wo, full, ga, gj, part_out, part_in, part_own, acc, out_buf, in_buf, ls, gs, gr, ss, sr, ks, kr):
+                w, wo, full, ga, gj, part_out, part_in, part_own, rows_out, edge, acc, out_buf, in_buf, ls, gs, gr, ss, sr, ks, kr, es, er,
+                reduce):
     y, c = place()
     peers = [at_chip(ring(y, k), c) for k in (1, 2, 3)]
     sibling = at_chip(y, 1 - c)
-    arrived = greet(peers + [sibling])
+    arrived = greet_owners(peers + [sibling], e)
     weights = load([(w_hbm.at[e], w)] + out_rows(wo_hbm, wo, e, y), ls)
     own_rows = grad[...].astype(BF)
     slot(full, y)[...] = own_rows
     arrived()
     gather_start(full, y, c, gs, gr)
+    reduce.begin(y, c)
     small[...] = jnp.zeros_like(small)
     small[2:3] = jnp.sum(own_rows.astype(F32), axis=0, keepdims=True)
     own, other = masks(c)
     out_wait(weights, wo, y)
     gather_wait(full, y, c, gs, gr)
+    reduce.middle(y, c)
     ga[...] = dot_nt(full[...], wo[...]).astype(BF)
     for h in range(SLOTS):
         at = h * HD
@@ -316,7 +326,9 @@
     swap = remote(part_out, part_in, ks, kr, sibling)
     swap.start()
     for at, size in chunks(D):
-        grad_out[:, at : at + size] = dot_tn(attended[...], full[:, at : at + size]).astype(BF)
+        rows_out[:, at : at + size] = dot_tn(attended[...], full[:, at : at + size]).astype(BF)
+    lend = remote(rows_out.at[0:HD], edge, es, er, at_chip(ring(y, 3), c))
+    lend.start()
     weights[0].wait()
     swap.wait()
     gj[:, : 2 * TH] = (part_own[...] + part_in[...].astype(F32)).astype(BF)
@@ -333,6 +345,217 @@
     small[0:1] = gain
     small[1:2] = shift
     grad_x[...] = grad[...] + back
+    lend.wait()
+
+    @pl.when(y < 3)
+    def _():
+        rows_out[256:320] = edge[...]
+
+    grad_out[...] = rows_out[pl.ds(pl.multiple_of(16 * y, 16), 272)]
+    reduce.finish()
+
+
+def plane():
+    s, r = lax.axis_index("section"), lax.axis_index("replica")
+    return s, r // 2, r % 2, s * 8 + r
+
+
+def at_plane(q):
+    return {"section": q // 8, "replica": lax.rem(q, 8)}
+
+
+def greet_owners(targets, layer):
+    s, x, h, me = plane()
+    barrier = pltpu.get_barrier_semaphore()
+    for target in targets:
+        pl.semaphore_signal(barrier, inc=1, device_id=target, device_id_type=MESH)
+
+    @pl.when(s == layer)
+    def _():
+        for j in range(1, 16):
+            q = lax.rem(me + j, 16)
+            pl.semaphore_signal(barrier, inc=1, device_id=at_plane(q), device_id_type=MESH)
+
+    return lambda: pl.semaphore_wait(barrier, len(targets) + jnp.where(s == layer, 7, 8))
+
+
+class Pieces:
+    def __init__(self, layer, groups, send, recv):
+        self.layer, self.groups, self.send, self.recv = layer, groups, send, recv
+
+    def copies(self):
+        s, x, h, me = plane()
+        for g, (half, pieces, landing, out) in enumerate(self.groups):
+            for dx in (2, 1, 3, 0):
+                xt = lax.rem(x + dx, 4)
+                owner = self.layer * 8 + xt * 2 + half
+                rel = lax.rem(me - owner + 15, 16)
+                copy = remote(pieces.at[xt], landing.at[rel], self.send.at[g, dx], self.recv.at[g, rel], at_plane(owner))
+                yield me != owner, copy
+
+    def start(self):
+        for remote_one, copy in self.copies():
+            pl.when(remote_one)(copy.start)
+
+    def finish(self):
+        s, x, h, me = plane()
+        for remote_one, copy in self.copies():
+            pl.when(remote_one)(copy.wait_send)
+        for g, (half, pieces, landing, out) in enumerate(self.groups):
+            mine = jnp.logical_and(s == self.layer, h == half)
+
+            def collect(g=g, pieces=pieces, landing=landing, out=out):
+                for rel in range(15):
+                    remote(pieces.at[x], landing.at[rel], self.send.at[g, 0], self.recv.at[g, rel], at_plane(me)).wait_recv()
+                for at in range(0, 136, 8):
+                    total = pieces[x, at : at + 8].astype(F32)
+                    for rel in range(15):
+                        total = total + landing[rel, at : at + 8].astype(F32)
+                    out[at : at + 8] = total.astype(BF)
+
+            pl.when(mine)(collect)
+
+
+class FeedReduce:
+    def __init__(self, layer, up, down, out, own, other, landing, ls, cs, cr, send, recv):
+        self.sources = (up, down)
+        self.out, self.own, self.other = out, own, other
+        self.ls, self.cs, self.cr = ls, cs, cr
+        self.pieces = Pieces(layer, [(0, own.at[0], landing, out), (1, own.at[1], landing, out)], send, recv)
+
+    def keeps(self, c):
+        up, down = self.sources
+        return [
+            pltpu.make_async_copy(up.at[:, c], self.own.at[0], self.ls.at[0]),
+            pltpu.make_async_copy(down.at[c], self.own.at[1], self.ls.at[1]),
+        ]
+
+    def swaps(self, y, c):
+        up, down = self.sources
+        sibling = at_chip(y, 1 - c)
+        return [
+            remote(up.at[:, 1 - c], self.other.at[0], self.cs.at[0], self.cr.at[0], sibling),
+            remote(down.at[1 - c], self.other.at[1], self.cs.at[1], self.cr.at[1], sibling),
+        ]
+
+    def begin(self, y, c):
+        for copy in self.keeps(c) + self.swaps(y, c):
+            copy.start()
+        self.out[...] = jnp.zeros_like(self.out)
+
+    def middle(self, y, c):
+        for copy in self.keeps(c) + self.swaps(y, c):
+            copy.wait()
+
+        def add(i, carry):
+            self.own[i // 4, i % 4] = (
+                self.own[i // 4, i % 4].astype(F32) + self.other[i // 4, i % 4].astype(F32)
+            ).astype(BF)
+            return carry
+
+        lax.fori_loop(0, 8, add, 0)
+        self.pieces.start()
+
+    def finish(self):
+        self.pieces.finish()
+
+
+FEED_SCRATCH = [
+    pltpu.VMEM((2, 4, 136, D), BF),
+    pltpu.VMEM((2, 4, 136, D), BF),
+    pltpu.VMEM((15, 136, D), BF),
+    DMA((2,)),
+    DMA((2,)),
+    DMA((2,)),
+    DMA((2, 4)),
+    DMA((2, 15)),
+]
+
+
+class AttendReduce:
+    def __init__(self, layer, wide, rows, out_a, out_b, out_o, own_w, other_w, own_r, other_r, pa, pb, po,
+                 land_a, land_b, land_o, ls, cs, cr, send, recv):
+        self.wide, self.rows = wide, rows
+        self.outs = (out_a, out_b, out_o)
+        self.own_w, self.other_w, self.own_r, self.other_r = own_w, other_w, own_r, other_r
+        self.pa, self.pb, self.po = pa, pb, po
+        self.ls, self.cs, self.cr = ls, cs, cr
+        self.pieces = Pieces(
+            layer, [(0, pa, land_a, out_a), (1, pb, land_b, out_b), (1, po, land_o, out_o)], send, recv
+        )
+
+    def keeps(self, c):
+        return [
+            pltpu.make_async_copy(self.wide.at[:, c], self.own_w, self.ls.at[0]),
+            pltpu.make_async_copy(self.rows.at[c], self.own_r, self.ls.at[1]),
+        ]
+
+    def swaps(self, y, c):
+        sibling = at_chip(y, 1 - c)
+        return [
+            remote(self.wide.at[:, 1 - c], self.other_w, self.cs.at[0], self.cr.at[0], sibling),
+            remote(self.rows.at[1 - c], self.other_r, self.cs.at[1], self.cr.at[1], sibling),
+        ]
+
+    def begin(self, y, c):
+        for copy in self.keeps(c) + self.swaps(y, c):
+            copy.start()
+        for out in self.outs:
+            out[...] = jnp.zeros_like(out)
+
+    def middle(self, y, c):
+        for copy in self.keeps(c) + self.swaps(y, c):
+            copy.wait()
+        for i in range(4):
+            block = self.own_w[i].astype(F32) + self.other_w[i].astype(F32)
+            self.pa[i] = block[:, :640].astype(BF)
+            self.pb[i] = block[:, 640:].astype(BF)
+            chunk = self.own_r[:, 256 * i : 256 * i + 256].astype(F32) + self.other_r[:, 256 * i : 256 * i + 256].astype(F32)
+            self.po[i, :, :256] = chunk.astype(BF)
+            if i < 3:
+                self.po[i, :, 256:] = jnp.zeros((136, HD), BF)
+        chunk = self.own_r[:, 1024:].astype(F32) + self.other_r[:, 1024:].astype(F32)
+        self.po[3, :, 256:] = chunk.astype(BF)
+        self.pieces.start()
+
+    def finish(self):
+        self.pieces.finish()
+
+
+ATTEND_SCRATCH = [
+    pltpu.VMEM((4, 136, TQKV), BF),
+    pltpu.VMEM((4, 136, TQKV), BF),
+    pltpu.VMEM((136, D), BF),
+    pltpu.VMEM((136, D), BF),
+    pltpu.VMEM((4, 136, 640), BF),
+    pltpu.VMEM((4, 136, 320), BF),
+    pltpu.VMEM((4, 136, 320), BF),
+    pltpu.VMEM((15, 136, 640), BF),
+    pltpu.VMEM((15, 136, 320), BF),
+    pltpu.VMEM((15, 136, 320), BF),
+    DMA((2,)),
+    DMA((2,)),
+    DMA((2,)),
+    DMA((3, 4)),
+    DMA((3, 15)),
+]
+
+
+def feed_back_reduce(e, layer, grad, wu_hbm, wd_hbm, vecs, middle, normed, hidden, active, wide, rows,
+                     grad_middle, grad_up, grad_down, small, out_a, out_b, out_o, *scratch):
+    own, extra = scratch[: 4 + len(MOVE)], scratch[4 + len(MOVE) :]
+    reduce = AttendReduce(layer, wide, rows, out_a, out_b, out_o, *extra)
+    feed_back(e, grad, wu_hbm, wd_hbm, vecs, middle, normed, hidden, active, grad_middle, grad_up, grad_down, small,
+              *own, reduce=reduce)
+
+
+def attend_back_reduce(e, grad, w_hbm, wo_hbm, vecs, x, normed, queries, kv, kv_other, logsum, attended, up, down,
+                       grad_x, grad_attn, grad_out, small, small_bias, out, *scratch):
+    extra = scratch[len(scratch) - len(FEED_SCRATCH) :]
+    own = scratch[: len(scratch) - len(FEED_SCRATCH)]
+    reduce = FeedReduce(e, up, down, out, *extra)
+    attend_back(e, grad, w_hbm, wo_hbm, vecs, x, normed, queries, kv, kv_other, logsum, attended,
+                grad_x, grad_attn, grad_out, small, small_bias, *own, reduce=reduce)
 
 
 def shape(dims, kind):
@@ -384,7 +607,12 @@
     return call(functools.partial(feed_forward, e), "feed_forward_%d" % e, 2 + e, outs, [VMEM, ANY, ANY, VMEM], scratch)(middle, wu, wd, vecs)
 
 
-def run_feed_back(e, grad, wu, wd, vecs, middle, normed, hidden, active):
+PIECE_A = shape((136, 640), BF)
+PIECE_B = shape((136, 320), BF)
+PIECE_U = shape((136, D), BF)
+
+
+def run_feed_back(e, grad, wu, wd, vecs, middle, normed, hidden, active, before=None):
     outs = [shape((BLK, D), F32), shape((D, D), BF), shape((D, D), BF), shape((8, D), F32)]
     scratch = [
         pltpu.VMEM((D, D), BF),
@@ -392,18 +620,26 @@
         pltpu.VMEM((ROWS, D), BF),
         pltpu.VMEM((ROWS, D), BF),
     ] + MOVE
-    return call(functools.partial(feed_back, e), "feed_back_%d" % e, 4 + e, outs, [VMEM, ANY, ANY] + [VMEM] * 5, scratch)(
-        grad, wu, wd, vecs, middle, normed, hidden, active
-    )
-
-
-def run_attend_back(e, grad, w, wo, vecs, x, saved):
+    ins = [VMEM, ANY, ANY] + [VMEM] * 5
+    if before is None:
+        return call(functools.partial(feed_back, e), "feed_back_%d" % e, 4 + e, outs, ins, scratch)(
+            grad, wu, wd, vecs, middle, normed, hidden, active
+        )
+    outs += [PIECE_A, PIECE_B, PIECE_B]
+    body = functools.partial(feed_back_reduce, e, 1 - e)
+    return call(body, "feed_back_%d" % e, 4 + e, outs, ins + [ANY, ANY], scratch + ATTEND_SCRATCH)(
+        grad, wu, wd, vecs, middle, normed, hidden, active, *before
+    )
+
+
+def run_attend_back(e, grad, w, wo, vecs, x, saved, up, down):
     outs = [
         shape((BLK, D), F32),
         shape((D, TQKV), BF),
-        shape((TH, D), BF),
+        shape((272, D), BF),
         shape((8, D), F32),
         shape((8, TQKV), F32),
+        PIECE_U,
     ]
     scratch = [
         pltpu.VMEM((D, TQKV), BF),
@@ -414,9 +650,12 @@
         pltpu.VMEM((ROWS, 2 * TH), BF),
         pltpu.VMEM((ROWS, 2 * TH), BF),
         pltpu.VMEM((ROWS, 2 * TH), F32),
-    ] + MOVE + [DMA, DMA]
-    return call(functools.partial(attend_back, e), "attend_back_%d" % e, 6 + e, outs, [VMEM, ANY, ANY] + [VMEM] * 8, scratch)(
-        grad, w, wo, vecs, x, *saved
+        pltpu.VMEM((TH, D), BF),
+        pltpu.VMEM((HD, D), BF),
+    ] + MOVE + [DMA, DMA, DMA, DMA] + FEED_SCRATCH
+    body = functools.partial(attend_back_reduce, e)
+    return call(body, "attend_back_%d" % e, 6 + e, outs, [VMEM, ANY, ANY] + [VMEM] * 8 + [ANY, ANY], scratch)(
+        grad, w, wo, vecs, x, *saved, up, down
     )
 
 
@@ -541,109 +780,167 @@
     )(a, u, d, o, v)
 
 
-def wide_start(wide, own_w, in_w, out_w, out_wide, keep, swap, y, c, ysend, yrecv):
-    keep.wait()
-    swap.wait()
-    for k in ORDER:
-        target = ring(y, k)
-        out_w[target] = (own_w[target].astype(F32) + in_w[target].astype(F32)).astype(BF)
-        remote(out_w.at[target], out_wide.at[y], ysend.at[k - 1], yrecv.at[k - 1], at_chip(target, c)).start()
-    out_wide[y] = (own_w[y].astype(F32) + in_w[y].astype(F32)).astype(BF)
-
-
-def wide_wait(out_w, out_wide, y, c, ysend, yrecv):
-    for k in (1, 3, 2):
-        remote(out_w.at[ring(y, k)], out_wide.at[ring(y, 4 - k)], ysend.at[k - 1], yrecv.at[k - 1],
-               at_chip(ring(y, k), c)).wait()
-
-
-def collect_feed(wide, tall, out_wide, out_tall, own_w, own_t, in_w, in_t, out_w, local, csend, crecv, ysend, yrecv):
+def build_small(buf, one, two, heads, y):
+    buf[...] = jnp.zeros_like(buf)
+    buf[0:2] = one[0:2]
+    buf[2:4] = two[0:2]
+    buf[4:5] = one[2:3]
+    buf[5:6] = two[3:4]
+    buf[6:10] = chip_row(y, two[2:3])
+    for row, at in ((10, 2 * TH), (11, TH)):
+        buf[row : row + 1, pl.ds(pl.multiple_of(256 * y, 256), 256)] = heads[0:1, at : at + 256]
+
+        @pl.when(y == 3)
+        def _(row=row, at=at):
+            buf[row : row + 1, 1024:D] = heads[0:1, at + 256 : at + TH]
+
+
+def gather_pieces(wide, rows, piece_u, in_a, in_b, in_o, one_0, two_0, heads_0, one_1, two_1, heads_1,
+                  up, down, out_a, out_b, out_o, out_small,
+                  red_a, red_b, red_o, small, small_c, small_y, small_x, small_z, gs, gr, cs, cr, ys, yr, zs, zr, *extra):
     y, c = place()
+    s, x, h, me = plane()
+    r = 2 * x + h
     sibling = at_chip(y, 1 - c)
-    arrived = greet([at_chip(ring(y, k), c) for k in (1, 2, 3)] + [sibling])
-    keeps = load([(wide.at[:, c], own_w), (tall.at[c], own_t)], local)
-    arrived()
-    swaps = [
-        remote(wide.at[:, 1 - c], in_w, csend.at[0], crecv.at[0], sibling),
-        remote(tall.at[1 - c], in_t, csend.at[1], crecv.at[1], sibling),
+    peers = [at_chip(ring(y, k), c) for k in (1, 2, 3)]
+    reduce = AttendReduce(0, wide, rows, red_a, red_b, red_o, *extra)
+    barrier = pltpu.get_barrier_semaphore()
+    others = [at_plane(lax.rem(me + j, 16)) for j in range(1, 16)]
+    sources = [
+        {"fsdp": 2 * ring(y, k) + c, "replica": 2 * y + half} for k in (1, 2, 3) for half in (0, 1)
     ]
-    for swap in swaps:
-        swap.start()
-    wide_start(wide, own_w, in_w, out_w, out_wide, keeps[0], swaps[0], y, c, ysend, yrecv)
-    keeps[1].wait()
-    swaps[1].wait()
-    out_tall[...] = (own_t[...].astype(F32) + in_t[...].astype(F32)).astype(BF)
-    wide_wait(out_w, out_wide, y, c, ysend, yrecv)
-
-
-def collect_attend(wide, rows, one, two, heads, out_wide, out_rows_ref, out_small,
-                   own_w, own_r, in_w, in_r, out_w, edge, small, in_small, in_small_y,
-                   local, csend, crecv, ysend, yrecv, esend, erecv, ssend, srecv):
-    y, c = place()
-    sibling = at_chip(y, 1 - c)
-    arrived = greet([at_chip(ring(y, k), c) for k in (1, 2, 3)] + [sibling])
-    keeps = load([(wide.at[:, c], own_w), (rows, own_r)], local)
-    small[...] = jnp.zeros_like(small)
-    small[0:2] = one[0:2]
-    small[2:4] = two[0:2]
-    small[4:5] = one[2:3]
-    small[5:6] = two[3:4]
-    small[6:10] = chip_row(y, two[2:3])
-    for row, at in ((10, 2 * TH), (11, TH)):
-        small[row : row + 1, pl.ds(pl.multiple_of(256 * y, 256), 256)] = heads[0:1, at : at + 256]
-
-        @pl.when(y == 3)
+    for target in peers + [sibling] + others + sources:
+        pl.semaphore_signal(barrier, inc=1, device_id=target, device_id_type=MESH)
+    build_small(small.at[0], one_0, two_0, heads_0, y)
+    build_small(small.at[1], one_1, two_1, heads_1, y)
+    pl.semaphore_wait(barrier, 19 + jnp.where(x == y, 0, 8))
+    reduce.begin(y, c)
+    cross = remote(small, small_c, cs, cr, sibling)
+    cross.start()
+
+    kinds = [
+        (piece_u, up, 0, True),
+        (piece_u, down, 1, False),
+        (red_a, out_a, 0, True),
+        (red_b, out_b, 1, True),
+        (red_o, out_o, 1, False),
+    ]
+
+    def sends(i):
+        piece, out, half, moves = kinds[i]
+        copies = []
+        for j in (4, 2, 6, 3, 5, 1, 7, 0):
+            target = lax.rem(r + j, 8)
+            row = x if moves else y
+            index = y if moves else x
+            copy = remote(piece, out.at[index], gs.at[i, j], gr.at[i, index], {"fsdp": 2 * row + c, "replica": target})
+            copies.append((j, copy))
+        return copies
+
+    def start(i):
+        piece, out, half, moves = kinds[i]
+
+        @pl.when(h == half)
         def _():
-            small[row : row + 1, 1024:D] = heads[0:1, at + 256 : at + TH]
-
-    arrived()
-    swaps = [
-        remote(wide.at[:, 1 - c], in_w, csend.at[0], crecv.at[0], sibling),
-        remote(rows, in_r, csend.at[1], crecv.at[1], sibling),
-        remote(small, in_small, csend.at[2], crecv.at[2], sibling),
+            for j, copy in sends(i):
+                if j:
+                    copy.start()
+                elif moves:
+                    pl.when(x != y)(copy.start)
+
+                    @pl.when(x == y)
+                    def _():
+                        out[y] = piece[...]
+                else:
+                    out[x] = piece[...]
+
+    def finish(i):
+        piece, out, half, moves = kinds[i]
+
+        @pl.when(h == half)
+        def _():
+            for j, copy in sends(i):
+                if j:
+                    copy.wait_send()
+                elif moves:
+                    pl.when(x != y)(copy.wait_send)
+
+        for index in range(4):
+            own = jnp.logical_and(h == half, index == (y if moves else x))
+            if moves:
+                own = jnp.logical_and(own, x == y)
+            copy = remote(piece, out.at[index], gs.at[i, 0], gr.at[i, index], sibling)
+            pl.when(jnp.logical_not(own))(copy.wait_recv)
+
+    start(0)
+    start(1)
+    reduce.middle(y, c)
+    cross.wait()
+    small[...] = small[...] + small_c[...]
+    hops = [remote(small, small_y.at[k - 1], ys.at[k - 1], yr.at[k - 1], peers[k - 1]) for k in (1, 2, 3)]
+    for hop in hops:
+        hop.start()
+    for hop in hops:
+        hop.wait()
+    small_x[...] = (small[...] + small_y[0] + small_y[1] + small_y[2]).astype(BF)
+
+    def plane_copies():
+        for j in range(1, 16):
+            q = lax.rem(me + j, 16)
+            yield remote(small_x.at[q // 8], small_z.at[15 - j], zs.at[j - 1], zr.at[15 - j], at_plane(q))
+
+    for copy in plane_copies():
+        copy.start()
+    reduce.finish()
+
+    @pl.when(s == 1)
+    def _():
+        red_a[...] = in_a[...]
+        red_b[...] = in_b[...]
+        red_o[...] = in_o[...]
+
+    for i in (2, 3, 4):
+        start(i)
+    total = small_x[s].astype(F32)
+    for j, copy in enumerate(plane_copies()):
+        copy.wait_send()
+    for j in range(15):
+        remote(small_x.at[0], small_z.at[j], zs.at[j], zr.at[j], sibling).wait_recv()
+        total = total + small_z[j].astype(F32)
+    out_small[...] = total
+    for i in range(5):
+        finish(i)
+
+
+def run_gather_pieces(wide, rows, piece_u, pieces, smalls):
+    outs = [
+        shape((4, 136, D), BF),
+        shape((4, 136, D), BF),
+        shape((4, 136, 640), BF),
+        shape((4, 136, 320), BF),
+        shape((4, 136, 320), BF),
+        shape((16, D), F32),
     ]
-    for swap in swaps:
-        swap.start()
-    wide_start(wide, own_w, in_w, out_w, out_wide, keeps[0], swaps[0], y, c, ysend, yrecv)
-    keeps[1].wait()
-    swaps[1].wait()
-    own_r[...] = (own_r[...].astype(F32) + in_r[...].astype(F32)).astype(BF)
-    shift = remote(own_r.at[0:HD], edge, esend, erecv, at_chip(ring(y, 3), c))
-    shift.start()
-    swaps[2].wait()
-    small[...] = small[...] + in_small[...]
-    for k in (1, 2, 3):
-        remote(small, in_small_y.at[k - 1], ssend.at[k - 1], srecv.at[k - 1], at_chip(ring(y, k), c)).start()
-    shift.wait()
-
-    @pl.when(y < 3)
-    def _():
-        own_r[256:320] = edge[...]
-
-    out_rows_ref[...] = own_r[pl.ds(pl.multiple_of(16 * y, 16), 272)]
-    total = small[...]
-    for k in (1, 2, 3):
-        remote(small, in_small_y.at[k - 1], ssend.at[k - 1], srecv.at[k - 1], at_chip(ring(y, k), c)).wait()
-        total = total + in_small_y[k - 1]
-    out_small[...] = total
-    wide_wait(out_w, out_wide, y, c, ysend, yrecv)
-
-
-def run_collect_feed(e, wide, tall):
-    outs = [shape((4, 136, D), BF), shape((544, D), BF)]
-    wide_buf, tall_buf = pltpu.VMEM((4, 136, D), BF), pltpu.VMEM((544, D), BF)
-    scratch = [wide_buf, tall_buf, wide_buf, tall_buf, wide_buf, DMA((2,)), DMA((2,)), DMA((2,)), DMA((3,)), DMA((3,))]
-    return call(collect_feed, "collect_feed_%d" % e, 9 + e, outs, [ANY] * 2, scratch)(wide, tall)
-
-
-def run_collect_attend(e, wide, rows, one, two, heads):
-    outs = [shape((4, 136, TQKV), BF), shape((272, D), BF), shape((16, D), F32)]
-    wide_buf, rows_buf, small_buf = pltpu.VMEM((4, 136, TQKV), BF), pltpu.VMEM((TH, D), BF), pltpu.VMEM((16, D), F32)
-    scratch = [wide_buf, rows_buf, wide_buf, rows_buf, wide_buf, pltpu.VMEM((HD, D), BF), small_buf, small_buf,
-               pltpu.VMEM((3, 16, D), F32), DMA((2,)), DMA((3,)), DMA((3,)), DMA((3,)), DMA((3,)), DMA, DMA,
-               DMA((3,)), DMA((3,))]
-    return call(collect_attend, "collect_attend_%d" % e, 11 + e, outs, [ANY] * 2 + [VMEM] * 3, scratch)(
-        wide, rows, one, two, heads
+    scratch = [
+        pltpu.VMEM((136, 640), BF),
+        pltpu.VMEM((136, 320), BF),
+        pltpu.VMEM((136, 320), BF),
+        pltpu.VMEM((2, 16, D), F32),
+        pltpu.VMEM((2, 16, D), F32),
+        pltpu.VMEM((3, 2, 16, D), F32),
+        pltpu.VMEM((2, 16, D), BF),
+        pltpu.VMEM((15, 16, D), BF),
+        DMA((5, 8)),
+        DMA((5, 4)),
+        DMA,
+        DMA,
+        DMA((3,)),
+        DMA((3,)),
+        DMA((15,)),
+        DMA((15,)),
+    ] + ATTEND_SCRATCH
+    return call(gather_pieces, "gather_pieces", 9, outs, [ANY, ANY] + [VMEM] * 10, scratch)(
+        wide, rows, piece_u, *pieces, *smalls
     )
 
 
@@ -696,32 +993,30 @@
         acts.append(result.astype(BF))
         stream = acts[-1].astype(F32)
     grad = lax.dynamic_index_in_dim(cotangent, s, 0, keepdims=False)[0].astype(F32)
-    in_grads, weight_grads = [None, None], [None, None]
+    in_grads, smalls, piece_u, before = [None, None], [None, None], [None, None], None
     for e in (1, 0):
         x, kept, middle, kept_two = saved[e]
-        grad_middle, grad_up, grad_down, two = run_feed_back(e, grad, wu, wd, vecs[e], middle, *kept_two)
-        if e == 0:
-            grad_up, weight_grads[1] = lax.optimization_barrier((grad_up, weight_grads[1]))
-        up, down = run_collect_feed(e, grad_up.reshape(4, 2, 136, D), grad_down.reshape(2, 544, D))
-        grad_middle, up, down = lax.optimization_barrier((grad_middle, up, down))
-        up, down = lax.psum((up, down), ("replica", "section"))
-        grad_x, grad_attn, grad_out, one, heads = run_attend_back(e, grad_middle, wa, wo, vecs[e], x, kept)
+        grad_middle, grad_up, grad_down, two, *pieces = run_feed_back(
+            e, grad, wu, wd, vecs[e], middle, *kept_two, before=before
+        )
+        grad_x, grad_attn, grad_out, one, heads, piece_u[e] = run_attend_back(
+            e, grad_middle, wa, wo, vecs[e], x, kept, grad_up.reshape(4, 2, 136, D), grad_down.reshape(2, 4, 136, D)
+        )
         in_grads[e] = grad_x.astype(BF)
         grad = in_grads[e].astype(F32)
-        attn, out, small = run_collect_attend(e, grad_attn.reshape(4, 2, 136, TQKV), grad_out, one, two, heads)
-        out = lax.dynamic_slice_in_dim(out, 136 * c, 136, 0)
-        out = jnp.concatenate([out, small.astype(BF)], axis=0)
-        grad, attn, out, up, down = lax.optimization_barrier((grad, attn, out, up, down))
-        attn, out = lax.psum((attn, out), ("section", "replica"))
-        out, small = out[:136], out[136:]
-        weight_grads[e] = (attn, out, up, down, small)
-    attn, out, up, down, small = (
-        jnp.where(s == 0, a, b).astype(F32) for a, b in zip(weight_grads[0], weight_grads[1])
-    )
+        before = (grad_attn.reshape(4, 2, 136, TQKV), grad_out.reshape(2, 136, D))
+        smalls[e] = (one, two, heads)
+    up, down, part_a, part_b, part_o, small = run_gather_pieces(
+        *before, jnp.where(s == 0, piece_u[0], piece_u[1]), pieces, smalls[0] + smalls[1]
+    )
+    up, part_a, part_b, part_o = (a.astype(F32) for a in (up, part_a, part_b, part_o))
+    attn = [jnp.concatenate([part_a[j], part_b[j]], axis=-1) for j in range(CHIPS)]
     attn = jnp.concatenate(
         [join_heads([attn[j][:, i * TH : (i + 1) * TH] for j in range(CHIPS)]) for i in (2, 0, 1)], axis=-1
     )
+    out = join_heads([part_o[j] for j in range(CHIPS)])
     up = jnp.concatenate([up[j] for j in range(CHIPS)], axis=-1)
+    down = down.reshape(544, D).astype(F32)
     pieces = lax.dynamic_slice(small, (0, 136 * f), (6, 136))
     piece_up = lax.dynamic_slice(small, (6 + y, 544 * c), (1, 544))
     piece_attn = lax.dynamic_slice(small, (10 + f // 4, 272 * (f % 4)), (1, 272))

time: 722 us -> 631 us (0.87)
  waiting for transfers between devices: 214 us -> 0.01 us
  Pallas kernels: 435 us -> 557 us
  between operations: 14.5 us -> 1.38 us
  local copies, waits for them, and re-layouts: 22.8 us -> 30.5 us
    psum x4 -> x0, waiting for transfers between devices: 210 us -> none  [the longest x2 149 us: on_device(): attn, out = lax.psum((attn, out), ('section', 'replica'))]
    pallas_call x8 -> x5, Pallas kernels: 206 us -> 328 us  [the longest x2 144 us: run_attend_back(): call(body, 'attend_back_%d' % e, 6 + e, outs, [VMEM, ANY, ANY] + [VMEM] *...]
    slice x4 -> x10, local copies, waits for them, and re-layouts: 0.44 us -> 7.73 us  [join_heads(): blocks[j][..., :256]]
  transfers between devices with their start and end apart: 7 -> 3, of which waited for: 5 -> 0; matrix products, arithmetic and copies ran while one was open for 4% -> 7% of each run, Pallas kernels for 19% -> 53%
where the time goes in v3:
time: 631 us; the launch traced here: 619 us
  Pallas kernels  557 us (88%)
  local copies, waits for them, and re-layouts  30.5 us (5%)
  other arithmetic  25.5 us (4%)
    pallas_call x2, Pallas kernels, run_attend_back(): call(body, 'attend_back_%d' % e, 6 + e, outs, [VMEM, ANY, ANY] + [VMEM] *...  144 us
    pallas_call x1, Pallas kernels, run_spread(): pl.pallas_call(spread, name='spread', out_shape=outs, in_specs=[ANY] * 5,...  128 us
    pallas_call x1, Pallas kernels, run_gather_pieces(): call(gather_pieces, 'gather_pieces', 9, outs, [ANY, ANY] + [VMEM] * 10, s...  108 us
    pallas_call x2, Pallas kernels, run_attend_forward(): call(functools.partial(attend_forward, e), 'attend_forward_%d' % e, e, ou...  54.9 us
    pallas_call x1, Pallas kernels, run_feed_back(): call(body, 'feed_back_%d' % e, 4 + e, outs, ins + [ANY, ANY], scratch + A...  51.8 us
    pallas_call x2, Pallas kernels, run_feed_forward(): call(functools.partial(feed_forward, e), 'feed_forward_%d' % e, 2 + e, ou...  46.3 us
    pallas_call x1, Pallas kernels, run_feed_back(): call(functools.partial(feed_back, e), 'feed_back_%d' % e, 4 + e, outs, in...  24.7 us
  transfers between devices with their start and end apart: 3, of which 0 were waited for; matrix products, arithmetic and copies ran while one was open for 7% of the time, Pallas kernels for 53%

profile of v3, /device:TPU:4, one launch (start us, length us, event | category | flops | bytes accessed | tf_op | source)
XLA Modules:
  0.0 618.6 jit_solution(2863141389353081802)
XLA Ops:
  0.7 1.0 slice_bitcast_fusion.23
  1.7 1.6 collective-permute-start
  3.3 1.1 fusion.1
  4.4 1.3 fusion
  6.1 1.6 bitcast_convert_fusion.2.x
  7.8 1.7 bitcast_convert_fusion.1.grad
  11.7 1.3 pad_maximum_fusion.1.send_u
  12.9 1.1 pad_maximum_fusion.2.send_a
  14.1 1.8 maximum_maximum_fusion.send_o
  15.9 127.5 %spread.1 = (bf16[2,4,2,136,960]{4,3,2,1,0:T(8,128)(2,1)}, bf16[2,4,2,136,1088]{4,3,2,1,0:T(8,128)(2,1)}, bf16[2,2,544,1088]{3,2,1,0:T(8,128)(2,1)}, bf16[2,2,19...) custom-call(bf16[4,136,960]{2,1,0:T(8,128)(2,1)} %pad_maximum_fusion.2.send_a, ...), custom_call_target="tpu_custom_call" | custom-call | tf_op jit(solution)/shard_map/spread/pallas_call | solution.py:772
  143.4 1.4 slice_bitcast_fusion.5
  144.8 1.0 slice_bitcast_fusion.14
  146.6 1.2 pad_maximum_fusion.wo_hbm
  147.8 28.1 %attend_forward_0.1 = (f32[64,1088]{1,0:T(8,128)}, bf16[256,1088]{1,0:T(8,128)(2,1)}, bf16[256,320]{1,0:T(8,128)(2,1)}, bf16[256,640]{1,0:T(8,128)(2,1)}, bf16[2...) custom-call(f32[64,1088]{1,0:T(8,128)} %bitcast_convert_fusion.2.x, ...), custom_call_target="tpu_custom_call" | custom-call | flops 10000000 | bytes 10000 | tf_op jit(solution)/shard_map/attend_forward_0/pallas_call | solution.py:601
  175.9 23.1 %feed_forward_0.1 = (f32[64,1088]{1,0:T(8,128)}, bf16[256,1088]{1,0:T(8,128)(2,1)}, f32[256,1088]{1,0:T(8,128)}, bf16[256,1088]{1,0:T(8,128)(2,1)}) custom-call(f32[64,1088]{1,0:T(8,128)} %get-tuple-element.71.middle, bf16[2,1088,1088]{2,1,0:T(8,128)(2,1)} %bitcast.112, bf16[2,1088,1088]{2,1,0:T(8,128)(2,1)} %bitcast.116, f32[16,1088]{1,0:T(8,128)} %get-tuple-element.183.vecs), custom_call_target="tpu_custom_call" | custom-call | flops 10000000 | bytes 10000 | tf_op jit(solution)/shard_map/feed_forward_0/pallas_call | solution.py:607
  199.0 1.7 convert_convert_fusion.1.x
  200.7 26.8 %attend_forward_1.1 = (f32[64,1088]{1,0:T(8,128)}, bf16[256,1088]{1,0:T(8,128)(2,1)}, bf16[256,320]{1,0:T(8,128)(2,1)}, bf16[256,640]{1,0:T(8,128)(2,1)}, bf16[2...) custom-call(f32[64,1088]{1,0:T(8,128)} %convert_convert_fusion.1.x, ...), custom_call_target="tpu_custom_call" | custom-call | flops 10000000 | bytes 10000 | tf_op jit(solution)/shard_map/attend_forward_1/pallas_call | solution.py:601
  227.5 23.2 %feed_forward_1.1 = (f32[64,1088]{1,0:T(8,128)}, bf16[256,1088]{1,0:T(8,128)(2,1)}, f32[256,1088]{1,0:T(8,128)}, bf16[256,1088]{1,0:T(8,128)(2,1)}) custom-call(f32[64,1088]{1,0:T(8,128)} %get-tuple-element.75.middle, bf16[2,1088,1088]{2,1,0:T(8,128)(2,1)} %bitcast.113, bf16[2,1088,1088]{2,1,0:T(8,128)(2,1)} %bitcast.117, f32[16,1088]{1,0:T(8,128)} %get-tuple-element.182.vecs), custom_call_target="tpu_custom_call" | custom-call | flops 10000000 | bytes 10000 | tf_op jit(solution)/shard_map/feed_forward_1/pallas_call | solution.py:607
  250.7 1.7 broadcast_select_fusion.3
  252.3 2.5 collective-permute-start.1
  254.8 24.7 %feed_back_1.1 = (f32[64,1088]{1,0:T(8,128)}, bf16[1088,1088]{1,0:T(8,128)(2,1)}, bf16[1088,1088]{1,0:T(8,128)(2,1)}, f32[8,1088]{1,0:T(8,128)}) custom-call(f32[64,1088]{1,0:T(8,128)} %bitcast_convert_fusion.1.grad, bf16[2,1088,1088]{2,1,0:T(8,128)(2,1)} %bitcast.114, bf16[2,1088,1088]{2,1,0:T(8,128)(2,1)} %bitcast.118, ...), custom_call_target="tpu_custom_call" | custom-call | flops 10000000 | bytes 10000 | tf_op jit(solution)/shard_map/feed_back_1/pallas_call | solution.py:625
  279.6 71.5 %attend_back_1.1 = (f32[64,1088]{1,0:T(8,128)}, bf16[1088,960]{1,0:T(8,128)(2,1)}, bf16[272,1088]{1,0:T(8,128)(2,1)}, f32[8,1088]{1,0:T(8,128)}, f32[8,960]{1,0:T(8,128)}, /*index=5*/bf16[136,1088]{1,0:T(8,128)(2,1)}) custom-call(f32[64,1088]{1,0:T(8,128)} %get-tuple-element.80.grad, bf16[2,1088,960]{2,1,0:T(8,128)(2,1)} %bitcast.122, ...), custom_call_target="tpu_custom_call" | custom-call | flops 10000000 | bytes 10000 | tf_op jit(solution)/shard_map/attend_back_1/pallas_call | solution.py:657
  351.0 1.7 convert_convert_fusion.grad
  352.7 51.8 %feed_back_0.1 = (f32[64,1088]{1,0:T(8,128)}, bf16[1088,1088]{1,0:T(8,128)(2,1)}, bf16[1088,1088]{1,0:T(8,128)(2,1)}, f32[8,1088]{1,0:T(8,128)}, bf16[136,640]{1...) custom-call(f32[64,1088]{1,0:T(8,128)} %convert_convert_fusion.grad, ...), custom_call_target="tpu_custom_call" | custom-call | flops 10000000 | bytes 10000 | tf_op jit(solution)/shard_map/feed_back_0/pallas_call | solution.py:630
  404.6 72.2 %attend_back_0.1 = (f32[64,1088]{1,0:T(8,128)}, bf16[1088,960]{1,0:T(8,128)(2,1)}, bf16[272,1088]{1,0:T(8,128)(2,1)}, f32[8,1088]{1,0:T(8,128)}, f32[8,960]{1,0:T(8,128)}, /*index=5*/bf16[136,1088]{1,0:T(8,128)(2,1)}) custom-call(f32[64,1088]{1,0:T(8,128)} %get-tuple-element.95.grad, bf16[2,1088,960]{2,1,0:T(8,128)(2,1)} %bitcast.123, ...), custom_call_target="tpu_custom_call" | custom-call | flops 10000000 | bytes 10000 | tf_op jit(solution)/shard_map/attend_back_0/pallas_call | solution.py:657
  476.8 1.7 broadcast_select_fusion.1
  478.5 1.7 broadcast_select_fusion.piece_u
  480.2 108.2 %gather_pieces.1 = (bf16[4,136,1088]{2,1,0:T(8,128)(2,1)}, bf16[4,136,1088]{2,1,0:T(8,128)(2,1)}, bf16[4,136,640]{2,1,0:T(8,128)(2,1)}, bf16[4,136,320]{2,1,0:T(...) custom-call(bf16[4,2,136,960]{3,2,1,0:T(8,128)(2,1)} %bitcast.129, bf16[2,136,1088]{2,1,0:T(8,128)(2,1)} %bitcast.140, ...), custom_call_target="tpu_custom_call" | custom-call | flops 10000000 | bytes 10000 | tf_op jit(solution)/shard_map/gather_pieces/pallas_call | solution.py:942
  588.4 1.1 convert_element_type.67
  589.5 0.8 slice_bitcast_fusion.19
  590.6 0.8 fusion.5
  591.3 0.8 fusion.4
  592.1 0.8 fusion.3
  593.7 1.2 copy-done.4
  595.3 1.1 copy-done.3
  596.4 1.6 bitcast_convert_fusion
  598.0 0.9 maximum_bitcast_fusion
  598.9 0.8 constant_dynamic-slice_fusion
  600.9 1.6 slice.320
  602.4 1.6 slice.322
  604.0 1.6 slice.324
  605.6 1.4 dynamic_slice.18
  606.9 1.4 dynamic_slice.20
  608.3 2.4 concatenate.42
  610.7 2.6 concatenate.40
  613.4 1.4 fusion.6
  614.9 0.9 select_bitcast_fusion.2
  616.6 0.9 select_bitcast_fusion
  (73 shorter events, 7.3 us)
Async XLA Ops:
  0.6 5.2 copy-start.2
  1.7 12.4 %collective-permute-start = (bf16[48,1088]{1,0:T(8,128)(2,1)S(1)}, bf16[48,1088]{1,0:T(8,128)(2,1)}, u32[]{:S(2)}, u32[]{:S(2)}) collective-permute-start(bf16[48,1088]{1,0:T(8,128)(2,1)S(1)} %slice_bitcast_fusion.23), channel_id=1, source_target_pairs={{0,16},{8,24},{16,32},{24,40},{32,48},{40,56},{48,0},{56,8},{1,17}... | collective-permute-start | bytes 313352 | tf_op jit(solution)/shard_map/ppermute | solution.py:970
  5.8 3.7 copy-start.12
  5.8 3.7 copy-start.13
  7.8 2.4 copy-start.16
  7.8 2.4 copy-start.17
  7.8 2.7 copy-start.15
  7.8 3.0 copy-start.14
  12.9 1.1 copy-start.9
  143.4 2.4 copy-start.8
  227.5 23.2 %copy-start = (f32[64,1088]{1,0:T(8,128)S(1)}, f32[64,1088]{1,0:T(8,128)}, u32[]{:S(2)}) copy-start(f32[64,1088]{1,0:T(8,128)} %get-tuple-element.74) | copy-start | bytes 835588
  252.3 362.5 %collective-permute-start.1 = (bf16[64,1088]{1,0:T(8,128)(2,1)}, bf16[64,1088]{1,0:T(8,128)(2,1)}, u32[]{:S(2)}, u32[]{:S(2)}) collective-permute-start(bf16[64,1088]{1,0:T(8,128)(2,1)} %broadcast_select_fusion.3), channel_id=1, source_target_pairs={{0,64},{64,0},{1,65},{65,1},{2,66},{66,2},{3,67},{67,3},{4,68},{68... | collective-permute-start | bytes 417800 | tf_op jit(solution)/shard_map/ppermute | solution.py:1027
  404.6 72.2 %copy-start.1 = (f32[64,1088]{1,0:T(8,128)S(1)}, f32[64,1088]{1,0:T(8,128)}, u32[]{:S(2)}) copy-start(f32[64,1088]{1,0:T(8,128)} %get-tuple-element.89) | copy-start | bytes 835588
  404.6 73.9 %copy-start.11 = (bf16[136,1088]{1,0:T(8,128)(2,1)S(1)}, bf16[136,1088]{1,0:T(8,128)(2,1)}, u32[]{:S(2)}) copy-start(bf16[136,1088]{1,0:T(8,128)(2,1)} %get-tuple-element.108) | copy-start | bytes 887812
  478.5 138.1 %collective-permute-start.2 = (bf16[64,1088]{1,0:T(8,128)(2,1)}, bf16[64,1088]{1,0:T(8,128)(2,1)}, u32[]{:S(2)}, u32[]{:S(2)}) collective-permute-start(bf16[64,1088]{1,0:T(8,128)(2,1)} %broadcast_select_fusion.1), channel_id=1, source_target_pairs={{0,64},{64,0},{1,65},{65,1},{2,66},{66,2},{3,67},{67,3},{4,68},{68... | collective-permute-start | bytes 417800 | tf_op jit(solution)/shard_map/ppermute | solution.py:1027
  588.4 2.0 copy-start.7
  590.6 3.0 copy-start.10
  593.6 1.3 copy-start.4
  595.1 1.3 copy-start.3
  610.7 4.1 copy-start.5
  613.4 3.2 copy-start.6

commit v4 on v3

--- a/solution.py
+++ b/solution.py
@@ -246,7 +246,7 @@
               wu, wd, full, gh, acc, out_buf, in_buf, ls, gs, gr, ss, sr, reduce=None):
     y, c = place()
     peers = [at_chip(ring(y, k), c) for k in (1, 2, 3)]
-    arrived = greet(peers) if reduce is None else greet_owners(peers + [at_chip(y, 1 - c)], reduce.pieces.layer)
+    arrived = greet(peers if reduce is None else peers + [at_chip(y, 1 - c)] + plane_peers())
     weights = load([(wu_hbm.at[e], wu), (wd_hbm.at[e], wd)], ls)
     own_rows = grad[...].astype(BF)
     slot(full, y)[...] = own_rows
@@ -290,7 +290,7 @@
     y, c = place()
     peers = [at_chip(ring(y, k), c) for k in (1, 2, 3)]
     sibling = at_chip(y, 1 - c)
-    arrived = greet_owners(peers + [sibling], e)
+    arrived = greet(peers + [sibling] + plane_peers())
     weights = load([(w_hbm.at[e], w)] + out_rows(wo_hbm, wo, e, y), ls)
     own_rows = grad[...].astype(BF)
     slot(full, y)[...] = own_rows
@@ -364,125 +364,160 @@
     return {"section": q // 8, "replica": lax.rem(q, 8)}
 
 
-def greet_owners(targets, layer):
+def x_peers(x, h):
+    return [{"replica": 2 * lax.rem(x + k, 4) + h} for k in (1, 2, 3)]
+
+
+def z_peers(s, h):
+    x = lax.axis_index("replica") // 2
+    return [
+        {"section": 1 - s},
+        {"section": 1 - s, "replica": 2 * x + 1 - h},
+        {"replica": 2 * x + 1 - h},
+    ]
+
+
+def plane_peers():
     s, x, h, me = plane()
-    barrier = pltpu.get_barrier_semaphore()
-    for target in targets:
-        pl.semaphore_signal(barrier, inc=1, device_id=target, device_id_type=MESH)
-
-    @pl.when(s == layer)
-    def _():
-        for j in range(1, 16):
-            q = lax.rem(me + j, 16)
-            pl.semaphore_signal(barrier, inc=1, device_id=at_plane(q), device_id_type=MESH)
-
-    return lambda: pl.semaphore_wait(barrier, len(targets) + jnp.where(s == layer, 7, 8))
-
-
-class Pieces:
-    def __init__(self, layer, groups, send, recv):
-        self.layer, self.groups, self.send, self.recv = layer, groups, send, recv
+    return x_peers(x, h) + z_peers(s, h)
+
+
+class AlongX:
+    def __init__(self, blocks, landing, out, send, recv):
+        self.blocks, self.landing, self.out, self.send, self.recv = blocks, landing, out, send, recv
 
     def copies(self):
         s, x, h, me = plane()
-        for g, (half, pieces, landing, out) in enumerate(self.groups):
-            for dx in (2, 1, 3, 0):
-                xt = lax.rem(x + dx, 4)
-                owner = self.layer * 8 + xt * 2 + half
-                rel = lax.rem(me - owner + 15, 16)
-                copy = remote(pieces.at[xt], landing.at[rel], self.send.at[g, dx], self.recv.at[g, rel], at_plane(owner))
-                yield me != owner, copy
+        targets = x_peers(x, h)
+        for k in ORDER:
+            yield remote(
+                self.blocks.at[lax.rem(x + k, 4)], self.landing.at[k - 1], self.send.at[k - 1], self.recv.at[k - 1],
+                targets[k - 1],
+            )
 
     def start(self):
-        for remote_one, copy in self.copies():
-            pl.when(remote_one)(copy.start)
+        for copy in self.copies():
+            copy.start()
 
     def finish(self):
         s, x, h, me = plane()
-        for remote_one, copy in self.copies():
-            pl.when(remote_one)(copy.wait_send)
-        for g, (half, pieces, landing, out) in enumerate(self.groups):
-            mine = jnp.logical_and(s == self.layer, h == half)
-
-            def collect(g=g, pieces=pieces, landing=landing, out=out):
-                for rel in range(15):
-                    remote(pieces.at[x], landing.at[rel], self.send.at[g, 0], self.recv.at[g, rel], at_plane(me)).wait_recv()
-                for at in range(0, 136, 8):
-                    total = pieces[x, at : at + 8].astype(F32)
-                    for rel in range(15):
-                        total = total + landing[rel, at : at + 8].astype(F32)
-                    out[at : at + 8] = total.astype(BF)
-
-            pl.when(mine)(collect)
+        for copy in self.copies():
+            copy.wait()
+
+        def add(i, carry):
+            rows = pl.ds(pl.multiple_of(8 * (i % 17), 8), 8)
+            total = self.blocks[x, i // 17, rows].astype(F32)
+            for k in range(3):
+                total = total + self.landing[k, i // 17, rows].astype(F32)
+            self.out[i // 17, rows] = total.astype(BF)
+            return carry
+
+        lax.fori_loop(0, 34, add, 0)
+
+
+def x_scratch(width):
+    return [pltpu.VMEM((4, 2, 136, width), BF), pltpu.VMEM((3, 2, 136, width), BF), DMA((3,)), DMA((3,))]
+
+
+class AlongZ:
+    def __init__(self, layer, blocks, landing, out, send, recv):
+        self.layer, self.blocks, self.landing, self.out, self.send, self.recv = layer, blocks, landing, out, send, recv
+
+    def copies(self):
+        s, x, h, me = plane()
+        for half in (0, 1):
+            owner = 2 * half + self.layer
+            rel = lax.rem(2 * h + s - owner + 3, 4)
+            target = {"section": jnp.int32(self.layer), "replica": 2 * x + half}
+            copy = remote(self.blocks.at[half], self.landing.at[rel], self.send.at[half], self.recv.at[rel], target)
+            yield 2 * h + s != owner, copy
+
+    def start(self):
+        for sends, copy in self.copies():
+            pl.when(sends)(copy.start)
+
+    def finish(self):
+        s, x, h, me = plane()
+        for sends, copy in self.copies():
+            pl.when(sends)(copy.wait_send)
+
+        @pl.when(s == self.layer)
+        def _():
+            for rel in range(3):
+                remote(self.blocks.at[0], self.landing.at[rel], self.send.at[0], self.recv.at[rel], {"section": 1 - s}).wait_recv()
+
+            def add(i, carry):
+                rows = pl.ds(pl.multiple_of(8 * i, 8), 8)
+                total = self.blocks[h, rows].astype(F32)
+                for rel in range(3):
+                    total = total + self.landing[rel, rows].astype(F32)
+                self.out[rows] = total.astype(BF)
+                return carry
+
+            lax.fori_loop(0, 17, add, 0)
+
+        @pl.when(s != self.layer)
+        def _():
+            self.out[...] = jnp.zeros_like(self.out)
+
+
+def z_scratch(width):
+    return [pltpu.VMEM((3, 136, width), BF), DMA((2,)), DMA((3,))]
 
 
 class FeedReduce:
-    def __init__(self, layer, up, down, out, own, other, landing, ls, cs, cr, send, recv):
+    def __init__(self, up, down, out, other, ls, cs, cr, *scratch):
         self.sources = (up, down)
-        self.out, self.own, self.other = out, own, other
-        self.ls, self.cs, self.cr = ls, cs, cr
-        self.pieces = Pieces(layer, [(0, own.at[0], landing, out), (1, own.at[1], landing, out)], send, recv)
+        self.other, self.ls, self.cs, self.cr = other, ls, cs, cr
+        self.along = AlongX(scratch[0], scratch[1], out, scratch[2], scratch[3])
+        self.blocks = scratch[0]
 
     def keeps(self, c):
         up, down = self.sources
         return [
-            pltpu.make_async_copy(up.at[:, c], self.own.at[0], self.ls.at[0]),
-            pltpu.make_async_copy(down.at[c], self.own.at[1], self.ls.at[1]),
+            pltpu.make_async_copy(up.at[:, c], self.blocks.at[:, 0], self.ls.at[0]),
+            pltpu.make_async_copy(down.at[c], self.blocks.at[:, 1], self.ls.at[1]),
         ]
 
     def swaps(self, y, c):
         up, down = self.sources
         sibling = at_chip(y, 1 - c)
         return [
-            remote(up.at[:, 1 - c], self.other.at[0], self.cs.at[0], self.cr.at[0], sibling),
-            remote(down.at[1 - c], self.other.at[1], self.cs.at[1], self.cr.at[1], sibling),
+            remote(up.at[:, 1 - c], self.other.at[:, 0], self.cs.at[0], self.cr.at[0], sibling),
+            remote(down.at[1 - c], self.other.at[:, 1], self.cs.at[1], self.cr.at[1], sibling),
         ]
 
     def begin(self, y, c):
         for copy in self.keeps(c) + self.swaps(y, c):
             copy.start()
-        self.out[...] = jnp.zeros_like(self.out)
 
     def middle(self, y, c):
         for copy in self.keeps(c) + self.swaps(y, c):
             copy.wait()
 
         def add(i, carry):
-            self.own[i // 4, i % 4] = (
-                self.own[i // 4, i % 4].astype(F32) + self.other[i // 4, i % 4].astype(F32)
+            self.blocks[i // 2, i % 2] = (
+                self.blocks[i // 2, i % 2].astype(F32) + self.other[i // 2, i % 2].astype(F32)
             ).astype(BF)
             return carry
 
         lax.fori_loop(0, 8, add, 0)
-        self.pieces.start()
+        self.along.start()
 
     def finish(self):
-        self.pieces.finish()
-
-
-FEED_SCRATCH = [
-    pltpu.VMEM((2, 4, 136, D), BF),
-    pltpu.VMEM((2, 4, 136, D), BF),
-    pltpu.VMEM((15, 136, D), BF),
-    DMA((2,)),
-    DMA((2,)),
-    DMA((2,)),
-    DMA((2, 4)),
-    DMA((2, 15)),
-]
+        self.along.finish()
+
+
+FEED_SCRATCH = [pltpu.VMEM((4, 2, 136, D), BF), DMA((2,)), DMA((2,)), DMA((2,))] + x_scratch(D)
 
 
 class AttendReduce:
-    def __init__(self, layer, wide, rows, out_a, out_b, out_o, own_w, other_w, own_r, other_r, pa, pb, po,
-                 land_a, land_b, land_o, ls, cs, cr, send, recv):
+    def __init__(self, wide, rows, out, own_w, other_w, own_r, other_r, ls, cs, cr, *scratch):
         self.wide, self.rows = wide, rows
-        self.outs = (out_a, out_b, out_o)
         self.own_w, self.other_w, self.own_r, self.other_r = own_w, other_w, own_r, other_r
-        self.pa, self.pb, self.po = pa, pb, po
         self.ls, self.cs, self.cr = ls, cs, cr
-        self.pieces = Pieces(
-            layer, [(0, pa, land_a, out_a), (1, pb, land_b, out_b), (1, po, land_o, out_o)], send, recv
-        )
+        self.along = AlongX(scratch[0], scratch[1], out, scratch[2], scratch[3])
+        self.blocks = scratch[0]
 
     def keeps(self, c):
         return [
@@ -500,26 +535,25 @@
     def begin(self, y, c):
         for copy in self.keeps(c) + self.swaps(y, c):
             copy.start()
-        for out in self.outs:
-            out[...] = jnp.zeros_like(out)
 
     def middle(self, y, c):
         for copy in self.keeps(c) + self.swaps(y, c):
             copy.wait()
+        blocks = self.blocks
         for i in range(4):
             block = self.own_w[i].astype(F32) + self.other_w[i].astype(F32)
-            self.pa[i] = block[:, :640].astype(BF)
-            self.pb[i] = block[:, 640:].astype(BF)
+            blocks[i, 0] = block[:, :640].astype(BF)
+            blocks[i, 1, :, :320] = block[:, 640:].astype(BF)
             chunk = self.own_r[:, 256 * i : 256 * i + 256].astype(F32) + self.other_r[:, 256 * i : 256 * i + 256].astype(F32)
-            self.po[i, :, :256] = chunk.astype(BF)
+            blocks[i, 1, :, 320:576] = chunk.astype(BF)
             if i < 3:
-                self.po[i, :, 256:] = jnp.zeros((136, HD), BF)
+                blocks[i, 1, :, 576:] = jnp.zeros((136, HD), BF)
         chunk = self.own_r[:, 1024:].astype(F32) + self.other_r[:, 1024:].astype(F32)
-        self.po[3, :, 256:] = chunk.astype(BF)
-        self.pieces.start()
+        blocks[3, 1, :, 576:] = chunk.astype(BF)
+        self.along.start()
 
     def finish(self):
-        self.pieces.finish()
+        self.along.finish()
 
 
 ATTEND_SCRATCH = [
@@ -527,35 +561,52 @@
     pltpu.VMEM((4, 136, TQKV), BF),
     pltpu.VMEM((136, D), BF),
     pltpu.VMEM((136, D), BF),
-    pltpu.VMEM((4, 136, 640), BF),
-    pltpu.VMEM((4, 136, 320), BF),
-    pltpu.VMEM((4, 136, 320), BF),
-    pltpu.VMEM((15, 136, 640), BF),
-    pltpu.VMEM((15, 136, 320), BF),
-    pltpu.VMEM((15, 136, 320), BF),
     DMA((2,)),
     DMA((2,)),
     DMA((2,)),
-    DMA((3, 4)),
-    DMA((3, 15)),
-]
-
-
-def feed_back_reduce(e, layer, grad, wu_hbm, wd_hbm, vecs, middle, normed, hidden, active, wide, rows,
-                     grad_middle, grad_up, grad_down, small, out_a, out_b, out_o, *scratch):
-    own, extra = scratch[: 4 + len(MOVE)], scratch[4 + len(MOVE) :]
-    reduce = AttendReduce(layer, wide, rows, out_a, out_b, out_o, *extra)
+] + x_scratch(640)
+
+
+class Both:
+    def __init__(self, first, along_z):
+        self.first, self.along_z = first, along_z
+
+    def begin(self, y, c):
+        self.first.begin(y, c)
+        if self.along_z is not None:
+            self.along_z.start()
+
+    def middle(self, y, c):
+        self.first.middle(y, c)
+
+    def finish(self):
+        self.first.finish()
+        if self.along_z is not None:
+            self.along_z.finish()
+
+
+def feed_back_reduce(e, grad, wu_hbm, wd_hbm, vecs, middle, normed, hidden, active, wide, rows, half_u,
+                     grad_middle, grad_up, grad_down, small, half_a, piece_u, *scratch):
+    count = 4 + len(MOVE)
+    own, extra, last = scratch[:count], scratch[count : count + len(ATTEND_SCRATCH)], scratch[count + len(ATTEND_SCRATCH) :]
+    reduce = Both(AttendReduce(wide, rows, half_a, *extra), AlongZ(1 - e, half_u, last[0], piece_u, *last[1:]))
     feed_back(e, grad, wu_hbm, wd_hbm, vecs, middle, normed, hidden, active, grad_middle, grad_up, grad_down, small,
               *own, reduce=reduce)
 
 
-def attend_back_reduce(e, grad, w_hbm, wo_hbm, vecs, x, normed, queries, kv, kv_other, logsum, attended, up, down,
-                       grad_x, grad_attn, grad_out, small, small_bias, out, *scratch):
-    extra = scratch[len(scratch) - len(FEED_SCRATCH) :]
-    own = scratch[: len(scratch) - len(FEED_SCRATCH)]
-    reduce = FeedReduce(e, up, down, out, *extra)
-    attend_back(e, grad, w_hbm, wo_hbm, vecs, x, normed, queries, kv, kv_other, logsum, attended,
-                grad_x, grad_attn, grad_out, small, small_bias, *own, reduce=reduce)
+def attend_back_reduce(e, later, grad, w_hbm, wo_hbm, vecs, x, normed, queries, kv, kv_other, logsum, attended, up, down,
+                       *refs):
+    refs = list(refs)
+    half_a = refs.pop(0) if later else None
+    outs, refs = refs[:5], refs[5:]
+    half_u = refs.pop(0)
+    piece_a = refs.pop(0) if later else None
+    count = 14 + len(MOVE)
+    own, extra, last = refs[:count], refs[count : count + len(FEED_SCRATCH)], refs[count + len(FEED_SCRATCH) :]
+    along_z = AlongZ(1 - e, half_a, last[0], piece_a, *last[1:]) if later else None
+    reduce = Both(FeedReduce(up, down, half_u, *extra), along_z)
+    attend_back(e, grad, w_hbm, wo_hbm, vecs, x, normed, queries, kv, kv_other, logsum, attended, *outs, *own,
+                reduce=reduce)
 
 
 def shape(dims, kind):
@@ -607,9 +658,8 @@
     return call(functools.partial(feed_forward, e), "feed_forward_%d" % e, 2 + e, outs, [VMEM, ANY, ANY, VMEM], scratch)(middle, wu, wd, vecs)
 
 
-PIECE_A = shape((136, 640), BF)
-PIECE_B = shape((136, 320), BF)
-PIECE_U = shape((136, D), BF)
+HALF_A, HALF_U = shape((2, 136, 640), BF), shape((2, 136, D), BF)
+PIECE_A, PIECE_U = shape((136, 640), BF), shape((136, D), BF)
 
 
 def run_feed_back(e, grad, wu, wd, vecs, middle, normed, hidden, active, before=None):
@@ -625,21 +675,21 @@
         return call(functools.partial(feed_back, e), "feed_back_%d" % e, 4 + e, outs, ins, scratch)(
             grad, wu, wd, vecs, middle, normed, hidden, active
         )
-    outs += [PIECE_A, PIECE_B, PIECE_B]
-    body = functools.partial(feed_back_reduce, e, 1 - e)
-    return call(body, "feed_back_%d" % e, 4 + e, outs, ins + [ANY, ANY], scratch + ATTEND_SCRATCH)(
+    outs += [HALF_A, PIECE_U]
+    scratch = scratch + ATTEND_SCRATCH + z_scratch(D)
+    return call(functools.partial(feed_back_reduce, e), "feed_back_%d" % e, 4 + e, outs, ins + [ANY, ANY, VMEM], scratch)(
         grad, wu, wd, vecs, middle, normed, hidden, active, *before
     )
 
 
-def run_attend_back(e, grad, w, wo, vecs, x, saved, up, down):
+def run_attend_back(e, grad, w, wo, vecs, x, saved, up, down, half_a=None):
     outs = [
         shape((BLK, D), F32),
         shape((D, TQKV), BF),
         shape((272, D), BF),
         shape((8, D), F32),
         shape((8, TQKV), F32),
-        PIECE_U,
+        HALF_U,
     ]
     scratch = [
         pltpu.VMEM((D, TQKV), BF),
@@ -653,13 +703,18 @@
         pltpu.VMEM((TH, D), BF),
         pltpu.VMEM((HD, D), BF),
     ] + MOVE + [DMA, DMA, DMA, DMA] + FEED_SCRATCH
-    body = functools.partial(attend_back_reduce, e)
-    return call(body, "attend_back_%d" % e, 6 + e, outs, [VMEM, ANY, ANY] + [VMEM] * 8 + [ANY, ANY], scratch)(
-        grad, w, wo, vecs, x, *saved, up, down
-    )
-
-
-def spread(send_a, send_u, send_d, send_o, send_v, wa, wu, wd, wo, wv, local, ysend, yrecv, zsend, zrecv, csend, crecv):
+    later = half_a is not None
+    body = functools.partial(attend_back_reduce, e, later)
+    ins = [VMEM, ANY, ANY] + [VMEM] * 8 + [ANY, ANY]
+    more = []
+    if later:
+        outs, scratch, ins, more = outs + [PIECE_A], scratch + z_scratch(640), ins + [VMEM], [half_a]
+    return call(body, "attend_back_%d" % e, 6 + e, outs, ins, scratch)(
+        grad, w, wo, vecs, x, *saved, up, down, *more
+    )
+
+
+def spread(send_a, send_u, send_d, send_o, send_v, wa, wu, wd, wo, wv, hold_a, hold_u, hold_d, hold_o, hold_v, local, ysend, yrecv, zsend, zrecv, csend, crecv):
     s = lax.axis_index("section")
     y, c = place()
     replica = lax.axis_index("replica")
@@ -669,15 +724,20 @@
     sibling = at_chip(y, 1 - c)
     peers = [at_chip(ring(y, k), c) for k in (1, 2, 3)]
     arrived = greet(peers + [sibling, near, far])
+    brought = load(
+        [(send_a.at[y], hold_a), (send_u.at[y], hold_u), (send_d, hold_d), (send_o, hold_o), (send_v, hold_v)], local.at[0]
+    )
+    for copy in brought:
+        copy.wait()
     keeps = load(
         [
-            (send_a.at[y], wa.at[s, y, c]),
-            (send_u.at[y], wu.at[s, y, c]),
-            (send_d, wd.at[s, c]),
-            (send_o, wo.at[s, c]),
-            (send_v, wv.at[s, y, c]),
+            (hold_a, wa.at[s, y, c]),
+            (hold_u, wu.at[s, y, c]),
+            (hold_d, wd.at[s, c]),
+            (hold_o, wo.at[s, c]),
+            (hold_v, wv.at[s, y, c]),
         ],
-        local,
+        local.at[1],
     )
     arrived()
 
@@ -775,7 +835,14 @@
         out_shape=outs,
         in_specs=[ANY] * 5,
         out_specs=[ANY] * 5,
-        scratch_shapes=[DMA((5,)), DMA((3, 3)), DMA((3, 3)), DMA((8,)), DMA((8,)), DMA((2, 5)), DMA((2, 5))],
+        scratch_shapes=[
+            pltpu.VMEM((136, TQKV), BF),
+            pltpu.VMEM((136, D), BF),
+            pltpu.VMEM((544, D), BF),
+            pltpu.VMEM((192, D), BF),
+            pltpu.VMEM((16, D), BF),
+            DMA((2, 5)), DMA((3, 3)), DMA((3, 3)), DMA((8,)), DMA((8,)), DMA((2, 5)), DMA((2, 5)),
+        ],
         compiler_params=pltpu.CompilerParams(collective_id=8, has_side_effects=True),
     )(a, u, d, o, v)
 
@@ -795,91 +862,104 @@
             buf[row : row + 1, 1024:D] = heads[0:1, at + 256 : at + TH]
 
 
-def gather_pieces(wide, rows, piece_u, in_a, in_b, in_o, one_0, two_0, heads_0, one_1, two_1, heads_1,
-                  up, down, out_a, out_b, out_o, out_small,
-                  red_a, red_b, red_o, small, small_c, small_y, small_x, small_z, gs, gr, cs, cr, ys, yr, zs, zr, *extra):
+class Gather:
+    def __init__(self, piece, moved, out, number, moves, keep_from, ts, tr, gs, gr):
+        self.piece, self.moved, self.out, self.i = piece, moved, out, number
+        self.moves, self.keep_from = moves, keep_from
+        self.ts, self.tr, self.gs, self.gr = ts, tr, gs, gr
+
+    def transpose(self):
+        y, c = place()
+        s, x, h, me = plane()
+        copy = remote(self.piece, self.moved, self.ts.at[self.i], self.tr.at[self.i], {"fsdp": 2 * x + c, "replica": 2 * y + h})
+        cond = x != y
+        return copy, cond if self.moves else jnp.logical_and(cond, h == 0)
+
+    def start(self):
+        copy, cond = self.transpose()
+        pl.when(cond)(copy.start)
+
+    def copies(self):
+        s, x, h, me = plane()
+        r = 2 * x + h
+        for j in (4, 2, 6, 3, 5, 1, 7):
+            yield j, remote(self.piece, self.out.at[h, x], self.gs.at[self.i, j], self.gr.at[self.i, j], {"replica": lax.rem(r + j, 8)})
+
+    def spread(self):
+        s, x, h, me = plane()
+        copy, cond = self.transpose()
+        pl.when(cond)(copy.wait)
+
+        @pl.when(jnp.logical_and(cond, h == 0))
+        def _():
+            self.piece[...] = self.moved[...]
+
+        if self.moves:
+            @pl.when(jnp.logical_and(cond, h == 1))
+            def _():
+                lane = lax.broadcasted_iota(jnp.int32, self.piece.shape, 1)
+                merged = jnp.where(lane < self.keep_from, self.moved[...].astype(F32), self.piece[...].astype(F32))
+                self.piece[...] = merged.astype(BF)
+
+        self.out[h, x] = self.piece[...]
+        for j, copy in self.copies():
+            copy.start()
+
+    def finish(self):
+        s, x, h, me = plane()
+        r = 2 * x + h
+        for j, copy in self.copies():
+            copy.wait_send()
+            source = lax.rem(r - j + 8, 8)
+            place_in = self.out.at[source % 2, source // 2]
+            remote(place_in, place_in, self.gs.at[self.i, j], self.gr.at[self.i, j], {"replica": lax.rem(r + j, 8)}).wait_recv()
+
+
+def gather_pieces(wide, rows, half_u, done_u, done_a, one_0, two_0, heads_0, one_1, two_1, heads_1,
+                  out_u, out_a, out_small,
+                  piece_u, moved_u, piece_a, moved_a, half_a, small, small_c, small_y, small_x, small_z,
+                  ts, tr, gs, gr, cs, cr, ys, yr, zs, zr, *extra):
     y, c = place()
     s, x, h, me = plane()
-    r = 2 * x + h
     sibling = at_chip(y, 1 - c)
     peers = [at_chip(ring(y, k), c) for k in (1, 2, 3)]
-    reduce = AttendReduce(0, wide, rows, red_a, red_b, red_o, *extra)
+    reduce = AttendReduce(wide, rows, half_a, *extra[: len(ATTEND_SCRATCH)])
+    extra = extra[len(ATTEND_SCRATCH) :]
+    z_u = AlongZ(0, half_u, extra[0], piece_u, extra[1], extra[2])
+    z_a = AlongZ(0, half_a, extra[3], piece_a, extra[4], extra[5])
+    g_u = Gather(piece_u, moved_u, out_u, 0, False, 0, ts, tr, gs, gr)
+    g_a = Gather(piece_a, moved_a, out_a, 1, True, 320, ts, tr, gs, gr)
     barrier = pltpu.get_barrier_semaphore()
-    others = [at_plane(lax.rem(me + j, 16)) for j in range(1, 16)]
-    sources = [
-        {"fsdp": 2 * ring(y, k) + c, "replica": 2 * y + half} for k in (1, 2, 3) for half in (0, 1)
-    ]
-    for target in peers + [sibling] + others + sources:
+    for target in peers + [sibling] + [at_plane(lax.rem(me + j, 16)) for j in range(1, 16)]:
         pl.semaphore_signal(barrier, inc=1, device_id=target, device_id_type=MESH)
+
+    @pl.when(x != y)
+    def _():
+        pl.semaphore_signal(barrier, inc=1, device_id={"fsdp": 2 * x + c, "replica": 2 * y + h}, device_id_type=MESH)
+
     build_small(small.at[0], one_0, two_0, heads_0, y)
     build_small(small.at[1], one_1, two_1, heads_1, y)
-    pl.semaphore_wait(barrier, 19 + jnp.where(x == y, 0, 8))
+    pl.semaphore_wait(barrier, 19 + jnp.where(x == y, 0, 1))
+    z_u.start()
     reduce.begin(y, c)
     cross = remote(small, small_c, cs, cr, sibling)
     cross.start()
-
-    kinds = [
-        (piece_u, up, 0, True),
-        (piece_u, down, 1, False),
-        (red_a, out_a, 0, True),
-        (red_b, out_b, 1, True),
-        (red_o, out_o, 1, False),
-    ]
-
-    def sends(i):
-        piece, out, half, moves = kinds[i]
-        copies = []
-        for j in (4, 2, 6, 3, 5, 1, 7, 0):
-            target = lax.rem(r + j, 8)
-            row = x if moves else y
-            index = y if moves else x
-            copy = remote(piece, out.at[index], gs.at[i, j], gr.at[i, index], {"fsdp": 2 * row + c, "replica": target})
-            copies.append((j, copy))
-        return copies
-
-    def start(i):
-        piece, out, half, moves = kinds[i]
-
-        @pl.when(h == half)
-        def _():
-            for j, copy in sends(i):
-                if j:
-                    copy.start()
-                elif moves:
-                    pl.when(x != y)(copy.start)
-
-                    @pl.when(x == y)
-                    def _():
-                        out[y] = piece[...]
-                else:
-                    out[x] = piece[...]
-
-    def finish(i):
-        piece, out, half, moves = kinds[i]
-
-        @pl.when(h == half)
-        def _():
-            for j, copy in sends(i):
-                if j:
-                    copy.wait_send()
-                elif moves:
-                    pl.when(x != y)(copy.wait_send)
-
-        for index in range(4):
-            own = jnp.logical_and(h == half, index == (y if moves else x))
-            if moves:
-                own = jnp.logical_and(own, x == y)
-            copy = remote(piece, out.at[index], gs.at[i, 0], gr.at[i, index], sibling)
-            pl.when(jnp.logical_not(own))(copy.wait_recv)
-
-    start(0)
-    start(1)
     reduce.middle(y, c)
     cross.wait()
     small[...] = small[...] + small_c[...]
     hops = [remote(small, small_y.at[k - 1], ys.at[k - 1], yr.at[k - 1], peers[k - 1]) for k in (1, 2, 3)]
     for hop in hops:
         hop.start()
+    z_u.finish()
+
+    @pl.when(s == 1)
+    def _():
+        piece_u[...] = done_u[...]
+
+    g_u.start()
+    reduce.finish()
+    z_a.start()
+    g_u.spread()
     for hop in hops:
         hop.wait()
     small_x[...] = (small[...] + small_y[0] + small_y[1] + small_y[2]).astype(BF)
@@ -891,56 +971,51 @@
 
     for copy in plane_copies():
         copy.start()
-    reduce.finish()
+    z_a.finish()
 
     @pl.when(s == 1)
     def _():
-        red_a[...] = in_a[...]
-        red_b[...] = in_b[...]
-        red_o[...] = in_o[...]
-
-    for i in (2, 3, 4):
-        start(i)
+        piece_a[...] = done_a[...]
+
+    g_a.start()
+    g_a.spread()
     total = small_x[s].astype(F32)
-    for j, copy in enumerate(plane_copies()):
+    for copy in plane_copies():
         copy.wait_send()
     for j in range(15):
         remote(small_x.at[0], small_z.at[j], zs.at[j], zr.at[j], sibling).wait_recv()
         total = total + small_z[j].astype(F32)
     out_small[...] = total
-    for i in range(5):
-        finish(i)
-
-
-def run_gather_pieces(wide, rows, piece_u, pieces, smalls):
-    outs = [
-        shape((4, 136, D), BF),
-        shape((4, 136, D), BF),
-        shape((4, 136, 640), BF),
-        shape((4, 136, 320), BF),
-        shape((4, 136, 320), BF),
-        shape((16, D), F32),
-    ]
+    g_u.finish()
+    g_a.finish()
+
+
+def run_gather_pieces(wide, rows, half_u, done_u, done_a, smalls):
+    outs = [shape((2, 4, 136, D), BF), shape((2, 4, 136, 640), BF), shape((16, D), F32)]
     scratch = [
+        pltpu.VMEM((136, D), BF),
+        pltpu.VMEM((136, D), BF),
         pltpu.VMEM((136, 640), BF),
-        pltpu.VMEM((136, 320), BF),
-        pltpu.VMEM((136, 320), BF),
+        pltpu.VMEM((136, 640), BF),
+        pltpu.VMEM((2, 136, 640), BF),
         pltpu.VMEM((2, 16, D), F32),
         pltpu.VMEM((2, 16, D), F32),
         pltpu.VMEM((3, 2, 16, D), F32),
         pltpu.VMEM((2, 16, D), BF),
         pltpu.VMEM((15, 16, D), BF),
-        DMA((5, 8)),
-        DMA((5, 4)),
+        DMA((2,)),
+        DMA((2,)),
+        DMA((2, 8)),
+        DMA((2, 8)),
         DMA,
         DMA,
         DMA((3,)),
         DMA((3,)),
         DMA((15,)),
         DMA((15,)),
-    ] + ATTEND_SCRATCH
-    return call(gather_pieces, "gather_pieces", 9, outs, [ANY, ANY] + [VMEM] * 10, scratch)(
-        wide, rows, piece_u, *pieces, *smalls
+    ] + ATTEND_SCRATCH + z_scratch(D) + z_scratch(640)
+    return call(gather_pieces, "gather_pieces", 9, outs, [ANY, ANY] + [VMEM] * 9, scratch)(
+        wide, rows, half_u, done_u, done_a, *smalls
     )
 
 
@@ -993,30 +1068,31 @@
         acts.append(result.astype(BF))
         stream = acts[-1].astype(F32)
     grad = lax.dynamic_index_in_dim(cotangent, s, 0, keepdims=False)[0].astype(F32)
-    in_grads, smalls, piece_u, before = [None, None], [None, None], [None, None], None
+    in_grads, smalls, before, half_a = [None, None], [None, None], None, None
     for e in (1, 0):
         x, kept, middle, kept_two = saved[e]
-        grad_middle, grad_up, grad_down, two, *pieces = run_feed_back(
+        grad_middle, grad_up, grad_down, two, *reduced = run_feed_back(
             e, grad, wu, wd, vecs[e], middle, *kept_two, before=before
         )
-        grad_x, grad_attn, grad_out, one, heads, piece_u[e] = run_attend_back(
-            e, grad_middle, wa, wo, vecs[e], x, kept, grad_up.reshape(4, 2, 136, D), grad_down.reshape(2, 4, 136, D)
+        if reduced:
+            half_a, done_u = reduced
+        grad_x, grad_attn, grad_out, one, heads, half_u, *done_a = run_attend_back(
+            e, grad_middle, wa, wo, vecs[e], x, kept, grad_up.reshape(4, 2, 136, D), grad_down.reshape(2, 4, 136, D),
+            half_a,
         )
         in_grads[e] = grad_x.astype(BF)
         grad = in_grads[e].astype(F32)
-        before = (grad_attn.reshape(4, 2, 136, TQKV), grad_out.reshape(2, 136, D))
+        before = (grad_attn.reshape(4, 2, 136, TQKV), grad_out.reshape(2, 136, D), half_u)
         smalls[e] = (one, two, heads)
-    up, down, part_a, part_b, part_o, small = run_gather_pieces(
-        *before, jnp.where(s == 0, piece_u[0], piece_u[1]), pieces, smalls[0] + smalls[1]
-    )
-    up, part_a, part_b, part_o = (a.astype(F32) for a in (up, part_a, part_b, part_o))
-    attn = [jnp.concatenate([part_a[j], part_b[j]], axis=-1) for j in range(CHIPS)]
+    all_u, all_a, small = run_gather_pieces(*before, done_u, *done_a, smalls[0] + smalls[1])
+    all_u, all_a = all_u.astype(F32), all_a.astype(F32)
+    attn = [jnp.concatenate([all_a[0, j], all_a[1, j, :, :320]], axis=-1) for j in range(CHIPS)]
     attn = jnp.concatenate(
         [join_heads([attn[j][:, i * TH : (i + 1) * TH] for j in range(CHIPS)]) for i in (2, 0, 1)], axis=-1
     )
-    out = join_heads([part_o[j] for j in range(CHIPS)])
-    up = jnp.concatenate([up[j] for j in range(CHIPS)], axis=-1)
-    down = down.reshape(544, D).astype(F32)
+    out = join_heads([all_a[1, j, :, 320:] for j in range(CHIPS)])
+    up = jnp.concatenate([all_u[0, j] for j in range(CHIPS)], axis=-1)
+    down = all_u[1].reshape(544, D)
     pieces = lax.dynamic_slice(small, (0, 136 * f), (6, 136))
     piece_up = lax.dynamic_slice(small, (6 + y, 544 * c), (1, 544))
     piece_attn = lax.dynamic_slice(small, (10 + f // 4, 272 * (f % 4)), (1, 272))

time: 631 us -> 485 us (0.77)
  the two profiles are of different devices: /device:TPU:4 before, /device:TPU:96 now
where the time goes in v4:
time: 485 us; the launch traced here: 479 us
  Pallas kernels  423 us (87%)
  local copies, waits for them, and re-layouts  31.1 us (6%)
  other arithmetic  19.6 us (4%)
    pallas_call x1, Pallas kernels, run_gather_pieces(): call(gather_pieces, 'gather_pieces', 9, outs, [ANY, ANY] + [VMEM] * 9, sc...  113 us
    pallas_call x2, Pallas kernels, run_attend_back(): call(body, 'attend_back_%d' % e, 6 + e, outs, ins, scratch)  90.5 us
    pallas_call x1, Pallas kernels, run_spread(): pl.pallas_call(spread, name='spread', out_shape=outs, in_specs=[ANY] * 5,...  59.3 us
    pallas_call x2, Pallas kernels, run_attend_forward(): call(functools.partial(attend_forward, e), 'attend_forward_%d' % e, e, ou...  55.2 us
    pallas_call x2, Pallas kernels, run_feed_forward(): call(functools.partial(feed_forward, e), 'feed_forward_%d' % e, 2 + e, ou...  46.2 us
    pallas_call x1, Pallas kernels, run_feed_back(): call(functools.partial(feed_back_reduce, e), 'feed_back_%d' % e, 4 + e, o...  33.4 us
    pallas_call x1, Pallas kernels, run_feed_back(): call(functools.partial(feed_back, e), 'feed_back_%d' % e, 4 + e, outs, in...  25.1 us
  transfers between devices with their start and end apart: 3, of which 0 were waited for; matrix products, arithmetic and copies ran while one was open for 7% of the time, Pallas kernels for 0%

profile of v4, /device:TPU:96, one launch (start us, length us, event | category | flops | bytes accessed | tf_op | source)
XLA Modules:
  0.0 479.0 jit_solution(15786874561674079845)
XLA Ops:
  0.7 1.0 slice_bitcast_fusion.23
  1.7 1.6 collective-permute-start
  3.3 1.1 fusion.1
  4.4 1.3 fusion
  6.2 1.7 bitcast_convert_fusion.1.x
  7.8 1.6 bitcast_convert_fusion.grad
  11.7 1.3 pad_maximum_fusion.1.send_u
  12.9 1.1 pad_maximum_fusion.2.send_a
  14.1 1.8 maximum_maximum_fusion.send_o
  15.9 59.3 %spread.1 = (bf16[2,4,2,136,960]{4,3,2,1,0:T(8,128)(2,1)}, bf16[2,4,2,136,1088]{4,3,2,1,0:T(8,128)(2,1)}, bf16[2,2,544,1088]{3,2,1,0:T(8,128)(2,1)}, bf16[2,2,19...) custom-call(bf16[4,136,960]{2,1,0:T(8,128)(2,1)} %pad_maximum_fusion.2.send_a, ...), custom_call_target="tpu_custom_call" | custom-call | tf_op jit(solution)/shard_map/spread/pallas_call | solution.py:832
  75.2 1.4 slice_bitcast_fusion.5
  76.6 1.0 slice_bitcast_fusion.14
  78.4 1.2 pad_maximum_fusion.wo_hbm
  79.6 28.3 %attend_forward_0.1 = (f32[64,1088]{1,0:T(8,128)}, bf16[256,1088]{1,0:T(8,128)(2,1)}, bf16[256,320]{1,0:T(8,128)(2,1)}, bf16[256,640]{1,0:T(8,128)(2,1)}, bf16[2...) custom-call(f32[64,1088]{1,0:T(8,128)} %bitcast_convert_fusion.1.x, ...), custom_call_target="tpu_custom_call" | custom-call | flops 10000000 | bytes 10000 | tf_op jit(solution)/shard_map/attend_forward_0/pallas_call | solution.py:652
  107.9 23.1 %feed_forward_0.1 = (f32[64,1088]{1,0:T(8,128)}, bf16[256,1088]{1,0:T(8,128)(2,1)}, f32[256,1088]{1,0:T(8,128)}, bf16[256,1088]{1,0:T(8,128)(2,1)}) custom-call(f32[64,1088]{1,0:T(8,128)} %get-tuple-element.68.middle, bf16[2,1088,1088]{2,1,0:T(8,128)(2,1)} %bitcast.109, bf16[2,1088,1088]{2,1,0:T(8,128)(2,1)} %bitcast.113, f32[16,1088]{1,0:T(8,128)} %get-tuple-element.177.vecs), custom_call_target="tpu_custom_call" | custom-call | flops 10000000 | bytes 10000 | tf_op jit(solution)/shard_map/feed_forward_0/pallas_call | solution.py:658
  131.0 1.7 convert_convert_fusion.1.x
  132.7 26.9 %attend_forward_1.1 = (f32[64,1088]{1,0:T(8,128)}, bf16[256,1088]{1,0:T(8,128)(2,1)}, bf16[256,320]{1,0:T(8,128)(2,1)}, bf16[256,640]{1,0:T(8,128)(2,1)}, bf16[2...) custom-call(f32[64,1088]{1,0:T(8,128)} %convert_convert_fusion.1.x, ...), custom_call_target="tpu_custom_call" | custom-call | flops 10000000 | bytes 10000 | tf_op jit(solution)/shard_map/attend_forward_1/pallas_call | solution.py:652
  159.6 23.1 %feed_forward_1.1 = (f32[64,1088]{1,0:T(8,128)}, bf16[256,1088]{1,0:T(8,128)(2,1)}, f32[256,1088]{1,0:T(8,128)}, bf16[256,1088]{1,0:T(8,128)(2,1)}) custom-call(f32[64,1088]{1,0:T(8,128)} %get-tuple-element.72.middle, bf16[2,1088,1088]{2,1,0:T(8,128)(2,1)} %bitcast.110, bf16[2,1088,1088]{2,1,0:T(8,128)(2,1)} %bitcast.114, f32[16,1088]{1,0:T(8,128)} %get-tuple-element.176.vecs), custom_call_target="tpu_custom_call" | custom-call | flops 10000000 | bytes 10000 | tf_op jit(solution)/shard_map/feed_forward_1/pallas_call | solution.py:658
  182.7 25.1 %feed_back_1.1 = (f32[64,1088]{1,0:T(8,128)}, bf16[1088,1088]{1,0:T(8,128)(2,1)}, bf16[1088,1088]{1,0:T(8,128)(2,1)}, f32[8,1088]{1,0:T(8,128)}) custom-call(f32[64,1088]{1,0:T(8,128)} %bitcast_convert_fusion.grad, bf16[2,1088,1088]{2,1,0:T(8,128)(2,1)} %bitcast.111, bf16[2,1088,1088]{2,1,0:T(8,128)(2,1)} %bitcast.115, f32[16,1088]{1,0:T(8,128)} %get-tuple-element.176.vecs, ...), custom_call_target="tpu_custom_call" | custom-call | flops 10000000 | bytes 10000 | tf_op jit(solution)/shard_map/feed_back_1/pallas_call | solution.py:675
  207.8 45.7 %attend_back_1.1 = (f32[64,1088]{1,0:T(8,128)}, bf16[1088,960]{1,0:T(8,128)(2,1)}, bf16[272,1088]{1,0:T(8,128)(2,1)}, f32[8,1088]{1,0:T(8,128)}, f32[8,960]{1,0:T(8,128)}, /*index=5*/bf16[2,136,1088]{2,1,0:T(8,128)(2,1)}) custom-call(f32[64,1088]{1,0:T(8,128)} %get-tuple-element.77.grad, bf16[2,1088,960]{2,1,0:T(8,128)(2,1)} %bitcast.119, ...), custom_call_target="tpu_custom_call" | custom-call | flops 10000000 | bytes 10000 | tf_op jit(solution)/shard_map/attend_back_1/pallas_call | solution.py:712
  253.5 1.7 convert_convert_fusion.grad
  255.2 33.4 %feed_back_0.1 = (f32[64,1088]{1,0:T(8,128)}, bf16[1088,1088]{1,0:T(8,128)(2,1)}, bf16[1088,1088]{1,0:T(8,128)(2,1)}, f32[8,1088]{1,0:T(8,128)}, bf16[2,136,640]...) custom-call(f32[64,1088]{1,0:T(8,128)} %convert_convert_fusion.grad, bf16[2,1088,1088]{2,1,0:T(8,128)(2,1)} %bitcast.112, ...), custom_call_target="tpu_custom_call" | custom-call | flops 10000000 | bytes 10000 | tf_op jit(solution)/shard_map/feed_back_0/pallas_call | solution.py:680
  288.6 44.8 %attend_back_0.1 = (f32[64,1088]{1,0:T(8,128)}, bf16[1088,960]{1,0:T(8,128)(2,1)}, bf16[272,1088]{1,0:T(8,128)(2,1)}, f32[8,1088]{1,0:T(8,128)}, f32[8,960]{1,0:...) custom-call(f32[64,1088]{1,0:T(8,128)} %get-tuple-element.93.grad, bf16[2,1088,960]{2,1,0:T(8,128)(2,1)} %bitcast.120, ...), custom_call_target="tpu_custom_call" | custom-call | flops 10000000 | bytes 10000 | tf_op jit(solution)/shard_map/attend_back_0/pallas_call | solution.py:712
  333.4 113.4 %gather_pieces.1 = (bf16[2,4,136,1088]{3,2,1,0:T(8,128)(2,1)}, bf16[2,4,136,640]{3,2,1,0:T(8,128)(2,1)}, f32[16,1088]{1,0:T(8,128)}) custom-call(bf16[4,2,136,960]{3,2,1,0:T(8,128)(2,1)} %bitcast.128, bf16[2,136,1088]{2,1,0:T(8,128)(2,1)} %bitcast.138, bf16[2,136,1088]{2,1,0:T(8,128)(2,1)} %get-tuple-element.106.half_u, ...), custom_call_target="tpu_custom_call" | custom-call | flops 10000000 | bytes 10000 | tf_op jit(solution)/shard_map/gather_pieces/pallas_call | solution.py:1017
  446.8 1.5 convert_element_type.48
  448.3 1.1 slice_bitcast_fusion.18
  449.5 0.8 copy-done.1
  450.5 0.7 broadcast_select_fusion.2
  451.2 0.7 broadcast_select_fusion
  451.8 2.0 collective-permute-start.2
  453.9 0.8 fusion.5
  454.6 0.8 fusion.4
  455.4 0.7 fusion.3
  456.1 0.8 fusion.2
  457.5 0.9 maximum_bitcast_fusion
  458.4 0.8 constant_dynamic-slice_fusion
  459.2 1.6 slice.353
  462.0 1.6 slice.324
  463.5 1.6 slice.326
  465.1 1.6 slice.328
  466.7 1.4 dynamic_slice.18
  468.1 1.4 dynamic_slice.20
  469.4 2.4 concatenate.42
  471.9 2.7 concatenate.40
  474.5 1.4 fusion.6
  476.0 1.0 select_bitcast_fusion.3
  477.0 0.8 maximum_bitcast_fusion.1
  477.8 0.8 maximum_bitcast_fusion.2
  (63 shorter events, 5.1 us)
Async XLA Ops:
  0.6 5.2 %copy-start.3 = (bf16[1,136,4352]{2,1,0:T(8,128)(2,1)S(1)}, bf16[1,136,4352]{2,1,0:T(8,128)(2,1)}, u32[]{:S(2)}) copy-start(bf16[1,136,4352]{2,1,0:T(8,128)(2,1)} %param.16) | copy-start | bytes 3551236
  1.7 12.4 %collective-permute-start = (bf16[48,1088]{1,0:T(8,128)(2,1)S(1)}, bf16[48,1088]{1,0:T(8,128)(2,1)}, u32[]{:S(2)}, u32[]{:S(2)}) collective-permute-start(bf16[48,1088]{1,0:T(8,128)(2,1)S(1)} %slice_bitcast_fusion.23), channel_id=1, source_target_pairs={{0,16},{8,24},{16,32},{24,40},{32,48},{40,56},{48,0},{56,8},{1,17}... | collective-permute-start | bytes 313352 | tf_op jit(solution)/shard_map/ppermute | solution.py:1045
  5.8 3.8 copy-start.9
  5.8 3.8 copy-start.10
  6.1 4.0 copy-start.13
  6.1 4.0 copy-start.14
  6.1 4.3 copy-start.12
  6.2 4.6 copy-start.11
  11.7 2.4 copy-start.8
  75.2 2.4 copy-start.7
  449.4 1.0 copy-start.1
  449.4 1.0 copy-start.4
  449.4 1.7 copy-start.2
  449.4 1.7 copy-start.5
  451.1 24.8 %collective-permute-start.1 = (bf16[64,1088]{1,0:T(8,128)(2,1)}, bf16[64,1088]{1,0:T(8,128)(2,1)}, u32[]{:S(2)}, u32[]{:S(2)}) collective-permute-start(bf16[64,1088]{1,0:T(8,128)(2,1)} %broadcast_select_fusion.2), channel_id=1, source_target_pairs={{0,64},{64,0},{1,65},{65,1},{2,66},{66,2},{3,67},{67,3},{4,68},{68... | collective-permute-start | bytes 417800 | tf_op jit(solution)/shard_map/ppermute | solution.py:1103
  451.8 5.2 %copy-start = (bf16[2,4,136,1088]{3,2,1,0:T(8,128)(2,1)S(1)}, bf16[2,4,136,1088]{3,2,1,0:T(8,128)(2,1)}, u32[]{:S(2)}) copy-start(bf16[2,4,136,1088]{3,2,1,0:T(8,128)(2,1)} %get-tuple-element.116) | copy-start | bytes 7102468
  451.8 25.9 %collective-permute-start.2 = (bf16[64,1088]{1,0:T(8,128)(2,1)}, bf16[64,1088]{1,0:T(8,128)(2,1)S(1)}, u32[]{:S(2)}, u32[]{:S(2)}) collective-permute-start(bf16[64,1088]{1,0:T(8,128)(2,1)} %broadcast_select_fusion), channel_id=1, source_target_pairs={{0,64},{64,0},{1,65},{65,1},{2,66},{66,2},{3,67},{67,3},{4,68},{68... | collective-permute-start | bytes 417800 | tf_op jit(solution)/shard_map/ppermute | solution.py:1103
  474.5 3.2 copy-start.6

commit v5 on v4

--- a/solution.py
+++ b/solution.py
@@ -179,7 +179,7 @@
     sibling = at_chip(y, 1 - c)
     arrived = greet(peers + [sibling])
     weights = load([(w_hbm.at[e], w)] + out_rows(wo_hbm, wo, e, y), ls)
-    slot(normed, y)[...] = norm(x[...], vecs[0:1], vecs[1:2]).astype(BF)
+    slot(normed, y)[...] = norm(x[...].astype(F32), vecs[0:1], vecs[1:2]).astype(BF)
     arrived()
     gather_start(normed, y, c, gs, gr)
     own, other = masks(c)
@@ -213,7 +213,7 @@
     for at, size in chunks(D):
         acc[:, at : at + size] = dot(mixed, wo[:, at : at + size])
     scatter_start(acc, out_buf, in_buf, y, c, ss, sr)
-    base = x[...] + vecs[4:5]
+    base = x[...].astype(F32) + vecs[4:5]
     middle[...] = base + scatter_wait(acc, out_buf, in_buf, y, c, ss, sr)
 
 
@@ -239,7 +239,7 @@
         acc[:, at : at + size] = dot(rows, wd[:, at : at + size])
     scatter_start(acc, out_buf, in_buf, y, c, ss, sr)
     base = middle[...] + vecs[5:6]
-    result[...] = base + scatter_wait(acc, out_buf, in_buf, y, c, ss, sr)
+    result[...] = (base + scatter_wait(acc, out_buf, in_buf, y, c, ss, sr)).astype(BF)
 
 
 def feed_back(e, grad, wu_hbm, wd_hbm, vecs, middle, normed, hidden, active, grad_middle, grad_up, grad_down, small,
@@ -248,7 +248,7 @@
     peers = [at_chip(ring(y, k), c) for k in (1, 2, 3)]
     arrived = greet(peers if reduce is None else peers + [at_chip(y, 1 - c)] + plane_peers())
     weights = load([(wu_hbm.at[e], wu), (wd_hbm.at[e], wd)], ls)
-    own_rows = grad[...].astype(BF)
+    own_rows = grad[...]
     slot(full, y)[...] = own_rows
     arrived()
     gather_start(full, y, c, gs, gr)
@@ -257,9 +257,9 @@
     small[...] = jnp.zeros_like(small)
     small[3:4] = jnp.sum(own_rows.astype(F32), axis=0, keepdims=True)
     weights[1].wait()
-    gather_wait(full, y, c, gs, gr)
     if reduce is not None:
         reduce.middle(y, c)
+    gather_wait(full, y, c, gs, gr)
     rows = full[...]
     for at, size in chunks(D):
         slope = gelu_slope(hidden[:, at : at + size])
@@ -278,7 +278,7 @@
     back, gain, shift = norm_back(d, middle[...], vecs[2:3])
     small[0:1] = gain
     small[1:2] = shift
-    grad_middle[...] = grad[...] + back
+    grad_middle[...] = grad[...].astype(F32) + back
     if reduce is not None:
         reduce.finish()
 
@@ -301,8 +301,8 @@
     small[2:3] = jnp.sum(own_rows.astype(F32), axis=0, keepdims=True)
     own, other = masks(c)
     out_wait(weights, wo, y)
+    reduce.middle(y, c)
     gather_wait(full, y, c, gs, gr)
-    reduce.middle(y, c)
     ga[...] = dot_nt(full[...], wo[...]).astype(BF)
     for h in range(SLOTS):
         at = h * HD
@@ -341,10 +341,10 @@
     small_bias[...] = jnp.zeros_like(small_bias)
     small_bias[0:1] = jnp.sum(gj[...].astype(F32), axis=0, keepdims=True)
     d = scatter_wait(acc, out_buf, in_buf, y, c, ss, sr)
-    back, gain, shift = norm_back(d, x[...], vecs[0:1])
+    back, gain, shift = norm_back(d, x[...].astype(F32), vecs[0:1])
     small[0:1] = gain
     small[1:2] = shift
-    grad_x[...] = grad[...] + back
+    grad_x[...] = (grad[...] + back).astype(BF)
     lend.wait()
 
     @pl.when(y < 3)
@@ -429,7 +429,7 @@
             owner = 2 * half + self.layer
             rel = lax.rem(2 * h + s - owner + 3, 4)
             target = {"section": jnp.int32(self.layer), "replica": 2 * x + half}
-            copy = remote(self.blocks.at[half], self.landing.at[rel], self.send.at[half], self.recv.at[rel], target)
+            copy = remote(self.blocks, self.landing.at[rel], self.send.at[half], self.recv.at[rel], target)
             yield 2 * h + s != owner, copy
 
     def start(self):
@@ -444,17 +444,17 @@
         @pl.when(s == self.layer)
         def _():
             for rel in range(3):
-                remote(self.blocks.at[0], self.landing.at[rel], self.send.at[0], self.recv.at[rel], {"section": 1 - s}).wait_recv()
+                remote(self.blocks, self.landing.at[rel], self.send.at[0], self.recv.at[rel], {"section": 1 - s}).wait_recv()
 
             def add(i, carry):
-                rows = pl.ds(pl.multiple_of(8 * i, 8), 8)
-                total = self.blocks[h, rows].astype(F32)
+                rows = pl.ds(pl.multiple_of(8 * (i % 17), 8), 8)
+                total = self.blocks[i // 17, rows].astype(F32)
                 for rel in range(3):
-                    total = total + self.landing[rel, rows].astype(F32)
-                self.out[rows] = total.astype(BF)
+                    total = total + self.landing[rel, i // 17, rows].astype(F32)
+                self.out[i // 17, rows] = total.astype(BF)
                 return carry
 
-            lax.fori_loop(0, 17, add, 0)
+            lax.fori_loop(0, 34, add, 0)
 
         @pl.when(s != self.layer)
         def _():
@@ -462,7 +462,7 @@
 
 
 def z_scratch(width):
-    return [pltpu.VMEM((3, 136, width), BF), DMA((2,)), DMA((3,))]
+    return [pltpu.VMEM((3, 2, 136, width), BF), DMA((2,)), DMA((3,))]
 
 
 class FeedReduce:
@@ -653,13 +653,12 @@
 
 
 def run_feed_forward(e, middle, wu, wd, vecs):
-    outs = [shape((BLK, D), F32), shape((ROWS, D), BF), shape((ROWS, D), F32), shape((ROWS, D), BF)]
+    outs = [shape((BLK, D), BF), shape((ROWS, D), BF), shape((ROWS, D), F32), shape((ROWS, D), BF)]
     scratch = [pltpu.VMEM((D, D), BF), pltpu.VMEM((D, D), BF)] + MOVE
     return call(functools.partial(feed_forward, e), "feed_forward_%d" % e, 2 + e, outs, [VMEM, ANY, ANY, VMEM], scratch)(middle, wu, wd, vecs)
 
 
 HALF_A, HALF_U = shape((2, 136, 640), BF), shape((2, 136, D), BF)
-PIECE_A, PIECE_U = shape((136, 640), BF), shape((136, D), BF)
 
 
 def run_feed_back(e, grad, wu, wd, vecs, middle, normed, hidden, active, before=None):
@@ -675,7 +674,7 @@
         return call(functools.partial(feed_back, e), "feed_back_%d" % e, 4 + e, outs, ins, scratch)(
             grad, wu, wd, vecs, middle, normed, hidden, active
         )
-    outs += [HALF_A, PIECE_U]
+    outs += [HALF_A, HALF_U]
     scratch = scratch + ATTEND_SCRATCH + z_scratch(D)
     return call(functools.partial(feed_back_reduce, e), "feed_back_%d" % e, 4 + e, outs, ins + [ANY, ANY, VMEM], scratch)(
         grad, wu, wd, vecs, middle, normed, hidden, active, *before
@@ -684,7 +683,7 @@
 
 def run_attend_back(e, grad, w, wo, vecs, x, saved, up, down, half_a=None):
     outs = [
-        shape((BLK, D), F32),
+        shape((BLK, D), BF),
         shape((D, TQKV), BF),
         shape((272, D), BF),
         shape((8, D), F32),
@@ -708,7 +707,7 @@
     ins = [VMEM, ANY, ANY] + [VMEM] * 8 + [ANY, ANY]
     more = []
     if later:
-        outs, scratch, ins, more = outs + [PIECE_A], scratch + z_scratch(640), ins + [VMEM], [half_a]
+        outs, scratch, ins, more = outs + [HALF_A], scratch + z_scratch(640), ins + [VMEM], [half_a]
     return call(body, "attend_back_%d" % e, 6 + e, outs, ins, scratch)(
         grad, w, wo, vecs, x, *saved, up, down, *more
     )
@@ -863,61 +862,58 @@
 
 
 class Gather:
-    def __init__(self, piece, moved, out, number, moves, keep_from, ts, tr, gs, gr):
-        self.piece, self.moved, self.out, self.i = piece, moved, out, number
-        self.moves, self.keep_from = moves, keep_from
+    def __init__(self, pair, moved, out, number, keep_from, ts, tr, gs, gr):
+        self.pair, self.moved, self.out, self.i, self.keep_from = pair, moved, out, number, keep_from
         self.ts, self.tr, self.gs, self.gr = ts, tr, gs, gr
 
     def transpose(self):
         y, c = place()
         s, x, h, me = plane()
-        copy = remote(self.piece, self.moved, self.ts.at[self.i], self.tr.at[self.i], {"fsdp": 2 * x + c, "replica": 2 * y + h})
-        cond = x != y
-        return copy, cond if self.moves else jnp.logical_and(cond, h == 0)
+        source = self.pair if self.keep_from else self.pair.at[0]
+        return remote(source, self.moved, self.ts.at[self.i], self.tr.at[self.i], {"fsdp": 2 * x + c, "replica": 2 * y + h})
 
     def start(self):
-        copy, cond = self.transpose()
-        pl.when(cond)(copy.start)
+        y, c = place()
+        s, x, h, me = plane()
+        pl.when(x != y)(self.transpose().start)
 
     def copies(self):
         s, x, h, me = plane()
-        r = 2 * x + h
-        for j in (4, 2, 6, 3, 5, 1, 7):
-            yield j, remote(self.piece, self.out.at[h, x], self.gs.at[self.i, j], self.gr.at[self.i, j], {"replica": lax.rem(r + j, 8)})
+        targets = x_peers(x, h)
+        for k in ORDER:
+            yield k, remote(self.pair, self.out.at[x], self.gs.at[self.i, k - 1], self.gr.at[self.i, k - 1], targets[k - 1])
 
     def spread(self):
+        y, c = place()
         s, x, h, me = plane()
-        copy, cond = self.transpose()
-        pl.when(cond)(copy.wait)
-
-        @pl.when(jnp.logical_and(cond, h == 0))
+
+        @pl.when(x != y)
         def _():
-            self.piece[...] = self.moved[...]
-
-        if self.moves:
-            @pl.when(jnp.logical_and(cond, h == 1))
-            def _():
-                lane = lax.broadcasted_iota(jnp.int32, self.piece.shape, 1)
-                merged = jnp.where(lane < self.keep_from, self.moved[...].astype(F32), self.piece[...].astype(F32))
-                self.piece[...] = merged.astype(BF)
-
-        self.out[h, x] = self.piece[...]
-        for j, copy in self.copies():
+            self.transpose().wait()
+            if self.keep_from:
+                self.pair[0] = self.moved[0]
+                lane = lax.broadcasted_iota(jnp.int32, self.pair.shape[1:], 1)
+                merged = jnp.where(lane < self.keep_from, self.moved[1].astype(F32), self.pair[1].astype(F32))
+                self.pair[1] = merged.astype(BF)
+            else:
+                self.pair[0] = self.moved[...]
+
+        for k, copy in self.copies():
             copy.start()
+        self.out[x] = self.pair[...]
 
     def finish(self):
         s, x, h, me = plane()
-        r = 2 * x + h
-        for j, copy in self.copies():
+        targets = x_peers(x, h)
+        for k, copy in self.copies():
             copy.wait_send()
-            source = lax.rem(r - j + 8, 8)
-            place_in = self.out.at[source % 2, source // 2]
-            remote(place_in, place_in, self.gs.at[self.i, j], self.gr.at[self.i, j], {"replica": lax.rem(r + j, 8)}).wait_recv()
+            place_in = self.out.at[lax.rem(x + 4 - k, 4)]
+            remote(place_in, place_in, self.gs.at[self.i, k - 1], self.gr.at[self.i, k - 1], targets[k - 1]).wait_recv()
 
 
 def gather_pieces(wide, rows, half_u, done_u, done_a, one_0, two_0, heads_0, one_1, two_1, heads_1,
-                  out_u, out_a, out_small,
-                  piece_u, moved_u, piece_a, moved_a, half_a, small, small_c, small_y, small_x, small_z,
+                  act_0, act_1, back_0, back_1, out_u, out_a, out_small, out_act, out_back,
+                  swap_act, swap_back, ws, wr, piece_u, moved_u, piece_a, moved_a, half_a, small, small_c, small_y, small_x, small_z,
                   ts, tr, gs, gr, cs, cr, ys, yr, zs, zr, *extra):
     y, c = place()
     s, x, h, me = plane()
@@ -927,8 +923,8 @@
     extra = extra[len(ATTEND_SCRATCH) :]
     z_u = AlongZ(0, half_u, extra[0], piece_u, extra[1], extra[2])
     z_a = AlongZ(0, half_a, extra[3], piece_a, extra[4], extra[5])
-    g_u = Gather(piece_u, moved_u, out_u, 0, False, 0, ts, tr, gs, gr)
-    g_a = Gather(piece_a, moved_a, out_a, 1, True, 320, ts, tr, gs, gr)
+    g_u = Gather(piece_u, moved_u, out_u, 0, 0, ts, tr, gs, gr)
+    g_a = Gather(piece_a, moved_a, out_a, 1, 320, ts, tr, gs, gr)
     barrier = pltpu.get_barrier_semaphore()
     for target in peers + [sibling] + [at_plane(lax.rem(me + j, 16)) for j in range(1, 16)]:
         pl.semaphore_signal(barrier, inc=1, device_id=target, device_id_type=MESH)
@@ -942,6 +938,14 @@
     pl.semaphore_wait(barrier, 19 + jnp.where(x == y, 0, 1))
     z_u.start()
     reduce.begin(y, c)
+    swap_act[...] = jnp.where(s == 0, act_1[...].astype(F32), act_0[...].astype(F32)).astype(BF)
+    swap_back[...] = jnp.where(s == 0, back_1[...].astype(F32), back_0[...].astype(F32)).astype(BF)
+    swaps = [
+        remote(swap_act, out_act.at[s], ws.at[0], wr.at[0], {"section": 1 - s}),
+        remote(swap_back, out_back.at[s], ws.at[1], wr.at[1], {"section": 1 - s}),
+    ]
+    out_act[s] = jnp.where(s == 0, act_0[...].astype(F32), act_1[...].astype(F32)).astype(BF)
+    out_back[s] = jnp.where(s == 0, back_0[...].astype(F32), back_1[...].astype(F32)).astype(BF)
     cross = remote(small, small_c, cs, cr, sibling)
     cross.start()
     reduce.middle(y, c)
@@ -978,6 +982,8 @@
         piece_a[...] = done_a[...]
 
     g_a.start()
+    for swap in swaps:
+        swap.start()
     g_a.spread()
     total = small_x[s].astype(F32)
     for copy in plane_copies():
@@ -986,17 +992,26 @@
         remote(small_x.at[0], small_z.at[j], zs.at[j], zr.at[j], sibling).wait_recv()
         total = total + small_z[j].astype(F32)
     out_small[...] = total
+    for i, swap in enumerate(swaps):
+        swap.wait_send()
+        place_in = (out_act, out_back)[i].at[1 - s]
+        remote(place_in, place_in, ws.at[i], wr.at[i], {"section": 1 - s}).wait_recv()
     g_u.finish()
     g_a.finish()
 
 
-def run_gather_pieces(wide, rows, half_u, done_u, done_a, smalls):
-    outs = [shape((2, 4, 136, D), BF), shape((2, 4, 136, 640), BF), shape((16, D), F32)]
+def run_gather_pieces(wide, rows, half_u, done_u, done_a, smalls, acts, backs):
+    both = shape((2, BLK, D), BF)
+    outs = [shape((4, 2, 136, D), BF), shape((4, 2, 136, 640), BF), shape((16, D), F32), both, both]
     scratch = [
+        pltpu.VMEM((BLK, D), BF),
+        pltpu.VMEM((BLK, D), BF),
+        DMA((2,)),
+        DMA((2,)),
+        pltpu.VMEM((2, 136, D), BF),
         pltpu.VMEM((136, D), BF),
-        pltpu.VMEM((136, D), BF),
-        pltpu.VMEM((136, 640), BF),
-        pltpu.VMEM((136, 640), BF),
+        pltpu.VMEM((2, 136, 640), BF),
+        pltpu.VMEM((2, 136, 640), BF),
         pltpu.VMEM((2, 136, 640), BF),
         pltpu.VMEM((2, 16, D), F32),
         pltpu.VMEM((2, 16, D), F32),
@@ -1005,8 +1020,8 @@
         pltpu.VMEM((15, 16, D), BF),
         DMA((2,)),
         DMA((2,)),
-        DMA((2, 8)),
-        DMA((2, 8)),
+        DMA((2, 3)),
+        DMA((2, 3)),
         DMA,
         DMA,
         DMA((3,)),
@@ -1014,9 +1029,49 @@
         DMA((15,)),
         DMA((15,)),
     ] + ATTEND_SCRATCH + z_scratch(D) + z_scratch(640)
-    return call(gather_pieces, "gather_pieces", 9, outs, [ANY, ANY] + [VMEM] * 9, scratch)(
-        wide, rows, half_u, done_u, done_a, *smalls
-    )
+    return call(gather_pieces, "gather_pieces", 9, outs, [ANY, ANY] + [VMEM] * 13, scratch)(
+        wide, rows, half_u, done_u, done_a, *smalls, *acts, *backs
+    )
+
+
+def assemble(all_u, all_a, small, attn, out, up, down, b_attn, b_out, b_up, b_down, gain, shift):
+    y, c = place()
+    f = 2 * y + c
+    for j in range(CHIPS):
+        up[:, j * D : (j + 1) * D] = all_u[j, 0].astype(F32)
+        down[j * 136 : (j + 1) * 136] = all_u[j, 1].astype(F32)
+        first, second = all_a[j, 0].astype(F32), all_a[j, 1].astype(F32)
+        parts = ((0, second[:, :TH]), (D, first[:, :TH]), (2 * D, first[:, TH:]))
+        for base, part in parts:
+            attn[:, base + 256 * j : base + 256 * j + 256] = part[:, :256]
+        out[:, 256 * j : 256 * j + 256] = second[:, TH : TH + 256]
+        if j == CHIPS - 1:
+            for base, part in parts:
+                attn[:, base + 1024 : base + D] = part[:, 256:]
+            out[:, 1024:] = second[:, TH + 256 :]
+
+    def pick(index, options):
+        total = jnp.where(index == 0, options[0], 0.0)
+        for i, option in enumerate(options[1:], 1):
+            total = total + jnp.where(index == i, option, 0.0)
+        return total
+
+    for row, ref, place_in in ((0, gain, 0), (1, shift, 0), (2, gain, 1), (3, shift, 1), (4, b_out, 0), (5, b_down, 0)):
+        ref[place_in : place_in + 1] = pick(f, [small[row : row + 1, 136 * i : 136 * i + 136] for i in range(8)])
+    b_up[...] = pick(f, [small[6 + i // 2 : 7 + i // 2, 544 * (i % 2) : 544 * (i % 2) + 544] for i in range(8)])
+    b_attn[...] = pick(f, [small[10 + i // 4 : 11 + i // 4, 272 * (i % 4) : 272 * (i % 4) + 272] for i in range(8)])
+
+
+def run_assemble(all_u, all_a, small):
+    sizes = [(136, 3 * D), (136, D), (136, FF), (544, D), (1, 272), (1, 136), (1, 544), (1, 136), (2, 136), (2, 136)]
+    return pl.pallas_call(
+        assemble,
+        name="assemble",
+        out_shape=[shape(dims, F32) for dims in sizes],
+        in_specs=[VMEM] * 3,
+        out_specs=[VMEM] * len(sizes),
+        compiler_params=pltpu.CompilerParams(vmem_limit_bytes=LIMIT),
+    )(all_u, all_a, small)
 
 
 def split_heads(block):
@@ -1025,10 +1080,6 @@
         jnp.concatenate([block[..., 256 * j : 256 * j + 256], block[..., 1024:] if j == 3 else zero], axis=-1)
         for j in range(CHIPS)
     ]
-
-
-def join_heads(blocks):
-    return jnp.concatenate([blocks[j][..., :256] for j in range(CHIPS)] + [blocks[3][..., 256:]], axis=-1)
 
 
 def on_device(inputs, cotangent, weight_attn, weight_out, weight_up, weight_down, bias_attn, bias_out, bias_up,
@@ -1058,16 +1109,15 @@
     wd = wd.reshape(2, D, D)
     wo = jnp.concatenate([wo[:, 1, 136:184], wo[:, 0, :136], wo[:, 1, :136]], axis=1)
     vecs = jnp.sum(wv.astype(F32), axis=(1, 2))
-    micro = lax.dynamic_index_in_dim(inputs, s, 0, keepdims=False)[0]
-    stream = micro.astype(F32)
+    stream = lax.dynamic_index_in_dim(inputs, s, 0, keepdims=False)[0]
     saved, acts = [], []
     for e in range(2):
         middle, *kept = run_attend_forward(e, stream, wa, wo, vecs[e])
         result, *kept_two = run_feed_forward(e, middle, wu, wd, vecs[e])
         saved.append((stream, kept, middle, kept_two))
-        acts.append(result.astype(BF))
-        stream = acts[-1].astype(F32)
-    grad = lax.dynamic_index_in_dim(cotangent, s, 0, keepdims=False)[0].astype(F32)
+        acts.append(result)
+        stream = result
+    grad = lax.dynamic_index_in_dim(cotangent, s, 0, keepdims=False)[0]
     in_grads, smalls, before, half_a = [None, None], [None, None], None, None
     for e in (1, 0):
         x, kept, middle, kept_two = saved[e]
@@ -1076,47 +1126,30 @@
         )
         if reduced:
             half_a, done_u = reduced
-        grad_x, grad_attn, grad_out, one, heads, half_u, *done_a = run_attend_back(
+        grad, grad_attn, grad_out, one, heads, half_u, *done_a = run_attend_back(
             e, grad_middle, wa, wo, vecs[e], x, kept, grad_up.reshape(4, 2, 136, D), grad_down.reshape(2, 4, 136, D),
             half_a,
         )
-        in_grads[e] = grad_x.astype(BF)
-        grad = in_grads[e].astype(F32)
+        in_grads[e] = grad
         before = (grad_attn.reshape(4, 2, 136, TQKV), grad_out.reshape(2, 136, D), half_u)
         smalls[e] = (one, two, heads)
-    all_u, all_a, small = run_gather_pieces(*before, done_u, *done_a, smalls[0] + smalls[1])
-    all_u, all_a = all_u.astype(F32), all_a.astype(F32)
-    attn = [jnp.concatenate([all_a[0, j], all_a[1, j, :, :320]], axis=-1) for j in range(CHIPS)]
-    attn = jnp.concatenate(
-        [join_heads([attn[j][:, i * TH : (i + 1) * TH] for j in range(CHIPS)]) for i in (2, 0, 1)], axis=-1
-    )
-    out = join_heads([all_a[1, j, :, 320:] for j in range(CHIPS)])
-    up = jnp.concatenate([all_u[0, j] for j in range(CHIPS)], axis=-1)
-    down = all_u[1].reshape(544, D)
-    pieces = lax.dynamic_slice(small, (0, 136 * f), (6, 136))
-    piece_up = lax.dynamic_slice(small, (6 + y, 544 * c), (1, 544))
-    piece_attn = lax.dynamic_slice(small, (10 + f // 4, 272 * (f % 4)), (1, 272))
-
-    def swap_layers(values):
-        mine = jnp.where(s == 0, values[0], values[1])
-        theirs = jnp.where(s == 0, values[1], values[0])
-        received = lax.ppermute(theirs, "section", [(0, 1), (1, 0)])
-        pair_up = jnp.stack([jnp.where(s == 0, mine, received), jnp.where(s == 0, received, mine)])
-        return pair_up[None, :, None]
-
+    all_u, all_a, small, all_acts, all_grads = run_gather_pieces(
+        *before, done_u, *done_a, smalls[0] + smalls[1], acts, in_grads
+    )
+    attn, out, up, down, b_attn, b_out, b_up, b_down, gain, shift = run_assemble(all_u, all_a, small)
     return (
-        swap_layers(acts),
-        swap_layers(in_grads),
+        all_acts[None, :, None],
+        all_grads[None, :, None],
         attn[None],
         out[None],
         up[None],
         down[None],
-        piece_attn,
-        pieces[4:5],
-        piece_up,
-        pieces[5:6],
-        pieces[0:4:2][None],
-        pieces[1:4:2][None],
+        b_attn,
+        b_out,
+        b_up,
+        b_down,
+        gain[None],
+        shift[None],
     )
 
 

time: 485 us -> 469 us (0.967)
  the two profiles are of different devices: /device:TPU:96 before, /device:TPU:4 now
where the time goes in v5:
time: 469 us; the launch traced here: 463 us
  Pallas kernels  442 us (94%)
  local copies, waits for them, and re-layouts  11.5 us (2%)
  other arithmetic  6.27 us (1%)
    pallas_call x1, Pallas kernels, run_gather_pieces(): call(gather_pieces, 'gather_pieces', 9, outs, [ANY, ANY] + [VMEM] * 13, s...  129 us
    pallas_call x2, Pallas kernels, run_attend_back(): call(body, 'attend_back_%d' % e, 6 + e, outs, ins, scratch)  87.2 us
    pallas_call x1, Pallas kernels, run_spread(): pl.pallas_call(spread, name='spread', out_shape=outs, in_specs=[ANY] * 5,...  60 us
    pallas_call x2, Pallas kernels, run_attend_forward(): call(functools.partial(attend_forward, e), 'attend_forward_%d' % e, e, ou...  55.3 us
    pallas_call x2, Pallas kernels, run_feed_forward(): call(functools.partial(feed_forward, e), 'feed_forward_%d' % e, 2 + e, ou...  45.8 us
    pallas_call x1, Pallas kernels, run_feed_back(): call(functools.partial(feed_back_reduce, e), 'feed_back_%d' % e, 4 + e, o...  33.9 us
    pallas_call x1, Pallas kernels, run_feed_back(): call(functools.partial(feed_back, e), 'feed_back_%d' % e, 4 + e, outs, in...  25.1 us
  transfers between devices with their start and end apart: 1, of which 0 were waited for; matrix products, arithmetic and copies ran while one was open for 2% of the time, Pallas kernels for 0%

profile of v5, /device:TPU:4, one launch (start us, length us, event | category | flops | bytes accessed | tf_op | source)
XLA Modules:
  0.0 462.7 jit_solution(2465457251378070124)
XLA Ops:
  0.7 1.0 slice_bitcast_fusion.7
  1.7 1.6 collective-permute-start
  3.3 1.1 fusion.1
  4.4 1.3 fusion
  5.8 0.0 copy-start.5
  5.8 0.0 copy-start.6
  5.8 0.0 copy-start.9
  5.8 0.0 copy-start.10
  5.8 0.0 copy-start.7
  5.8 0.0 copy-start.8
  5.9 0.3 slice_bitcast_fusion.5
  6.2 0.1 pad.8.clone
  6.2 0.2 copy-done.5
  6.4 0.0 copy-done.6
  6.5 0.0 copy-done.9
  6.5 0.0 copy-done.10
  6.5 0.2 dynamic_update_slice.9
  6.8 0.3 dynamic_update_slice.10
  7.1 0.0 copy-done.8
  7.1 0.3 dynamic_update_slice.11
  7.4 0.6 pad_maximum_fusion.3.send_v
  8.0 1.7 dynamic-slice_bitcast_fusion
  9.7 0.1 maximum_bitcast_fusion
  9.9 0.1 concatenate.22
  10.0 0.1 concatenate.24
  10.1 0.1 concatenate.23
  10.3 1.3 pad_maximum_fusion.1.send_u
  11.5 1.1 pad_maximum_fusion.2.send_a
  12.7 0.0 collective-permute-done
  12.7 1.8 maximum_maximum_fusion.send_o
  14.5 60.0 %spread.1 = (bf16[2,4,2,136,960]{4,3,2,1,0:T(8,128)(2,1)}, bf16[2,4,2,136,1088]{4,3,2,1,0:T(8,128)(2,1)}, bf16[2,2,544,1088]{3,2,1,0:T(8,128)(2,1)}, bf16[2,2,19...) custom-call(bf16[4,136,960]{2,1,0:T(8,128)(2,1)} %pad_maximum_fusion.2.send_a, ...), custom_call_target="tpu_custom_call" | custom-call | tf_op jit(solution)/shard_map/spread/pallas_call | solution.py:831
  74.5 1.0 slice_bitcast_fusion.6
  75.5 1.4 slice_bitcast_fusion.1
  76.9 0.1 convert_reduce_fusion
  77.0 0.7 slice_bitcast_fusion.8
  77.7 1.2 pad_maximum_fusion.wo_hbm
  78.9 28.4 %attend_forward_0.1 = (f32[64,1088]{1,0:T(8,128)}, bf16[256,1088]{1,0:T(8,128)(2,1)}, bf16[256,320]{1,0:T(8,128)(2,1)}, bf16[256,640]{1,0:T(8,128)(2,1)}, bf16[2...) custom-call(bf16[64,1088]{1,0:T(8,128)(2,1)} %get-tuple-element.178.x, ...), custom_call_target="tpu_custom_call" | custom-call | flops 10000000 | bytes 10000 | tf_op jit(solution)/shard_map/attend_forward_0/pallas_call | solution.py:652
  107.3 22.8 %feed_forward_0.1 = (bf16[64,1088]{1,0:T(8,128)(2,1)}, bf16[256,1088]{1,0:T(8,128)(2,1)}, f32[256,1088]{1,0:T(8,128)}, bf16[256,1088]{1,0:T(8,128)(2,1)}) custom-call(f32[64,1088]{1,0:T(8,128)} %get-tuple-element.82.middle, bf16[2,1088,1088]{2,1,0:T(8,128)(2,1)} %bitcast.64, bf16[2,1088,1088]{2,1,0:T(8,128)(2,1)} %bitcast.68, f32[16,1088]{1,0:T(8,128)} %get-tuple-element.172.vecs), custom_call_target="tpu_custom_call" | custom-call | flops 10000000 | bytes 10000 | tf_op jit(solution)/shard_map/feed_forward_0/pallas_call | solution.py:658
  130.1 27.0 %attend_forward_1.1 = (f32[64,1088]{1,0:T(8,128)}, bf16[256,1088]{1,0:T(8,128)(2,1)}, bf16[256,320]{1,0:T(8,128)(2,1)}, bf16[256,640]{1,0:T(8,128)(2,1)}, bf16[2...) custom-call(bf16[64,1088]{1,0:T(8,128)(2,1)} %get-tuple-element.83.x.act_0, ...), custom_call_target="tpu_custom_call" | custom-call | flops 10000000 | bytes 10000 | tf_op jit(solution)/shard_map/attend_forward_1/pallas_call | solution.py:652
  157.0 23.0 %feed_forward_1.1 = (bf16[64,1088]{1,0:T(8,128)(2,1)}, bf16[256,1088]{1,0:T(8,128)(2,1)}, f32[256,1088]{1,0:T(8,128)}, bf16[256,1088]{1,0:T(8,128)(2,1)}) custom-call(f32[64,1088]{1,0:T(8,128)} %get-tuple-element.84.middle, bf16[2,1088,1088]{2,1,0:T(8,128)(2,1)} %bitcast.65, bf16[2,1088,1088]{2,1,0:T(8,128)(2,1)} %bitcast.69, f32[16,1088]{1,0:T(8,128)} %get-tuple-element.173.vecs), custom_call_target="tpu_custom_call" | custom-call | flops 10000000 | bytes 10000 | tf_op jit(solution)/shard_map/feed_forward_1/pallas_call | solution.py:658
  180.0 25.1 %feed_back_1.1 = (f32[64,1088]{1,0:T(8,128)}, bf16[1088,1088]{1,0:T(8,128)(2,1)}, bf16[1088,1088]{1,0:T(8,128)(2,1)}, f32[8,1088]{1,0:T(8,128)}) custom-call(bf16[64,1088]{1,0:T(8,128)(2,1)} %get-tuple-element.179.grad, bf16[2,1088,1088]{2,1,0:T(8,128)(2,1)} %bitcast.66, bf16[2,1088,1088]{2,1,0:T(8,128)(2,1)} %bitcast.70, ...), custom_call_target="tpu_custom_call" | custom-call | flops 10000000 | bytes 10000 | tf_op jit(solution)/shard_map/feed_back_1/pallas_call | solution.py:674
  205.1 42.9 %attend_back_1.1 = (bf16[64,1088]{1,0:T(8,128)(2,1)}, bf16[1088,960]{1,0:T(8,128)(2,1)}, bf16[272,1088]{1,0:T(8,128)(2,1)}, f32[8,1088]{1,0:T(8,128)}, f32[8,960]{1,0:T(8,128)}, /*index=5*/bf16[2,136,1088]{2,1,0:T(8,128)(2,1)}) custom-call(f32[64,1088]{1,0:T(8,128)} %get-tuple-element.88.grad, bf16[2,1088,960]{2,1,0:T(8,128)(2,1)} %bitcast.74, ...), custom_call_target="tpu_custom_call" | custom-call | flops 10000000 | bytes 10000 | tf_op jit(solution)/shard_map/attend_back_1/pallas_call | solution.py:711
  248.1 33.9 %feed_back_0.1 = (f32[64,1088]{1,0:T(8,128)}, bf16[1088,1088]{1,0:T(8,128)(2,1)}, bf16[1088,1088]{1,0:T(8,128)(2,1)}, f32[8,1088]{1,0:T(8,128)}, bf16[2,136,640]...) custom-call(bf16[64,1088]{1,0:T(8,128)(2,1)} %get-tuple-element.97.grad.back_1, bf16[2,1088,1088]{2,1,0:T(8,128)(2,1)} %bitcast.67, ...), custom_call_target="tpu_custom_call" | custom-call | flops 10000000 | bytes 10000 | tf_op jit(solution)/shard_map/feed_back_0/pallas_call | solution.py:679
  281.9 44.3 %attend_back_0.1 = (bf16[64,1088]{1,0:T(8,128)(2,1)}, bf16[1088,960]{1,0:T(8,128)(2,1)}, bf16[272,1088]{1,0:T(8,128)(2,1)}, f32[8,1088]{1,0:T(8,128)}, f32[8,960...) custom-call(f32[64,1088]{1,0:T(8,128)} %get-tuple-element.104.grad, ...), custom_call_target="tpu_custom_call" | custom-call | flops 10000000 | bytes 10000 | tf_op jit(solution)/shard_map/attend_back_0/pallas_call | solution.py:711
  326.2 128.9 %gather_pieces.1 = (bf16[4,2,136,1088]{3,2,1,0:T(8,128)(2,1)}, bf16[4,2,136,640]{3,2,1,0:T(8,128)(2,1)}, f32[16,1088]{1,0:T(8,128)}, bf16[2,64,1088]{2,1,0:T(8,128)(2,1)}, bf16[2,64,1088]{2,1,0:T(8,128)(2,1)}) custom-call(bf16[4,2,136,960]{3,2,1,0:T(8,128)(2,1)} %bitcast.80, bf16[2,136,1088]{2,1,0:T(8,128)(2,1)} %bitcast.89, ...), custom_call_target="tpu_custom_call" | custom-call | flops 10000000 | bytes 10000 | tf_op jit(solution)/shard_map/gather_pieces/pallas_call | solution.py:1032
  455.2 5.8 %assemble.1 = (f32[136,3264]{1,0:T(8,128)}, f32[136,1088]{1,0:T(8,128)}, f32[136,4352]{1,0:T(8,128)}, f32[544,1088]{1,0:T(8,128)}, f32[1,272]{1,0:T(1,128)}, /*i...) custom-call(bf16[4,2,136,1088]{3,2,1,0:T(8,128)(2,1)} %get-tuple-element.129.al, ...), custom_call_target="tpu_custom_call" | custom-call | tf_op jit(solution)/shard_map/assemble/pallas_call | solution.py:1067
  461.0 0.7 copy.38
  461.7 0.7 copy.39
  (18 shorter events, 0.1 us)
Async XLA Ops:
  0.6 5.2 %copy-start = (bf16[1,136,4352]{2,1,0:T(8,128)(2,1)S(1)}, bf16[1,136,4352]{2,1,0:T(8,128)(2,1)}, u32[]{:S(2)}) copy-start(bf16[1,136,4352]{2,1,0:T(8,128)(2,1)} %param.16) | copy-start | bytes 3551236
  1.7 11.0 %collective-permute-start = (bf16[48,1088]{1,0:T(8,128)(2,1)S(1)}, bf16[48,1088]{1,0:T(8,128)(2,1)}, u32[]{:S(2)}, u32[]{:S(2)}) collective-permute-start(bf16[48,1088]{1,0:T(8,128)(2,1)S(1)} %slice_bitcast_fusion.7), channel_id=1, source_target_pairs={{0,16},{8,24},{16,32},{24,40},{32,48},{40,56},{48,0},{56,8},{1,17}... | collective-permute-start | bytes 313352 | tf_op jit(solution)/shard_map/ppermute | solution.py:1096
  5.8 0.7 copy-start.5
  5.8 0.7 copy-start.6
  5.8 0.7 copy-start.9
  5.8 0.7 copy-start.10
  5.8 1.0 copy-start.7
  5.8 1.3 copy-start.8
  11.5 1.1 copy-start.2
  74.5 2.4 copy-start.1
  455.2 5.8 %copy-start.4 = (bf16[2,64,1088]{2,1,0:T(8,128)(2,1)S(1)}, bf16[2,64,1088]{2,1,0:T(8,128)(2,1)}, u32[]{:S(2)}) copy-start(bf16[2,64,1088]{2,1,0:T(8,128)(2,1)} %get-tuple-element.127) | copy-start | bytes 835588
  455.2 6.5 %copy-start.3 = (bf16[2,64,1088]{2,1,0:T(8,128)(2,1)S(1)}, bf16[2,64,1088]{2,1,0:T(8,128)(2,1)}, u32[]{:S(2)}) copy-start(bf16[2,64,1088]{2,1,0:T(8,128)(2,1)} %get-tuple-element.128) | copy-start | bytes 835588

commit v6 on v5

--- a/solution.py
+++ b/solution.py
@@ -243,11 +243,10 @@
 
 
 def feed_back(e, grad, wu_hbm, wd_hbm, vecs, middle, normed, hidden, active, grad_middle, grad_up, grad_down, small,
-              wu, wd, full, gh, acc, out_buf, in_buf, ls, gs, gr, ss, sr, reduce=None):
+              wu, wd, full, gh, acc, out_buf, in_buf, ls, gs, gr, ss, sr, arrived, reduce=None, weights=None):
     y, c = place()
-    peers = [at_chip(ring(y, k), c) for k in (1, 2, 3)]
-    arrived = greet(peers if reduce is None else peers + [at_chip(y, 1 - c)] + plane_peers())
-    weights = load([(wu_hbm.at[e], wu), (wd_hbm.at[e], wd)], ls)
+    if weights is None:
+        weights = load([(wu_hbm.at[e], wu), (wd_hbm.at[e], wd)], ls)
     own_rows = grad[...]
     slot(full, y)[...] = own_rows
     arrived()
@@ -271,6 +270,8 @@
     for at, size in chunks(D):
         acc[:, at : at + size] = dot_nt(rows, wu[at : at + size, :])
     scatter_start(acc, out_buf, in_buf, y, c, ss, sr)
+    if reduce is not None:
+        reduce.late()
     for at, size in chunks(D):
         grad_up[at : at + size, :] = dot_tn(normed[:, at : at + size], gh[...]).astype(BF)
         grad_down[at : at + size, :] = dot_tn(active[:, at : at + size], full[...]).astype(BF)
@@ -286,11 +287,9 @@
 def attend_back(e, grad, w_hbm, wo_hbm, vecs, x, normed, queries, kv, kv_other, logsum, attended,
                 grad_x, grad_attn, grad_out, small, small_bias,
                 w, wo, full, ga, gj, part_out, part_in, part_own, rows_out, edge, acc, out_buf, in_buf, ls, gs, gr, ss, sr, ks, kr, es, er,
-                reduce):
+                arrived, reduce):
     y, c = place()
-    peers = [at_chip(ring(y, k), c) for k in (1, 2, 3)]
     sibling = at_chip(y, 1 - c)
-    arrived = greet(peers + [sibling] + plane_peers())
     weights = load([(w_hbm.at[e], w)] + out_rows(wo_hbm, wo, e, y), ls)
     own_rows = grad[...].astype(BF)
     slot(full, y)[...] = own_rows
@@ -336,8 +335,20 @@
     for at, size in chunks(D):
         acc[:, at : at + size] = dot_nt(rows, w[at : at + size, :])
     scatter_start(acc, out_buf, in_buf, y, c, ss, sr)
-    for at, size in chunks(D):
-        grad_attn[at : at + size, :] = dot_tn(normed[:, at : at + size], gj[...]).astype(BF)
+    for j in range(CHIPS):
+        part = dot_tn(normed[:, 272 * j : 272 * j + 272], gj[...])
+        grad_attn[j, 0] = part[:136].astype(BF)
+        grad_attn[j, 1] = part[136:].astype(BF)
+    lend.wait()
+
+    @pl.when(y < 3)
+    def _():
+        rows_out[256:320] = edge[...]
+
+    chip_rows = rows_out[pl.ds(pl.multiple_of(16 * y, 16), 272)].astype(F32)
+    grad_out[0] = chip_rows[:136].astype(BF)
+    grad_out[1] = chip_rows[136:].astype(BF)
+    reduce.ready(y, c)
     small_bias[...] = jnp.zeros_like(small_bias)
     small_bias[0:1] = jnp.sum(gj[...].astype(F32), axis=0, keepdims=True)
     d = scatter_wait(acc, out_buf, in_buf, y, c, ss, sr)
@@ -345,13 +356,6 @@
     small[0:1] = gain
     small[1:2] = shift
     grad_x[...] = (grad[...] + back).astype(BF)
-    lend.wait()
-
-    @pl.when(y < 3)
-    def _():
-        rows_out[256:320] = edge[...]
-
-    grad_out[...] = rows_out[pl.ds(pl.multiple_of(16 * y, 16), 272)]
     reduce.finish()
 
 
@@ -512,18 +516,12 @@
 
 
 class AttendReduce:
-    def __init__(self, wide, rows, out, own_w, other_w, own_r, other_r, ls, cs, cr, *scratch):
+    def __init__(self, wide, rows, out, other_w, other_r, cs, cr, *scratch):
         self.wide, self.rows = wide, rows
-        self.own_w, self.other_w, self.own_r, self.other_r = own_w, other_w, own_r, other_r
-        self.ls, self.cs, self.cr = ls, cs, cr
+        self.other_w, self.other_r = other_w, other_r
+        self.cs, self.cr = cs, cr
         self.along = AlongX(scratch[0], scratch[1], out, scratch[2], scratch[3])
         self.blocks = scratch[0]
-
-    def keeps(self, c):
-        return [
-            pltpu.make_async_copy(self.wide.at[:, c], self.own_w, self.ls.at[0]),
-            pltpu.make_async_copy(self.rows.at[c], self.own_r, self.ls.at[1]),
-        ]
 
     def swaps(self, y, c):
         sibling = at_chip(y, 1 - c)
@@ -533,22 +531,22 @@
         ]
 
     def begin(self, y, c):
-        for copy in self.keeps(c) + self.swaps(y, c):
+        for copy in self.swaps(y, c):
             copy.start()
 
     def middle(self, y, c):
-        for copy in self.keeps(c) + self.swaps(y, c):
+        for copy in self.swaps(y, c):
             copy.wait()
         blocks = self.blocks
         for i in range(4):
-            block = self.own_w[i].astype(F32) + self.other_w[i].astype(F32)
+            block = self.wide[i, c].astype(F32) + self.other_w[i].astype(F32)
             blocks[i, 0] = block[:, :640].astype(BF)
             blocks[i, 1, :, :320] = block[:, 640:].astype(BF)
-            chunk = self.own_r[:, 256 * i : 256 * i + 256].astype(F32) + self.other_r[:, 256 * i : 256 * i + 256].astype(F32)
+            chunk = self.rows[c, :, 256 * i : 256 * i + 256].astype(F32) + self.other_r[:, 256 * i : 256 * i + 256].astype(F32)
             blocks[i, 1, :, 320:576] = chunk.astype(BF)
             if i < 3:
                 blocks[i, 1, :, 576:] = jnp.zeros((136, HD), BF)
-        chunk = self.own_r[:, 1024:].astype(F32) + self.other_r[:, 1024:].astype(F32)
+        chunk = self.rows[c, :, 1024:].astype(F32) + self.other_r[:, 1024:].astype(F32)
         blocks[3, 1, :, 576:] = chunk.astype(BF)
         self.along.start()
 
@@ -558,55 +556,108 @@
 
 ATTEND_SCRATCH = [
     pltpu.VMEM((4, 136, TQKV), BF),
-    pltpu.VMEM((4, 136, TQKV), BF),
-    pltpu.VMEM((136, D), BF),
     pltpu.VMEM((136, D), BF),
     DMA((2,)),
     DMA((2,)),
-    DMA((2,)),
 ] + x_scratch(640)
 
 
-class Both:
-    def __init__(self, first, along_z):
-        self.first, self.along_z = first, along_z
+BLOCKS = [pltpu.VMEM((4, 2, 136, TQKV), BF), pltpu.VMEM((2, 136, D), BF)]
+
+
+class Hooks:
+    def __init__(self, begin=(), middle=(), late=(), ready=()):
+        self.steps = begin, middle, late, ready
 
     def begin(self, y, c):
-        self.first.begin(y, c)
-        if self.along_z is not None:
-            self.along_z.start()
+        for step in self.steps[0]:
+            step(y, c)
 
     def middle(self, y, c):
-        self.first.middle(y, c)
+        for step in self.steps[1]:
+            step(y, c)
+
+    def late(self):
+        for step in self.steps[2]:
+            step()
+
+    def ready(self, y, c):
+        for step in self.steps[3]:
+            step(y, c)
 
     def finish(self):
-        self.first.finish()
-        if self.along_z is not None:
-            self.along_z.finish()
-
-
-def feed_back_reduce(e, grad, wu_hbm, wd_hbm, vecs, middle, normed, hidden, active, wide, rows, half_u,
-                     grad_middle, grad_up, grad_down, small, half_a, piece_u, *scratch):
-    count = 4 + len(MOVE)
-    own, extra, last = scratch[:count], scratch[count : count + len(ATTEND_SCRATCH)], scratch[count + len(ATTEND_SCRATCH) :]
-    reduce = Both(AttendReduce(wide, rows, half_a, *extra), AlongZ(1 - e, half_u, last[0], piece_u, *last[1:]))
-    feed_back(e, grad, wu_hbm, wd_hbm, vecs, middle, normed, hidden, active, grad_middle, grad_up, grad_down, small,
-              *own, reduce=reduce)
-
-
-def attend_back_reduce(e, later, grad, w_hbm, wo_hbm, vecs, x, normed, queries, kv, kv_other, logsum, attended, up, down,
-                       *refs):
-    refs = list(refs)
-    half_a = refs.pop(0) if later else None
-    outs, refs = refs[:5], refs[5:]
-    half_u = refs.pop(0)
-    piece_a = refs.pop(0) if later else None
-    count = 14 + len(MOVE)
-    own, extra, last = refs[:count], refs[count : count + len(FEED_SCRATCH)], refs[count + len(FEED_SCRATCH) :]
-    along_z = AlongZ(1 - e, half_a, last[0], piece_a, *last[1:]) if later else None
-    reduce = Both(FeedReduce(up, down, half_u, *extra), along_z)
-    attend_back(e, grad, w_hbm, wo_hbm, vecs, x, normed, queries, kv, kv_other, logsum, attended, *outs, *own,
-                reduce=reduce)
+        pass
+
+
+def split(refs, *counts):
+    parts, at = [], 0
+    for count in counts:
+        parts.append(refs[at : at + count])
+        at += count
+    assert at == len(refs)
+    return parts
+
+
+def feed_back_alone(e, *refs):
+    y, c = place()
+    feed_back(e, *refs, greet([at_chip(ring(y, k), c) for k in (1, 2, 3)]))
+
+
+def backward_middle(*refs):
+    a_in, updown, f_in, a_out, half_u, f_out, half_a, a_scr, u_scr, f_scr, grads, w_scr = split(
+        refs, 11, 2, 7, 3, 1, 4, 1, len(ATTEND_OWN), len(FEED_SCRATCH), len(FEED_OWN), 2, len(ATTEND_SCRATCH)
+    )
+    y, c = place()
+    s, x, h, me = plane()
+    arrived = greet([at_chip(ring(y, k), c) for k in (1, 2, 3)] + [at_chip(y, 1 - c)] + x_peers(x, h))
+    wu_hbm, wd_hbm, vecs, *kept = f_in
+    weights = load([(wu_hbm.at[0], f_scr[0]), (wd_hbm.at[0], f_scr[1])], f_scr[7])
+    feed = FeedReduce(*updown, half_u[0], *u_scr)
+    attend = AttendReduce(*grads, half_a[0], *w_scr)
+    grad_x, small, small_bias = a_out
+    attend_back(1, *a_in, grad_x, *grads, small, small_bias, *a_scr, arrived,
+                Hooks(begin=[feed.begin], middle=[feed.middle], ready=[attend.begin]))
+    feed_back(0, grad_x, wu_hbm, wd_hbm, vecs, *kept, *f_out, *f_scr, lambda: None,
+              Hooks(middle=[attend.middle], late=[feed.finish]), weights)
+    attend.finish()
+
+
+def backward_end(*refs):
+    a_in, updown, halves, rest, a_out, g_out, a_scr, u_scr, grads, w_scr, z_scr, g_scr = split(
+        refs, 11, 2, 2, 8, 1, 5, len(ATTEND_OWN), len(FEED_SCRATCH), 2, len(ATTEND_SCRATCH), 12 + 4 + 3, len(GATHER_OWN)
+    )
+    y, c = place()
+    s, x, h, me = plane()
+    sibling = at_chip(y, 1 - c)
+    peers = [at_chip(ring(y, k), c) for k in (1, 2, 3)]
+    barrier = pltpu.get_barrier_semaphore()
+    for target in peers + [sibling] + [at_plane(lax.rem(me + j, 16)) for j in range(1, 16)]:
+        pl.semaphore_signal(barrier, inc=1, device_id=target, device_id_type=MESH)
+
+    @pl.when(x != y)
+    def _():
+        pl.semaphore_signal(barrier, inc=1, device_id={"fsdp": 2 * x + c, "replica": 2 * y + h}, device_id_type=MESH)
+
+    def arrived():
+        pl.semaphore_wait(barrier, 19 + jnp.where(x == y, 0, 1))
+
+    half_u1, half_a1 = halves
+    z_u1, z_a1, z_u0, z_a0 = z_scr[0:3], z_scr[3:6], z_scr[6:9], z_scr[9:12]
+    pair_u1, pair_a1, half_u0, half_a0, small, small_bias, grad_back = z_scr[12:]
+    (grad_x,) = a_out
+    feed = FeedReduce(*updown, half_u0, *u_scr)
+    attend = AttendReduce(*grads, half_a0, *w_scr)
+    first_u = AlongZ(1, half_u1, z_u1[0], pair_u1, z_u1[1], z_u1[2])
+    first_a = AlongZ(1, half_a1, z_a1[0], pair_a1, z_a1[1], z_a1[2])
+
+    def start_first(y, c):
+        first_u.start()
+        first_a.start()
+
+    attend_back(0, *a_in, grad_x, *grads, small, small_bias, *a_scr, arrived,
+                Hooks(begin=[feed.begin, start_first], middle=[feed.middle], ready=[attend.begin]))
+    gather_pieces(feed, attend, first_u, first_a, half_u0, half_a0, z_u0, z_a0, pair_u1, pair_a1,
+                  small, small_bias, *rest, grad_x, *g_out, *g_scr)
 
 
 def shape(dims, kind):
@@ -661,55 +712,84 @@
 HALF_A, HALF_U = shape((2, 136, 640), BF), shape((2, 136, D), BF)
 
 
-def run_feed_back(e, grad, wu, wd, vecs, middle, normed, hidden, active, before=None):
-    outs = [shape((BLK, D), F32), shape((D, D), BF), shape((D, D), BF), shape((8, D), F32)]
-    scratch = [
-        pltpu.VMEM((D, D), BF),
-        pltpu.VMEM((D, D), BF),
-        pltpu.VMEM((ROWS, D), BF),
-        pltpu.VMEM((ROWS, D), BF),
-    ] + MOVE
-    ins = [VMEM, ANY, ANY] + [VMEM] * 5
-    if before is None:
-        return call(functools.partial(feed_back, e), "feed_back_%d" % e, 4 + e, outs, ins, scratch)(
-            grad, wu, wd, vecs, middle, normed, hidden, active
-        )
-    outs += [HALF_A, HALF_U]
-    scratch = scratch + ATTEND_SCRATCH + z_scratch(D)
-    return call(functools.partial(feed_back_reduce, e), "feed_back_%d" % e, 4 + e, outs, ins + [ANY, ANY, VMEM], scratch)(
-        grad, wu, wd, vecs, middle, normed, hidden, active, *before
-    )
-
-
-def run_attend_back(e, grad, w, wo, vecs, x, saved, up, down, half_a=None):
-    outs = [
-        shape((BLK, D), BF),
-        shape((D, TQKV), BF),
-        shape((272, D), BF),
-        shape((8, D), F32),
-        shape((8, TQKV), F32),
-        HALF_U,
+FEED_OWN = [
+    pltpu.VMEM((D, D), BF),
+    pltpu.VMEM((D, D), BF),
+    pltpu.VMEM((ROWS, D), BF),
+    pltpu.VMEM((ROWS, D), BF),
+] + MOVE
+ATTEND_OWN = [
+    pltpu.VMEM((D, TQKV), BF),
+    pltpu.VMEM((TH, D), BF),
+    pltpu.VMEM((ROWS, D), BF),
+    pltpu.VMEM((ROWS, TH), BF),
+    pltpu.VMEM((ROWS, TQKV), BF),
+    pltpu.VMEM((ROWS, 2 * TH), BF),
+    pltpu.VMEM((ROWS, 2 * TH), BF),
+    pltpu.VMEM((ROWS, 2 * TH), F32),
+    pltpu.VMEM((TH, D), BF),
+    pltpu.VMEM((HD, D), BF),
+] + MOVE + [DMA, DMA, DMA, DMA]
+GATHER_OWN = [
+    pltpu.VMEM((BLK, D), BF),
+    pltpu.VMEM((BLK, D), BF),
+    DMA((2,)),
+    DMA((2,)),
+    pltpu.VMEM((2, 136, D), BF),
+    pltpu.VMEM((136, D), BF),
+    pltpu.VMEM((2, 136, 640), BF),
+    pltpu.VMEM((2, 136, 640), BF),
+    pltpu.VMEM((2, 16, D), F32),
+    pltpu.VMEM((2, 16, D), F32),
+    pltpu.VMEM((3, 2, 16, D), F32),
+    pltpu.VMEM((2, 16, D), BF),
+    pltpu.VMEM((15, 16, D), BF),
+    DMA((2,)),
+    DMA((2,)),
+    DMA((2, 3)),
+    DMA((2, 3)),
+    DMA,
+    DMA,
+    DMA((3,)),
+    DMA((3,)),
+    DMA((15,)),
+    DMA((15,)),
+]
+FEED_OUTS = [shape((BLK, D), F32), shape((D, D), BF), shape((D, D), BF), shape((8, D), F32)]
+SMALLS = [shape((8, D), F32), shape((8, TQKV), F32)]
+
+
+def run_feed_back(grad, wu, wd, vecs, middle, normed, hidden, active):
+    return call(functools.partial(feed_back_alone, 1), "feed_back_1", 4, FEED_OUTS, [VMEM, ANY, ANY] + [VMEM] * 5, FEED_OWN)(
+        grad, wu, wd, vecs, middle, normed, hidden, active
+    )
+
+
+def run_backward_middle(attend_args, up, down, feed_args):
+    outs = [shape((BLK, D), BF)] + SMALLS + [HALF_U] + FEED_OUTS + [HALF_A]
+    ins = [VMEM, ANY, ANY] + [VMEM] * 8 + [ANY] * 4 + [VMEM] * 5
+    scratch = ATTEND_OWN + FEED_SCRATCH + FEED_OWN + BLOCKS + ATTEND_SCRATCH
+    return call(backward_middle, "backward_middle", 5, outs, ins, scratch)(*attend_args, up, down, *feed_args)
+
+
+def run_backward_end(attend_args, up, down, half_u, half_a, rest):
+    both = shape((2, BLK, D), BF)
+    outs = [shape((BLK, D), BF)]
+    outs += [shape((4, 2, 136, D), BF), shape((4, 2, 136, 640), BF), shape((16, D), F32), both, both]
+    ins = [VMEM, ANY, ANY] + [VMEM] * 8 + [ANY] * 2 + [VMEM] * (2 + len(rest))
+    pairs = [
+        pltpu.VMEM((2, 136, D), BF),
+        pltpu.VMEM((2, 136, 640), BF),
+        pltpu.VMEM((2, 136, D), BF),
+        pltpu.VMEM((2, 136, 640), BF),
+        pltpu.VMEM((8, D), F32),
+        pltpu.VMEM((8, TQKV), F32),
+        pltpu.VMEM((8, 128), F32),
     ]
-    scratch = [
-        pltpu.VMEM((D, TQKV), BF),
-        pltpu.VMEM((TH, D), BF),
-        pltpu.VMEM((ROWS, D), BF),
-        pltpu.VMEM((ROWS, TH), BF),
-        pltpu.VMEM((ROWS, TQKV), BF),
-        pltpu.VMEM((ROWS, 2 * TH), BF),
-        pltpu.VMEM((ROWS, 2 * TH), BF),
-        pltpu.VMEM((ROWS, 2 * TH), F32),
-        pltpu.VMEM((TH, D), BF),
-        pltpu.VMEM((HD, D), BF),
-    ] + MOVE + [DMA, DMA, DMA, DMA] + FEED_SCRATCH
-    later = half_a is not None
-    body = functools.partial(attend_back_reduce, e, later)
-    ins = [VMEM, ANY, ANY] + [VMEM] * 8 + [ANY, ANY]
-    more = []
-    if later:
-        outs, scratch, ins, more = outs + [HALF_A], scratch + z_scratch(640), ins + [VMEM], [half_a]
-    return call(body, "attend_back_%d" % e, 6 + e, outs, ins, scratch)(
-        grad, w, wo, vecs, x, *saved, up, down, *more
+    zs = (z_scratch(D) + z_scratch(640)) * 2
+    scratch = ATTEND_OWN + FEED_SCRATCH + BLOCKS + ATTEND_SCRATCH + zs + pairs + GATHER_OWN
+    return call(backward_end, "backward_end", 6, outs, ins, scratch)(
+        *attend_args, up, down, half_u, half_a, *rest
     )
 
 
@@ -911,33 +991,23 @@
             remote(place_in, place_in, self.gs.at[self.i, k - 1], self.gr.at[self.i, k - 1], targets[k - 1]).wait_recv()
 
 
-def gather_pieces(wide, rows, half_u, done_u, done_a, one_0, two_0, heads_0, one_1, two_1, heads_1,
-                  act_0, act_1, back_0, back_1, out_u, out_a, out_small, out_act, out_back,
-                  swap_act, swap_back, ws, wr, piece_u, moved_u, piece_a, moved_a, half_a, small, small_c, small_y, small_x, small_z,
-                  ts, tr, gs, gr, cs, cr, ys, yr, zs, zr, *extra):
+def gather_pieces(feed, attend, first_u, first_a, half_u, half_a, z_u, z_a, done_u, done_a, one_0, heads_0,
+                  two_0, one_1, two_1, heads_1, act_0, act_1, back_1, spare, back_0, out_u, out_a, out_small, out_act, out_back,
+                  swap_act, swap_back, ws, wr, piece_u, moved_u, piece_a, moved_a, small, small_c, small_y, small_x, small_z,
+                  ts, tr, gs, gr, cs, cr, ys, yr, zs, zr):
     y, c = place()
     s, x, h, me = plane()
     sibling = at_chip(y, 1 - c)
     peers = [at_chip(ring(y, k), c) for k in (1, 2, 3)]
-    reduce = AttendReduce(wide, rows, half_a, *extra[: len(ATTEND_SCRATCH)])
-    extra = extra[len(ATTEND_SCRATCH) :]
-    z_u = AlongZ(0, half_u, extra[0], piece_u, extra[1], extra[2])
-    z_a = AlongZ(0, half_a, extra[3], piece_a, extra[4], extra[5])
+    z_u = AlongZ(0, half_u, z_u[0], piece_u, z_u[1], z_u[2])
+    z_a = AlongZ(0, half_a, z_a[0], piece_a, z_a[1], z_a[2])
     g_u = Gather(piece_u, moved_u, out_u, 0, 0, ts, tr, gs, gr)
     g_a = Gather(piece_a, moved_a, out_a, 1, 320, ts, tr, gs, gr)
-    barrier = pltpu.get_barrier_semaphore()
-    for target in peers + [sibling] + [at_plane(lax.rem(me + j, 16)) for j in range(1, 16)]:
-        pl.semaphore_signal(barrier, inc=1, device_id=target, device_id_type=MESH)
-
-    @pl.when(x != y)
-    def _():
-        pl.semaphore_signal(barrier, inc=1, device_id={"fsdp": 2 * x + c, "replica": 2 * y + h}, device_id_type=MESH)
-
+    attend.middle(y, c)
+    feed.finish()
+    z_u.start()
     build_small(small.at[0], one_0, two_0, heads_0, y)
     build_small(small.at[1], one_1, two_1, heads_1, y)
-    pl.semaphore_wait(barrier, 19 + jnp.where(x == y, 0, 1))
-    z_u.start()
-    reduce.begin(y, c)
     swap_act[...] = jnp.where(s == 0, act_1[...].astype(F32), act_0[...].astype(F32)).astype(BF)
     swap_back[...] = jnp.where(s == 0, back_1[...].astype(F32), back_0[...].astype(F32)).astype(BF)
     swaps = [
@@ -948,12 +1018,15 @@
     out_back[s] = jnp.where(s == 0, back_0[...].astype(F32), back_1[...].astype(F32)).astype(BF)
     cross = remote(small, small_c, cs, cr, sibling)
     cross.start()
-    reduce.middle(y, c)
     cross.wait()
     small[...] = small[...] + small_c[...]
     hops = [remote(small, small_y.at[k - 1], ys.at[k - 1], yr.at[k - 1], peers[k - 1]) for k in (1, 2, 3)]
     for hop in hops:
         hop.start()
+    first_u.finish()
+    first_a.finish()
+    attend.finish()
+    z_a.start()
     z_u.finish()
 
     @pl.when(s == 1)
@@ -961,8 +1034,6 @@
         piece_u[...] = done_u[...]
 
     g_u.start()
-    reduce.finish()
-    z_a.start()
     g_u.spread()
     for hop in hops:
         hop.wait()
@@ -1000,40 +1071,6 @@
     g_a.finish()
 
 
-def run_gather_pieces(wide, rows, half_u, done_u, done_a, smalls, acts, backs):
-    both = shape((2, BLK, D), BF)
-    outs = [shape((4, 2, 136, D), BF), shape((4, 2, 136, 640), BF), shape((16, D), F32), both, both]
-    scratch = [
-        pltpu.VMEM((BLK, D), BF),
-        pltpu.VMEM((BLK, D), BF),
-        DMA((2,)),
-        DMA((2,)),
-        pltpu.VMEM((2, 136, D), BF),
-        pltpu.VMEM((136, D), BF),
-        pltpu.VMEM((2, 136, 640), BF),
-        pltpu.VMEM((2, 136, 640), BF),
-        pltpu.VMEM((2, 136, 640), BF),
-        pltpu.VMEM((2, 16, D), F32),
-        pltpu.VMEM((2, 16, D), F32),
-        pltpu.VMEM((3, 2, 16, D), F32),
-        pltpu.VMEM((2, 16, D), BF),
-        pltpu.VMEM((15, 16, D), BF),
-        DMA((2,)),
-        DMA((2,)),
-        DMA((2, 3)),
-        DMA((2, 3)),
-        DMA,
-        DMA,
-        DMA((3,)),
-        DMA((3,)),
-        DMA((15,)),
-        DMA((15,)),
-    ] + ATTEND_SCRATCH + z_scratch(D) + z_scratch(640)
-    return call(gather_pieces, "gather_pieces", 9, outs, [ANY, ANY] + [VMEM] * 13, scratch)(
-        wide, rows, half_u, done_u, done_a, *smalls, *acts, *backs
-    )
-
-
 def assemble(all_u, all_a, small, attn, out, up, down, b_attn, b_out, b_up, b_down, gain, shift):
     y, c = place()
     f = 2 * y + c
@@ -1118,23 +1155,22 @@
         acts.append(result)
         stream = result
     grad = lax.dynamic_index_in_dim(cotangent, s, 0, keepdims=False)[0]
-    in_grads, smalls, before, half_a = [None, None], [None, None], None, None
-    for e in (1, 0):
-        x, kept, middle, kept_two = saved[e]
-        grad_middle, grad_up, grad_down, two, *reduced = run_feed_back(
-            e, grad, wu, wd, vecs[e], middle, *kept_two, before=before
-        )
-        if reduced:
-            half_a, done_u = reduced
-        grad, grad_attn, grad_out, one, heads, half_u, *done_a = run_attend_back(
-            e, grad_middle, wa, wo, vecs[e], x, kept, grad_up.reshape(4, 2, 136, D), grad_down.reshape(2, 4, 136, D),
-            half_a,
-        )
-        in_grads[e] = grad
-        before = (grad_attn.reshape(4, 2, 136, TQKV), grad_out.reshape(2, 136, D), half_u)
-        smalls[e] = (one, two, heads)
-    all_u, all_a, small, all_acts, all_grads = run_gather_pieces(
-        *before, done_u, *done_a, smalls[0] + smalls[1], acts, in_grads
+    x_1, kept_1, middle_1, kept_two_1 = saved[1]
+    x_0, kept_0, middle_0, kept_two_0 = saved[0]
+    grad_middle, up, down, two_1 = run_feed_back(grad, wu, wd, vecs[1], middle_1, *kept_two_1)
+    back_1, one_1, heads_1, half_u, grad_middle, up_0, down_0, two_0, half_a = run_backward_middle(
+        (grad_middle, wa, wo, vecs[1], x_1, *kept_1),
+        up.reshape(4, 2, 136, D),
+        down.reshape(2, 4, 136, D),
+        (wu, wd, vecs[0], middle_0, *kept_two_0),
+    )
+    back_0, all_u, all_a, small, all_acts, all_grads = run_backward_end(
+        (grad_middle, wa, wo, vecs[0], x_0, *kept_0),
+        up_0.reshape(4, 2, 136, D),
+        down_0.reshape(2, 4, 136, D),
+        half_u,
+        half_a,
+        (two_0, one_1, two_1, heads_1, *acts, back_1, two_0),
     )
     attn, out, up, down, b_attn, b_out, b_up, b_down, gain, shift = run_assemble(all_u, all_a, small)
     return (

time: 469 us -> 452 us (0.964)
  Pallas kernels: 442 us -> 425 us
    pallas_call x5 -> x3, Pallas kernels: 275 us -> 258 us  [the longest x1 175 us: run_backward_end(): call(backward_end, 'backward_end', 6, outs, ins, scratch)]
where the time goes in v6:
time: 452 us; the launch traced here: 446 us
  Pallas kernels  425 us (94%)
  local copies, waits for them, and re-layouts  11.5 us (3%)
  other arithmetic  6.27 us (1%)
    pallas_call x1, Pallas kernels, run_backward_end(): call(backward_end, 'backward_end', 6, outs, ins, scratch)  175 us
    pallas_call x1, Pallas kernels, run_spread(): pl.pallas_call(spread, name='spread', out_shape=outs, in_specs=[ANY] * 5,...  60 us
    pallas_call x1, Pallas kernels, run_backward_middle(): call(backward_middle, 'backward_middle', 5, outs, ins, scratch)  58 us
    pallas_call x2, Pallas kernels, run_attend_forward(): call(functools.partial(attend_forward, e), 'attend_forward_%d' % e, e, ou...  55.4 us
    pallas_call x2, Pallas kernels, run_feed_forward(): call(functools.partial(feed_forward, e), 'feed_forward_%d' % e, 2 + e, ou...  45.8 us
    pallas_call x1, Pallas kernels, run_feed_back(): call(functools.partial(feed_back_alone, 1), 'feed_back_1', 4, FEED_OUTS,...  25.1 us
  transfers between devices with their start and end apart: 1, of which 0 were waited for; matrix products, arithmetic and copies ran while one was open for 2% of the time, Pallas kernels for 0%

profile of v6, /device:TPU:4, one launch (start us, length us, event | category | flops | bytes accessed | tf_op | source)
XLA Modules:
  0.0 445.6 jit_solution(16953344816585970431)
XLA Ops:
  0.7 1.0 slice_bitcast_fusion.7
  1.7 1.6 collective-permute-start
  3.3 1.1 fusion.1
  4.4 1.3 fusion
  5.8 0.0 copy-start.5
  5.8 0.0 copy-start.6
  5.8 0.0 copy-start.9
  5.8 0.0 copy-start.10
  5.8 0.0 copy-start.7
  5.8 0.0 copy-start.8
  5.9 0.3 slice_bitcast_fusion.5
  6.2 0.1 pad.8.clone
  6.2 0.2 copy-done.5
  6.4 0.0 copy-done.6
  6.5 0.0 copy-done.9
  6.5 0.0 copy-done.10
  6.5 0.2 dynamic_update_slice.9
  6.8 0.3 dynamic_update_slice.10
  7.1 0.0 copy-done.8
  7.1 0.3 dynamic_update_slice.11
  7.4 0.6 pad_maximum_fusion.3.send_v
  8.0 1.7 dynamic-slice_bitcast_fusion
  9.7 0.1 maximum_bitcast_fusion
  9.9 0.1 concatenate.22
  10.0 0.1 concatenate.24
  10.1 0.1 concatenate.23
  10.3 1.3 pad_maximum_fusion.1.send_u
  11.5 1.1 pad_maximum_fusion.2.send_a
  12.7 0.0 collective-permute-done
  12.7 0.0 copy-done.2
  12.7 1.8 maximum_maximum_fusion.send_o
  14.5 60.0 %spread.1 = (bf16[2,4,2,136,960]{4,3,2,1,0:T(8,128)(2,1)}, bf16[2,4,2,136,1088]{4,3,2,1,0:T(8,128)(2,1)}, bf16[2,2,544,1088]{3,2,1,0:T(8,128)(2,1)}, bf16[2,2,19...) custom-call(bf16[4,136,960]{2,1,0:T(8,128)(2,1)} %pad_maximum_fusion.2.send_a, ...), custom_call_target="tpu_custom_call" | custom-call | tf_op jit(solution)/shard_map/spread/pallas_call | solution.py:911
  74.5 0.0 copy-start.1
  74.5 1.0 slice_bitcast_fusion.6
  75.5 1.4 slice_bitcast_fusion.1
  76.9 0.1 convert_reduce_fusion
  77.0 0.7 slice_bitcast_fusion.8
  77.7 1.2 pad_maximum_fusion.wo_hbm.refs_2_
  78.9 28.4 %attend_forward_0.1 = (f32[64,1088]{1,0:T(8,128)}, bf16[256,1088]{1,0:T(8,128)(2,1)}, bf16[256,320]{1,0:T(8,128)(2,1)}, bf16[256,640]{1,0:T(8,128)(2,1)}, bf16[2...) custom-call(bf16[64,1088]{1,0:T(8,128)(2,1)} %get-tuple-element.158.x.refs_4_, ...), custom_call_target="tpu_custom_call" | custom-call | flops 10000000 | bytes 10000 | tf_op jit(solution)/shard_map/attend_forward_0/pallas_call | solution.py:703
  107.3 22.7 %feed_forward_0.1 = (bf16[64,1088]{1,0:T(8,128)(2,1)}, bf16[256,1088]{1,0:T(8,128)(2,1)}, f32[256,1088]{1,0:T(8,128)}, bf16[256,1088]{1,0:T(8,128)(2,1)}) custom-call(f32[64,1088]{1,0:T(8,128)} %get-tuple-element.72.middle.refs_16_, bf16[2,1088,1088]{2,1,0:T(8,128)(2,1)} %bitcast.60, bf16[2,1088,1088]{2,1,0:T(8,128)(2,1)} %bitcast.64, ...), custom_call_target="tpu_custom_call" | custom-call | flops 10000000 | bytes 10000 | tf_op jit(solution)/shard_map/feed_forward_0/pallas_call | solution.py:709
  130.0 27.0 %attend_forward_1.1 = (f32[64,1088]{1,0:T(8,128)}, bf16[256,1088]{1,0:T(8,128)(2,1)}, bf16[256,320]{1,0:T(8,128)(2,1)}, bf16[256,640]{1,0:T(8,128)(2,1)}, bf16[2...) custom-call(bf16[64,1088]{1,0:T(8,128)(2,1)} %get-tuple-element.73.x.refs_4_.refs_19_, ...), custom_call_target="tpu_custom_call" | custom-call | flops 10000000 | bytes 10000 | tf_op jit(solution)/shard_map/attend_forward_1/pallas_call | solution.py:703
  157.1 23.0 %feed_forward_1.1 = (bf16[64,1088]{1,0:T(8,128)(2,1)}, bf16[256,1088]{1,0:T(8,128)(2,1)}, f32[256,1088]{1,0:T(8,128)}, bf16[256,1088]{1,0:T(8,128)(2,1)}) custom-call(f32[64,1088]{1,0:T(8,128)} %get-tuple-element.74.middle.refs_4_, bf16[2,1088,1088]{2,1,0:T(8,128)(2,1)} %bitcast.61, bf16[2,1088,1088]{2,1,0:T(8,128)(2,1)} %bitcast.65, ...), custom_call_target="tpu_custom_call" | custom-call | flops 10000000 | bytes 10000 | tf_op jit(solution)/shard_map/feed_forward_1/pallas_call | solution.py:709
  180.1 25.1 %feed_back_1.1 = (f32[64,1088]{1,0:T(8,128)}, bf16[1088,1088]{1,0:T(8,128)(2,1)}, bf16[1088,1088]{1,0:T(8,128)(2,1)}, f32[8,1088]{1,0:T(8,128)}) custom-call(bf16[64,1088]{1,0:T(8,128)(2,1)} %get-tuple-element.159.refs_0_, bf16[2,1088,1088]{2,1,0:T(8,128)(2,1)} %bitcast.62, bf16[2,1088,1088]{2,1,0:T(8,128)(2,1)} %bitcast.66, ...), custom_call_target="tpu_custom_call" | custom-call | flops 10000000 | bytes 10000 | tf_op jit(solution)/shard_map/feed_back_1/pallas_call | solution.py:763
  205.1 58.0 %backward_middle.1 = (bf16[64,1088]{1,0:T(8,128)(2,1)}, f32[8,1088]{1,0:T(8,128)}, f32[8,960]{1,0:T(8,128)}, bf16[2,136,1088]{2,1,0:T(8,128)(2,1)}, f32[64,1088]...) custom-call(f32[64,1088]{1,0:T(8,128)} %get-tuple-element.78.refs_0_, ...), custom_call_target="tpu_custom_call" | custom-call | flops 10000000 | bytes 10000 | tf_op jit(solution)/shard_map/backward_middle/pallas_call | solution.py:772
  263.1 175.0 %backward_end.1 = (bf16[64,1088]{1,0:T(8,128)(2,1)}, bf16[4,2,136,1088]{3,2,1,0:T(8,128)(2,1)}, bf16[4,2,136,640]{3,2,1,0:T(8,128)(2,1)}, f32[16,1088]{1,0:T(8,1...) custom-call(f32[64,1088]{1,0:T(8,128)} %get-tuple-element.90.refs_0_, bf16[2,1088,960]{2,1,0:T(8,128)(2,1)} %bitcast.71, ...), custom_call_target="tpu_custom_call" | custom-call | flops 10000000 | bytes 10000 | tf_op jit(solution)/shard_map/backward_end/pallas_call | solution.py:791
  438.1 5.8 %assemble.1 = (f32[136,3264]{1,0:T(8,128)}, f32[136,1088]{1,0:T(8,128)}, f32[136,4352]{1,0:T(8,128)}, f32[544,1088]{1,0:T(8,128)}, f32[1,272]{1,0:T(1,128)}, /*i...) custom-call(bf16[4,2,136,1088]{3,2,1,0:T(8,128)(2,1)} %get-tuple-element.109.al, ...), custom_call_target="tpu_custom_call" | custom-call | tf_op jit(solution)/shard_map/assemble/pallas_call | solution.py:1104
  443.9 0.7 copy.38
  444.6 0.7 copy.39
  (16 shorter events, 0.1 us)
Async XLA Ops:
  0.6 5.2 %copy-start = (bf16[1,136,4352]{2,1,0:T(8,128)(2,1)S(1)}, bf16[1,136,4352]{2,1,0:T(8,128)(2,1)}, u32[]{:S(2)}) copy-start(bf16[1,136,4352]{2,1,0:T(8,128)(2,1)} %param.16) | copy-start | bytes 3551236
  1.7 11.0 %collective-permute-start = (bf16[48,1088]{1,0:T(8,128)(2,1)S(1)}, bf16[48,1088]{1,0:T(8,128)(2,1)}, u32[]{:S(2)}, u32[]{:S(2)}) collective-permute-start(bf16[48,1088]{1,0:T(8,128)(2,1)S(1)} %slice_bitcast_fusion.7), channel_id=1, source_target_pairs={{0,16},{8,24},{16,32},{24,40},{32,48},{40,56},{48,0},{56,8},{1,17}... | collective-permute-start | bytes 313352 | tf_op jit(solution)/shard_map/ppermute | solution.py:1133
  5.8 0.7 copy-start.5
  5.8 0.7 copy-start.6
  5.8 0.7 copy-start.9
  5.8 0.7 copy-start.10
  5.8 1.0 copy-start.7
  5.8 1.3 copy-start.8
  11.5 1.1 copy-start.2
  74.5 2.4 copy-start.1
  438.1 5.8 %copy-start.4 = (bf16[2,64,1088]{2,1,0:T(8,128)(2,1)S(1)}, bf16[2,64,1088]{2,1,0:T(8,128)(2,1)}, u32[]{:S(2)}) copy-start(bf16[2,64,1088]{2,1,0:T(8,128)(2,1)} %get-tuple-element.107) | copy-start | bytes 835588
  438.1 6.5 %copy-start.3 = (bf16[2,64,1088]{2,1,0:T(8,128)(2,1)S(1)}, bf16[2,64,1088]{2,1,0:T(8,128)(2,1)}, u32[]{:S(2)}) copy-start(bf16[2,64,1088]{2,1,0:T(8,128)(2,1)} %get-tuple-element.108) | copy-start | bytes 835588

commit v7 on v6

--- a/solution.py
+++ b/solution.py
@@ -386,16 +386,21 @@
     return x_peers(x, h) + z_peers(s, h)
 
 
+def block_of(x, y):
+    return lax.rem(x - y + 8, 4)
+
+
 class AlongX:
     def __init__(self, blocks, landing, out, send, recv):
         self.blocks, self.landing, self.out, self.send, self.recv = blocks, landing, out, send, recv
 
     def copies(self):
+        y, c = place()
         s, x, h, me = plane()
         targets = x_peers(x, h)
         for k in ORDER:
             yield remote(
-                self.blocks.at[lax.rem(x + k, 4)], self.landing.at[k - 1], self.send.at[k - 1], self.recv.at[k - 1],
+                self.blocks.at[block_of(x + k, y)], self.landing.at[k - 1], self.send.at[k - 1], self.recv.at[k - 1],
                 targets[k - 1],
             )
 
@@ -404,27 +409,29 @@
             copy.start()
 
     def finish(self):
+        y, c = place()
         s, x, h, me = plane()
+        own = block_of(x, y)
         for copy in self.copies():
             copy.wait()
 
         def add(i, carry):
             rows = pl.ds(pl.multiple_of(8 * (i % 17), 8), 8)
-            total = self.blocks[x, i // 17, rows].astype(F32)
+            total = self.blocks[own, i // 17, rows].astype(F32)
             for k in range(3):
                 total = total + self.landing[k, i // 17, rows].astype(F32)
             self.out[i // 17, rows] = total.astype(BF)
             return carry
 
-        lax.fori_loop(0, 34, add, 0)
-
-
-def x_scratch(width):
-    return [pltpu.VMEM((4, 2, 136, width), BF), pltpu.VMEM((3, 2, 136, width), BF), DMA((3,)), DMA((3,))]
+        lax.fori_loop(0, 17 * self.out.shape[0], add, 0)
+
+
+def x_scratch(count, width):
+    return [pltpu.VMEM((4, count, 136, width), BF), pltpu.VMEM((3, count, 136, width), BF), DMA((3,)), DMA((3,))]
 
 
 class AlongZ:
-    def __init__(self, layer, blocks, landing, out, send, recv):
+    def __init__(self, layer, blocks, out, landing, send, recv):
         self.layer, self.blocks, self.landing, self.out, self.send, self.recv = layer, blocks, landing, out, send, recv
 
     def copies(self):
@@ -458,61 +465,49 @@
                 self.out[i // 17, rows] = total.astype(BF)
                 return carry
 
-            lax.fori_loop(0, 34, add, 0)
-
-        @pl.when(s != self.layer)
-        def _():
-            self.out[...] = jnp.zeros_like(self.out)
-
-
-def z_scratch(width):
-    return [pltpu.VMEM((3, 2, 136, width), BF), DMA((2,)), DMA((3,))]
+            lax.fori_loop(0, 17 * self.out.shape[0], add, 0)
+
+
+def z_scratch(count, width):
+    return [pltpu.VMEM((3, count, 136, width), BF), DMA((2,)), DMA((3,))]
 
 
 class FeedReduce:
-    def __init__(self, up, down, out, other, ls, cs, cr, *scratch):
+    def __init__(self, up, down, out_up, out_down, other, ls, cs, cr, *scratch):
         self.sources = (up, down)
         self.other, self.ls, self.cs, self.cr = other, ls, cs, cr
-        self.along = AlongX(scratch[0], scratch[1], out, scratch[2], scratch[3])
-        self.blocks = scratch[0]
-
-    def keeps(self, c):
-        up, down = self.sources
-        return [
-            pltpu.make_async_copy(up.at[:, c], self.blocks.at[:, 0], self.ls.at[0]),
-            pltpu.make_async_copy(down.at[c], self.blocks.at[:, 1], self.ls.at[1]),
-        ]
-
-    def swaps(self, y, c):
+        self.up = AlongX(scratch[0], scratch[1], out_up, *scratch[2:4])
+        self.down = AlongX(scratch[4], scratch[5], out_down, *scratch[6:8])
+
+    def copies(self, y, c):
         up, down = self.sources
         sibling = at_chip(y, 1 - c)
-        return [
-            remote(up.at[:, 1 - c], self.other.at[:, 0], self.cs.at[0], self.cr.at[0], sibling),
-            remote(down.at[1 - c], self.other.at[:, 1], self.cs.at[1], self.cr.at[1], sibling),
-        ]
+        for i, (unit, own, theirs) in enumerate(
+            ((self.up, up.at[:, c], up.at[:, 1 - c]), (self.down, down.at[c], down.at[1 - c]))
+        ):
+            keep = pltpu.make_async_copy(own, unit.blocks.at[:, 0], self.ls.at[i])
+            swap = remote(theirs, self.other.at[:, i], self.cs.at[i], self.cr.at[i], sibling)
+            yield unit, keep, swap
 
     def begin(self, y, c):
-        for copy in self.keeps(c) + self.swaps(y, c):
-            copy.start()
+        for unit, keep, swap in self.copies(y, c):
+            swap.start()
+            keep.start()
 
     def middle(self, y, c):
-        for copy in self.keeps(c) + self.swaps(y, c):
-            copy.wait()
-
-        def add(i, carry):
-            self.blocks[i // 2, i % 2] = (
-                self.blocks[i // 2, i % 2].astype(F32) + self.other[i // 2, i % 2].astype(F32)
-            ).astype(BF)
-            return carry
-
-        lax.fori_loop(0, 8, add, 0)
-        self.along.start()
-
-    def finish(self):
-        self.along.finish()
-
-
-FEED_SCRATCH = [pltpu.VMEM((4, 2, 136, D), BF), DMA((2,)), DMA((2,)), DMA((2,))] + x_scratch(D)
+        for at, (unit, keep, swap) in enumerate(self.copies(y, c)):
+            keep.wait()
+            swap.wait()
+
+            def add(i, carry, unit=unit, at=at):
+                unit.blocks[i, 0] = (unit.blocks[i, 0].astype(F32) + self.other[i, at].astype(F32)).astype(BF)
+                return carry
+
+            lax.fori_loop(0, 4, add, 0)
+            unit.start()
+
+
+FEED_SCRATCH = [pltpu.VMEM((4, 2, 136, D), BF), DMA((2,)), DMA((2,)), DMA((2,))] + x_scratch(1, D) * 2
 
 
 class AttendReduce:
@@ -559,7 +554,7 @@
     pltpu.VMEM((136, D), BF),
     DMA((2,)),
     DMA((2,)),
-] + x_scratch(640)
+] + x_scratch(2, 640)
 
 
 BLOCKS = [pltpu.VMEM((4, 2, 136, TQKV), BF), pltpu.VMEM((2, 136, D), BF)]
@@ -605,59 +600,53 @@
 
 def backward_middle(*refs):
     a_in, updown, f_in, a_out, half_u, f_out, half_a, a_scr, u_scr, f_scr, grads, w_scr = split(
-        refs, 11, 2, 7, 3, 1, 4, 1, len(ATTEND_OWN), len(FEED_SCRATCH), len(FEED_OWN), 2, len(ATTEND_SCRATCH)
+        refs, 11, 2, 7, 3, 2, 4, 1, len(ATTEND_OWN), len(FEED_SCRATCH), len(FEED_OWN), 2, len(ATTEND_SCRATCH)
     )
     y, c = place()
     s, x, h, me = plane()
     arrived = greet([at_chip(ring(y, k), c) for k in (1, 2, 3)] + [at_chip(y, 1 - c)] + x_peers(x, h))
     wu_hbm, wd_hbm, vecs, *kept = f_in
     weights = load([(wu_hbm.at[0], f_scr[0]), (wd_hbm.at[0], f_scr[1])], f_scr[7])
-    feed = FeedReduce(*updown, half_u[0], *u_scr)
+    feed = FeedReduce(*updown, *half_u, *u_scr)
     attend = AttendReduce(*grads, half_a[0], *w_scr)
     grad_x, small, small_bias = a_out
     attend_back(1, *a_in, grad_x, *grads, small, small_bias, *a_scr, arrived,
                 Hooks(begin=[feed.begin], middle=[feed.middle], ready=[attend.begin]))
     feed_back(0, grad_x, wu_hbm, wd_hbm, vecs, *kept, *f_out, *f_scr, lambda: None,
-              Hooks(middle=[attend.middle], late=[feed.finish]), weights)
+              Hooks(middle=[attend.middle], late=[feed.up.finish, feed.down.finish]), weights)
     attend.finish()
 
 
 def backward_end(*refs):
-    a_in, updown, halves, rest, a_out, g_out, a_scr, u_scr, grads, w_scr, z_scr, g_scr = split(
-        refs, 11, 2, 2, 8, 1, 5, len(ATTEND_OWN), len(FEED_SCRATCH), 2, len(ATTEND_SCRATCH), 12 + 4 + 3, len(GATHER_OWN)
+    a_in, updown, halves, rest, a_out, g_out, a_scr, u_scr, grads, w_scr, z_scr, own, g_scr = split(
+        refs, 11, 2, 3, 7, 1, 6, len(ATTEND_OWN), len(FEED_SCRATCH), 2, len(ATTEND_SCRATCH), 18, 11, len(GATHER_OWN)
     )
     y, c = place()
     s, x, h, me = plane()
     sibling = at_chip(y, 1 - c)
     peers = [at_chip(ring(y, k), c) for k in (1, 2, 3)]
-    barrier = pltpu.get_barrier_semaphore()
-    for target in peers + [sibling] + [at_plane(lax.rem(me + j, 16)) for j in range(1, 16)]:
-        pl.semaphore_signal(barrier, inc=1, device_id=target, device_id_type=MESH)
-
-    @pl.when(x != y)
-    def _():
-        pl.semaphore_signal(barrier, inc=1, device_id={"fsdp": 2 * x + c, "replica": 2 * y + h}, device_id_type=MESH)
-
-    def arrived():
-        pl.semaphore_wait(barrier, 19 + jnp.where(x == y, 0, 1))
-
-    half_u1, half_a1 = halves
-    z_u1, z_a1, z_u0, z_a0 = z_scr[0:3], z_scr[3:6], z_scr[6:9], z_scr[9:12]
-    pair_u1, pair_a1, half_u0, half_a0, small, small_bias, grad_back = z_scr[12:]
+    arrived = greet(peers + [sibling] + [at_plane(lax.rem(me + j, 16)) for j in range(1, 16)])
+    half_up, half_down, half_a, sum_up, sum_down, sum_a, late_up, late_down, late_a, small, small_bias = own
     (grad_x,) = a_out
-    feed = FeedReduce(*updown, half_u0, *u_scr)
-    attend = AttendReduce(*grads, half_a0, *w_scr)
-    first_u = AlongZ(1, half_u1, z_u1[0], pair_u1, z_u1[1], z_u1[2])
-    first_a = AlongZ(1, half_a1, z_a1[0], pair_a1, z_a1[1], z_a1[2])
+    feed = FeedReduce(*updown, half_up, half_down, *u_scr)
+    attend = AttendReduce(*grads, half_a, *w_scr)
+    first = [AlongZ(1, half, out, *z_scr[3 * i : 3 * i + 3]) for i, (half, out) in enumerate(zip(halves, (sum_up, sum_down, sum_a)))]
+    last = [
+        AlongZ(0, half, out, *z_scr[9 + 3 * i : 12 + 3 * i])
+        for i, (half, out) in enumerate(zip((half_up, half_down, half_a), (late_up, late_down, late_a)))
+    ]
 
     def start_first(y, c):
-        first_u.start()
-        first_a.start()
+        for unit in first:
+            unit.start()
+
+    def up_along_z(y, c):
+        feed.up.finish()
+        last[0].start()
 
     attend_back(0, *a_in, grad_x, *grads, small, small_bias, *a_scr, arrived,
-                Hooks(begin=[feed.begin, start_first], middle=[feed.middle], ready=[attend.begin]))
-    gather_pieces(feed, attend, first_u, first_a, half_u0, half_a0, z_u0, z_a0, pair_u1, pair_a1,
-                  small, small_bias, *rest, grad_x, *g_out, *g_scr)
+                Hooks(begin=[feed.begin, start_first], middle=[feed.middle], ready=[attend.begin, up_along_z]))
+    gather_pieces(feed, attend, first, last, small, small_bias, *rest, grad_x, *g_out, *g_scr)
 
 
 def shape(dims, kind):
@@ -709,7 +698,7 @@
     return call(functools.partial(feed_forward, e), "feed_forward_%d" % e, 2 + e, outs, [VMEM, ANY, ANY, VMEM], scratch)(middle, wu, wd, vecs)
 
 
-HALF_A, HALF_U = shape((2, 136, 640), BF), shape((2, 136, D), BF)
+HALF_A, HALF_U = shape((2, 136, 640), BF), shape((1, 136, D), BF)
 
 
 FEED_OWN = [
@@ -735,19 +724,17 @@
     pltpu.VMEM((BLK, D), BF),
     DMA((2,)),
     DMA((2,)),
-    pltpu.VMEM((2, 136, D), BF),
-    pltpu.VMEM((136, D), BF),
-    pltpu.VMEM((2, 136, 640), BF),
+    pltpu.VMEM((1, 136, D), BF),
     pltpu.VMEM((2, 136, 640), BF),
     pltpu.VMEM((2, 16, D), F32),
     pltpu.VMEM((2, 16, D), F32),
     pltpu.VMEM((3, 2, 16, D), F32),
     pltpu.VMEM((2, 16, D), BF),
     pltpu.VMEM((15, 16, D), BF),
-    DMA((2,)),
-    DMA((2,)),
-    DMA((2, 3)),
-    DMA((2, 3)),
+    DMA((3,)),
+    DMA((3,)),
+    DMA((3, 3)),
+    DMA((3, 3)),
     DMA,
     DMA,
     DMA((3,)),
@@ -766,31 +753,22 @@
 
 
 def run_backward_middle(attend_args, up, down, feed_args):
-    outs = [shape((BLK, D), BF)] + SMALLS + [HALF_U] + FEED_OUTS + [HALF_A]
+    outs = [shape((BLK, D), BF)] + SMALLS + [HALF_U, HALF_U] + FEED_OUTS + [HALF_A]
     ins = [VMEM, ANY, ANY] + [VMEM] * 8 + [ANY] * 4 + [VMEM] * 5
     scratch = ATTEND_OWN + FEED_SCRATCH + FEED_OWN + BLOCKS + ATTEND_SCRATCH
     return call(backward_middle, "backward_middle", 5, outs, ins, scratch)(*attend_args, up, down, *feed_args)
 
 
-def run_backward_end(attend_args, up, down, half_u, half_a, rest):
+def run_backward_end(attend_args, up, down, halves, rest):
     both = shape((2, BLK, D), BF)
-    outs = [shape((BLK, D), BF)]
-    outs += [shape((4, 2, 136, D), BF), shape((4, 2, 136, 640), BF), shape((16, D), F32), both, both]
-    ins = [VMEM, ANY, ANY] + [VMEM] * 8 + [ANY] * 2 + [VMEM] * (2 + len(rest))
-    pairs = [
-        pltpu.VMEM((2, 136, D), BF),
-        pltpu.VMEM((2, 136, 640), BF),
-        pltpu.VMEM((2, 136, D), BF),
-        pltpu.VMEM((2, 136, 640), BF),
-        pltpu.VMEM((8, D), F32),
-        pltpu.VMEM((8, TQKV), F32),
-        pltpu.VMEM((8, 128), F32),
-    ]
-    zs = (z_scratch(D) + z_scratch(640)) * 2
-    scratch = ATTEND_OWN + FEED_SCRATCH + BLOCKS + ATTEND_SCRATCH + zs + pairs + GATHER_OWN
-    return call(backward_end, "backward_end", 6, outs, ins, scratch)(
-        *attend_args, up, down, half_u, half_a, *rest
-    )
+    outs = [shape((BLK, D), BF), shape((4, 1, 136, D), BF), shape((4, 1, 136, D), BF), shape((4, 2, 136, 640), BF)]
+    outs += [shape((16, D), F32), both, both]
+    ins = [VMEM, ANY, ANY] + [VMEM] * 8 + [ANY] * 2 + [VMEM] * (3 + len(rest))
+    units = [pltpu.VMEM((1, 136, D), BF), pltpu.VMEM((1, 136, D), BF), pltpu.VMEM((2, 136, 640), BF)]
+    zs = (z_scratch(1, D) + z_scratch(1, D) + z_scratch(2, 640)) * 2
+    smalls = [pltpu.VMEM((8, D), F32), pltpu.VMEM((8, TQKV), F32)]
+    scratch = ATTEND_OWN + FEED_SCRATCH + BLOCKS + ATTEND_SCRATCH + zs + units * 3 + smalls + GATHER_OWN
+    return call(backward_end, "backward_end", 6, outs, ins, scratch)(*attend_args, up, down, *halves, *rest)
 
 
 def spread(send_a, send_u, send_d, send_o, send_v, wa, wu, wd, wo, wv, hold_a, hold_u, hold_d, hold_o, hold_v, local, ysend, yrecv, zsend, zrecv, csend, crecv):
@@ -942,72 +920,86 @@
 
 
 class Gather:
-    def __init__(self, pair, moved, out, number, keep_from, ts, tr, gs, gr):
-        self.pair, self.moved, self.out, self.i, self.keep_from = pair, moved, out, number, keep_from
+    def __init__(self, unit, moved, keep_from, out, ts, tr, gs, gr):
+        self.unit, self.moved, self.out, self.keep_from = unit, moved, out, keep_from
         self.ts, self.tr, self.gs, self.gr = ts, tr, gs, gr
 
     def transpose(self):
         y, c = place()
         s, x, h, me = plane()
-        source = self.pair if self.keep_from else self.pair.at[0]
-        return remote(source, self.moved, self.ts.at[self.i], self.tr.at[self.i], {"fsdp": 2 * x + c, "replica": 2 * y + h})
-
-    def start(self):
+        return remote(self.unit, self.moved, self.ts, self.tr, at_chip(block_of(x, y), c))
+
+    def elsewhere(self):
         y, c = place()
         s, x, h, me = plane()
-        pl.when(x != y)(self.transpose().start)
+        return block_of(x, y) != y
+
+    def start(self):
+        pl.when(self.elsewhere())(self.transpose().start)
+
+    def arrive(self):
+        @pl.when(self.elsewhere())
+        def _():
+            self.transpose().wait()
+            self.unit[0] = self.moved[0]
+            if self.keep_from:
+                lane = lax.broadcasted_iota(jnp.int32, self.unit.shape[1:], 1)
+                merged = jnp.where(lane < self.keep_from, self.moved[1].astype(F32), self.unit[1].astype(F32))
+                self.unit[1] = merged.astype(BF)
 
     def copies(self):
+        y, c = place()
         s, x, h, me = plane()
         targets = x_peers(x, h)
         for k in ORDER:
-            yield k, remote(self.pair, self.out.at[x], self.gs.at[self.i, k - 1], self.gr.at[self.i, k - 1], targets[k - 1])
+            yield k, remote(self.unit, self.out.at[block_of(x, y)], self.gs.at[k - 1], self.gr.at[k - 1], targets[k - 1])
 
     def spread(self):
         y, c = place()
         s, x, h, me = plane()
-
-        @pl.when(x != y)
-        def _():
-            self.transpose().wait()
-            if self.keep_from:
-                self.pair[0] = self.moved[0]
-                lane = lax.broadcasted_iota(jnp.int32, self.pair.shape[1:], 1)
-                merged = jnp.where(lane < self.keep_from, self.moved[1].astype(F32), self.pair[1].astype(F32))
-                self.pair[1] = merged.astype(BF)
-            else:
-                self.pair[0] = self.moved[...]
-
         for k, copy in self.copies():
             copy.start()
-        self.out[x] = self.pair[...]
+        self.out[block_of(x, y)] = self.unit[...]
 
     def finish(self):
+        y, c = place()
         s, x, h, me = plane()
         targets = x_peers(x, h)
         for k, copy in self.copies():
             copy.wait_send()
-            place_in = self.out.at[lax.rem(x + 4 - k, 4)]
-            remote(place_in, place_in, self.gs.at[self.i, k - 1], self.gr.at[self.i, k - 1], targets[k - 1]).wait_recv()
-
-
-def gather_pieces(feed, attend, first_u, first_a, half_u, half_a, z_u, z_a, done_u, done_a, one_0, heads_0,
-                  two_0, one_1, two_1, heads_1, act_0, act_1, back_1, spare, back_0, out_u, out_a, out_small, out_act, out_back,
-                  swap_act, swap_back, ws, wr, piece_u, moved_u, piece_a, moved_a, small, small_c, small_y, small_x, small_z,
+            place_in = self.out.at[block_of(x - k + 4, y)]
+            remote(place_in, place_in, self.gs.at[k - 1], self.gr.at[k - 1], targets[k - 1]).wait_recv()
+
+
+def gather_pieces(feed, attend, first, last, one_0, heads_0,
+                  two_0, one_1, two_1, heads_1, act_0, act_1, back_1, back_0,
+                  out_up, out_down, out_a, out_small, out_act, out_back,
+                  swap_act, swap_back, ws, wr, moved_up, moved_a, small, small_c, small_y, small_x, small_z,
                   ts, tr, gs, gr, cs, cr, ys, yr, zs, zr):
     y, c = place()
     s, x, h, me = plane()
     sibling = at_chip(y, 1 - c)
     peers = [at_chip(ring(y, k), c) for k in (1, 2, 3)]
-    z_u = AlongZ(0, half_u, z_u[0], piece_u, z_u[1], z_u[2])
-    z_a = AlongZ(0, half_a, z_a[0], piece_a, z_a[1], z_a[2])
-    g_u = Gather(piece_u, moved_u, out_u, 0, 0, ts, tr, gs, gr)
-    g_a = Gather(piece_a, moved_a, out_a, 1, 320, ts, tr, gs, gr)
+    gathers = [
+        Gather(last[i].out, moved, keep, out, ts.at[i], tr.at[i], gs.at[i], gr.at[i])
+        for i, (moved, keep, out) in enumerate(((moved_up, 0, out_up), (None, 0, out_down), (moved_a, 320, out_a)))
+    ]
+
+    def sum_along_z(i):
+        first[i].finish()
+        last[i].finish()
+
+        @pl.when(s == 1)
+        def _():
+            last[i].out[...] = first[i].out[...]
+
     attend.middle(y, c)
-    feed.finish()
-    z_u.start()
+    feed.down.finish()
+    last[1].start()
     build_small(small.at[0], one_0, two_0, heads_0, y)
     build_small(small.at[1], one_1, two_1, heads_1, y)
+    cross = remote(small, small_c, cs, cr, sibling)
+    cross.start()
     swap_act[...] = jnp.where(s == 0, act_1[...].astype(F32), act_0[...].astype(F32)).astype(BF)
     swap_back[...] = jnp.where(s == 0, back_1[...].astype(F32), back_0[...].astype(F32)).astype(BF)
     swaps = [
@@ -1016,25 +1008,13 @@
     ]
     out_act[s] = jnp.where(s == 0, act_0[...].astype(F32), act_1[...].astype(F32)).astype(BF)
     out_back[s] = jnp.where(s == 0, back_0[...].astype(F32), back_1[...].astype(F32)).astype(BF)
-    cross = remote(small, small_c, cs, cr, sibling)
-    cross.start()
     cross.wait()
     small[...] = small[...] + small_c[...]
     hops = [remote(small, small_y.at[k - 1], ys.at[k - 1], yr.at[k - 1], peers[k - 1]) for k in (1, 2, 3)]
     for hop in hops:
         hop.start()
-    first_u.finish()
-    first_a.finish()
-    attend.finish()
-    z_a.start()
-    z_u.finish()
-
-    @pl.when(s == 1)
-    def _():
-        piece_u[...] = done_u[...]
-
-    g_u.start()
-    g_u.spread()
+    sum_along_z(0)
+    gathers[0].start()
     for hop in hops:
         hop.wait()
     small_x[...] = (small[...] + small_y[0] + small_y[1] + small_y[2]).astype(BF)
@@ -1044,18 +1024,20 @@
             q = lax.rem(me + j, 16)
             yield remote(small_x.at[q // 8], small_z.at[15 - j], zs.at[j - 1], zr.at[15 - j], at_plane(q))
 
+    attend.finish()
+    last[2].start()
+    gathers[0].arrive()
+    gathers[0].spread()
+    sum_along_z(1)
+    gathers[1].spread()
     for copy in plane_copies():
         copy.start()
-    z_a.finish()
-
-    @pl.when(s == 1)
-    def _():
-        piece_a[...] = done_a[...]
-
-    g_a.start()
+    sum_along_z(2)
+    gathers[2].start()
     for swap in swaps:
         swap.start()
-    g_a.spread()
+    gathers[2].arrive()
+    gathers[2].spread()
     total = small_x[s].astype(F32)
     for copy in plane_copies():
         copy.wait_send()
@@ -1067,16 +1049,16 @@
         swap.wait_send()
         place_in = (out_act, out_back)[i].at[1 - s]
         remote(place_in, place_in, ws.at[i], wr.at[i], {"section": 1 - s}).wait_recv()
-    g_u.finish()
-    g_a.finish()
-
-
-def assemble(all_u, all_a, small, attn, out, up, down, b_attn, b_out, b_up, b_down, gain, shift):
+    for gather in gathers:
+        gather.finish()
+
+
+def assemble(all_up, all_down, all_a, small, attn, out, up, down, b_attn, b_out, b_up, b_down, gain, shift):
     y, c = place()
     f = 2 * y + c
     for j in range(CHIPS):
-        up[:, j * D : (j + 1) * D] = all_u[j, 0].astype(F32)
-        down[j * 136 : (j + 1) * 136] = all_u[j, 1].astype(F32)
+        up[:, j * D : (j + 1) * D] = all_up[j, 0].astype(F32)
+        down[j * 136 : (j + 1) * 136] = all_down[j, 0].astype(F32)
         first, second = all_a[j, 0].astype(F32), all_a[j, 1].astype(F32)
         parts = ((0, second[:, :TH]), (D, first[:, :TH]), (2 * D, first[:, TH:]))
         for base, part in parts:
@@ -1099,16 +1081,16 @@
     b_attn[...] = pick(f, [small[10 + i // 4 : 11 + i // 4, 272 * (i % 4) : 272 * (i % 4) + 272] for i in range(8)])
 
 
-def run_assemble(all_u, all_a, small):
+def run_assemble(*gathered):
     sizes = [(136, 3 * D), (136, D), (136, FF), (544, D), (1, 272), (1, 136), (1, 544), (1, 136), (2, 136), (2, 136)]
     return pl.pallas_call(
         assemble,
         name="assemble",
         out_shape=[shape(dims, F32) for dims in sizes],
-        in_specs=[VMEM] * 3,
+        in_specs=[VMEM] * 4,
         out_specs=[VMEM] * len(sizes),
         compiler_params=pltpu.CompilerParams(vmem_limit_bytes=LIMIT),
-    )(all_u, all_a, small)
+    )(*gathered)
 
 
 def split_heads(block):
@@ -1158,21 +1140,20 @@
     x_1, kept_1, middle_1, kept_two_1 = saved[1]
     x_0, kept_0, middle_0, kept_two_0 = saved[0]
     grad_middle, up, down, two_1 = run_feed_back(grad, wu, wd, vecs[1], middle_1, *kept_two_1)
-    back_1, one_1, heads_1, half_u, grad_middle, up_0, down_0, two_0, half_a = run_backward_middle(
+    back_1, one_1, heads_1, half_up, half_down, grad_middle, up_0, down_0, two_0, half_a = run_backward_middle(
         (grad_middle, wa, wo, vecs[1], x_1, *kept_1),
         up.reshape(4, 2, 136, D),
         down.reshape(2, 4, 136, D),
         (wu, wd, vecs[0], middle_0, *kept_two_0),
     )
-    back_0, all_u, all_a, small, all_acts, all_grads = run_backward_end(
+    back_0, all_up, all_down, all_a, small, all_acts, all_grads = run_backward_end(
         (grad_middle, wa, wo, vecs[0], x_0, *kept_0),
         up_0.reshape(4, 2, 136, D),
         down_0.reshape(2, 4, 136, D),
-        half_u,
-        half_a,
-        (two_0, one_1, two_1, heads_1, *acts, back_1, two_0),
-    )
-    attn, out, up, down, b_attn, b_out, b_up, b_down, gain, shift = run_assemble(all_u, all_a, small)
+        (half_up, half_down, half_a),
+        (two_0, one_1, two_1, heads_1, *acts, back_1),
+    )
+    attn, out, up, down, b_attn, b_out, b_up, b_down, gain, shift = run_assemble(all_up, all_down, all_a, small)
     return (
         all_acts[None, :, None],
         all_grads[None, :, None],

time: 452 us -> 389 us (0.86)
  Pallas kernels: 425 us -> 361 us
    pallas_call x1, Pallas kernels: 175 us -> 113 us  [run_backward_end(): call(backward_end, 'backward_end', 6, outs, ins, scratch)]
where the time goes in v7:
time: 389 us; the launch traced here: 381 us
  Pallas kernels  361 us (93%)
  local copies, waits for them, and re-layouts  11.5 us (3%)
  other arithmetic  6.27 us (2%)
    pallas_call x1, Pallas kernels, run_backward_end(): call(backward_end, 'backward_end', 6, outs, ins, scratch)  113 us
    pallas_call x1, Pallas kernels, run_spread(): pl.pallas_call(spread, name='spread', out_shape=outs, in_specs=[ANY] * 5,...  60 us
    pallas_call x1, Pallas kernels, run_backward_middle(): call(backward_middle, 'backward_middle', 5, outs, ins, scratch)  56 us
    pallas_call x2, Pallas kernels, run_attend_forward(): call(functools.partial(attend_forward, e), 'attend_forward_%d' % e, e, ou...  55.4 us
    pallas_call x2, Pallas kernels, run_feed_forward(): call(functools.partial(feed_forward, e), 'feed_forward_%d' % e, 2 + e, ou...  45.8 us
    pallas_call x1, Pallas kernels, run_feed_back(): call(functools.partial(feed_back_alone, 1), 'feed_back_1', 4, FEED_OUTS,...  25.1 us
  transfers between devices with their start and end apart: 1, of which 0 were waited for; matrix products, arithmetic and copies ran while one was open for 2% of the time, Pallas kernels for 0%

profile of v7, /device:TPU:4, one launch (start us, length us, event | category | flops | bytes accessed | tf_op | source)
XLA Modules:
  0.0 381.3 jit_solution(8099425759309750368)
XLA Ops:
  0.6 0.0 copy-start
  0.7 1.0 slice_bitcast_fusion.7
  1.7 1.6 collective-permute-start
  3.3 1.1 fusion.1
  4.4 1.3 fusion
  5.8 0.0 copy-start.5
  5.8 0.0 copy-start.6
  5.8 0.0 copy-start.9
  5.8 0.0 copy-start.10
  5.8 0.0 copy-start.7
  5.8 0.0 copy-start.8
  5.9 0.3 slice_bitcast_fusion.5
  6.2 0.1 pad.8.clone
  6.2 0.2 copy-done.5
  6.4 0.0 copy-done.6
  6.5 0.0 copy-done.9
  6.5 0.0 copy-done.10
  6.5 0.2 dynamic_update_slice.9
  6.8 0.3 dynamic_update_slice.10
  7.1 0.3 dynamic_update_slice.11
  7.4 0.6 pad_maximum_fusion.3.send_v
  8.0 1.7 dynamic-slice_bitcast_fusion
  9.7 0.1 maximum_bitcast_fusion
  9.9 0.1 concatenate.22
  10.0 0.1 concatenate.24
  10.1 0.1 concatenate.23
  10.3 1.3 pad_maximum_fusion.1.send_u
  11.5 1.1 pad_maximum_fusion.2.send_a
  12.7 0.0 collective-permute-done
  12.7 1.8 maximum_maximum_fusion.send_o
  14.5 60.0 %spread.1 = (bf16[2,4,2,136,960]{4,3,2,1,0:T(8,128)(2,1)}, bf16[2,4,2,136,1088]{4,3,2,1,0:T(8,128)(2,1)}, bf16[2,2,544,1088]{3,2,1,0:T(8,128)(2,1)}, bf16[2,2,19...) custom-call(bf16[4,136,960]{2,1,0:T(8,128)(2,1)} %pad_maximum_fusion.2.send_a, ...), custom_call_target="tpu_custom_call" | custom-call | tf_op jit(solution)/shard_map/spread/pallas_call | solution.py:889
  74.5 0.0 copy-start.1
  74.5 1.0 slice_bitcast_fusion.6
  75.5 1.4 slice_bitcast_fusion.1
  76.9 0.0 copy-done.1
  76.9 0.1 convert_reduce_fusion
  77.0 0.7 slice_bitcast_fusion.8
  77.7 1.2 pad_maximum_fusion.wo_hbm.refs_2_
  78.9 28.1 %attend_forward_0.1 = (f32[64,1088]{1,0:T(8,128)}, bf16[256,1088]{1,0:T(8,128)(2,1)}, bf16[256,320]{1,0:T(8,128)(2,1)}, bf16[256,640]{1,0:T(8,128)(2,1)}, bf16[2...) custom-call(bf16[64,1088]{1,0:T(8,128)(2,1)} %get-tuple-element.162.x.refs_4_, ...), custom_call_target="tpu_custom_call" | custom-call | flops 10000000 | bytes 10000 | tf_op jit(solution)/shard_map/attend_forward_0/pallas_call | solution.py:692
  107.0 22.8 %feed_forward_0.1 = (bf16[64,1088]{1,0:T(8,128)(2,1)}, bf16[256,1088]{1,0:T(8,128)(2,1)}, f32[256,1088]{1,0:T(8,128)}, bf16[256,1088]{1,0:T(8,128)(2,1)}) custom-call(f32[64,1088]{1,0:T(8,128)} %get-tuple-element.74.middle.refs_16_, bf16[2,1088,1088]{2,1,0:T(8,128)(2,1)} %bitcast.60, bf16[2,1088,1088]{2,1,0:T(8,128)(2,1)} %bitcast.64, ...), custom_call_target="tpu_custom_call" | custom-call | flops 10000000 | bytes 10000 | tf_op jit(solution)/shard_map/feed_forward_0/pallas_call | solution.py:698
  129.8 27.3 %attend_forward_1.1 = (f32[64,1088]{1,0:T(8,128)}, bf16[256,1088]{1,0:T(8,128)(2,1)}, bf16[256,320]{1,0:T(8,128)(2,1)}, bf16[256,640]{1,0:T(8,128)(2,1)}, bf16[2...) custom-call(bf16[64,1088]{1,0:T(8,128)(2,1)} %get-tuple-element.75.x.refs_4_.refs_20_, ...), custom_call_target="tpu_custom_call" | custom-call | flops 10000000 | bytes 10000 | tf_op jit(solution)/shard_map/attend_forward_1/pallas_call | solution.py:692
  157.1 23.0 %feed_forward_1.1 = (bf16[64,1088]{1,0:T(8,128)(2,1)}, bf16[256,1088]{1,0:T(8,128)(2,1)}, f32[256,1088]{1,0:T(8,128)}, bf16[256,1088]{1,0:T(8,128)(2,1)}) custom-call(f32[64,1088]{1,0:T(8,128)} %get-tuple-element.76.middle.refs_4_, bf16[2,1088,1088]{2,1,0:T(8,128)(2,1)} %bitcast.61, bf16[2,1088,1088]{2,1,0:T(8,128)(2,1)} %bitcast.65, ...), custom_call_target="tpu_custom_call" | custom-call | flops 10000000 | bytes 10000 | tf_op jit(solution)/shard_map/feed_forward_1/pallas_call | solution.py:698
  180.2 25.1 %feed_back_1.1 = (f32[64,1088]{1,0:T(8,128)}, bf16[1088,1088]{1,0:T(8,128)(2,1)}, bf16[1088,1088]{1,0:T(8,128)(2,1)}, f32[8,1088]{1,0:T(8,128)}) custom-call(bf16[64,1088]{1,0:T(8,128)(2,1)} %get-tuple-element.163.refs_0_, bf16[2,1088,1088]{2,1,0:T(8,128)(2,1)} %bitcast.62, bf16[2,1088,1088]{2,1,0:T(8,128)(2,1)} %bitcast.66, ...), custom_call_target="tpu_custom_call" | custom-call | flops 10000000 | bytes 10000 | tf_op jit(solution)/shard_map/feed_back_1/pallas_call | solution.py:750
  205.2 56.0 %backward_middle.1 = (bf16[64,1088]{1,0:T(8,128)(2,1)}, f32[8,1088]{1,0:T(8,128)}, f32[8,960]{1,0:T(8,128)}, bf16[1,136,1088]{2,1,0:T(8,128)(2,1)}, bf16[1,136,1...) custom-call(f32[64,1088]{1,0:T(8,128)} %get-tuple-element.80.refs_0_, ...), custom_call_target="tpu_custom_call" | custom-call | flops 10000000 | bytes 10000 | tf_op jit(solution)/shard_map/backward_middle/pallas_call | solution.py:759
  261.2 112.6 %backward_end.1 = (bf16[64,1088]{1,0:T(8,128)(2,1)}, bf16[4,1,136,1088]{3,2,1,0:T(8,128)(2,1)}, bf16[4,1,136,1088]{3,2,1,0:T(8,128)(2,1)}, bf16[4,2,136,640]{3,2...) custom-call(f32[64,1088]{1,0:T(8,128)} %get-tuple-element.92.refs_0_, ...), custom_call_target="tpu_custom_call" | custom-call | flops 10000000 | bytes 10000 | tf_op jit(solution)/shard_map/backward_end/pallas_call | solution.py:771
  373.8 5.7 %assemble.1 = (f32[136,3264]{1,0:T(8,128)}, f32[136,1088]{1,0:T(8,128)}, f32[136,4352]{1,0:T(8,128)}, f32[544,1088]{1,0:T(8,128)}, f32[1,272]{1,0:T(1,128)}, /*i...) custom-call(bf16[4,1,136,1088]{3,2,1,0:T(8,128)(2,1)} %get-tuple-element.112.al, ...), custom_call_target="tpu_custom_call" | custom-call | tf_op jit(solution)/shard_map/assemble/pallas_call | solution.py:1086
  379.6 0.7 copy.38
  380.3 0.7 copy.39
  (16 shorter events, 0.1 us)
Async XLA Ops:
  0.6 5.2 %copy-start = (bf16[1,136,4352]{2,1,0:T(8,128)(2,1)S(1)}, bf16[1,136,4352]{2,1,0:T(8,128)(2,1)}, u32[]{:S(2)}) copy-start(bf16[1,136,4352]{2,1,0:T(8,128)(2,1)} %param.16) | copy-start | bytes 3551236
  1.7 11.0 %collective-permute-start = (bf16[48,1088]{1,0:T(8,128)(2,1)S(1)}, bf16[48,1088]{1,0:T(8,128)(2,1)}, u32[]{:S(2)}, u32[]{:S(2)}) collective-permute-start(bf16[48,1088]{1,0:T(8,128)(2,1)S(1)} %slice_bitcast_fusion.7), channel_id=1, source_target_pairs={{0,16},{8,24},{16,32},{24,40},{32,48},{40,56},{48,0},{56,8},{1,17}... | collective-permute-start | bytes 313352 | tf_op jit(solution)/shard_map/ppermute | solution.py:1115
  5.8 0.7 copy-start.5
  5.8 0.7 copy-start.6
  5.8 0.7 copy-start.9
  5.8 0.7 copy-start.10
  5.8 1.0 copy-start.7
  5.8 1.3 copy-start.8
  11.5 1.1 copy-start.2
  74.5 2.4 copy-start.1
  373.8 5.8 %copy-start.4 = (bf16[2,64,1088]{2,1,0:T(8,128)(2,1)S(1)}, bf16[2,64,1088]{2,1,0:T(8,128)(2,1)}, u32[]{:S(2)}) copy-start(bf16[2,64,1088]{2,1,0:T(8,128)(2,1)} %get-tuple-element.110) | copy-start | bytes 835588
  373.8 6.5 %copy-start.3 = (bf16[2,64,1088]{2,1,0:T(8,128)(2,1)S(1)}, bf16[2,64,1088]{2,1,0:T(8,128)(2,1)}, u32[]{:S(2)}) copy-start(bf16[2,64,1088]{2,1,0:T(8,128)(2,1)} %get-tuple-element.111) | copy-start | bytes 835588

commit v8 on v7

--- a/solution.py
+++ b/solution.py
@@ -173,12 +173,11 @@
 
 
 def attend_forward(e, x, w_hbm, wo_hbm, vecs, middle, normed, queries, kv, kv_other, logsum, attended,
-                   w, wo, acc, out_buf, in_buf, ls, gs, gr, ss, sr, ks, kr):
+                   w, wo, acc, out_buf, in_buf, ls, gs, gr, ss, sr, ks, kr, arrived, weights=None):
     y, c = place()
-    peers = [at_chip(ring(y, k), c) for k in (1, 2, 3)]
     sibling = at_chip(y, 1 - c)
-    arrived = greet(peers + [sibling])
-    weights = load([(w_hbm.at[e], w)] + out_rows(wo_hbm, wo, e, y), ls)
+    if weights is None:
+        weights = load([(w_hbm.at[e], w)] + out_rows(wo_hbm, wo, e, y), ls)
     slot(normed, y)[...] = norm(x[...].astype(F32), vecs[0:1], vecs[1:2]).astype(BF)
     arrived()
     gather_start(normed, y, c, gs, gr)
@@ -217,11 +216,9 @@
     middle[...] = base + scatter_wait(acc, out_buf, in_buf, y, c, ss, sr)
 
 
-def feed_forward(e, middle, wu_hbm, wd_hbm, vecs, result, normed, hidden, active,
-                 wu, wd, acc, out_buf, in_buf, ls, gs, gr, ss, sr):
+def feed_forward(middle, vecs, result, normed, hidden, active,
+                 wu, wd, acc, out_buf, in_buf, gs, gr, ss, sr, arrived, weights, defer=False):
     y, c = place()
-    arrived = greet([at_chip(ring(y, k), c) for k in (1, 2, 3)])
-    weights = load([(wu_hbm.at[e], wu), (wd_hbm.at[e], wd)], ls)
     slot(normed, y)[...] = norm(middle[...], vecs[2:3], vecs[3:4]).astype(BF)
     arrived()
     gather_start(normed, y, c, gs, gr)
@@ -238,19 +235,26 @@
     for at, size in chunks(D):
         acc[:, at : at + size] = dot(rows, wd[:, at : at + size])
     scatter_start(acc, out_buf, in_buf, y, c, ss, sr)
-    base = middle[...] + vecs[5:6]
-    result[...] = (base + scatter_wait(acc, out_buf, in_buf, y, c, ss, sr)).astype(BF)
+
+    def finish():
+        base = middle[...] + vecs[5:6]
+        result[...] = (base + scatter_wait(acc, out_buf, in_buf, y, c, ss, sr)).astype(BF)
+
+    if defer:
+        return finish
+    finish()
 
 
 def feed_back(e, grad, wu_hbm, wd_hbm, vecs, middle, normed, hidden, active, grad_middle, grad_up, grad_down, small,
-              wu, wd, full, gh, acc, out_buf, in_buf, ls, gs, gr, ss, sr, arrived, reduce=None, weights=None):
+              wu, wd, full, gh, acc, out_buf, in_buf, ls, gs, gr, ss, sr, arrived, reduce=None, weights=None, early=False):
     y, c = place()
     if weights is None:
         weights = load([(wu_hbm.at[e], wu), (wd_hbm.at[e], wd)], ls)
     own_rows = grad[...]
-    slot(full, y)[...] = own_rows
-    arrived()
-    gather_start(full, y, c, gs, gr)
+    if not early:
+        slot(full, y)[...] = own_rows
+        arrived()
+        gather_start(full, y, c, gs, gr)
     if reduce is not None:
         reduce.begin(y, c)
     small[...] = jnp.zeros_like(small)
@@ -593,9 +597,42 @@
     return parts
 
 
-def feed_back_alone(e, *refs):
+def attend_forward_first(*refs):
     y, c = place()
-    feed_back(e, *refs, greet([at_chip(ring(y, k), c) for k in (1, 2, 3)]))
+    arrived = greet([at_chip(ring(y, k), c) for k in (1, 2, 3)] + [at_chip(y, 1 - c)])
+    attend_forward(0, refs[0].at[lax.axis_index("section"), 0], *refs[1:], arrived)
+
+
+class Loaded:
+    def wait(self):
+        pass
+
+
+def forward_rest(middle_0, wu_hbm, wd_hbm, w_hbm, wo_hbm, vecs_0, vecs_1, cotangent, *refs):
+    f0_out, a_out, result_1, back_out, f0_scr, a_scr, f1_kept, f1_scr, b_scr, loads = split(
+        refs, 4, 7, 1, 4, 2 + len(FEED_MOVE), 2 + len(MOVE) + 2, 3, 2 + len(FEED_MOVE), 2 + len(MOVE), 1
+    )
+    y, c = place()
+    arrived = greet([at_chip(ring(y, k), c) for k in (1, 2, 3)] + [at_chip(y, 1 - c)])
+    weights_0 = load([(wu_hbm.at[0], f0_scr[0]), (wd_hbm.at[0], f0_scr[1])], loads[0].at[0])
+    weights_a = load([(w_hbm.at[1], a_scr[0])] + out_rows(wo_hbm, a_scr[1], 1, y), a_scr[5])
+    weights_1 = load([(wu_hbm.at[1], f1_scr[0]), (wd_hbm.at[1], f1_scr[1])], loads[0].at[1])
+    grad = cotangent.at[lax.axis_index("section"), 0]
+    full, gs, gr = b_scr[0], b_scr[6], b_scr[7]
+    slot(full, y)[...] = grad[...]
+
+    def begin():
+        arrived()
+
+    result_0 = f0_out[0]
+    feed_forward(middle_0, vecs_0, *f0_out, *f0_scr, begin, weights_0)
+    gather_start(full, y, c, gs, gr)
+    attend_forward(1, result_0, w_hbm, wo_hbm, vecs_1, *a_out, *a_scr, lambda: None, weights_a)
+    middle_1 = a_out[0]
+    normed, hidden, active = f1_kept
+    finish = feed_forward(middle_1, vecs_1, result_1[0], normed, hidden, active, *f1_scr, lambda: None, weights_1, True)
+    feed_back(1, grad, wu_hbm, wd_hbm, vecs_1, middle_1, normed, hidden, active, *back_out,
+              f1_scr[0], f1_scr[1], *b_scr, lambda: None, Hooks(late=[finish]), [Loaded(), Loaded()], True)
 
 
 def backward_middle(*refs):
@@ -628,6 +665,7 @@
     arrived = greet(peers + [sibling] + [at_plane(lax.rem(me + j, 16)) for j in range(1, 16)])
     half_up, half_down, half_a, sum_up, sum_down, sum_a, late_up, late_down, late_a, small, small_bias = own
     (grad_x,) = a_out
+    a_in = [*a_in[:4], a_in[4].at[s, 0], *a_in[5:]]
     feed = FeedReduce(*updown, half_up, half_down, *u_scr)
     attend = AttendReduce(*grads, half_a, *w_scr)
     first = [AlongZ(1, half, out, *z_scr[3 * i : 3 * i + 3]) for i, (half, out) in enumerate(zip(halves, (sum_up, sum_down, sum_a)))]
@@ -678,27 +716,37 @@
     )
 
 
-def run_attend_forward(e, x, w, wo, vecs):
-    outs = [
-        shape((BLK, D), F32),
-        shape((ROWS, D), BF),
-        shape((ROWS, TH), BF),
-        shape((ROWS, 2 * TH), BF),
-        shape((ROWS, 2 * TH), BF),
-        shape((ROWS, 128), F32),
-        shape((ROWS, TH), BF),
-    ]
-    scratch = [pltpu.VMEM((D, TQKV), BF), pltpu.VMEM((TH, D), BF)] + MOVE + [DMA, DMA]
-    return call(functools.partial(attend_forward, e), "attend_forward_%d" % e, e, outs, [VMEM, ANY, ANY, VMEM], scratch)(x, w, wo, vecs)
-
-
-def run_feed_forward(e, middle, wu, wd, vecs):
-    outs = [shape((BLK, D), BF), shape((ROWS, D), BF), shape((ROWS, D), F32), shape((ROWS, D), BF)]
-    scratch = [pltpu.VMEM((D, D), BF), pltpu.VMEM((D, D), BF)] + MOVE
-    return call(functools.partial(feed_forward, e), "feed_forward_%d" % e, 2 + e, outs, [VMEM, ANY, ANY, VMEM], scratch)(middle, wu, wd, vecs)
-
-
 HALF_A, HALF_U = shape((2, 136, 640), BF), shape((1, 136, D), BF)
+FEED_OUTS = [shape((BLK, D), F32), shape((D, D), BF), shape((D, D), BF), shape((8, D), F32)]
+ATTEND_KEPT = [
+    shape((BLK, D), F32),
+    shape((ROWS, D), BF),
+    shape((ROWS, TH), BF),
+    shape((ROWS, 2 * TH), BF),
+    shape((ROWS, 2 * TH), BF),
+    shape((ROWS, 128), F32),
+    shape((ROWS, TH), BF),
+]
+FEED_KEPT = [shape((ROWS, D), BF), shape((ROWS, D), F32), shape((ROWS, D), BF)]
+ATTEND_WEIGHTS = [pltpu.VMEM((D, TQKV), BF), pltpu.VMEM((TH, D), BF)]
+FEED_WEIGHTS = [pltpu.VMEM((D, D), BF), pltpu.VMEM((D, D), BF)]
+FEED_MOVE = MOVE[:3] + MOVE[4:]
+
+
+def run_attend_forward(x, w, wo, vecs):
+    scratch = ATTEND_WEIGHTS + MOVE + [DMA, DMA]
+    return call(attend_forward_first, "attend_forward_0", 0, ATTEND_KEPT, [VMEM, ANY, ANY, VMEM], scratch)(x, w, wo, vecs)
+
+
+def run_forward_rest(middle, wu, wd, wa, wo, vecs, cotangent):
+    outs = [shape((BLK, D), BF)] + FEED_KEPT + ATTEND_KEPT + [shape((BLK, D), BF)] + FEED_OUTS
+    kept = [pltpu.VMEM(kind.shape, kind.dtype) for kind in FEED_KEPT]
+    rows = pltpu.VMEM((ROWS, D), BF)
+    scratch = FEED_WEIGHTS + FEED_MOVE + ATTEND_WEIGHTS + MOVE + [DMA, DMA] + kept + FEED_WEIGHTS + FEED_MOVE
+    scratch = scratch + [rows, rows] + MOVE + [DMA((2, 2))]
+    return call(forward_rest, "forward_rest", 2, outs, [VMEM] + [ANY] * 4 + [VMEM] * 3, scratch)(
+        middle, wu, wd, wa, wo, vecs[0], vecs[1], cotangent
+    )
 
 
 FEED_OWN = [
@@ -742,14 +790,7 @@
     DMA((15,)),
     DMA((15,)),
 ]
-FEED_OUTS = [shape((BLK, D), F32), shape((D, D), BF), shape((D, D), BF), shape((8, D), F32)]
 SMALLS = [shape((8, D), F32), shape((8, TQKV), F32)]
-
-
-def run_feed_back(grad, wu, wd, vecs, middle, normed, hidden, active):
-    return call(functools.partial(feed_back_alone, 1), "feed_back_1", 4, FEED_OUTS, [VMEM, ANY, ANY] + [VMEM] * 5, FEED_OWN)(
-        grad, wu, wd, vecs, middle, normed, hidden, active
-    )
 
 
 def run_backward_middle(attend_args, up, down, feed_args):
@@ -1128,18 +1169,10 @@
     wd = wd.reshape(2, D, D)
     wo = jnp.concatenate([wo[:, 1, 136:184], wo[:, 0, :136], wo[:, 1, :136]], axis=1)
     vecs = jnp.sum(wv.astype(F32), axis=(1, 2))
-    stream = lax.dynamic_index_in_dim(inputs, s, 0, keepdims=False)[0]
-    saved, acts = [], []
-    for e in range(2):
-        middle, *kept = run_attend_forward(e, stream, wa, wo, vecs[e])
-        result, *kept_two = run_feed_forward(e, middle, wu, wd, vecs[e])
-        saved.append((stream, kept, middle, kept_two))
-        acts.append(result)
-        stream = result
-    grad = lax.dynamic_index_in_dim(cotangent, s, 0, keepdims=False)[0]
-    x_1, kept_1, middle_1, kept_two_1 = saved[1]
-    x_0, kept_0, middle_0, kept_two_0 = saved[0]
-    grad_middle, up, down, two_1 = run_feed_back(grad, wu, wd, vecs[1], middle_1, *kept_two_1)
+    middle_0, *kept_0 = run_attend_forward(inputs, wa, wo, vecs[0])
+    rest = run_forward_rest(middle_0, wu, wd, wa, wo, vecs, cotangent)
+    (x_1, *kept_two_0), (middle_1, *kept_1), (result_1,), (grad_middle, up, down, two_1) = split(rest, 4, 7, 1, 4)
+    acts = [x_1, result_1]
     back_1, one_1, heads_1, half_up, half_down, grad_middle, up_0, down_0, two_0, half_a = run_backward_middle(
         (grad_middle, wa, wo, vecs[1], x_1, *kept_1),
         up.reshape(4, 2, 136, D),
@@ -1147,7 +1180,7 @@
         (wu, wd, vecs[0], middle_0, *kept_two_0),
     )
     back_0, all_up, all_down, all_a, small, all_acts, all_grads = run_backward_end(
-        (grad_middle, wa, wo, vecs[0], x_0, *kept_0),
+        (grad_middle, wa, wo, vecs[0], inputs, *kept_0),
         up_0.reshape(4, 2, 136, D),
         down_0.reshape(2, 4, 136, D),
         (half_up, half_down, half_a),

time: 389 us -> 368 us (0.946)
  the two profiles are of different devices: /device:TPU:4 before, /device:TPU:1 now
where the time goes in v8:
time: 368 us; the launch traced here: 363 us
  Pallas kernels  343 us (93%)
  local copies, waits for them, and re-layouts  10.1 us (3%)
  other arithmetic  6.27 us (2%)
    pallas_call x1, Pallas kernels, run_backward_end(): call(backward_end, 'backward_end', 6, outs, ins, scratch)  111 us
    pallas_call x1, Pallas kernels, run_forward_rest(): call(forward_rest, 'forward_rest', 2, outs, [VMEM] + [ANY] * 4 + [VMEM] *...  80.8 us
    pallas_call x1, Pallas kernels, run_spread(): pl.pallas_call(spread, name='spread', out_shape=outs, in_specs=[ANY] * 5,...  60.6 us
    pallas_call x1, Pallas kernels, run_backward_middle(): call(backward_middle, 'backward_middle', 5, outs, ins, scratch)  56.8 us
    pallas_call x1, Pallas kernels, run_attend_forward(): call(attend_forward_first, 'attend_forward_0', 0, ATTEND_KEPT, [VMEM, ANY...  27.9 us
  transfers between devices with their start and end apart: 1, of which 0 were waited for; matrix products, arithmetic and copies ran while one was open for 2% of the time, Pallas kernels for 0%

profile of v8, /device:TPU:1, one launch (start us, length us, event | category | flops | bytes accessed | tf_op | source)
XLA Modules:
  0.0 362.7 jit_solution(2109184325592715917)
XLA Ops:
  0.6 0.0 copy-start
  0.7 1.0 slice_bitcast_fusion.7
  1.7 2.2 collective-permute-start
  3.9 1.1 fusion.1
  5.0 1.3 fusion
  6.3 0.0 copy-start.5
  6.3 0.0 copy-start.6
  6.3 0.0 copy-start.9
  6.4 0.0 copy-start.10
  6.4 0.0 copy-start.7
  6.4 0.0 copy-start.8
  6.4 0.0 copy-done
  6.4 0.3 slice_bitcast_fusion.5
  6.7 0.1 pad.8.clone
  6.8 0.2 copy-done.5
  7.0 0.0 copy-done.6
  7.0 0.0 copy-done.9
  7.0 0.0 copy-done.10
  7.1 0.3 dynamic_update_slice.9
  7.4 0.0 copy-done.7
  7.4 0.4 dynamic_update_slice.10
  7.8 0.0 copy-done.8
  7.8 0.4 dynamic_update_slice.11
  8.2 0.6 pad_maximum_fusion.3.send_v
  8.9 0.1 maximum_bitcast_fusion
  9.0 0.1 concatenate.22
  9.2 0.1 concatenate.24
  9.3 0.1 concatenate.23
  9.4 1.3 pad_maximum_fusion.1.send_u
  10.7 1.1 pad_maximum_fusion.2.send_a
  11.8 0.0 collective-permute-done
  11.8 0.0 copy-done.2
  11.8 1.8 maximum_maximum_fusion.send_o
  13.6 60.6 %spread.1 = (bf16[2,4,2,136,960]{4,3,2,1,0:T(8,128)(2,1)}, bf16[2,4,2,136,1088]{4,3,2,1,0:T(8,128)(2,1)}, bf16[2,2,544,1088]{3,2,1,0:T(8,128)(2,1)}, bf16[2,2,19...) custom-call(bf16[4,136,960]{2,1,0:T(8,128)(2,1)} %pad_maximum_fusion.2.send_a, ...), custom_call_target="tpu_custom_call" | custom-call | tf_op jit(solution)/shard_map/spread/pallas_call | solution.py:930
  74.2 0.0 copy-start.1
  74.3 1.0 slice_bitcast_fusion.6
  75.3 1.4 slice_bitcast_fusion.1
  76.7 0.0 copy-done.1
  76.7 0.1 convert_reduce_fusion
  76.8 0.7 slice_bitcast_fusion.8
  77.4 1.2 pad_maximum_fusion.refs_2_.wo_hbm
  78.6 27.9 %attend_forward_0.1 = (f32[64,1088]{1,0:T(8,128)}, bf16[256,1088]{1,0:T(8,128)(2,1)}, bf16[256,320]{1,0:T(8,128)(2,1)}, bf16[256,640]{1,0:T(8,128)(2,1)}, bf16[2...) custom-call(bf16[2,1,64,1088]{3,2,1,0:T(8,128)(2,1)} %refs_4_.1, bf16[2,1088,960]{2,1,0:T(8,128)(2,1)} %bitcast.56, ...), custom_call_target="tpu_custom_call" | custom-call | flops 10000000 | bytes 10000 | tf_op jit(solution)/shard_map/attend_forward_0/pallas_call | solution.py:738
  106.6 80.8 %forward_rest.1 = (bf16[64,1088]{1,0:T(8,128)(2,1)}, bf16[256,1088]{1,0:T(8,128)(2,1)}, f32[256,1088]{1,0:T(8,128)}, bf16[256,1088]{1,0:T(8,128)(2,1)}, f32[64,1...) custom-call(f32[64,1088]{1,0:T(8,128)} %get-tuple-element.68.middle_, ...), custom_call_target="tpu_custom_call" | custom-call | flops 10000000 | bytes 10000 | tf_op jit(solution)/shard_map/forward_rest/pallas_call | solution.py:747
  187.4 56.8 %backward_middle.1 = (bf16[64,1088]{1,0:T(8,128)(2,1)}, f32[8,1088]{1,0:T(8,128)}, f32[8,960]{1,0:T(8,128)}, bf16[1,136,1088]{2,1,0:T(8,128)(2,1)}, bf16[1,136,1...) custom-call(f32[64,1088]{1,0:T(8,128)} %get-tuple-element.71.refs_0_, ...), custom_call_target="tpu_custom_call" | custom-call | flops 10000000 | bytes 10000 | tf_op jit(solution)/shard_map/backward_middle/pallas_call | solution.py:800
  244.3 110.9 %backward_end.1 = (bf16[64,1088]{1,0:T(8,128)(2,1)}, bf16[4,1,136,1088]{3,2,1,0:T(8,128)(2,1)}, bf16[4,1,136,1088]{3,2,1,0:T(8,128)(2,1)}, bf16[4,2,136,640]{3,2...) custom-call(f32[64,1088]{1,0:T(8,128)} %get-tuple-element.84.refs_0_, ...), custom_call_target="tpu_custom_call" | custom-call | flops 10000000 | bytes 10000 | tf_op jit(solution)/shard_map/backward_end/pallas_call | solution.py:812
  355.2 5.7 %assemble.1 = (f32[136,3264]{1,0:T(8,128)}, f32[136,1088]{1,0:T(8,128)}, f32[136,4352]{1,0:T(8,128)}, f32[544,1088]{1,0:T(8,128)}, f32[1,272]{1,0:T(1,128)}, /*i...) custom-call(bf16[4,1,136,1088]{3,2,1,0:T(8,128)(2,1)} %get-tuple-element.104.al, ...), custom_call_target="tpu_custom_call" | custom-call | tf_op jit(solution)/shard_map/assemble/pallas_call | solution.py:1127
  361.0 0.7 copy.38
  361.7 0.7 copy.39
  (12 shorter events, 0.1 us)
Async XLA Ops:
  0.6 5.8 %copy-start = (bf16[1,136,4352]{2,1,0:T(8,128)(2,1)S(1)}, bf16[1,136,4352]{2,1,0:T(8,128)(2,1)}, u32[]{:S(2)}) copy-start(bf16[1,136,4352]{2,1,0:T(8,128)(2,1)} %param.16) | copy-start | bytes 3551236
  1.7 10.2 %collective-permute-start = (bf16[48,1088]{1,0:T(8,128)(2,1)S(1)}, bf16[48,1088]{1,0:T(8,128)(2,1)}, u32[]{:S(2)}, u32[]{:S(2)}) collective-permute-start(bf16[48,1088]{1,0:T(8,128)(2,1)S(1)} %slice_bitcast_fusion.7), channel_id=1, source_target_pairs={{0,16},{8,24},{16,32},{24,40},{32,48},{40,56},{48,0},{56,8},{1,17}... | collective-permute-start | bytes 313352 | tf_op jit(solution)/shard_map/ppermute | solution.py:1156
  6.3 0.7 copy-start.5
  6.3 0.7 copy-start.6
  6.3 0.7 copy-start.9
  6.4 0.7 copy-start.10
  6.4 1.1 copy-start.7
  6.4 1.5 copy-start.8
  10.7 1.1 copy-start.2
  74.2 2.4 copy-start.1
  355.2 5.8 %copy-start.4 = (bf16[2,64,1088]{2,1,0:T(8,128)(2,1)S(1)}, bf16[2,64,1088]{2,1,0:T(8,128)(2,1)}, u32[]{:S(2)}) copy-start(bf16[2,64,1088]{2,1,0:T(8,128)(2,1)} %get-tuple-element.102) | copy-start | bytes 835588
  355.2 6.5 %copy-start.3 = (bf16[2,64,1088]{2,1,0:T(8,128)(2,1)S(1)}, bf16[2,64,1088]{2,1,0:T(8,128)(2,1)}, u32[]{:S(2)}) copy-start(bf16[2,64,1088]{2,1,0:T(8,128)(2,1)} %get-tuple-element.103) | copy-start | bytes 835588

commit v9 on v8

--- a/solution.py
+++ b/solution.py
@@ -173,7 +173,7 @@
 
 
 def attend_forward(e, x, w_hbm, wo_hbm, vecs, middle, normed, queries, kv, kv_other, logsum, attended,
-                   w, wo, acc, out_buf, in_buf, ls, gs, gr, ss, sr, ks, kr, arrived, weights=None):
+                   w, wo, acc, out_buf, in_buf, ls, gs, gr, ss, sr, ks, kr, arrived, weights=None, hooks=None):
     y, c = place()
     sibling = at_chip(y, 1 - c)
     if weights is None:
@@ -181,6 +181,8 @@
     slot(normed, y)[...] = norm(x[...].astype(F32), vecs[0:1], vecs[1:2]).astype(BF)
     arrived()
     gather_start(normed, y, c, gs, gr)
+    if hooks is not None:
+        hooks.begin(y, c)
     own, other = masks(c)
     weights[0].wait()
     gather_wait(normed, y, c, gs, gr)
@@ -212,6 +214,8 @@
     for at, size in chunks(D):
         acc[:, at : at + size] = dot(mixed, wo[:, at : at + size])
     scatter_start(acc, out_buf, in_buf, y, c, ss, sr)
+    if hooks is not None:
+        hooks.late()
     base = x[...].astype(F32) + vecs[4:5]
     middle[...] = base + scatter_wait(acc, out_buf, in_buf, y, c, ss, sr)
 
@@ -597,10 +601,48 @@
     return parts
 
 
-def attend_forward_first(*refs):
+def attend_forward_first(x, w_hbm, wo_hbm, vecs, part, *refs):
+    kept, (wu,), own, (hold, ls, zs, zr, cs, cr) = split(refs, 7, 1, 2 + len(MOVE) + 2, 6)
     y, c = place()
-    arrived = greet([at_chip(ring(y, k), c) for k in (1, 2, 3)] + [at_chip(y, 1 - c)])
-    attend_forward(0, refs[0].at[lax.axis_index("section"), 0], *refs[1:], arrived)
+    s, _, h, me = plane()
+    sibling = at_chip(y, 1 - c)
+    near, far = z_peers(s, h)[:2]
+    arrived = greet([at_chip(ring(y, k), c) for k in (1, 2, 3)] + [sibling, near, far])
+    bring = pltpu.make_async_copy(part, hold, ls.at[0])
+    bring.start()
+
+    def along_z(layer):
+        return [
+            remote(hold.at[0:2], wu.at[layer, 0:2, c], zs.at[0], zr.at[0], near),
+            remote(hold.at[2:4], wu.at[layer, 2:4, c], zs.at[1], zr.at[1], far),
+        ]
+
+    def across(layer, i, core):
+        rows = wu.at[layer, :, core]
+        return remote(hold if i == 0 else rows, rows, cs.at[i], cr.at[i], sibling)
+
+    keep = pltpu.make_async_copy(hold, wu.at[s, :, c], ls.at[1])
+
+    def begin(y, c):
+        bring.wait()
+        keep.start()
+        for copy in along_z(s):
+            copy.start()
+        across(s, 0, c).start()
+
+    def late():
+        for copy in along_z(1 - s):
+            copy.wait_recv()
+        across(1 - s, 1, c).start()
+
+    attend_forward(0, x.at[s, 0], w_hbm, wo_hbm, vecs, *kept, *own, arrived, hooks=Hooks(begin=[begin], late=[late]))
+    across(s, 0, 1 - c).wait_recv()
+    across(1 - s, 1, 1 - c).wait_recv()
+    for copy in along_z(s):
+        copy.wait_send()
+    across(s, 0, c).wait_send()
+    across(1 - s, 1, c).wait_send()
+    keep.wait()
 
 
 class Loaded:
@@ -703,13 +745,13 @@
 ]
 
 
-def call(body, name, number, outs, ins, scratch):
+def call(body, name, number, outs, ins, scratch, out_specs=None):
     return pl.pallas_call(
         body,
         name=name,
         out_shape=outs,
         in_specs=ins,
-        out_specs=[VMEM] * len(outs),
+        out_specs=out_specs or [VMEM] * len(outs),
         scratch_shapes=scratch,
         cost_estimate=COST,
         compiler_params=pltpu.CompilerParams(collective_id=number, has_side_effects=True, vmem_limit_bytes=LIMIT),
@@ -733,9 +775,12 @@
 FEED_MOVE = MOVE[:3] + MOVE[4:]
 
 
-def run_attend_forward(x, w, wo, vecs):
+def run_attend_forward(x, w, wo, vecs, part):
     scratch = ATTEND_WEIGHTS + MOVE + [DMA, DMA]
-    return call(attend_forward_first, "attend_forward_0", 0, ATTEND_KEPT, [VMEM, ANY, ANY, VMEM], scratch)(x, w, wo, vecs)
+    scratch += [pltpu.VMEM((4, 136, D), BF), DMA((2,)), DMA((2,)), DMA((2,)), DMA((2,)), DMA((2,))]
+    outs = ATTEND_KEPT + [shape((2, 4, 2, 136, D), BF)]
+    return call(attend_forward_first, "attend_forward_0", 0, outs, [VMEM, ANY, ANY, VMEM, ANY], scratch,
+                [VMEM] * 7 + [ANY])(x, w, wo, vecs, part)
 
 
 def run_forward_rest(middle, wu, wd, wa, wo, vecs, cotangent):
@@ -781,8 +826,8 @@
     pltpu.VMEM((15, 16, D), BF),
     DMA((3,)),
     DMA((3,)),
-    DMA((3, 3)),
-    DMA((3, 3)),
+    DMA((3, 4)),
+    DMA((3, 4)),
     DMA,
     DMA,
     DMA((3,)),
@@ -830,7 +875,7 @@
     keeps = load(
         [
             (hold_a, wa.at[s, y, c]),
-            (hold_u, wu.at[s, y, c]),
+            (hold_u, wu.at[y]),
             (hold_d, wd.at[s, c]),
             (hold_o, wo.at[s, c]),
             (hold_v, wv.at[s, y, c]),
@@ -845,7 +890,7 @@
         return [
             remote(send_v, wv.at[s, place_in, c], ysend.at[0, k - 1], yrecv.at[0, k - 1], at_chip(target, c)),
             remote(send_a.at[target], wa.at[s, place_in, c], ysend.at[1, k - 1], yrecv.at[1, k - 1], at_chip(target, c)),
-            remote(send_u.at[target], wu.at[s, place_in, c], ysend.at[2, k - 1], yrecv.at[2, k - 1], at_chip(target, c)),
+            remote(send_u.at[target], wu.at[place_in], ysend.at[2, k - 1], yrecv.at[2, k - 1], at_chip(target, c)),
         ]
 
     def along_z(layer):
@@ -854,10 +899,8 @@
             remote(wa.at[layer, 0:2, c], wa.at[layer, 0:2, c], zsend.at[1], zrecv.at[1], near),
             remote(wa.at[layer, 2:4, c], wa.at[layer, 2:4, c], zsend.at[2], zrecv.at[2], far),
             remote(wo.at[layer, c], wo.at[layer, c], zsend.at[3], zrecv.at[3], far),
-            remote(wu.at[layer, 0:2, c], wu.at[layer, 0:2, c], zsend.at[4], zrecv.at[4], near),
-            remote(wu.at[layer, 2:4, c], wu.at[layer, 2:4, c], zsend.at[5], zrecv.at[5], far),
-            remote(wd.at[layer, c, 0:272], wd.at[layer, c, 0:272], zsend.at[6], zrecv.at[6], near),
-            remote(wd.at[layer, c, 272:544], wd.at[layer, c, 272:544], zsend.at[7], zrecv.at[7], far),
+            remote(wd.at[layer, c, 0:272], wd.at[layer, c, 0:272], zsend.at[4], zrecv.at[4], near),
+            remote(wd.at[layer, c, 272:544], wd.at[layer, c, 272:544], zsend.at[5], zrecv.at[5], far),
         ]
 
     def across(layer, i, core):
@@ -865,8 +908,7 @@
             remote(wv.at[layer, :, core], wv.at[layer, :, core], csend.at[i, 0], crecv.at[i, 0], sibling),
             remote(wa.at[layer, :, core], wa.at[layer, :, core], csend.at[i, 1], crecv.at[i, 1], sibling),
             remote(wo.at[layer, core], wo.at[layer, core], csend.at[i, 2], crecv.at[i, 2], sibling),
-            remote(wu.at[layer, :, core], wu.at[layer, :, core], csend.at[i, 3], crecv.at[i, 3], sibling),
-            remote(wd.at[layer, core], wd.at[layer, core], csend.at[i, 4], crecv.at[i, 4], sibling),
+            remote(wd.at[layer, core], wd.at[layer, core], csend.at[i, 3], crecv.at[i, 3], sibling),
         ]
 
     sent_y = [along_y(k, False) for k in (1, 2, 3)]
@@ -881,9 +923,9 @@
     sent_z[3].start()
     sent_c[0][2].start()
     keeps[2].wait()
-    sent_z[6].start()
-    sent_z[7].start()
-    sent_c[0][4].start()
+    sent_z[4].start()
+    sent_z[5].start()
+    sent_c[0][3].start()
     for kind, keep, zs, cross in ((0, 4, (0,), 0), (1, 0, (1, 2), 1)):
         keeps[keep].wait()
         for k in range(3):
@@ -893,36 +935,30 @@
         sent_c[0][cross].start()
     for k in (1, 0, 2):
         sent_y[k][2].start()
-    for zs, cross in (((3,), 2), ((6, 7), 4), ((0,), 0), ((1, 2), 1)):
+    for zs, cross in (((3,), 2), ((4, 5), 3), ((0,), 0), ((1, 2), 1)):
         for z in zs:
             got_z[z].wait_recv()
         sent_c[1][cross].start()
     keeps[1].wait()
     for k in range(3):
         got_y[k][2].wait_recv()
-    for z in (4, 5):
-        sent_z[z].start()
-    sent_c[0][3].start()
-    for z in (4, 5):
-        got_z[z].wait_recv()
-    sent_c[1][3].start()
     for i in range(2):
-        for cross in range(5):
+        for cross in range(4):
             got_c[i][cross].wait_recv()
     for k in range(3):
         for kind in range(3):
             sent_y[k][kind].wait_send()
-    for z in range(8):
+    for z in range(6):
         sent_z[z].wait_send()
     for i in range(2):
-        for cross in range(5):
+        for cross in range(4):
             sent_c[i][cross].wait_send()
 
 
 def run_spread(a, u, d, o, v):
     outs = [
         shape((2, 4, 2, 136, TQKV), BF),
-        shape((2, 4, 2, 136, D), BF),
+        shape((4, 136, D), BF),
         shape((2, 2, 544, D), BF),
         shape((2, 2, 192, D), BF),
         shape((2, 4, 2, 16, D), BF),
@@ -939,7 +975,7 @@
             pltpu.VMEM((544, D), BF),
             pltpu.VMEM((192, D), BF),
             pltpu.VMEM((16, D), BF),
-            DMA((2, 5)), DMA((3, 3)), DMA((3, 3)), DMA((8,)), DMA((8,)), DMA((2, 5)), DMA((2, 5)),
+            DMA((2, 5)), DMA((3, 3)), DMA((3, 3)), DMA((6,)), DMA((6,)), DMA((2, 4)), DMA((2, 4)),
         ],
         compiler_params=pltpu.CompilerParams(collective_id=8, has_side_effects=True),
     )(a, u, d, o, v)
@@ -992,24 +1028,54 @@
         y, c = place()
         s, x, h, me = plane()
         targets = x_peers(x, h)
-        for k in ORDER:
-            yield k, remote(self.unit, self.out.at[block_of(x, y)], self.gs.at[k - 1], self.gr.at[k - 1], targets[k - 1])
+        for k in (1, 3):
+            yield remote(self.unit, self.out.at[block_of(x, y)], self.gs.at[k], self.gr.at[k], targets[k - 1])
+
+    def half(self, x, second):
+        y, c = place()
+        block = self.out.at[block_of(x, y)]
+        if self.unit.shape[0] == 2:
+            return block.at[1] if second else block.at[0]
+        return block.at[0, :, 512:] if second else block.at[0, :, 0:512]
+
+    def arrivals(self):
+        s, x, h, me = plane()
+        targets = x_peers(x, h)
+        y, c = place()
+        for k in (1, 3):
+            place_in = self.out.at[block_of(x - k + 4, y)]
+            yield remote(place_in, place_in, self.gs.at[k], self.gr.at[k], targets[k - 1])
+
+    def forwards(self):
+        s, x, h, me = plane()
+        targets = x_peers(x, h)
+        for i, k in enumerate((1, 3)):
+            part = self.half(x - k + 4, i)
+            yield remote(part, part, self.gs.at[2 * i], self.gr.at[2 * i], targets[k - 1])
 
     def spread(self):
         y, c = place()
         s, x, h, me = plane()
-        for k, copy in self.copies():
+        for copy in self.copies():
             copy.start()
         self.out[block_of(x, y)] = self.unit[...]
 
+    def forward(self):
+        for copy in self.arrivals():
+            copy.wait_recv()
+        for copy in self.forwards():
+            copy.start()
+
     def finish(self):
-        y, c = place()
         s, x, h, me = plane()
         targets = x_peers(x, h)
-        for k, copy in self.copies():
+        for copy in self.copies():
             copy.wait_send()
-            place_in = self.out.at[block_of(x - k + 4, y)]
-            remote(place_in, place_in, self.gs.at[k - 1], self.gr.at[k - 1], targets[k - 1]).wait_recv()
+        for copy in self.forwards():
+            copy.wait_send()
+        for i, k in enumerate((1, 3)):
+            part = self.half(x + 2, i)
+            remote(part, part, self.gs.at[2 * i], self.gr.at[2 * i], targets[k - 1]).wait_recv()
 
 
 def gather_pieces(feed, attend, first, last, one_0, heads_0,
@@ -1073,10 +1139,12 @@
     gathers[1].spread()
     for copy in plane_copies():
         copy.start()
+    gathers[0].forward()
     sum_along_z(2)
     gathers[2].start()
     for swap in swaps:
         swap.start()
+    gathers[1].forward()
     gathers[2].arrive()
     gathers[2].spread()
     total = small_x[s].astype(F32)
@@ -1086,6 +1154,7 @@
         remote(small_x.at[0], small_z.at[j], zs.at[j], zr.at[j], sibling).wait_recv()
         total = total + small_z[j].astype(F32)
     out_small[...] = total
+    gathers[2].forward()
     for i, swap in enumerate(swaps):
         swap.wait_send()
         place_in = (out_act, out_back)[i].at[1 - s]
@@ -1165,11 +1234,11 @@
     )
     wa, wu, wd, wo, wv = run_spread(send_a, send_u, weight_down[0], send_o, send_v)
     wa = wa.reshape(2, D, TQKV)
-    wu = wu.reshape(2, D, D)
     wd = wd.reshape(2, D, D)
     wo = jnp.concatenate([wo[:, 1, 136:184], wo[:, 0, :136], wo[:, 1, :136]], axis=1)
     vecs = jnp.sum(wv.astype(F32), axis=(1, 2))
-    middle_0, *kept_0 = run_attend_forward(inputs, wa, wo, vecs[0])
+    middle_0, *kept_0, wu = run_attend_forward(inputs, wa, wo, vecs[0], wu)
+    wu = wu.reshape(2, D, D)
     rest = run_forward_rest(middle_0, wu, wd, wa, wo, vecs, cotangent)
     (x_1, *kept_two_0), (middle_1, *kept_1), (result_1,), (grad_middle, up, down, two_1) = split(rest, 4, 7, 1, 4)
     acts = [x_1, result_1]

time: 368 us -> 344 us (0.935)
  the two profiles are of different devices: /device:TPU:1 before, /device:TPU:8 now
where the time goes in v9:
time: 344 us; the launch traced here: 338 us
  Pallas kernels  319 us (93%)
  local copies, waits for them, and re-layouts  10 us (3%)
  other arithmetic  6.27 us (2%)
    pallas_call x1, Pallas kernels, run_backward_end(): call(backward_end, 'backward_end', 6, outs, ins, scratch)  102 us
    pallas_call x1, Pallas kernels, run_forward_rest(): call(forward_rest, 'forward_rest', 2, outs, [VMEM] + [ANY] * 4 + [VMEM] *...  81.3 us
    pallas_call x1, Pallas kernels, run_backward_middle(): call(backward_middle, 'backward_middle', 5, outs, ins, scratch)  56.8 us
    pallas_call x1, Pallas kernels, run_spread(): pl.pallas_call(spread, name='spread', out_shape=outs, in_specs=[ANY] * 5,...  45.8 us
    pallas_call x1, Pallas kernels, run_attend_forward(): call(attend_forward_first, 'attend_forward_0', 0, outs, [VMEM, ANY, ANY,...  27.2 us
  transfers between devices with their start and end apart: 1, of which 0 were waited for; matrix products, arithmetic and copies ran while one was open for 2% of the time, Pallas kernels for 0%

profile of v9, /device:TPU:8, one launch (start us, length us, event | category | flops | bytes accessed | tf_op | source)
XLA Modules:
  0.0 338.0 jit_solution(17716779795739079722)
XLA Ops:
  0.6 0.0 copy-start
  0.7 1.0 slice_bitcast_fusion.7
  1.7 1.6 collective-permute-start
  3.3 1.1 fusion.1
  4.4 1.3 fusion
  5.8 0.0 copy-start.5
  5.8 0.0 copy-start.6
  5.8 0.0 copy-start.9
  5.8 0.0 copy-start.10
  5.8 0.0 copy-start.7
  5.8 0.0 copy-start.8
  5.9 0.0 copy-done
  5.9 0.3 slice_bitcast_fusion.5
  6.2 0.1 pad.8.clone
  6.2 0.2 copy-done.5
  6.4 0.0 copy-done.6
  6.5 0.0 copy-done.9
  6.5 0.0 copy-done.10
  6.5 0.3 dynamic_update_slice.9
  6.9 0.0 copy-done.7
  6.9 0.3 dynamic_update_slice.10
  7.2 0.4 dynamic_update_slice.11
  7.6 0.6 pad_maximum_fusion.3.send_v
  8.2 0.1 maximum_bitcast_fusion
  8.4 0.1 concatenate.22
  8.5 0.1 concatenate.24
  8.6 0.1 concatenate.23
  8.8 1.3 pad_maximum_fusion.1.send_u
  10.0 1.1 pad_maximum_fusion.2.send_a
  11.2 0.0 collective-permute-done
  11.2 0.0 copy-done.2
  11.2 1.8 maximum_maximum_fusion.send_o
  13.0 45.8 %spread.1 = (bf16[2,4,2,136,960]{4,3,2,1,0:T(8,128)(2,1)}, bf16[4,136,1088]{2,1,0:T(8,128)(2,1)}, bf16[2,2,544,1088]{3,2,1,0:T(8,128)(2,1)}, bf16[2,2,192,1088]{...) custom-call(bf16[4,136,960]{2,1,0:T(8,128)(2,1)} %pad_maximum_fusion.2.send_a, bf16[4,136,1088]{2,1,0:T(8,128)(2,1)} %pad_maximum_fusion.1.send_u, ...), custom_call_target="tpu_custom_call" | custom-call | tf_op jit(solution)/shard_map/spread/pallas_call | solution.py:966
  58.8 1.0 slice_bitcast_fusion.6
  59.8 1.4 slice_bitcast_fusion.1
  61.2 0.1 convert_reduce_fusion
  61.3 0.7 slice_bitcast_fusion.8
  62.0 1.2 pad_maximum_fusion.wo_hbm.refs_2_
  63.2 27.2 %attend_forward_0.1 = (f32[64,1088]{1,0:T(8,128)}, bf16[256,1088]{1,0:T(8,128)(2,1)}, bf16[256,320]{1,0:T(8,128)(2,1)}, bf16[256,640]{1,0:T(8,128)(2,1)}, bf16[2...) custom-call(bf16[2,1,64,1088]{3,2,1,0:T(8,128)(2,1)} %refs_4_.1, ...), custom_call_target="tpu_custom_call" | custom-call | flops 10000000 | bytes 10000 | tf_op jit(solution)/shard_map/attend_forward_0/pallas_call | solution.py:782
  90.4 81.3 %forward_rest.1 = (bf16[64,1088]{1,0:T(8,128)(2,1)}, bf16[256,1088]{1,0:T(8,128)(2,1)}, f32[256,1088]{1,0:T(8,128)}, bf16[256,1088]{1,0:T(8,128)(2,1)}, f32[64,1...) custom-call(f32[64,1088]{1,0:T(8,128)} %get-tuple-element.70.middle_, ...), custom_call_target="tpu_custom_call" | custom-call | flops 10000000 | bytes 10000 | tf_op jit(solution)/shard_map/forward_rest/pallas_call | solution.py:792
  171.7 56.8 %backward_middle.1 = (bf16[64,1088]{1,0:T(8,128)(2,1)}, f32[8,1088]{1,0:T(8,128)}, f32[8,960]{1,0:T(8,128)}, bf16[1,136,1088]{2,1,0:T(8,128)(2,1)}, bf16[1,136,1...) custom-call(f32[64,1088]{1,0:T(8,128)} %get-tuple-element.73.refs_0_, ...), custom_call_target="tpu_custom_call" | custom-call | flops 10000000 | bytes 10000 | tf_op jit(solution)/shard_map/backward_middle/pallas_call | solution.py:845
  228.5 102.0 %backward_end.1 = (bf16[64,1088]{1,0:T(8,128)(2,1)}, bf16[4,1,136,1088]{3,2,1,0:T(8,128)(2,1)}, bf16[4,1,136,1088]{3,2,1,0:T(8,128)(2,1)}, bf16[4,2,136,640]{3,2...) custom-call(f32[64,1088]{1,0:T(8,128)} %get-tuple-element.86.refs_0_, ...), custom_call_target="tpu_custom_call" | custom-call | flops 10000000 | bytes 10000 | tf_op jit(solution)/shard_map/backward_end/pallas_call | solution.py:857
  330.5 0.0 copy-start.4
  330.5 0.0 copy-start.3
  330.5 5.7 %assemble.1 = (f32[136,3264]{1,0:T(8,128)}, f32[136,1088]{1,0:T(8,128)}, f32[136,4352]{1,0:T(8,128)}, f32[544,1088]{1,0:T(8,128)}, f32[1,272]{1,0:T(1,128)}, /*i...) custom-call(bf16[4,1,136,1088]{3,2,1,0:T(8,128)(2,1)} %get-tuple-element.106.al, ...), custom_call_target="tpu_custom_call" | custom-call | tf_op jit(solution)/shard_map/assemble/pallas_call | solution.py:1196
  336.3 0.0 copy-done.4
  336.3 0.7 copy.38
  337.0 0.7 copy.39
  (12 shorter events, 0.1 us)
Async XLA Ops:
  0.6 5.2 %copy-start = (bf16[1,136,4352]{2,1,0:T(8,128)(2,1)S(1)}, bf16[1,136,4352]{2,1,0:T(8,128)(2,1)}, u32[]{:S(2)}) copy-start(bf16[1,136,4352]{2,1,0:T(8,128)(2,1)} %param.16) | copy-start | bytes 3551236
  1.7 9.5 %collective-permute-start = (bf16[48,1088]{1,0:T(8,128)(2,1)S(1)}, bf16[48,1088]{1,0:T(8,128)(2,1)}, u32[]{:S(2)}, u32[]{:S(2)}) collective-permute-start(bf16[48,1088]{1,0:T(8,128)(2,1)S(1)} %slice_bitcast_fusion.7), channel_id=1, source_target_pairs={{0,16},{8,24},{16,32},{24,40},{32,48},{40,56},{48,0},{56,8},{1,17}... | collective-permute-start | bytes 313352 | tf_op jit(solution)/shard_map/ppermute | solution.py:1225
  5.8 0.7 copy-start.5
  5.8 0.7 copy-start.6
  5.8 0.7 copy-start.9
  5.8 0.7 copy-start.10
  5.8 1.1 copy-start.7
  5.8 1.3 copy-start.8
  10.0 1.1 copy-start.2
  58.8 2.4 copy-start.1
  330.5 5.8 %copy-start.4 = (bf16[2,64,1088]{2,1,0:T(8,128)(2,1)S(1)}, bf16[2,64,1088]{2,1,0:T(8,128)(2,1)}, u32[]{:S(2)}) copy-start(bf16[2,64,1088]{2,1,0:T(8,128)(2,1)} %get-tuple-element.104) | copy-start | bytes 835588
  330.5 6.5 %copy-start.3 = (bf16[2,64,1088]{2,1,0:T(8,128)(2,1)S(1)}, bf16[2,64,1088]{2,1,0:T(8,128)(2,1)}, u32[]{:S(2)}) copy-start(bf16[2,64,1088]{2,1,0:T(8,128)(2,1)} %get-tuple-element.105) | copy-start | bytes 835588

commit v10 on v9

--- a/solution.py
+++ b/solution.py
@@ -273,6 +273,8 @@
         part = (dot_nt(rows, wd[at : at + size, :]) * slope).astype(BF)
         gh[:, at : at + size] = part
         small[2:3, at : at + size] = jnp.sum(part.astype(F32), axis=0, keepdims=True)
+    if reduce is not None:
+        reduce.relay(y, c)
     weights[0].wait()
     rows = gh[...]
     for at, size in chunks(D):
@@ -311,6 +313,7 @@
     reduce.middle(y, c)
     gather_wait(full, y, c, gs, gr)
     ga[...] = dot_nt(full[...], wo[...]).astype(BF)
+    reduce.relay(y, c)
     for h in range(SLOTS):
         at = h * HD
         q = queries[:, at : at + HD]
@@ -398,44 +401,75 @@
     return lax.rem(x - y + 8, 4)
 
 
+def halves(block, second):
+    cut = 512 if block.shape[-1] == D else 384
+    return block.at[:, :, cut:] if second else block.at[:, :, 0:cut]
+
+
 class AlongX:
-    def __init__(self, blocks, landing, out, send, recv):
-        self.blocks, self.landing, self.out, self.send, self.recv = blocks, landing, out, send, recv
-
-    def copies(self):
+    def __init__(self, blocks, landing, passing, out, send, recv):
+        self.blocks, self.landing, self.passing, self.out = blocks, landing, passing, out
+        self.send, self.recv = send, recv
+
+    def parts(self):
         y, c = place()
         s, x, h, me = plane()
         targets = x_peers(x, h)
-        for k in ORDER:
-            yield remote(
-                self.blocks.at[block_of(x + k, y)], self.landing.at[k - 1], self.send.at[k - 1], self.recv.at[k - 1],
-                targets[k - 1],
-            )
+        ahead, behind = targets[0], targets[2]
+        opposite = self.blocks.at[block_of(x + 2, y)]
+        to_ahead, to_behind = self.blocks.at[block_of(x + 1, y)], self.blocks.at[block_of(x + 3, y)]
+        moves = [
+            (halves(opposite, 0), halves(self.passing, 0), ahead),
+            (halves(opposite, 1), halves(self.passing, 1), behind),
+            (halves(to_ahead, 1), halves(self.landing.at[0], 1), ahead),
+            (halves(to_behind, 0), halves(self.landing.at[1], 0), behind),
+            (halves(to_ahead, 0), halves(self.landing.at[0], 0), ahead),
+            (halves(to_behind, 1), halves(self.landing.at[1], 1), behind),
+        ]
+        return [remote(source, to, self.send.at[i], self.recv.at[i], target) for i, (source, to, target) in enumerate(moves)]
 
     def start(self):
-        for copy in self.copies():
+        for copy in self.parts()[:4]:
             copy.start()
+
+    def relay(self):
+        y, c = place()
+        s, x, h, me = plane()
+        copies = self.parts()
+        for second, step in ((0, 1), (1, 3)):
+            copies[second].wait_recv()
+            block, passed = halves(self.blocks.at[block_of(x + step, y)], second), halves(self.passing, second)
+            block[...] = (block[...].astype(F32) + passed[...].astype(F32)).astype(BF)
+            copies[4 + second].start()
 
     def finish(self):
         y, c = place()
         s, x, h, me = plane()
         own = block_of(x, y)
-        for copy in self.copies():
-            copy.wait()
+        copies = self.parts()
+        for copy in copies:
+            copy.wait_send()
+        for copy in copies[2:]:
+            copy.wait_recv()
 
         def add(i, carry):
-            rows = pl.ds(pl.multiple_of(8 * (i % 17), 8), 8)
-            total = self.blocks[own, i // 17, rows].astype(F32)
-            for k in range(3):
-                total = total + self.landing[k, i // 17, rows].astype(F32)
-            self.out[i // 17, rows] = total.astype(BF)
+            rows = pl.ds(pl.multiple_of(8 * i, 8), 8)
+            total = self.blocks[own, 0, rows].astype(F32)
+            total = total + self.landing[0, 0, rows].astype(F32) + self.landing[1, 0, rows].astype(F32)
+            self.out[0, rows] = total.astype(BF)
             return carry
 
-        lax.fori_loop(0, 17 * self.out.shape[0], add, 0)
-
-
-def x_scratch(count, width):
-    return [pltpu.VMEM((4, count, 136, width), BF), pltpu.VMEM((3, count, 136, width), BF), DMA((3,)), DMA((3,))]
+        lax.fori_loop(0, 17, add, 0)
+
+
+def x_scratch(width):
+    return [
+        pltpu.VMEM((4, 1, 136, width), BF),
+        pltpu.VMEM((2, 1, 136, width), BF),
+        pltpu.VMEM((1, 136, width), BF),
+        DMA((6,)),
+        DMA((6,)),
+    ]
 
 
 class AlongZ:
@@ -484,8 +518,8 @@
     def __init__(self, up, down, out_up, out_down, other, ls, cs, cr, *scratch):
         self.sources = (up, down)
         self.other, self.ls, self.cs, self.cr = other, ls, cs, cr
-        self.up = AlongX(scratch[0], scratch[1], out_up, *scratch[2:4])
-        self.down = AlongX(scratch[4], scratch[5], out_down, *scratch[6:8])
+        self.up = AlongX(*scratch[0:3], out_up, *scratch[3:5])
+        self.down = AlongX(*scratch[5:8], out_down, *scratch[8:10])
 
     def copies(self, y, c):
         up, down = self.sources
@@ -514,17 +548,20 @@
             lax.fori_loop(0, 4, add, 0)
             unit.start()
 
-
-FEED_SCRATCH = [pltpu.VMEM((4, 2, 136, D), BF), DMA((2,)), DMA((2,)), DMA((2,))] + x_scratch(1, D) * 2
+    def relay(self, y, c):
+        self.up.relay()
+        self.down.relay()
+
+
+FEED_SCRATCH = [pltpu.VMEM((4, 2, 136, D), BF), DMA((2,)), DMA((2,)), DMA((2,))] + x_scratch(D) * 2
 
 
 class AttendReduce:
-    def __init__(self, wide, rows, out, other_w, other_r, cs, cr, *scratch):
+    def __init__(self, wide, rows, outs, other_w, other_r, cs, cr, *scratch):
         self.wide, self.rows = wide, rows
         self.other_w, self.other_r = other_w, other_r
         self.cs, self.cr = cs, cr
-        self.along = AlongX(scratch[0], scratch[1], out, scratch[2], scratch[3])
-        self.blocks = scratch[0]
+        self.units = [AlongX(*scratch[0:3], outs[0], *scratch[3:5]), AlongX(*scratch[5:8], outs[1], *scratch[8:10])]
 
     def swaps(self, y, c):
         sibling = at_chip(y, 1 - c)
@@ -540,21 +577,24 @@
     def middle(self, y, c):
         for copy in self.swaps(y, c):
             copy.wait()
-        blocks = self.blocks
+        first, second = (unit.blocks for unit in self.units)
         for i in range(4):
             block = self.wide[i, c].astype(F32) + self.other_w[i].astype(F32)
-            blocks[i, 0] = block[:, :640].astype(BF)
-            blocks[i, 1, :, :320] = block[:, 640:].astype(BF)
+            first[i, 0] = block[:, :640].astype(BF)
+            second[i, 0, :, :320] = block[:, 640:].astype(BF)
+        self.units[0].start()
+        for i in range(4):
             chunk = self.rows[c, :, 256 * i : 256 * i + 256].astype(F32) + self.other_r[:, 256 * i : 256 * i + 256].astype(F32)
-            blocks[i, 1, :, 320:576] = chunk.astype(BF)
+            second[i, 0, :, 320:576] = chunk.astype(BF)
             if i < 3:
-                blocks[i, 1, :, 576:] = jnp.zeros((136, HD), BF)
+                second[i, 0, :, 576:] = jnp.zeros((136, HD), BF)
         chunk = self.rows[c, :, 1024:].astype(F32) + self.other_r[:, 1024:].astype(F32)
-        blocks[3, 1, :, 576:] = chunk.astype(BF)
-        self.along.start()
-
-    def finish(self):
-        self.along.finish()
+        second[3, 0, :, 576:] = chunk.astype(BF)
+        self.units[1].start()
+
+    def relay(self, y, c):
+        for unit in self.units:
+            unit.relay()
 
 
 ATTEND_SCRATCH = [
@@ -562,15 +602,15 @@
     pltpu.VMEM((136, D), BF),
     DMA((2,)),
     DMA((2,)),
-] + x_scratch(2, 640)
+] + x_scratch(640) * 2
 
 
 BLOCKS = [pltpu.VMEM((4, 2, 136, TQKV), BF), pltpu.VMEM((2, 136, D), BF)]
 
 
 class Hooks:
-    def __init__(self, begin=(), middle=(), late=(), ready=()):
-        self.steps = begin, middle, late, ready
+    def __init__(self, begin=(), middle=(), late=(), ready=(), relay=()):
+        self.steps = begin, middle, late, ready, relay
 
     def begin(self, y, c):
         for step in self.steps[0]:
@@ -586,6 +626,10 @@
 
     def ready(self, y, c):
         for step in self.steps[3]:
+            step(y, c)
+
+    def relay(self, y, c):
+        for step in self.steps[4]:
             step(y, c)
 
     def finish(self):
@@ -679,7 +723,7 @@
 
 def backward_middle(*refs):
     a_in, updown, f_in, a_out, half_u, f_out, half_a, a_scr, u_scr, f_scr, grads, w_scr = split(
-        refs, 11, 2, 7, 3, 2, 4, 1, len(ATTEND_OWN), len(FEED_SCRATCH), len(FEED_OWN), 2, len(ATTEND_SCRATCH)
+        refs, 11, 2, 7, 3, 2, 4, 2, len(ATTEND_OWN), len(FEED_SCRATCH), len(FEED_OWN), 2, len(ATTEND_SCRATCH)
     )
     y, c = place()
     s, x, h, me = plane()
@@ -687,33 +731,34 @@
     wu_hbm, wd_hbm, vecs, *kept = f_in
     weights = load([(wu_hbm.at[0], f_scr[0]), (wd_hbm.at[0], f_scr[1])], f_scr[7])
     feed = FeedReduce(*updown, *half_u, *u_scr)
-    attend = AttendReduce(*grads, half_a[0], *w_scr)
+    attend = AttendReduce(*grads, half_a, *w_scr)
     grad_x, small, small_bias = a_out
     attend_back(1, *a_in, grad_x, *grads, small, small_bias, *a_scr, arrived,
-                Hooks(begin=[feed.begin], middle=[feed.middle], ready=[attend.begin]))
+                Hooks(begin=[feed.begin], middle=[feed.middle], relay=[feed.relay], ready=[attend.begin]))
     feed_back(0, grad_x, wu_hbm, wd_hbm, vecs, *kept, *f_out, *f_scr, lambda: None,
-              Hooks(middle=[attend.middle], late=[feed.up.finish, feed.down.finish]), weights)
-    attend.finish()
+              Hooks(middle=[attend.middle], relay=[attend.relay], late=[feed.up.finish, feed.down.finish]), weights)
+    for unit in attend.units:
+        unit.finish()
 
 
 def backward_end(*refs):
     a_in, updown, halves, rest, a_out, g_out, a_scr, u_scr, grads, w_scr, z_scr, own, g_scr = split(
-        refs, 11, 2, 3, 7, 1, 6, len(ATTEND_OWN), len(FEED_SCRATCH), 2, len(ATTEND_SCRATCH), 18, 11, len(GATHER_OWN)
+        refs, 11, 2, 4, 7, 1, 7, len(ATTEND_OWN), len(FEED_SCRATCH), 2, len(ATTEND_SCRATCH), 24, 14, len(GATHER_OWN)
     )
     y, c = place()
     s, x, h, me = plane()
     sibling = at_chip(y, 1 - c)
     peers = [at_chip(ring(y, k), c) for k in (1, 2, 3)]
     arrived = greet(peers + [sibling] + [at_plane(lax.rem(me + j, 16)) for j in range(1, 16)])
-    half_up, half_down, half_a, sum_up, sum_down, sum_a, late_up, late_down, late_a, small, small_bias = own
+    mine, sums, lates, (small, small_bias) = split(own, 4, 4, 4, 2)
     (grad_x,) = a_out
     a_in = [*a_in[:4], a_in[4].at[s, 0], *a_in[5:]]
-    feed = FeedReduce(*updown, half_up, half_down, *u_scr)
-    attend = AttendReduce(*grads, half_a, *w_scr)
-    first = [AlongZ(1, half, out, *z_scr[3 * i : 3 * i + 3]) for i, (half, out) in enumerate(zip(halves, (sum_up, sum_down, sum_a)))]
+    feed = FeedReduce(*updown, mine[0], mine[1], *u_scr)
+    attend = AttendReduce(*grads, mine[2:], *w_scr)
+    first = [AlongZ(1, half, out, *z_scr[3 * i : 3 * i + 3]) for i, (half, out) in enumerate(zip(halves, sums))]
     last = [
-        AlongZ(0, half, out, *z_scr[9 + 3 * i : 12 + 3 * i])
-        for i, (half, out) in enumerate(zip((half_up, half_down, half_a), (late_up, late_down, late_a)))
+        AlongZ(0, half, out, *z_scr[12 + 3 * i : 15 + 3 * i])
+        for i, (half, out) in enumerate(zip(mine, lates))
     ]
 
     def start_first(y, c):
@@ -725,7 +770,7 @@
         last[0].start()
 
     attend_back(0, *a_in, grad_x, *grads, small, small_bias, *a_scr, arrived,
-                Hooks(begin=[feed.begin, start_first], middle=[feed.middle], ready=[attend.begin, up_along_z]))
+                Hooks(begin=[feed.begin, start_first], middle=[feed.middle], relay=[feed.relay], ready=[attend.begin, up_along_z]))
     gather_pieces(feed, attend, first, last, small, small_bias, *rest, grad_x, *g_out, *g_scr)
 
 
@@ -758,7 +803,7 @@
     )
 
 
-HALF_A, HALF_U = shape((2, 136, 640), BF), shape((1, 136, D), BF)
+HALF_A, HALF_U = shape((1, 136, 640), BF), shape((1, 136, D), BF)
 FEED_OUTS = [shape((BLK, D), F32), shape((D, D), BF), shape((D, D), BF), shape((8, D), F32)]
 ATTEND_KEPT = [
     shape((BLK, D), F32),
@@ -818,16 +863,17 @@
     DMA((2,)),
     DMA((2,)),
     pltpu.VMEM((1, 136, D), BF),
-    pltpu.VMEM((2, 136, 640), BF),
+    pltpu.VMEM((1, 136, 640), BF),
+    pltpu.VMEM((1, 136, 640), BF),
     pltpu.VMEM((2, 16, D), F32),
     pltpu.VMEM((2, 16, D), F32),
     pltpu.VMEM((3, 2, 16, D), F32),
     pltpu.VMEM((2, 16, D), BF),
     pltpu.VMEM((15, 16, D), BF),
-    DMA((3,)),
-    DMA((3,)),
-    DMA((3, 4)),
-    DMA((3, 4)),
+    DMA((4,)),
+    DMA((4,)),
+    DMA((4, 4)),
+    DMA((4, 4)),
     DMA,
     DMA,
     DMA((3,)),
@@ -839,7 +885,7 @@
 
 
 def run_backward_middle(attend_args, up, down, feed_args):
-    outs = [shape((BLK, D), BF)] + SMALLS + [HALF_U, HALF_U] + FEED_OUTS + [HALF_A]
+    outs = [shape((BLK, D), BF)] + SMALLS + [HALF_U, HALF_U] + FEED_OUTS + [HALF_A, HALF_A]
     ins = [VMEM, ANY, ANY] + [VMEM] * 8 + [ANY] * 4 + [VMEM] * 5
     scratch = ATTEND_OWN + FEED_SCRATCH + FEED_OWN + BLOCKS + ATTEND_SCRATCH
     return call(backward_middle, "backward_middle", 5, outs, ins, scratch)(*attend_args, up, down, *feed_args)
@@ -847,11 +893,11 @@
 
 def run_backward_end(attend_args, up, down, halves, rest):
     both = shape((2, BLK, D), BF)
-    outs = [shape((BLK, D), BF), shape((4, 1, 136, D), BF), shape((4, 1, 136, D), BF), shape((4, 2, 136, 640), BF)]
+    outs = [shape((BLK, D), BF), shape((4, 1, 136, D), BF), shape((4, 1, 136, D), BF), shape((4, 1, 136, 640), BF)] + [shape((4, 1, 136, 640), BF)]
     outs += [shape((16, D), F32), both, both]
-    ins = [VMEM, ANY, ANY] + [VMEM] * 8 + [ANY] * 2 + [VMEM] * (3 + len(rest))
-    units = [pltpu.VMEM((1, 136, D), BF), pltpu.VMEM((1, 136, D), BF), pltpu.VMEM((2, 136, 640), BF)]
-    zs = (z_scratch(1, D) + z_scratch(1, D) + z_scratch(2, 640)) * 2
+    ins = [VMEM, ANY, ANY] + [VMEM] * 8 + [ANY] * 2 + [VMEM] * (4 + len(rest))
+    units = [pltpu.VMEM((1, 136, D), BF), pltpu.VMEM((1, 136, D), BF)] + [pltpu.VMEM((1, 136, 640), BF)] * 2
+    zs = (z_scratch(1, D) + z_scratch(1, D) + z_scratch(1, 640) * 2) * 2
     smalls = [pltpu.VMEM((8, D), F32), pltpu.VMEM((8, TQKV), F32)]
     scratch = ATTEND_OWN + FEED_SCRATCH + BLOCKS + ATTEND_SCRATCH + zs + units * 3 + smalls + GATHER_OWN
     return call(backward_end, "backward_end", 6, outs, ins, scratch)(*attend_args, up, down, *halves, *rest)
@@ -1018,11 +1064,12 @@
         @pl.when(self.elsewhere())
         def _():
             self.transpose().wait()
-            self.unit[0] = self.moved[0]
             if self.keep_from:
                 lane = lax.broadcasted_iota(jnp.int32, self.unit.shape[1:], 1)
-                merged = jnp.where(lane < self.keep_from, self.moved[1].astype(F32), self.unit[1].astype(F32))
-                self.unit[1] = merged.astype(BF)
+                merged = jnp.where(lane < self.keep_from, self.moved[0].astype(F32), self.unit[0].astype(F32))
+                self.unit[0] = merged.astype(BF)
+            else:
+                self.unit[0] = self.moved[0]
 
     def copies(self):
         y, c = place()
@@ -1033,10 +1080,7 @@
 
     def half(self, x, second):
         y, c = place()
-        block = self.out.at[block_of(x, y)]
-        if self.unit.shape[0] == 2:
-            return block.at[1] if second else block.at[0]
-        return block.at[0, :, 512:] if second else block.at[0, :, 0:512]
+        return halves(self.out.at[block_of(x, y)], second)
 
     def arrivals(self):
         s, x, h, me = plane()
@@ -1080,8 +1124,8 @@
 
 def gather_pieces(feed, attend, first, last, one_0, heads_0,
                   two_0, one_1, two_1, heads_1, act_0, act_1, back_1, back_0,
-                  out_up, out_down, out_a, out_small, out_act, out_back,
-                  swap_act, swap_back, ws, wr, moved_up, moved_a, small, small_c, small_y, small_x, small_z,
+                  out_up, out_down, out_a, out_b, out_small, out_act, out_back,
+                  swap_act, swap_back, ws, wr, moved_up, moved_a, moved_b, small, small_c, small_y, small_x, small_z,
                   ts, tr, gs, gr, cs, cr, ys, yr, zs, zr):
     y, c = place()
     s, x, h, me = plane()
@@ -1089,7 +1133,7 @@
     peers = [at_chip(ring(y, k), c) for k in (1, 2, 3)]
     gathers = [
         Gather(last[i].out, moved, keep, out, ts.at[i], tr.at[i], gs.at[i], gr.at[i])
-        for i, (moved, keep, out) in enumerate(((moved_up, 0, out_up), (None, 0, out_down), (moved_a, 320, out_a)))
+        for i, (moved, keep, out) in enumerate(((moved_up, 0, out_up), (None, 0, out_down), (moved_a, 0, out_a), (moved_b, 320, out_b)))
     ]
 
     def sum_along_z(i):
@@ -1103,6 +1147,7 @@
     attend.middle(y, c)
     feed.down.finish()
     last[1].start()
+    attend.relay(y, c)
     build_small(small.at[0], one_0, two_0, heads_0, y)
     build_small(small.at[1], one_1, two_1, heads_1, y)
     cross = remote(small, small_c, cs, cr, sibling)
@@ -1131,10 +1176,12 @@
             q = lax.rem(me + j, 16)
             yield remote(small_x.at[q // 8], small_z.at[15 - j], zs.at[j - 1], zr.at[15 - j], at_plane(q))
 
-    attend.finish()
+    attend.units[0].finish()
     last[2].start()
     gathers[0].arrive()
     gathers[0].spread()
+    attend.units[1].finish()
+    last[3].start()
     sum_along_z(1)
     gathers[1].spread()
     for copy in plane_copies():
@@ -1142,11 +1189,16 @@
     gathers[0].forward()
     sum_along_z(2)
     gathers[2].start()
+    gathers[1].forward()
     for swap in swaps:
         swap.start()
-    gathers[1].forward()
     gathers[2].arrive()
     gathers[2].spread()
+    sum_along_z(3)
+    gathers[3].start()
+    gathers[2].forward()
+    gathers[3].arrive()
+    gathers[3].spread()
     total = small_x[s].astype(F32)
     for copy in plane_copies():
         copy.wait_send()
@@ -1154,7 +1206,7 @@
         remote(small_x.at[0], small_z.at[j], zs.at[j], zr.at[j], sibling).wait_recv()
         total = total + small_z[j].astype(F32)
     out_small[...] = total
-    gathers[2].forward()
+    gathers[3].forward()
     for i, swap in enumerate(swaps):
         swap.wait_send()
         place_in = (out_act, out_back)[i].at[1 - s]
@@ -1163,13 +1215,13 @@
         gather.finish()
 
 
-def assemble(all_up, all_down, all_a, small, attn, out, up, down, b_attn, b_out, b_up, b_down, gain, shift):
+def assemble(all_up, all_down, all_a, all_b, small, attn, out, up, down, b_attn, b_out, b_up, b_down, gain, shift):
     y, c = place()
     f = 2 * y + c
     for j in range(CHIPS):
         up[:, j * D : (j + 1) * D] = all_up[j, 0].astype(F32)
         down[j * 136 : (j + 1) * 136] = all_down[j, 0].astype(F32)
-        first, second = all_a[j, 0].astype(F32), all_a[j, 1].astype(F32)
+        first, second = all_a[j, 0].astype(F32), all_b[j, 0].astype(F32)
         parts = ((0, second[:, :TH]), (D, first[:, :TH]), (2 * D, first[:, TH:]))
         for base, part in parts:
             attn[:, base + 256 * j : base + 256 * j + 256] = part[:, :256]
@@ -1197,7 +1249,7 @@
         assemble,
         name="assemble",
         out_shape=[shape(dims, F32) for dims in sizes],
-        in_specs=[VMEM] * 4,
+        in_specs=[VMEM] * 5,
         out_specs=[VMEM] * len(sizes),
         compiler_params=pltpu.CompilerParams(vmem_limit_bytes=LIMIT),
     )(*gathered)
@@ -1242,20 +1294,20 @@
     rest = run_forward_rest(middle_0, wu, wd, wa, wo, vecs, cotangent)
     (x_1, *kept_two_0), (middle_1, *kept_1), (result_1,), (grad_middle, up, down, two_1) = split(rest, 4, 7, 1, 4)
     acts = [x_1, result_1]
-    back_1, one_1, heads_1, half_up, half_down, grad_middle, up_0, down_0, two_0, half_a = run_backward_middle(
+    back_1, one_1, heads_1, half_up, half_down, grad_middle, up_0, down_0, two_0, *half_a = run_backward_middle(
         (grad_middle, wa, wo, vecs[1], x_1, *kept_1),
         up.reshape(4, 2, 136, D),
         down.reshape(2, 4, 136, D),
         (wu, wd, vecs[0], middle_0, *kept_two_0),
     )
-    back_0, all_up, all_down, all_a, small, all_acts, all_grads = run_backward_end(
+    back_0, all_up, all_down, all_a, all_b, small, all_acts, all_grads = run_backward_end(
         (grad_middle, wa, wo, vecs[0], inputs, *kept_0),
         up_0.reshape(4, 2, 136, D),
         down_0.reshape(2, 4, 136, D),
-        (half_up, half_down, half_a),
+        (half_up, half_down, *half_a),
         (two_0, one_1, two_1, heads_1, *acts, back_1),
     )
-    attn, out, up, down, b_attn, b_out, b_up, b_down, gain, shift = run_assemble(all_up, all_down, all_a, small)
+    attn, out, up, down, b_attn, b_out, b_up, b_down, gain, shift = run_assemble(all_up, all_down, all_a, all_b, small)
     return (
         all_acts[None, :, None],
         all_grads[None, :, None],

time: 344 us -> 359 us (1.044)
  the two profiles are of different devices: /device:TPU:8 before, /device:TPU:10 now
where the time goes in v10:
time: 359 us; the launch traced here: 354 us
  Pallas kernels  334 us (93%)
  local copies, waits for them, and re-layouts  10 us (3%)
  other arithmetic  6.27 us (2%)
    pallas_call x1, Pallas kernels, run_backward_end(): call(backward_end, 'backward_end', 6, outs, ins, scratch)  113 us
    pallas_call x1, Pallas kernels, run_forward_rest(): call(forward_rest, 'forward_rest', 2, outs, [VMEM] + [ANY] * 4 + [VMEM] *...  81.4 us
    pallas_call x1, Pallas kernels, run_backward_middle(): call(backward_middle, 'backward_middle', 5, outs, ins, scratch)  61 us
    pallas_call x1, Pallas kernels, run_spread(): pl.pallas_call(spread, name='spread', out_shape=outs, in_specs=[ANY] * 5,...  45.8 us
    pallas_call x1, Pallas kernels, run_attend_forward(): call(attend_forward_first, 'attend_forward_0', 0, outs, [VMEM, ANY, ANY,...  27.2 us
  transfers between devices with their start and end apart: 1, of which 0 were waited for; matrix products, arithmetic and copies ran while one was open for 2% of the time, Pallas kernels for 0%

profile of v10, /device:TPU:10, one launch (start us, length us, event | category | flops | bytes accessed | tf_op | source)
XLA Modules:
  0.0 353.8 jit_solution(976806007018114022)
XLA Ops:
  0.6 0.0 copy-start
  0.7 1.0 slice_bitcast_fusion.7
  1.7 1.6 collective-permute-start
  3.3 1.1 fusion.1
  4.4 1.3 fusion
  5.8 0.0 copy-start.5
  5.8 0.0 copy-start.6
  5.8 0.0 copy-start.9
  5.8 0.0 copy-start.10
  5.8 0.0 copy-start.7
  5.8 0.0 copy-start.8
  5.9 0.0 copy-done
  5.9 0.3 slice_bitcast_fusion.5
  6.2 0.1 pad.8.clone
  6.2 0.2 copy-done.5
  6.4 0.0 copy-done.6
  6.5 0.0 copy-done.9
  6.5 0.0 copy-done.10
  6.5 0.3 dynamic_update_slice.9
  6.9 0.0 copy-done.7
  6.9 0.3 dynamic_update_slice.10
  7.2 0.0 copy-done.8
  7.2 0.4 dynamic_update_slice.11
  7.6 0.6 pad_maximum_fusion.3.send_v
  8.2 0.1 maximum_bitcast_fusion
  8.4 0.1 concatenate.22
  8.5 0.1 concatenate.24
  8.6 0.1 concatenate.23
  8.8 1.3 pad_maximum_fusion.1.send_u
  10.0 1.1 pad_maximum_fusion.2.send_a
  11.2 0.0 collective-permute-done
  11.2 0.0 copy-done.2
  11.2 1.8 maximum_maximum_fusion.send_o
  13.0 45.8 %spread.1 = (bf16[2,4,2,136,960]{4,3,2,1,0:T(8,128)(2,1)}, bf16[4,136,1088]{2,1,0:T(8,128)(2,1)}, bf16[2,2,544,1088]{3,2,1,0:T(8,128)(2,1)}, bf16[2,2,192,1088]{...) custom-call(bf16[4,136,960]{2,1,0:T(8,128)(2,1)} %pad_maximum_fusion.2.send_a, bf16[4,136,1088]{2,1,0:T(8,128)(2,1)} %pad_maximum_fusion.1.send_u, ...), custom_call_target="tpu_custom_call" | custom-call | tf_op jit(solution)/shard_map/spread/pallas_call | solution.py:1012
  58.8 0.0 copy-start.1
  58.8 1.0 slice_bitcast_fusion.6
  59.8 1.4 slice_bitcast_fusion.1
  61.2 0.0 copy-done.1
  61.2 0.1 convert_reduce_fusion
  61.3 0.7 slice_bitcast_fusion.8
  62.0 1.2 pad_maximum_fusion.wo_hbm.refs_2_
  63.2 27.2 %attend_forward_0.1 = (f32[64,1088]{1,0:T(8,128)}, bf16[256,1088]{1,0:T(8,128)(2,1)}, bf16[256,320]{1,0:T(8,128)(2,1)}, bf16[256,640]{1,0:T(8,128)(2,1)}, bf16[2...) custom-call(bf16[2,1,64,1088]{3,2,1,0:T(8,128)(2,1)} %refs_4_.1, ...), custom_call_target="tpu_custom_call" | custom-call | flops 10000000 | bytes 10000 | tf_op jit(solution)/shard_map/attend_forward_0/pallas_call | solution.py:827
  90.4 81.4 %forward_rest.1 = (bf16[64,1088]{1,0:T(8,128)(2,1)}, bf16[256,1088]{1,0:T(8,128)(2,1)}, f32[256,1088]{1,0:T(8,128)}, bf16[256,1088]{1,0:T(8,128)(2,1)}, f32[64,1...) custom-call(f32[64,1088]{1,0:T(8,128)} %get-tuple-element.72.middle_, ...), custom_call_target="tpu_custom_call" | custom-call | flops 10000000 | bytes 10000 | tf_op jit(solution)/shard_map/forward_rest/pallas_call | solution.py:837
  171.8 61.0 %backward_middle.1 = (bf16[64,1088]{1,0:T(8,128)(2,1)}, f32[8,1088]{1,0:T(8,128)}, f32[8,960]{1,0:T(8,128)}, bf16[1,136,1088]{2,1,0:T(8,128)(2,1)}, bf16[1,136,1...) custom-call(f32[64,1088]{1,0:T(8,128)} %get-tuple-element.75.refs_0_, ...), custom_call_target="tpu_custom_call" | custom-call | flops 10000000 | bytes 10000 | tf_op jit(solution)/shard_map/backward_middle/pallas_call | solution.py:891
  232.8 113.3 %backward_end.1 = (bf16[64,1088]{1,0:T(8,128)(2,1)}, bf16[4,1,136,1088]{3,2,1,0:T(8,128)(2,1)}, bf16[4,1,136,1088]{3,2,1,0:T(8,128)(2,1)}, bf16[4,1,136,640]{3,2...) custom-call(f32[64,1088]{1,0:T(8,128)} %get-tuple-element.88.refs_0_, ...), custom_call_target="tpu_custom_call" | custom-call | flops 10000000 | bytes 10000 | tf_op jit(solution)/shard_map/backward_end/pallas_call | solution.py:903
  346.2 5.7 %assemble.1 = (f32[136,3264]{1,0:T(8,128)}, f32[136,1088]{1,0:T(8,128)}, f32[136,4352]{1,0:T(8,128)}, f32[544,1088]{1,0:T(8,128)}, f32[1,272]{1,0:T(1,128)}, /*i...) custom-call(bf16[4,1,136,1088]{3,2,1,0:T(8,128)(2,1)} %get-tuple-element.109.al, ...), custom_call_target="tpu_custom_call" | custom-call | tf_op jit(solution)/shard_map/assemble/pallas_call | solution.py:1248
  351.9 0.7 copy.38
  352.6 0.7 copy.39
  (12 shorter events, 0.1 us)
Async XLA Ops:
  0.6 5.2 %copy-start = (bf16[1,136,4352]{2,1,0:T(8,128)(2,1)S(1)}, bf16[1,136,4352]{2,1,0:T(8,128)(2,1)}, u32[]{:S(2)}) copy-start(bf16[1,136,4352]{2,1,0:T(8,128)(2,1)} %param.16) | copy-start | bytes 3551236
  1.7 9.5 %collective-permute-start = (bf16[48,1088]{1,0:T(8,128)(2,1)S(1)}, bf16[48,1088]{1,0:T(8,128)(2,1)}, u32[]{:S(2)}, u32[]{:S(2)}) collective-permute-start(bf16[48,1088]{1,0:T(8,128)(2,1)S(1)} %slice_bitcast_fusion.7), channel_id=1, source_target_pairs={{0,16},{8,24},{16,32},{24,40},{32,48},{40,56},{48,0},{56,8},{1,17}... | collective-permute-start | bytes 313352 | tf_op jit(solution)/shard_map/ppermute | solution.py:1277
  5.8 0.7 copy-start.5
  5.8 0.7 copy-start.6
  5.8 0.7 copy-start.9
  5.8 0.7 copy-start.10
  5.8 1.1 copy-start.7
  5.8 1.3 copy-start.8
  10.0 1.1 copy-start.2
  58.8 2.4 copy-start.1
  346.1 5.7 %copy-start.4 = (bf16[2,64,1088]{2,1,0:T(8,128)(2,1)S(1)}, bf16[2,64,1088]{2,1,0:T(8,128)(2,1)}, u32[]{:S(2)}) copy-start(bf16[2,64,1088]{2,1,0:T(8,128)(2,1)} %get-tuple-element.107) | copy-start | bytes 835588
  346.2 6.5 %copy-start.3 = (bf16[2,64,1088]{2,1,0:T(8,128)(2,1)S(1)}, bf16[2,64,1088]{2,1,0:T(8,128)(2,1)}, u32[]{:S(2)}) copy-start(bf16[2,64,1088]{2,1,0:T(8,128)(2,1)} %get-tuple-element.108) | copy-start | bytes 835588

commit v11 on v10

--- a/solution.py
+++ b/solution.py
@@ -273,14 +273,13 @@
         part = (dot_nt(rows, wd[at : at + size, :]) * slope).astype(BF)
         gh[:, at : at + size] = part
         small[2:3, at : at + size] = jnp.sum(part.astype(F32), axis=0, keepdims=True)
-    if reduce is not None:
-        reduce.relay(y, c)
     weights[0].wait()
     rows = gh[...]
     for at, size in chunks(D):
         acc[:, at : at + size] = dot_nt(rows, wu[at : at + size, :])
     scatter_start(acc, out_buf, in_buf, y, c, ss, sr)
     if reduce is not None:
+        reduce.relay(y, c)
         reduce.late()
     for at, size in chunks(D):
         grad_up[at : at + size, :] = dot_tn(normed[:, at : at + size], gh[...]).astype(BF)
@@ -313,7 +312,6 @@
     reduce.middle(y, c)
     gather_wait(full, y, c, gs, gr)
     ga[...] = dot_nt(full[...], wo[...]).astype(BF)
-    reduce.relay(y, c)
     for h in range(SLOTS):
         at = h * HD
         q = queries[:, at : at + HD]
@@ -339,6 +337,7 @@
         rows_out[:, at : at + size] = dot_tn(attended[...], full[:, at : at + size]).astype(BF)
     lend = remote(rows_out.at[0:HD], edge, es, er, at_chip(ring(y, 3), c))
     lend.start()
+    reduce.relay(y, c)
     weights[0].wait()
     swap.wait()
     gj[:, : 2 * TH] = (part_own[...] + part_in[...].astype(F32)).astype(BF)
@@ -903,7 +902,7 @@
     return call(backward_end, "backward_end", 6, outs, ins, scratch)(*attend_args, up, down, *halves, *rest)
 
 
-def spread(send_a, send_u, send_d, send_o, send_v, wa, wu, wd, wo, wv, hold_a, hold_u, hold_d, hold_o, hold_v, local, ysend, yrecv, zsend, zrecv, csend, crecv):
+def spread(send_a, send_u, send_d, send_o, send_v, send_t, wa, wu, wd, wo, wv, wt, hold_a, hold_u, hold_d, hold_o, hold_v, local, ysend, yrecv, zsend, zrecv, csend, crecv, tsend, trecv):
     s = lax.axis_index("section")
     y, c = place()
     replica = lax.axis_index("replica")
@@ -957,6 +956,13 @@
             remote(wd.at[layer, core], wd.at[layer, core], csend.at[i, 3], crecv.at[i, 3], sibling),
         ]
 
+    def tail_z(layer):
+        return remote(wt.at[layer, c], wt.at[layer, c], tsend.at[1], trecv.at[1], far)
+
+    def tail_c(layer, i, core):
+        return remote(wt.at[layer, core], wt.at[layer, core], tsend.at[2 + i], trecv.at[2 + i], sibling)
+
+    tail_y = remote(send_t, wt.at[s, c], tsend.at[0], trecv.at[0], peers[0])
     sent_y = [along_y(k, False) for k in (1, 2, 3)]
     got_y = [along_y(k, True) for k in (1, 2, 3)]
     sent_z, got_z = along_z(s), along_z(1 - s)
@@ -965,6 +971,7 @@
     for kind in (0, 1):
         for k in (1, 0, 2):
             sent_y[k][kind].start()
+    tail_y.start()
     keeps[3].wait()
     sent_z[3].start()
     sent_c[0][2].start()
@@ -981,16 +988,26 @@
         sent_c[0][cross].start()
     for k in (1, 0, 2):
         sent_y[k][2].start()
+    tail_y.wait()
+    tail_z(s).start()
+    tail_c(s, 0, c).start()
     for zs, cross in (((3,), 2), ((4, 5), 3), ((0,), 0), ((1, 2), 1)):
         for z in zs:
             got_z[z].wait_recv()
         sent_c[1][cross].start()
+    tail_z(1 - s).wait_recv()
+    tail_c(1 - s, 1, c).start()
     keeps[1].wait()
     for k in range(3):
         got_y[k][2].wait_recv()
     for i in range(2):
         for cross in range(4):
             got_c[i][cross].wait_recv()
+    tail_c(s, 0, 1 - c).wait_recv()
+    tail_c(1 - s, 1, 1 - c).wait_recv()
+    tail_z(s).wait_send()
+    tail_c(s, 0, c).wait_send()
+    tail_c(1 - s, 1, c).wait_send()
     for k in range(3):
         for kind in range(3):
             sent_y[k][kind].wait_send()
@@ -1001,30 +1018,31 @@
             sent_c[i][cross].wait_send()
 
 
-def run_spread(a, u, d, o, v):
+def run_spread(a, u, d, o, v, t):
     outs = [
         shape((2, 4, 2, 136, TQKV), BF),
         shape((4, 136, D), BF),
         shape((2, 2, 544, D), BF),
-        shape((2, 2, 192, D), BF),
+        shape((2, 2, 136, D), BF),
         shape((2, 4, 2, 16, D), BF),
+        shape((2, 2, 48, D), BF),
     ]
     return pl.pallas_call(
         spread,
         name="spread",
         out_shape=outs,
-        in_specs=[ANY] * 5,
-        out_specs=[ANY] * 5,
+        in_specs=[ANY] * 6,
+        out_specs=[ANY] * 6,
         scratch_shapes=[
             pltpu.VMEM((136, TQKV), BF),
             pltpu.VMEM((136, D), BF),
             pltpu.VMEM((544, D), BF),
-            pltpu.VMEM((192, D), BF),
+            pltpu.VMEM((136, D), BF),
             pltpu.VMEM((16, D), BF),
-            DMA((2, 5)), DMA((3, 3)), DMA((3, 3)), DMA((6,)), DMA((6,)), DMA((2, 4)), DMA((2, 4)),
+            DMA((2, 5)), DMA((3, 3)), DMA((3, 3)), DMA((6,)), DMA((6,)), DMA((2, 4)), DMA((2, 4)), DMA((4,)), DMA((4,)),
         ],
         compiler_params=pltpu.CompilerParams(collective_id=8, has_side_effects=True),
-    )(a, u, d, o, v)
+    )(a, u, d, o, v, t)
 
 
 def build_small(buf, one, two, heads, y):
@@ -1274,8 +1292,6 @@
         [jnp.concatenate([k_blocks[j], v_blocks[j], q_blocks[j]], axis=-1) for j in range(CHIPS)]
     )
     send_u = jnp.stack([weight_up[0][:, j * D : (j + 1) * D] for j in range(CHIPS)])
-    tail = lax.ppermute(weight_out[0, 88:], "fsdp", [(i, (i + 2) % 8) for i in range(8)])
-    send_o = jnp.concatenate([weight_out[0], tail, jnp.zeros((8, D), BF)], axis=0)
     vectors = jnp.stack([norm_gain[0, 0], norm_bias[0, 0], norm_gain[0, 1], norm_bias[0, 1], bias_out[0], bias_down[0]])
     send_v = jnp.concatenate(
         [
@@ -1284,10 +1300,12 @@
             lax.dynamic_update_slice(jnp.zeros((6, D), BF), bias_attn, (f // 4, 272 * (f % 4))),
         ]
     )
-    wa, wu, wd, wo, wv = run_spread(send_a, send_u, weight_down[0], send_o, send_v)
+    wa, wu, wd, wo, wv, wt = run_spread(
+        send_a, send_u, weight_down[0], weight_out[0], send_v, weight_out[0, 88:]
+    )
     wa = wa.reshape(2, D, TQKV)
     wd = wd.reshape(2, D, D)
-    wo = jnp.concatenate([wo[:, 1, 136:184], wo[:, 0, :136], wo[:, 1, :136]], axis=1)
+    wo = jnp.concatenate([wt[:, 1], wo[:, 0], wo[:, 1]], axis=1)
     vecs = jnp.sum(wv.astype(F32), axis=(1, 2))
     middle_0, *kept_0, wu = run_attend_forward(inputs, wa, wo, vecs[0], wu)
     wu = wu.reshape(2, D, D)

time: 359 us -> 345 us (0.961)
  the two profiles are of different devices: /device:TPU:10 before, /device:TPU:8 now
where the time goes in v11:
time: 345 us; the launch traced here: 340 us
  Pallas kernels  322 us (93%)
  local copies, waits for them, and re-layouts  10.9 us (3%)
  other arithmetic  5.65 us (2%)
    pallas_call x1, Pallas kernels, run_backward_end(): call(backward_end, 'backward_end', 6, outs, ins, scratch)  108 us
    pallas_call x1, Pallas kernels, run_forward_rest(): call(forward_rest, 'forward_rest', 2, outs, [VMEM] + [ANY] * 4 + [VMEM] *...  81.8 us
    pallas_call x1, Pallas kernels, run_backward_middle(): call(backward_middle, 'backward_middle', 5, outs, ins, scratch)  54.4 us
    pallas_call x1, Pallas kernels, run_spread(): pl.pallas_call(spread, name='spread', out_shape=outs, in_specs=[ANY] * 6,...  44.4 us
    pallas_call x1, Pallas kernels, run_attend_forward(): call(attend_forward_first, 'attend_forward_0', 0, outs, [VMEM, ANY, ANY,...  27.5 us

profile of v11, /device:TPU:8, one launch (start us, length us, event | category | flops | bytes accessed | tf_op | source)
XLA Modules:
  0.0 339.6 jit_solution(14836474503652680355)
XLA Ops:
  0.6 0.0 copy-start.2
  0.7 0.8 slice_bitcast_fusion.10
  1.5 0.7 stack.43
  2.2 0.9 dynamic_update_slice.10
  3.1 1.0 dynamic_update_slice.11
  4.2 0.3 dynamic_update_slice.9
  4.5 0.6 pad_maximum_fusion.3.send_v
  5.1 1.5 slice_bitcast_fusion.7.send_t
  6.7 1.1 fusion.1
  7.8 0.1 maximum_bitcast_fusion
  7.9 0.0 copy-done.2
  7.9 0.1 fusion
  8.1 0.1 concatenate.19
  8.2 0.1 concatenate.21
  8.3 0.1 concatenate.20
  8.5 0.0 copy-start
  8.5 1.1 pad_maximum_fusion.2.send_a
  9.6 0.5 copy-done
  10.1 0.3 slice_bitcast_fusion.5
  10.4 1.3 pad_maximum_fusion.1.send_u
  11.7 44.4 %spread.1 = (bf16[2,4,2,136,960]{4,3,2,1,0:T(8,128)(2,1)}, bf16[4,136,1088]{2,1,0:T(8,128)(2,1)}, bf16[2,2,544,1088]{3,2,1,0:T(8,128)(2,1)}, bf16[2,2,136,1088]{...) custom-call(bf16[4,136,960]{2,1,0:T(8,128)(2,1)} %pad_maximum_fusion.2.send_a, ...), custom_call_target="tpu_custom_call" | custom-call | tf_op jit(solution)/shard_map/spread/pallas_call | solution.py:1030
  56.1 0.0 copy-start.1
  56.1 1.3 convert_reduce_fusion
  57.3 0.7 slice_bitcast_fusion.8
  58.0 1.0 slice_bitcast_fusion.6
  59.0 0.0 copy-done.1
  59.0 0.1 slice_bitcast_fusion.1
  59.1 1.2 pad_maximum_fusion.wo_hbm.refs_2_
  60.3 27.5 %attend_forward_0.1 = (f32[64,1088]{1,0:T(8,128)}, bf16[256,1088]{1,0:T(8,128)(2,1)}, bf16[256,320]{1,0:T(8,128)(2,1)}, bf16[256,640]{1,0:T(8,128)(2,1)}, bf16[2...) custom-call(bf16[2,1,64,1088]{3,2,1,0:T(8,128)(2,1)} %refs_4_.1, ...), custom_call_target="tpu_custom_call" | custom-call | flops 10000000 | bytes 10000 | tf_op jit(solution)/shard_map/attend_forward_0/pallas_call | solution.py:826
  87.8 81.8 %forward_rest.1 = (bf16[64,1088]{1,0:T(8,128)(2,1)}, bf16[256,1088]{1,0:T(8,128)(2,1)}, f32[256,1088]{1,0:T(8,128)}, bf16[256,1088]{1,0:T(8,128)(2,1)}, f32[64,1...) custom-call(f32[64,1088]{1,0:T(8,128)} %get-tuple-element.74.middle_, ...), custom_call_target="tpu_custom_call" | custom-call | flops 10000000 | bytes 10000 | tf_op jit(solution)/shard_map/forward_rest/pallas_call | solution.py:836
  169.7 54.4 %backward_middle.1 = (bf16[64,1088]{1,0:T(8,128)(2,1)}, f32[8,1088]{1,0:T(8,128)}, f32[8,960]{1,0:T(8,128)}, bf16[1,136,1088]{2,1,0:T(8,128)(2,1)}, bf16[1,136,1...) custom-call(f32[64,1088]{1,0:T(8,128)} %get-tuple-element.77.refs_0_, ...), custom_call_target="tpu_custom_call" | custom-call | flops 10000000 | bytes 10000 | tf_op jit(solution)/shard_map/backward_middle/pallas_call | solution.py:890
  224.1 108.1 %backward_end.1 = (bf16[64,1088]{1,0:T(8,128)(2,1)}, bf16[4,1,136,1088]{3,2,1,0:T(8,128)(2,1)}, bf16[4,1,136,1088]{3,2,1,0:T(8,128)(2,1)}, bf16[4,1,136,640]{3,2...) custom-call(f32[64,1088]{1,0:T(8,128)} %get-tuple-element.90.refs_0_, ...), custom_call_target="tpu_custom_call" | custom-call | flops 10000000 | bytes 10000 | tf_op jit(solution)/shard_map/backward_end/pallas_call | solution.py:902
  332.2 0.0 copy-start.4
  332.2 0.0 copy-start.3
  332.2 5.7 %assemble.1 = (f32[136,3264]{1,0:T(8,128)}, f32[136,1088]{1,0:T(8,128)}, f32[136,4352]{1,0:T(8,128)}, f32[544,1088]{1,0:T(8,128)}, f32[1,272]{1,0:T(1,128)}, /*i...) custom-call(bf16[4,1,136,1088]{3,2,1,0:T(8,128)(2,1)} %get-tuple-element.111.al, ...), custom_call_target="tpu_custom_call" | custom-call | tf_op jit(solution)/shard_map/assemble/pallas_call | solution.py:1266
  337.9 0.0 copy-done.4
  337.9 0.7 copy.38
  338.7 0.0 copy-done.3
  338.7 0.7 copy.39
  (4 shorter events, 0.0 us)
Async XLA Ops:
  0.6 7.3 %copy-start.2 = (bf16[1,136,3264]{2,1,0:T(8,128)(2,1)S(1)}, bf16[1,136,3264]{2,1,0:T(8,128)(2,1)}, u32[]{:S(2)}) copy-start(bf16[1,136,3264]{2,1,0:T(8,128)(2,1)} %param.14) | copy-start | bytes 2663428
  8.5 1.7 copy-start
  56.1 2.9 copy-start.1
  332.2 5.7 %copy-start.4 = (bf16[2,64,1088]{2,1,0:T(8,128)(2,1)S(1)}, bf16[2,64,1088]{2,1,0:T(8,128)(2,1)}, u32[]{:S(2)}) copy-start(bf16[2,64,1088]{2,1,0:T(8,128)(2,1)} %get-tuple-element.109) | copy-start | bytes 835588
  332.2 6.5 %copy-start.3 = (bf16[2,64,1088]{2,1,0:T(8,128)(2,1)S(1)}, bf16[2,64,1088]{2,1,0:T(8,128)(2,1)}, u32[]{:S(2)}) copy-start(bf16[2,64,1088]{2,1,0:T(8,128)(2,1)} %get-tuple-element.110) | copy-start | bytes 835588
